TPU v7x, 256 devices: a whole 4x4x8 slice. The times are simulated.
256 devices in a mesh: subj: 8 (over y, core), slab: 32 (over z, x).
Axes of the slice: x: 4, y: 4, z: 8, core: 2. Of those that a mesh axis runs over, the one named last changes fastest.
Arguments:
- template: float32 [64, 256, 512], P('slab'), may hold values from -6 to 6
- images: float32 [8, 64, 256, 512], P('subj', 'slab'), may hold values from -6 to 6
- fractions: bfloat16 [8, 3, 64, 256, 512], P('subj', None, 'slab'), may hold values from 0 to 1
- requests: int32 [8, 32, 9, 128], P('subj', 'slab'), may hold values from 0 to 511, as said below
- corners: int32 [8, 4, 64, 256], P('subj', None, 'slab'), may hold values from 0 to 1151, as said below
Outputs:
- new_template: float32 [64, 256, 512], P('slab')
- image_force: float32 [8, 3, 64, 256, 512], P('subj', None, 'slab')
Inputs may be any that keep to these rules, and one draw needn't show every extreme that they name: requests[s, d, j, c] is a line of source slab device d + j - 4, numbered plane * 256 + row within its 2 planes; the 128 lines of one list are distinct; lists whose source lies outside the grid are never used. corners[s, k, z, x] is a slot j * 128 + c with d + j - 4 a slab device of the grid, d = z // 2; for each subject every such slot of a destination device is named by at least one corner.
All inputs are finite; a program needn't handle non-finite values.
Results may differ from a plain program's by a relative error of at most 0.0003.
Values sent between devices are 32-bit elements; how exact they have to be, the bound alone decides.
No kernel may reach another device: no remote copies, remote signals or barrier semaphores. Data moves between devices by JAX's collectives and lax.ppermute only.
A program may use at most 64 MiB of HBM per device.

v0:
```python
import jax
import jax.numpy as jnp
from jax import lax
from jax.sharding import PartitionSpec as P

SMOOTH = 2
REACH = 4


diffusion = 0.15


def from_behind(block, axis, distance):
    devices = range(lax.axis_size(axis))
    route = [(i - distance, i) for i in devices if i - distance in devices]
    return lax.ppermute(block, axis, route)


def padded_2(cells, sides, width):
    for axis, dim in sides:
        count = lax.axis_size(axis)
        ends = count - 1
        head = lax.slice_in_dim(cells, 0, width, axis=dim)
        tail = lax.slice_in_dim(cells, cells.shape[dim] - width, cells.shape[dim], axis=dim)
        cells = jnp.concatenate(
            [
                lax.ppermute(tail, axis, [(i, (i + 1) % count) for i in range(ends)]),
                cells,
                lax.ppermute(head, axis, [((i + 1) % count, i) for i in range(ends)]),
            ],
            axis=dim,
        )
    return cells


def corner_weights(fraction):
    depth_part = fraction[:, 0]
    row_part = fraction[:, 1]
    return jnp.stack(
        [
            (1.0 - depth_part) * (1.0 - row_part),
            (1.0 - depth_part) * row_part,
            depth_part * (1.0 - row_part),
            depth_part * row_part,
        ],
        axis=1,
    )


def relax_once(padded):
    extended = jnp.pad(padded, ((0, 0), (0, 0), (1, 1)))
    centre = extended[1:-1, 1:-1, 1:-1]
    beside = extended[2:, 1:-1, 1:-1] + extended[:-2, 1:-1, 1:-1]
    beside = beside + extended[1:-1, 2:, 1:-1] + extended[1:-1, :-2, 1:-1]
    beside = beside + extended[1:-1, 1:-1, 2:] + extended[1:-1, 1:-1, :-2]
    return centre + diffusion * (beside - 6.0 * centre)


def on_device(template, images, fractions, requests, corners):
    subj_local, plane_count, row_count, cell_count = images.shape
    line_count = plane_count * row_count
    band_count = requests.shape[2]
    capacity = requests.shape[3]
    flat_template = template.reshape(line_count, cell_count)
    fraction = fractions.astype(jnp.float32).reshape(subj_local, 3, line_count, cell_count)
    across = fraction[:, 2][:, None]
    weights = corner_weights(fraction)
    slot_ids = corners.reshape(subj_local, 4, line_count)
    asked_lines = requests[:, 0]
    sources = []
    wanted_all = []
    for band_pos in range(band_count):
        offset = band_pos - REACH
        if offset == 0:
            wanted_part = asked_lines[:, band_pos]
            sources.append(jnp.take(flat_template, wanted_part, axis=0))
        else:
            wanted_part = from_behind(asked_lines[:, band_pos], "slab", offset)
            outgoing = jnp.take(flat_template, wanted_part, axis=0)
            sources.append(from_behind(outgoing, "slab", -offset))
        wanted_all.append(wanted_part)
    buffer = jnp.stack(sources, axis=1).reshape(subj_local, band_count * capacity, cell_count)
    corner_lines = jax.vmap(lambda held_lines, chosen: jnp.take(held_lines, chosen, axis=0))(
        buffer, slot_ids
    )
    shifted = jnp.concatenate(
        [corner_lines[..., 1:], jnp.zeros_like(corner_lines[..., :1])], axis=-1
    )
    warped = jnp.sum(weights * ((1.0 - across) * corner_lines + across * shifted), axis=1)
    mismatch = warped - images.reshape(subj_local, line_count, cell_count)
    volume = warped.reshape(subj_local, plane_count, row_count, cell_count)
    rimmed = padded_2(volume, (("slab", 1),), 1)
    depth_diff = 0.5 * (rimmed[:, 2:] - rimmed[:, :-2])
    row_pad = jnp.pad(volume, ((0, 0), (0, 0), (1, 1), (0, 0)))
    row_diff = 0.5 * (row_pad[:, :, 2:] - row_pad[:, :, :-2])
    cell_pad = jnp.pad(volume, ((0, 0), (0, 0), (0, 0), (1, 1)))
    cell_diff = 0.5 * (cell_pad[..., 2:] - cell_pad[..., :-2])
    negative = -mismatch.reshape(volume.shape)
    image_force = jnp.stack(
        [negative * depth_diff, negative * row_diff, negative * cell_diff], axis=1
    )
    scaled = weights * mismatch[:, None]
    pushed = (1.0 - across) * scaled + jnp.concatenate(
        [jnp.zeros_like(scaled[..., :1]), (across * scaled)[..., :-1]], axis=-1
    )
    flat_pushed = pushed.reshape(subj_local, 4 * line_count, cell_count)
    pooled = jax.vmap(
        lambda values, chosen: jax.ops.segment_sum(
            values, chosen, num_segments=band_count * capacity
        )
    )(flat_pushed, slot_ids.reshape(subj_local, 4 * line_count))
    pooled = pooled.reshape(subj_local, band_count, capacity, cell_count)
    received = []
    for band_pos in range(band_count):
        offset = band_pos - REACH
        block_grad = pooled[:, band_pos]
        if offset != 0:
            block_grad = from_behind(block_grad, "slab", offset)
        received.append(block_grad)
    returned = jnp.stack(received, axis=1)
    wanted = jnp.stack(wanted_all, axis=1)
    local_grad = jax.ops.segment_sum(
        returned.reshape(-1, cell_count), wanted.reshape(-1), num_segments=line_count
    )
    subject_total = subj_local * lax.axis_size("subj")
    grid_grad = local_grad.reshape(plane_count, row_count, cell_count)
    smoothed = lax.psum(grid_grad, "subj")
    for repeat in range(SMOOTH):
        rimmed_grad = padded_2(smoothed, (("slab", 0),), 1)
        smoothed = relax_once(jnp.pad(rimmed_grad, ((0, 0), (1, 1), (0, 0))))
    new_template = template - smoothed / subject_total
    return (new_template, image_force)


def solution(mesh):
    return jax.shard_map(
        on_device,
        mesh=mesh,
        in_specs=(
            P("slab", None, None),
            P("subj", "slab", None, None),
            P("subj", None, "slab", None, None),
            P("subj", "slab", None, None),
            P("subj", None, "slab", None),
        ),
        out_specs=(P("slab", None, None), P("subj", None, "slab", None, None)),
        check_vma=False,
    )
```

profile of v0, /device:TPU:152, one launch (start us, length us, event | category | flops | bytes accessed | tf_op | source)
XLA Modules:
  0.0 335.4 jit_solution(7846086620897287123)
XLA Ops:
  7.9 2.0 collective-permute-start
  9.9 2.9 collective-permute-start.1
  12.9 4.2 %collective-permute-start.2 = (s32[1,128]{1,0:T(1,128)S(1)}, s32[1,128]{1,0:T(1,128)S(1)}, u32[]{:S(2)}, u32[]{:S(2)}) collective-permute-start(s32[1,128]{1,0:T(1,128)S(1)} %get-tuple-element.33), channel_id=1, source_target_pairs={{2,0},{3,1},{4,2},{5,3},{6,4},{7,5},{8,6},{9,7},{10,8},{11,9},{12,... | collective-permute-start | bytes 1544 | tf_op jit(solution)/shard_map/ppermute | solution.py:16
  17.1 3.3 collective-permute-start.3
  25.8 2.9 subtract_bitcast_fusion
  30.5 2.5 collective-permute-start.4
  33.0 3.2 collective-permute-start.5
  37.9 4.9 %collective-permute-start.9 = (f32[1,128,512]{2,1,0:T(8,128)}, f32[1,128,512]{2,1,0:T(8,128)}, u32[]{:S(2)}, u32[]{:S(2)}) collective-permute-start(f32[1,128,512]{2,1,0:T(8,128)} %bitcast_select_fusion.7), channel_id=1, source_target_pairs={{0,3},{1,4},{2,5},{3,6},{4,7},{5,8},{6,9},{7,10},{8,11},{9,12},{10... | collective-permute-start | bytes 786440 | tf_op jit(solution)/shard_map/ppermute | solution.py:16
  43.7 3.8 %collective-permute-start.8 = (f32[1,128,512]{2,1,0:T(8,128)S(1)}, f32[1,128,512]{2,1,0:T(8,128)S(1)}, u32[]{:S(2)}, u32[]{:S(2)}) collective-permute-start(f32[1,128,512]{2,1,0:T(8,128)S(1)} %bitcast_select_fusion.8), channel_id=1, source_target_pairs={{0,4},{1,5},{2,6},{3,7},{4,8},{5,9},{6,10},{7,11},{8,12},{9,13},{1... | collective-permute-start | bytes 786440 | tf_op jit(solution)/shard_map/ppermute | solution.py:16
  49.1 5.8 %collective-permute-start.10 = (f32[1,128,512]{2,1,0:T(8,128)}, f32[1,128,512]{2,1,0:T(8,128)}, u32[]{:S(2)}, u32[]{:S(2)}) collective-permute-start(f32[1,128,512]{2,1,0:T(8,128)} %bitcast_select_fusion.6), channel_id=1, source_target_pairs={{0,2},{1,3},{2,4},{3,5},{4,6},{5,7},{6,8},{7,9},{8,10},{9,11},{10,... | collective-permute-start | bytes 786440 | tf_op jit(solution)/shard_map/ppermute | solution.py:16
  56.5 1.9 collective-permute-start.11
  58.5 4.6 %collective-permute-start.6 = (s32[1,128]{1,0:T(1,128)S(1)}, s32[1,128]{1,0:T(1,128)S(1)}, u32[]{:S(2)}, u32[]{:S(2)}) collective-permute-start(s32[1,128]{1,0:T(1,128)S(1)} %get-tuple-element.28), channel_id=1, source_target_pairs={{0,3},{1,4},{2,5},{3,6},{4,7},{5,8},{6,9},{7,10},{8,11},{9,12},{10... | collective-permute-start | bytes 1544 | tf_op jit(solution)/shard_map/ppermute | solution.py:16
  66.0 1.9 collective-permute-start.7
  68.7 3.9 %collective-permute-done.7 = s32[1,128]{1,0:T(1,128)S(1)} collective-permute-done((s32[1,128]{1,0:T(1,128)S(1)}, s32[1,128]{1,0:T(1,128)S(1)}, u32[]{:S(2)}, u32[]{:S(2)}) %collective-permute-start.7) | collective-permute-done | bytes 544 | tf_op jit(solution)/shard_map/ppermute | solution.py:16
  72.7 5.1 %collective-permute-start.12 = (f32[1,128,512]{2,1,0:T(8,128)}, f32[1,128,512]{2,1,0:T(8,128)}, u32[]{:S(2)}, u32[]{:S(2)}) collective-permute-start(f32[1,128,512]{2,1,0:T(8,128)} %bitcast_select_fusion.3), channel_id=1, source_target_pairs={{1,0},{2,1},{3,2},{4,3},{5,4},{6,5},{7,6},{8,7},{9,8},{10,9},{11,1... | collective-permute-start | bytes 786440 | tf_op jit(solution)/shard_map/ppermute | solution.py:16
  81.7 2.4 collective-permute-start.13
  85.2 1.9 collective-permute-start.14
  88.1 2.1 collective-permute-start.15
  93.7 2.6 collective-permute-done.14
  96.3 3.4 %collective-permute-done.15 = f32[1,128,512]{2,1,0:T(8,128)S(1)} collective-permute-done((f32[1,128,512]{2,1,0:T(8,128)S(1)}, f32[1,128,512]{2,1,0:T(8,128)S(1)}, u32[]{:S(2)}, u32[]{:S(2)}) %collective-permute-start.15) | collective-permute-done | bytes 262176 | tf_op jit(solution)/shard_map/ppermute | solution.py:16
  99.7 20.5 %gather_fusion = f32[2048,512]{1,0:T(8,128)} fusion(f32[1,1152,512]{2,1,0:T(8,128)S(1)} %bitcast.196, s32[2048]{0:T(1024)S(1)} %bitcast.206), kind=kCustom, calls=%fused_computation.9 | custom fusion | bytes 8404992 | tf_op jit(solution)/shard_map/vmap(jit(_take))/gather | solution.py:83
  120.2 2.6 broadcast_select_fusion
  129.5 3.0 pad_add_fusion
  132.5 14.7 %scatter_custom_fusion.1 = f32[1152,512]{1,0:T(8,128)} fusion(s32[2048]{0:T(1024)S(1)} %broadcast_select_fusion.1, f32[2048,512]{1,0:T(8,128)} %bitcast.213, f32[]{:T(128)} %constant.8.clone.1), kind=kCustom, calls=%fused_computation.33 | custom fusion | flops 1048576 | bytes 2359808
  148.7 4.9 %collective-permute-start.16 = (f32[1,128,512]{2,1,0:T(8,128)S(1)}, f32[1,128,512]{2,1,0:T(8,128)S(1)}, u32[]{:S(2)}, u32[]{:S(2)}) collective-permute-start(f32[1,128,512]{2,1,0:T(8,128)S(1)} %get-tuple-element.17), channel_id=1, source_target_pairs={{4,0},{5,1},{6,2},{7,3},{8,4},{9,5},{10,6},{11,7},{12,8},{13,9},{1... | collective-permute-start | bytes 786440 | tf_op jit(solution)/shard_map/ppermute | solution.py:16
  153.6 1.9 collective-permute-start.17
  155.5 1.9 collective-permute-start.18
  157.4 4.6 %collective-permute-start.19 = (f32[1,128,512]{2,1,0:T(8,128)S(1)}, f32[1,128,512]{2,1,0:T(8,128)S(1)}, u32[]{:S(2)}, u32[]{:S(2)}) collective-permute-start(f32[1,128,512]{2,1,0:T(8,128)S(1)} %get-tuple-element.14), channel_id=1, source_target_pairs={{1,0},{2,1},{3,2},{4,3},{5,4},{6,5},{7,6},{8,7},{9,8},{10,9},{11,1... | collective-permute-start | bytes 786440 | tf_op jit(solution)/shard_map/ppermute | solution.py:16
  162.1 6.2 %collective-permute-done.17 = f32[1,128,512]{2,1,0:T(8,128)S(1)} collective-permute-done((f32[1,128,512]{2,1,0:T(8,128)S(1)}, f32[1,128,512]{2,1,0:T(8,128)S(1)}, u32[]{:S(2)}, u32[]{:S(2)}) %collective-permute-start.17) | collective-permute-done | bytes 262176 | tf_op jit(solution)/shard_map/ppermute | solution.py:16
  169.5 2.8 collective-permute-done.19
  174.6 1.9 collective-permute-start.20
  176.6 5.8 %collective-permute-start.21 = (f32[1,128,512]{2,1,0:T(8,128)}, f32[1,128,512]{2,1,0:T(8,128)}, u32[]{:S(2)}, u32[]{:S(2)}) collective-permute-start(f32[1,128,512]{2,1,0:T(8,128)} %get-tuple-element.11), channel_id=1, source_target_pairs={{0,2},{1,3},{2,4},{3,5},{4,6},{5,7},{6,8},{7,9},{8,10},{9,11},{10,... | collective-permute-start | bytes 786440 | tf_op jit(solution)/shard_map/ppermute | solution.py:16
  182.4 3.0 collective-permute-start.22
  185.4 4.3 %collective-permute-start.23 = (f32[1,128,512]{2,1,0:T(8,128)S(1)}, f32[1,128,512]{2,1,0:T(8,128)S(1)}, u32[]{:S(2)}, u32[]{:S(2)}) collective-permute-start(f32[1,128,512]{2,1,0:T(8,128)S(1)} %get-tuple-element.9), channel_id=1, source_target_pairs={{0,4},{1,5},{2,6},{3,7},{4,8},{5,9},{6,10},{7,11},{8,12},{9,13},{1... | collective-permute-start | bytes 786440 | tf_op jit(solution)/shard_map/ppermute | solution.py:16
  197.0 11.2 %scatter_custom_fusion = f32[512,512]{1,0:T(8,128)} fusion(s32[1152]{0:T(1024)S(1)} %bitcast.217, f32[1152,512]{1,0:T(8,128)} %bitcast.216, f32[]{:T(128)} %constant.8.clone.1), kind=kCustom, calls=%fused_computation.76 | custom fusion | flops 589824 | bytes 1049088 | tf_op jit(solution)/shard_map/scatter-add | solution.py:122
  208.2 70.1 %all-reduce.10.cloned.1.call-done = f32[2,256,512]{2,1,0:T(8,128)} async-done(((f32[2,256,512]{2,1,0:T(8,128)}), f32[2,256,512]{2,1,0:T(8,128)}) %all-reduce.10.cloned.1.call-update) | async-done | bytes 1048592 | tf_op jit(solution)/shard_map/psum | solution.py:127
  279.7 4.5 %collective-permute-start.24 = (f32[1,256,512]{2,1,0:T(8,128)S(1)}, f32[1,256,512]{2,1,0:T(8,128)S(1)}, u32[]{:S(2)}, u32[]{:S(2)}) collective-permute-start(f32[1,256,512]{2,1,0:T(8,128)S(1)} %get-tuple-element.26), channel_id=1, source_target_pairs={{1,0},{2,1},{3,2},{4,3},{5,4},{6,5},{7,6},{8,7},{9,8},{10,9},{11,1... | collective-permute-start | bytes 1572872 | tf_op jit(solution)/shard_map/ppermute | solution.py:29
  284.2 1.9 collective-permute-start.25
  286.2 7.2 %collective-permute-start.28 = (f32[1,1,256,512]{3,2,1,0:T(8,128)S(1)}, f32[1,1,256,512]{3,2,1,0:T(8,128)S(1)}, u32[]{:S(2)}, u32[]{:S(2)}) collective-permute-start(f32[1,1,256,512]{3,2,1,0:T(8,128)S(1)} %get-tuple-element.21), channel_id=1, source_target_pairs={{1,0},{2,1},{3,2},{4,3},{5,4},{6,5},{7,6},{8,7},{9,8},{10,9},{11,1... | collective-permute-start | bytes 1572872 | tf_op jit(solution)/shard_map/ppermute | solution.py:29
  293.4 1.9 collective-permute-start.29
  296.4 7.7 %collective-permute-done.25 = f32[1,256,512]{2,1,0:T(8,128)S(1)} collective-permute-done((f32[1,256,512]{2,1,0:T(8,128)S(1)}, f32[1,256,512]{2,1,0:T(8,128)S(1)}, u32[]{:S(2)}, u32[]{:S(2)}) %collective-permute-start.25) | collective-permute-done | bytes 524320 | tf_op jit(solution)/shard_map/ppermute | solution.py:27
  305.5 1.9 collective-permute-start.26
  307.5 3.9 %collective-permute-start.27 = (f32[1,256,512]{2,1,0:T(8,128)S(1)}, f32[1,256,512]{2,1,0:T(8,128)S(1)}, u32[]{:S(2)}, u32[]{:S(2)}) collective-permute-start(f32[1,256,512]{2,1,0:T(8,128)S(1)} %get-tuple-element.23), channel_id=1, source_target_pairs={{0,1},{1,2},{2,3},{3,4},{4,5},{5,6},{6,7},{7,8},{8,9},{9,10},{10,1... | collective-permute-start | bytes 1572872 | tf_op jit(solution)/shard_map/ppermute | solution.py:27
  311.4 4.0 %collective-permute-done.29 = f32[1,1,256,512]{3,2,1,0:T(8,128)S(1)} collective-permute-done((f32[1,1,256,512]{3,2,1,0:T(8,128)S(1)}, f32[1,1,256,512]{3,2,1,0:T(8,128)S(1)}, u32[]{:S(2)}, u32[]{:S(2)}) %collective-permute-start.29) | collective-permute-done | bytes 524320 | tf_op jit(solution)/shard_map/ppermute | solution.py:27
  316.1 2.0 pad_maximum_fusion.1
  318.1 2.8 collective-permute-done.26
  320.9 5.5 %collective-permute-done.27 = f32[1,256,512]{2,1,0:T(8,128)S(1)} collective-permute-done((f32[1,256,512]{2,1,0:T(8,128)S(1)}, f32[1,256,512]{2,1,0:T(8,128)S(1)}, u32[]{:S(2)}, u32[]{:S(2)}) %collective-permute-start.27) | collective-permute-done | bytes 524320 | tf_op jit(solution)/shard_map/ppermute | solution.py:27
  326.7 1.9 fusion.19
  (152 shorter events, 50.1 us)
Async XLA Ops:
  7.2 271.1 %all-reduce.10.cloned.1.call-start = ((), (), s32[]{:S(2)}) async-start(), calls=%async_computation | async-start | bytes 2097152 | tf_op jit(solution)/shard_map/psum | solution.py:127
  7.9 22.5 %collective-permute-start = (s32[1,128]{1,0:T(1,128)S(1)}, s32[1,128]{1,0:T(1,128)S(1)}, u32[]{:S(2)}, u32[]{:S(2)}) collective-permute-start(s32[1,128]{1,0:T(1,128)S(1)} %get-tuple-element.35), channel_id=1, source_target_pairs={{4,0},{5,1},{6,2},{7,3},{8,4},{9,5},{10,6},{11,7},{12,8},{13,9},{1... | collective-permute-start | bytes 1544 | tf_op jit(solution)/shard_map/ppermute | solution.py:16
  9.9 20.5 %collective-permute-start.1 = (s32[1,128]{1,0:T(1,128)S(1)}, s32[1,128]{1,0:T(1,128)S(1)}, u32[]{:S(2)}, u32[]{:S(2)}) collective-permute-start(s32[1,128]{1,0:T(1,128)S(1)} %get-tuple-element.34), channel_id=1, source_target_pairs={{3,0},{4,1},{5,2},{6,3},{7,4},{8,5},{9,6},{10,7},{11,8},{12,9},{13... | collective-permute-start | bytes 1544 | tf_op jit(solution)/shard_map/ppermute | solution.py:16
  12.9 17.6 %collective-permute-start.2 = (s32[1,128]{1,0:T(1,128)S(1)}, s32[1,128]{1,0:T(1,128)S(1)}, u32[]{:S(2)}, u32[]{:S(2)}) collective-permute-start(s32[1,128]{1,0:T(1,128)S(1)} %get-tuple-element.33), channel_id=1, source_target_pairs={{2,0},{3,1},{4,2},{5,3},{6,4},{7,5},{8,6},{9,7},{10,8},{11,9},{12,... | collective-permute-start | bytes 1544 | tf_op jit(solution)/shard_map/ppermute | solution.py:16
  17.1 13.4 %collective-permute-start.3 = (s32[1,128]{1,0:T(1,128)S(1)}, s32[1,128]{1,0:T(1,128)S(1)}, u32[]{:S(2)}, u32[]{:S(2)}) collective-permute-start(s32[1,128]{1,0:T(1,128)S(1)} %get-tuple-element.32), channel_id=1, source_target_pairs={{1,0},{2,1},{3,2},{4,3},{5,4},{6,5},{7,6},{8,7},{9,8},{10,9},{11,1... | collective-permute-start | bytes 1544 | tf_op jit(solution)/shard_map/ppermute | solution.py:16
  25.8 3.0 copy-start.15
  25.8 3.0 copy-start.16
  25.8 3.2 copy-start
  28.7 1.8 copy-start.14
  30.5 26.0 %collective-permute-start.4 = (s32[1,128]{1,0:T(1,128)S(1)}, s32[1,128]{1,0:T(1,128)S(1)}, u32[]{:S(2)}, u32[]{:S(2)}) collective-permute-start(s32[1,128]{1,0:T(1,128)S(1)} %get-tuple-element.30), channel_id=1, source_target_pairs={{0,1},{1,2},{2,3},{3,4},{4,5},{5,6},{6,7},{7,8},{8,9},{9,10},{10,1... | collective-permute-start | bytes 1544 | tf_op jit(solution)/shard_map/ppermute | solution.py:16
  33.0 25.4 %collective-permute-start.5 = (s32[1,128]{1,0:T(1,128)S(1)}, s32[1,128]{1,0:T(1,128)S(1)}, u32[]{:S(2)}, u32[]{:S(2)}) collective-permute-start(s32[1,128]{1,0:T(1,128)S(1)} %get-tuple-element.29), channel_id=1, source_target_pairs={{0,2},{1,3},{2,4},{3,5},{4,6},{5,7},{6,8},{7,9},{8,10},{9,11},{10,... | collective-permute-start | bytes 1544 | tf_op jit(solution)/shard_map/ppermute | solution.py:16
  37.9 47.2 %collective-permute-start.9 = (f32[1,128,512]{2,1,0:T(8,128)}, f32[1,128,512]{2,1,0:T(8,128)}, u32[]{:S(2)}, u32[]{:S(2)}) collective-permute-start(f32[1,128,512]{2,1,0:T(8,128)} %bitcast_select_fusion.7), channel_id=1, source_target_pairs={{0,3},{1,4},{2,5},{3,6},{4,7},{5,8},{6,9},{7,10},{8,11},{9,12},{10... | collective-permute-start | bytes 786440 | tf_op jit(solution)/shard_map/ppermute | solution.py:16
  43.7 37.3 %collective-permute-start.8 = (f32[1,128,512]{2,1,0:T(8,128)S(1)}, f32[1,128,512]{2,1,0:T(8,128)S(1)}, u32[]{:S(2)}, u32[]{:S(2)}) collective-permute-start(f32[1,128,512]{2,1,0:T(8,128)S(1)} %bitcast_select_fusion.8), channel_id=1, source_target_pairs={{0,4},{1,5},{2,6},{3,7},{4,8},{5,9},{6,10},{7,11},{8,12},{9,13},{1... | collective-permute-start | bytes 786440 | tf_op jit(solution)/shard_map/ppermute | solution.py:16
  49.1 38.9 %collective-permute-start.10 = (f32[1,128,512]{2,1,0:T(8,128)}, f32[1,128,512]{2,1,0:T(8,128)}, u32[]{:S(2)}, u32[]{:S(2)}) collective-permute-start(f32[1,128,512]{2,1,0:T(8,128)} %bitcast_select_fusion.6), channel_id=1, source_target_pairs={{0,2},{1,3},{2,4},{3,5},{4,6},{5,7},{6,8},{7,9},{8,10},{9,11},{10,... | collective-permute-start | bytes 786440 | tf_op jit(solution)/shard_map/ppermute | solution.py:16
  56.5 34.6 %collective-permute-start.11 = (f32[1,128,512]{2,1,0:T(8,128)}, f32[1,128,512]{2,1,0:T(8,128)}, u32[]{:S(2)}, u32[]{:S(2)}) collective-permute-start(f32[1,128,512]{2,1,0:T(8,128)} %bitcast_select_fusion.5), channel_id=1, source_target_pairs={{0,1},{1,2},{2,3},{3,4},{4,5},{5,6},{6,7},{7,8},{8,9},{9,10},{10,1... | collective-permute-start | bytes 786440 | tf_op jit(solution)/shard_map/ppermute | solution.py:16
  58.5 7.5 %collective-permute-start.6 = (s32[1,128]{1,0:T(1,128)S(1)}, s32[1,128]{1,0:T(1,128)S(1)}, u32[]{:S(2)}, u32[]{:S(2)}) collective-permute-start(s32[1,128]{1,0:T(1,128)S(1)} %get-tuple-element.28), channel_id=1, source_target_pairs={{0,3},{1,4},{2,5},{3,6},{4,7},{5,8},{6,9},{7,10},{8,11},{9,12},{10... | collective-permute-start | bytes 1544 | tf_op jit(solution)/shard_map/ppermute | solution.py:16
  66.0 6.6 %collective-permute-start.7 = (s32[1,128]{1,0:T(1,128)S(1)}, s32[1,128]{1,0:T(1,128)S(1)}, u32[]{:S(2)}, u32[]{:S(2)}) collective-permute-start(s32[1,128]{1,0:T(1,128)S(1)} %get-tuple-element.27), channel_id=1, source_target_pairs={{0,4},{1,5},{2,6},{3,7},{4,8},{5,9},{6,10},{7,11},{8,12},{9,13},{1... | collective-permute-start | bytes 1544 | tf_op jit(solution)/shard_map/ppermute | solution.py:16
  72.7 19.6 %collective-permute-start.12 = (f32[1,128,512]{2,1,0:T(8,128)}, f32[1,128,512]{2,1,0:T(8,128)}, u32[]{:S(2)}, u32[]{:S(2)}) collective-permute-start(f32[1,128,512]{2,1,0:T(8,128)} %bitcast_select_fusion.3), channel_id=1, source_target_pairs={{1,0},{2,1},{3,2},{4,3},{5,4},{6,5},{7,6},{8,7},{9,8},{10,9},{11,1... | collective-permute-start | bytes 786440 | tf_op jit(solution)/shard_map/ppermute | solution.py:16
  80.9 11.2 %copy-start.11 = (f32[128,512]{1,0:T(8,128)S(1)}, f32[128,512]{1,0:T(8,128)}, u32[]{:S(2)}) copy-start(f32[128,512]{1,0:T(8,128)} %gather_fusion.5) | copy-start | bytes 786436
  81.0 0.7 copy-start.12
  81.7 11.9 %collective-permute-start.13 = (f32[1,128,512]{2,1,0:T(8,128)}, f32[1,128,512]{2,1,0:T(8,128)S(1)}, u32[]{:S(2)}, u32[]{:S(2)}) collective-permute-start(f32[1,128,512]{2,1,0:T(8,128)} %bitcast_select_fusion.2), channel_id=1, source_target_pairs={{2,0},{3,1},{4,2},{5,3},{6,4},{7,5},{8,6},{9,7},{10,8},{11,9},{12,... | collective-permute-start | bytes 786440 | tf_op jit(solution)/shard_map/ppermute | solution.py:16
  85.2 11.2 %collective-permute-start.14 = (f32[1,128,512]{2,1,0:T(8,128)}, f32[1,128,512]{2,1,0:T(8,128)S(1)}, u32[]{:S(2)}, u32[]{:S(2)}) collective-permute-start(f32[1,128,512]{2,1,0:T(8,128)} %bitcast_select_fusion.1), channel_id=1, source_target_pairs={{3,0},{4,1},{5,2},{6,3},{7,4},{8,5},{9,6},{10,7},{11,8},{12,9},{13... | collective-permute-start | bytes 786440 | tf_op jit(solution)/shard_map/ppermute | solution.py:16
  88.1 11.7 %collective-permute-start.15 = (f32[1,128,512]{2,1,0:T(8,128)S(1)}, f32[1,128,512]{2,1,0:T(8,128)S(1)}, u32[]{:S(2)}, u32[]{:S(2)}) collective-permute-start(f32[1,128,512]{2,1,0:T(8,128)S(1)} %bitcast_select_fusion), channel_id=1, source_target_pairs={{4,0},{5,1},{6,2},{7,3},{8,4},{9,5},{10,6},{11,7},{12,8},{13,9},{1... | collective-permute-start | bytes 786440 | tf_op jit(solution)/shard_map/ppermute | solution.py:16
  120.2 3.8 %copy-start.6 = (f32[512,512]{1,0:T(8,128)S(1)}, f32[512,512]{1,0:T(8,128)}, u32[]{:S(2)}) copy-start(f32[512,512]{1,0:T(8,128)} %get-tuple-element.3) | copy-start | bytes 3145732
  120.2 3.8 %copy-start.7 = (f32[512,512]{1,0:T(8,128)S(1)}, f32[512,512]{1,0:T(8,128)}, u32[]{:S(2)}) copy-start(f32[512,512]{1,0:T(8,128)} %get-tuple-element.6) | copy-start | bytes 3145732
  122.8 2.2 copy-start.1
  122.8 2.5 copy-start.2
  122.9 2.8 copy-start.3
  122.9 3.1 copy-start.4
  122.9 3.4 %copy-start.5 = (f32[1,1,512,512]{3,2,1,0:T(8,128)S(1)}, f32[1,1,512,512]{3,2,1,0:T(8,128)}, u32[]{:S(2)}) copy-start(f32[1,1,512,512]{3,2,1,0:T(8,128)} %get-tuple-element.8) | copy-start | bytes 3145732
  126.2 1.6 copy-start.10
  147.3 25.1 %copy-start.8 = (f32[1152,512]{1,0:T(8,128)S(1)}, f32[1152,512]{1,0:T(8,128)}, u32[]{:S(2)}) copy-start(f32[1152,512]{1,0:T(8,128)} %scatter_custom_fusion.1) | copy-start | bytes 7077892
  148.7 13.4 %collective-permute-start.16 = (f32[1,128,512]{2,1,0:T(8,128)S(1)}, f32[1,128,512]{2,1,0:T(8,128)S(1)}, u32[]{:S(2)}, u32[]{:S(2)}) collective-permute-start(f32[1,128,512]{2,1,0:T(8,128)S(1)} %get-tuple-element.17), channel_id=1, source_target_pairs={{4,0},{5,1},{6,2},{7,3},{8,4},{9,5},{10,6},{11,7},{12,8},{13,9},{1... | collective-permute-start | bytes 786440 | tf_op jit(solution)/shard_map/ppermute | solution.py:16
  153.6 14.7 %collective-permute-start.17 = (f32[1,128,512]{2,1,0:T(8,128)S(1)}, f32[1,128,512]{2,1,0:T(8,128)S(1)}, u32[]{:S(2)}, u32[]{:S(2)}) collective-permute-start(f32[1,128,512]{2,1,0:T(8,128)S(1)} %get-tuple-element.16), channel_id=1, source_target_pairs={{3,0},{4,1},{5,2},{6,3},{7,4},{8,5},{9,6},{10,7},{11,8},{12,9},{13... | collective-permute-start | bytes 786440 | tf_op jit(solution)/shard_map/ppermute | solution.py:16
  155.5 14.0 %collective-permute-start.18 = (f32[1,128,512]{2,1,0:T(8,128)S(1)}, f32[1,128,512]{2,1,0:T(8,128)S(1)}, u32[]{:S(2)}, u32[]{:S(2)}) collective-permute-start(f32[1,128,512]{2,1,0:T(8,128)S(1)} %get-tuple-element.15), channel_id=1, source_target_pairs={{2,0},{3,1},{4,2},{5,3},{6,4},{7,5},{8,6},{9,7},{10,8},{11,9},{12,... | collective-permute-start | bytes 786440 | tf_op jit(solution)/shard_map/ppermute | solution.py:16
  157.4 14.9 %collective-permute-start.19 = (f32[1,128,512]{2,1,0:T(8,128)S(1)}, f32[1,128,512]{2,1,0:T(8,128)S(1)}, u32[]{:S(2)}, u32[]{:S(2)}) collective-permute-start(f32[1,128,512]{2,1,0:T(8,128)S(1)} %get-tuple-element.14), channel_id=1, source_target_pairs={{1,0},{2,1},{3,2},{4,3},{5,4},{6,5},{7,6},{8,7},{9,8},{10,9},{11,1... | collective-permute-start | bytes 786440 | tf_op jit(solution)/shard_map/ppermute | solution.py:16
  173.2 1.4 copy-start.13
  174.6 16.0 %collective-permute-start.20 = (f32[1,128,512]{2,1,0:T(8,128)}, f32[1,128,512]{2,1,0:T(8,128)}, u32[]{:S(2)}, u32[]{:S(2)}) collective-permute-start(f32[1,128,512]{2,1,0:T(8,128)} %get-tuple-element.12), channel_id=1, source_target_pairs={{0,1},{1,2},{2,3},{3,4},{4,5},{5,6},{6,7},{7,8},{8,9},{9,10},{10,1... | collective-permute-start | bytes 786440 | tf_op jit(solution)/shard_map/ppermute | solution.py:16
  176.6 15.8 %collective-permute-start.21 = (f32[1,128,512]{2,1,0:T(8,128)}, f32[1,128,512]{2,1,0:T(8,128)}, u32[]{:S(2)}, u32[]{:S(2)}) collective-permute-start(f32[1,128,512]{2,1,0:T(8,128)} %get-tuple-element.11), channel_id=1, source_target_pairs={{0,2},{1,3},{2,4},{3,5},{4,6},{5,7},{6,8},{7,9},{8,10},{9,11},{10,... | collective-permute-start | bytes 786440 | tf_op jit(solution)/shard_map/ppermute | solution.py:16
  182.4 13.2 %collective-permute-start.22 = (f32[1,128,512]{2,1,0:T(8,128)}, f32[1,128,512]{2,1,0:T(8,128)S(1)}, u32[]{:S(2)}, u32[]{:S(2)}) collective-permute-start(f32[1,128,512]{2,1,0:T(8,128)} %get-tuple-element.10), channel_id=1, source_target_pairs={{0,3},{1,4},{2,5},{3,6},{4,7},{5,8},{6,9},{7,10},{8,11},{9,12},{10... | collective-permute-start | bytes 786440 | tf_op jit(solution)/shard_map/ppermute | solution.py:16
  185.4 10.8 %collective-permute-start.23 = (f32[1,128,512]{2,1,0:T(8,128)S(1)}, f32[1,128,512]{2,1,0:T(8,128)S(1)}, u32[]{:S(2)}, u32[]{:S(2)}) collective-permute-start(f32[1,128,512]{2,1,0:T(8,128)S(1)} %get-tuple-element.9), channel_id=1, source_target_pairs={{0,4},{1,5},{2,6},{3,7},{4,8},{5,9},{6,10},{7,11},{8,12},{9,13},{1... | collective-permute-start | bytes 786440 | tf_op jit(solution)/shard_map/ppermute | solution.py:16
  278.3 25.9 %copy-start.9 = (f32[2,256,512]{2,1,0:T(8,128)S(1)}, f32[2,256,512]{2,1,0:T(8,128)}, u32[]{:S(2)}) copy-start(f32[2,256,512]{2,1,0:T(8,128)} %all-reduce.10.cloned.1.call-done) | copy-start | bytes 3145732
  279.7 16.8 %collective-permute-start.24 = (f32[1,256,512]{2,1,0:T(8,128)S(1)}, f32[1,256,512]{2,1,0:T(8,128)S(1)}, u32[]{:S(2)}, u32[]{:S(2)}) collective-permute-start(f32[1,256,512]{2,1,0:T(8,128)S(1)} %get-tuple-element.26), channel_id=1, source_target_pairs={{1,0},{2,1},{3,2},{4,3},{5,4},{6,5},{7,6},{8,7},{9,8},{10,9},{11,1... | collective-permute-start | bytes 1572872 | tf_op jit(solution)/shard_map/ppermute | solution.py:29
  284.2 20.0 %collective-permute-start.25 = (f32[1,256,512]{2,1,0:T(8,128)S(1)}, f32[1,256,512]{2,1,0:T(8,128)S(1)}, u32[]{:S(2)}, u32[]{:S(2)}) collective-permute-start(f32[1,256,512]{2,1,0:T(8,128)S(1)} %get-tuple-element.25), channel_id=1, source_target_pairs={{0,1},{1,2},{2,3},{3,4},{4,5},{5,6},{6,7},{7,8},{8,9},{9,10},{10,1... | collective-permute-start | bytes 1572872 | tf_op jit(solution)/shard_map/ppermute | solution.py:27
  286.2 25.2 %collective-permute-start.28 = (f32[1,1,256,512]{3,2,1,0:T(8,128)S(1)}, f32[1,1,256,512]{3,2,1,0:T(8,128)S(1)}, u32[]{:S(2)}, u32[]{:S(2)}) collective-permute-start(f32[1,1,256,512]{3,2,1,0:T(8,128)S(1)} %get-tuple-element.21), channel_id=1, source_target_pairs={{1,0},{2,1},{3,2},{4,3},{5,4},{6,5},{7,6},{8,7},{9,8},{10,9},{11,1... | collective-permute-start | bytes 1572872 | tf_op jit(solution)/shard_map/ppermute | solution.py:29
  293.4 22.0 %collective-permute-start.29 = (f32[1,1,256,512]{3,2,1,0:T(8,128)S(1)}, f32[1,1,256,512]{3,2,1,0:T(8,128)S(1)}, u32[]{:S(2)}, u32[]{:S(2)}) collective-permute-start(f32[1,1,256,512]{3,2,1,0:T(8,128)S(1)} %get-tuple-element.22), channel_id=1, source_target_pairs={{0,1},{1,2},{2,3},{3,4},{4,5},{5,6},{6,7},{7,8},{8,9},{9,10},{10,1... | collective-permute-start | bytes 1572872 | tf_op jit(solution)/shard_map/ppermute | solution.py:27
  305.5 15.3 %collective-permute-start.26 = (f32[1,256,512]{2,1,0:T(8,128)S(1)}, f32[1,256,512]{2,1,0:T(8,128)S(1)}, u32[]{:S(2)}, u32[]{:S(2)}) collective-permute-start(f32[1,256,512]{2,1,0:T(8,128)S(1)} %get-tuple-element.24), channel_id=1, source_target_pairs={{1,0},{2,1},{3,2},{4,3},{5,4},{6,5},{7,6},{8,7},{9,8},{10,9},{11,1... | collective-permute-start | bytes 1572872 | tf_op jit(solution)/shard_map/ppermute | solution.py:29
  307.5 18.9 %collective-permute-start.27 = (f32[1,256,512]{2,1,0:T(8,128)S(1)}, f32[1,256,512]{2,1,0:T(8,128)S(1)}, u32[]{:S(2)}, u32[]{:S(2)}) collective-permute-start(f32[1,256,512]{2,1,0:T(8,128)S(1)} %get-tuple-element.23), channel_id=1, source_target_pairs={{0,1},{1,2},{2,3},{3,4},{4,5},{5,6},{6,7},{7,8},{8,9},{9,10},{10,1... | collective-permute-start | bytes 1572872 | tf_op jit(solution)/shard_map/ppermute | solution.py:27
Sparse Core Ops, SparseCore 0:
  208.3 69.9 all-reduce.9
where the time goes:
time: 337 us; the launch traced here: 335 us
  waiting for transfers between devices  116 us (34%)
  starting transfers between devices  103 us (31%)
  other arithmetic  52.4 us (16%)
  local copies, waits for them, and re-layouts  49.9 us (15%)
  between operations  14.9 us (4%)
    ppermute x24, starting transfers between devices, from_behind(): return lax.ppermute(block, axis, route)  81.1 us
    psum x1, waiting for transfers between devices, on_device(): smoothed = lax.psum(grid_grad, 'subj')  70.1 us
    ppermute x24, waiting for transfers between devices, from_behind(): return lax.ppermute(block, axis, route)  24.4 us
    gather x2, local copies, waits for them, and re-layouts, on_device(): jnp.take(held_lines, chosen, axis=0)  20.5 us
    ppermute x3, waiting for transfers between devices, padded_2(): lax.ppermute(tail, axis, [(i, (i + 1) % count) for i in range(ends)])  17.3 us
    unnamed x6, other arithmetic  15 us
    unnamed x57, local copies, waits for them, and re-layouts  14.1 us
    ppermute x3, starting transfers between devices, padded_2(): lax.ppermute(head, axis, [((i + 1) % count, i) for i in range(ends)])  13.7 us
  transfers between devices with their start and end apart: 31, of which 16 were waited for; matrix products, arithmetic and copies ran while one was open for 10% of the time, Pallas kernels for 0%

commit v1 on v0

v1 whole, which is shorter than its diff:
```python
import functools

import jax
import jax.numpy as jnp
from jax import lax
from jax.experimental import pallas as pl
from jax.experimental.pallas import tpu as pltpu
from jax.sharding import PartitionSpec as P

SMOOTH = 2
REACH = 4
RING = 4
diffusion = 0.15
HALO = SMOOTH

F32 = jnp.float32
BF16 = jnp.bfloat16
I32 = jnp.int32
VMEM = pl.BlockSpec(memory_space=pltpu.VMEM)
SMEM = pl.BlockSpec(memory_space=pltpu.SMEM)
ANY = pl.BlockSpec(memory_space=pl.ANY)
LIMIT = 48 * 2**20


def call(body, outs, in_specs, out_specs, scratch=(), cost=2**20):
    return pl.pallas_call(
        body,
        out_shape=outs,
        in_specs=in_specs,
        out_specs=out_specs,
        scratch_shapes=list(scratch),
        compiler_params=pltpu.CompilerParams(vmem_limit_bytes=LIMIT),
        cost_estimate=pl.CostEstimate(flops=cost, bytes_accessed=cost, transcendentals=0),
    )


def f32s(*shape):
    return jax.ShapeDtypeStruct(shape, F32)


def along_x(value, step):
    count = lax.axis_size("slab")
    route = [(i, i // RING * RING + (i + step) % RING) for i in range(count)]
    return lax.ppermute(value, "slab", route)


def along_slab(value, step):
    count = lax.axis_size("slab")
    return lax.ppermute(value, "slab", [(i, (i + step) % count) for i in range(count)])


def along_z(value, step):
    return along_slab(value, RING * step)


def other_core(value):
    count = lax.axis_size("subj")
    return lax.ppermute(value, "subj", [(i, i ^ 1) for i in range(count)])


def along_y(value, step):
    count = lax.axis_size("subj")
    return lax.ppermute(value, "subj", [(i, (i + 2 * step) % count) for i in range(count)])


def copy_lines(list_ref, list_row, source_ref, out_ref, flip, base):
    capacity = out_ref.shape[0]

    def group(block, carry):
        for unit in range(8):
            place = block * 8 + unit
            line = (list_ref[list_row, place] ^ flip) + base
            out_ref[pl.ds(place, 1), :] = source_ref[pl.ds(line, 1), :]
        return carry

    lax.fori_loop(0, capacity // 8, group, 0)


def own_lines_kernel(place_ref, lists_0, lists_1, lists_2, lists_3, lines_ref, out_0, out_1, out_2, out_3):
    here = place_ref[0]
    for step, lists, out in ((0, lists_0, out_0), (1, lists_1, out_1), (2, lists_2, out_2), (3, lists_3, out_3)):
        there = lax.rem(here + step, RING)
        copy_lines(lists, here - there + REACH, lines_ref, out, 0, 0)


def cross_lines_kernel(
    place_ref, lists_0, lists_1, lists_2, lists_3, low_a, low_b, high_a, high_b,
    out_low, out_high, out_1, out_2, out_3, held, sems,
):
    here = place_ref[0]
    half = low_a.shape[0]
    flip = place_ref[1] * half
    copies = [
        pltpu.make_async_copy(part, held.at[pl.ds(at * half, half)], sems.at[at])
        for at, part in enumerate((low_a, low_b, high_a, high_b))
    ]
    for copy in copies:
        copy.start()
    for copy in copies:
        copy.wait()
    copy_lines(lists_0, 0, held, out_low, flip, 0)
    copy_lines(lists_0, 2 * REACH, held, out_high, flip, 2 * half)
    for step, lists, out in ((1, lists_1, out_1), (2, lists_2, out_2), (3, lists_3, out_3)):
        there = lax.rem(here + step, RING)
        above = (there > here).astype(I32)
        copy_lines(lists, here - there + 2 * REACH * above, held, out, flip, 2 * half * above)


def split_parts(value):
    high = value.astype(BF16)
    low = (value - high.astype(F32)).astype(BF16)
    return high, low


def shift_down(value):
    width = value.shape[1]
    lane = lax.broadcasted_iota(I32, value.shape, 1)
    return jnp.where(lane == width - 1, 0.0, pltpu.roll(value, width - 1, 1))


def shift_up(value):
    lane = lax.broadcasted_iota(I32, value.shape, 1)
    return jnp.where(lane == 0, 0.0, pltpu.roll(value, 1, 1))


def warp_kernel(*refs):
    slot_ref, ids_ref, fraction_ref, image_ref = refs[:4]
    blocks = refs[4:13]
    warped_refs = refs[13:15]
    pooled_refs = refs[15:24]
    held, stage, push_high, push_low, sems = refs[24:]
    capacity = blocks[0].shape[0]
    line_count = image_ref.shape[0]
    rows_plane = line_count // 2
    rows = 16
    copies = [
        pltpu.make_async_copy(block, held.at[pl.ds(at * capacity, capacity)], sems.at[at])
        for at, block in enumerate(blocks)
    ]
    for copy in copies:
        copy.start()
    for copy in copies:
        copy.wait()

    for plane in range(2):
        def step(block, carry):
            local = pl.multiple_of(block * rows, rows)
            first = pl.multiple_of(plane * rows_plane + block * rows, rows)
            for corner in range(4):
                for row in range(rows):
                    line = slot_ref[corner, first + row]
                    stage[pl.ds(corner * rows + row, 1), :] = held[pl.ds(line, 1), :]
            depth_part = fraction_ref[0, pl.ds(first, rows), :].astype(F32)
            row_part = fraction_ref[1, pl.ds(first, rows), :].astype(F32)
            across = fraction_ref[2, pl.ds(first, rows), :].astype(F32)
            depth_rest, row_rest, rest = 1.0 - depth_part, 1.0 - row_part, 1.0 - across
            weights = (
                depth_rest * row_rest, depth_rest * row_part,
                depth_part * row_rest, depth_part * row_part,
            )
            warped = None
            for corner in range(4):
                lines = stage[corner * rows:(corner + 1) * rows, :]
                term = weights[corner] * (rest * lines + across * shift_down(lines))
                warped = term if warped is None else warped + term
            warped_refs[plane][pl.ds(local, rows), :] = warped
            mismatch = warped - image_ref[pl.ds(first, rows), :]
            for corner in range(4):
                scaled = weights[corner] * mismatch
                pushed = rest * scaled + shift_up(across * scaled)
                high, low = split_parts(pushed)
                at = pl.multiple_of(corner * line_count + plane * rows_plane + block * rows, rows)
                push_high[pl.ds(at, rows), :] = high
                push_low[pl.ds(at, rows), :] = low
            return carry

        lax.fori_loop(0, rows_plane // rows, step, 0)

    group = 3
    total = 4 * line_count
    slot = lax.broadcasted_iota(I32, (group * capacity, total), 0)
    for first in range(0, 9, group):
        chosen = (ids_ref[...] == slot + first * capacity)
        hot = jnp.where(chosen, 1.0, 0.0).astype(BF16)
        summed = jnp.dot(hot, push_high[...], preferred_element_type=F32)
        summed = summed + jnp.dot(hot, push_low[...], preferred_element_type=F32)
        for at in range(group):
            pooled_refs[first + at][...] = summed[at * capacity:(at + 1) * capacity]


def add_lines(target_rows, ids, values, outs):
    high_refs, low_refs = values
    for out, first, count in outs:
        hot = jnp.where(target_rows[first:first + count] == ids, 1.0, 0.0).astype(BF16)
        out[...] = jnp.dot(hot, high_refs, preferred_element_type=F32) + jnp.dot(
            hot, low_refs, preferred_element_type=F32
        )


def own_back_kernel(
    place_ref, lists_0, lists_1, lists_2, lists_3, rows_ref, in_0, in_1, in_2, in_3, keep, send
):
    here = place_ref[0]
    ids = []
    for step, lists in enumerate((lists_0, lists_1, lists_2, lists_3)):
        there = lax.rem(here + step, RING)
        ids.append(lists[pl.ds(here - there + REACH, 1), :])
    values = jnp.concatenate([in_0[...], in_1[...], in_2[...], in_3[...]], axis=0)
    count = keep.shape[0]
    add_lines(rows_ref[...], jnp.concatenate(ids, axis=1), split_parts(values),
              ((keep, 0, count), (send, count, count)))


def cross_back_kernel(
    place_ref, lists_0, lists_1, lists_2, lists_3, rows_ref, in_low, in_high, in_1, in_2, in_3,
    keep_low, keep_high, send_low, send_high,
):
    here = place_ref[0]
    span = 2 * REACH * in_low.shape[0]
    ids = [lists_0[0:1, :], lists_0[2 * REACH:2 * REACH + 1, :] + span]
    for step, lists in enumerate((lists_1, lists_2, lists_3), 1):
        there = lax.rem(here + step, RING)
        above = (there > here).astype(I32)
        ids.append(lists[pl.ds(here - there + 2 * REACH * above, 1), :] + span * above)
    ids = jnp.concatenate(ids, axis=1)
    values = split_parts(jnp.concatenate([in_low[...], in_high[...], in_1[...], in_2[...], in_3[...]], axis=0))
    count = keep_low.shape[0]
    rows = rows_ref[...]
    add_lines(rows, ids, values, ((keep_low, 0, count), (send_low, count, count)))
    add_lines(rows, ids - span, values, ((keep_high, 0, count), (send_high, count, count)))


def smooth_kernel(place_ref, before, piece, after, template_ref, out, field):
    device, last, core, chip = place_ref[2], place_ref[3], place_ref[1], place_ref[4]
    size = piece.shape[0]
    rows = size // 2
    total = 3 * size
    zero = jnp.zeros(piece.shape, F32)
    field[0:size, :] = jnp.where(device > 0, before[...], zero)
    field[size:2 * size, :] = piece[...]
    field[2 * size:3 * size, :] = jnp.where(device < last, after[...], zero)
    width = piece.shape[1]
    at = lax.broadcasted_iota(I32, (total, width), 0)
    row = lax.rem(at, rows)
    per_piece = rows - 2 * HALO
    index = core * RING + chip
    row = row + index * per_piece - HALO
    inside = (row >= 0) & (row < 2 * RING * per_piece)
    inside = inside & ((at >= size) | (device > 0)) & ((at < 2 * size) | (device < last))
    current = field[...]
    for repeat in range(SMOOTH):
        beside = pltpu.roll(current, rows, 0) + pltpu.roll(current, total - rows, 0)
        beside = beside + pltpu.roll(current, 1, 0) + pltpu.roll(current, total - 1, 0)
        beside = beside + shift_up(current) + shift_down(current)
        current = current + diffusion * (beside - 6.0 * current)
        if repeat < SMOOTH - 1:
            current = jnp.where(inside, current, 0.0)
    field[...] = current
    subjects = place_ref[5].astype(F32)
    plane_rows = template_ref.shape[0] // 2
    for plane in range(2):
        start = pl.multiple_of(plane * plane_rows + index * per_piece, per_piece)
        found = field[pl.ds(size + plane * rows + HALO, per_piece), :]
        out[plane * per_piece:(plane + 1) * per_piece, :] = (
            template_ref[pl.ds(start, per_piece), :] - found / subjects
        )


def assemble_kernel(place_ref, *refs):
    pieces, out, sems = refs[:2 * RING], refs[2 * RING], refs[2 * RING + 1]
    core, chip = place_ref[1], place_ref[4]
    count = pieces[0].shape[0] // 2
    plane_rows = out.shape[0] // 2
    copies = []
    for at, piece in enumerate(pieces):
        part = core if at < RING else 1 - core
        index = part * RING + lax.rem(chip + RING - at % RING, RING)
        for plane in range(2):
            start = pl.multiple_of(plane * plane_rows + index * count, count)
            copies.append(
                pltpu.make_async_copy(
                    piece.at[pl.ds(plane * count, count)], out.at[pl.ds(start, count)], sems.at[2 * at + plane]
                )
            )
    for copy in copies:
        copy.start()
    for copy in copies:
        copy.wait()


def force_kernel(place_ref, before, plane_0, plane_1, after, image_ref, out):
    device, last = place_ref[2], place_ref[3]
    rows_plane, width = plane_0.shape
    rows = 32
    row = lax.broadcasted_iota(I32, (rows, width), 0)
    for plane, (previous, current, following) in enumerate(
        ((before, plane_0, plane_1), (plane_0, plane_1, after))
    ):
        def step(block, carry):
            first = pl.multiple_of(block * rows, rows)
            centre = current[pl.ds(first, rows), :]
            negative = image_ref[pl.ds(plane * rows_plane + first, rows), :] - centre
            back, ahead = previous[pl.ds(first, rows), :], following[pl.ds(first, rows), :]
            if plane == 0:
                back = jnp.where(device > 0, back, 0.0)
            else:
                ahead = jnp.where(device < last, ahead, 0.0)
            out[0, plane, pl.ds(first, rows), :] = negative * (0.5 * (ahead - back))
            above = current[pl.ds(jnp.maximum(first - 1, 0), 1), :]
            above = jnp.where(first > 0, above, 0.0)
            below = current[pl.ds(jnp.minimum(first + rows, rows_plane - 1), 1), :]
            below = jnp.where(first + rows < rows_plane, below, 0.0)
            up = jnp.where(row == 0, above, pltpu.roll(centre, 1, 0))
            down = jnp.where(row == rows - 1, below, pltpu.roll(centre, rows - 1, 0))
            out[1, plane, pl.ds(first, rows), :] = negative * (0.5 * (down - up))
            out[2, plane, pl.ds(first, rows), :] = negative * (0.5 * (shift_down(centre) - shift_up(centre)))
            return carry

        lax.fori_loop(0, rows_plane // rows, step, 0)


def on_device(template, images, fractions, requests, corners):
    _, plane_count, row_count, cell_count = images.shape
    line_count = plane_count * row_count
    band_count, capacity = requests.shape[2:]
    slab = lax.axis_index("slab")
    subject = lax.axis_index("subj")
    last = lax.axis_size("slab") - 1
    here = slab % RING
    core = subject % 2
    chip = subject // 2
    place = jnp.stack([here, core, slab, jnp.int32(last), chip, jnp.int32(lax.axis_size("subj"))]).astype(I32)
    lists = requests.reshape(band_count, capacity)
    lines = template.reshape(line_count, cell_count)
    block = f32s(capacity, cell_count)

    asked = [lists] + [along_x(lists, -step) for step in (1, 2, 3)]
    plane = lax.dynamic_index_in_dim(template, core, 0, keepdims=False)
    from_low = along_z(plane, 1)
    from_high = along_z(plane, -1)

    own = call(
        own_lines_kernel, (block,) * 4, [SMEM] * 5 + [VMEM], (VMEM,) * 4
    )(place, *asked, lines)
    got_own = [along_x(own[step], step) for step in (1, 2, 3)]
    from_low_b, from_high_b = other_core(from_low), other_core(from_high)
    cross = call(
        cross_lines_kernel, (block,) * 5, [SMEM] * 5 + [ANY] * 4, (VMEM,) * 5,
        [pltpu.VMEM((2 * line_count, cell_count), F32), pltpu.SemaphoreType.DMA((4,))],
    )(place, *asked, from_low, from_low_b, from_high, from_high_b)
    got_cross = [along_x(cross[1 + step], step) for step in (1, 2, 3)]

    slot_ids = corners.reshape(4, line_count)
    offset = slot_ids // capacity - REACH
    source = here + offset
    outside = (source < 0) | (source >= RING)
    behind = (here - source) % RING
    held_at = jnp.where(
        behind == 0,
        jnp.where(offset == 0, 0, jnp.where(offset < 0, 1, 2)),
        1 + 2 * behind + outside.astype(I32),
    )
    slot_ids = held_at * capacity + slot_ids % capacity

    blocks = [own[0], cross[0], cross[1]]
    for at in range(3):
        blocks += [got_own[at], got_cross[at]]
    half = f32s(row_count, cell_count)
    results = call(
        warp_kernel,
        (half,) * 2 + (block,) * 9,
        [SMEM] + [VMEM] * 3 + [ANY] * 9,
        (VMEM,) * 11,
        [
            pltpu.VMEM((band_count * capacity, cell_count), F32),
            pltpu.VMEM((64, cell_count), F32),
            pltpu.VMEM((4 * line_count, cell_count), BF16),
            pltpu.VMEM((4 * line_count, cell_count), BF16),
            pltpu.SemaphoreType.DMA((9,)),
        ],
        2**24,
    )(
        slot_ids, slot_ids.reshape(1, 4 * line_count),
        fractions.reshape(3, line_count, cell_count), images.reshape(line_count, cell_count), *blocks,
    )
    warped_0, warped_1 = results[:2]
    pooled = results[2:]

    back_cross = [along_x(pooled[2 + 2 * step], -step) for step in (1, 2, 3)]
    back_own = [along_x(pooled[1 + 2 * step], -step) for step in (1, 2, 3)]

    per_piece = row_count // (2 * RING)
    wide = per_piece + 2 * HALO
    at = jnp.arange(2 * RING * 2 * wide, dtype=I32)
    piece = at // (2 * wide)
    part = jnp.where(piece < RING, core, 1 - core)
    index = part * RING + (chip + piece) % RING
    row = index * per_piece - HALO + at % wide
    target = jnp.where((row >= 0) & (row < row_count), at // wide % 2 * row_count + row, -(2**20))
    target = target.reshape(-1, 1)
    core_part = f32s(RING * 2 * wide, cell_count)
    keep_low, keep_high, send_low, send_high = call(
        cross_back_kernel, (core_part,) * 4, [SMEM] + [VMEM] * 10, (VMEM,) * 4, (), 2**22
    )(place, *asked, target, pooled[1], pooled[2], *back_cross)
    sum_low = keep_low + other_core(send_low)
    sum_high = keep_high + other_core(send_high)
    in_from_high = along_z(sum_low, -1)
    in_from_low = along_z(sum_high, 1)
    keep_own, send_own = call(
        own_back_kernel, (core_part,) * 2, [SMEM] + [VMEM] * 9, (VMEM,) * 2, (), 2**22
    )(place, *asked, target, pooled[0], *back_own)
    total = keep_own + other_core(send_own) + in_from_high + in_from_low

    size = 2 * wide
    pieces = [total[at * size:(at + 1) * size] for at in range(RING)]
    piece_sum = pieces[0] + along_y(pieces[1], 1) + along_y(pieces[2], 2) + along_y(pieces[3], 3)
    before, after = along_slab(piece_sum, 1), along_slab(piece_sum, -1)
    new_piece = call(
        smooth_kernel, f32s(2 * per_piece, cell_count), [SMEM] + [VMEM] * 4, VMEM,
        [pltpu.VMEM((3 * size, cell_count), F32)],
    )(place, before, piece_sum, after, lines)

    edge_0, edge_1, _ = lax.optimization_barrier((warped_0, warped_1, keep_own))
    edge_before, edge_after = along_slab(edge_1, 1), along_slab(edge_0, -1)
    image_force = call(
        force_kernel, f32s(3, plane_count, row_count, cell_count), [SMEM] + [VMEM] * 5, VMEM, (), 2**22
    )(place, edge_before, warped_0, warped_1, edge_after, images.reshape(line_count, cell_count))

    mine = [new_piece] + [along_y(new_piece, step) for step in (1, 2, 3)]
    theirs = [other_core(value) for value in mine]
    new_template = call(
        assemble_kernel, f32s(line_count, cell_count), [SMEM] + [ANY] * 8, ANY,
        [pltpu.SemaphoreType.DMA((16,))],
    )(place, *mine, *theirs)
    return new_template.reshape(template.shape), image_force[None]


def solution(mesh):
    return jax.shard_map(
        on_device,
        mesh=mesh,
        in_specs=(
            P("slab", None, None),
            P("subj", "slab", None, None),
            P("subj", None, "slab", None, None),
            P("subj", "slab", None, None),
            P("subj", None, "slab", None),
        ),
        out_specs=(P("slab", None, None), P("subj", None, "slab", None, None)),
        check_vma=False,
    )
```

time: 337 us -> 177 us (0.53)
  the two profiles are of different devices: /device:TPU:152 before, /device:TPU:1 now
where the time goes in v1:
time: 177 us
  waiting for transfers between devices  79.2 us (45%)
  starting transfers between devices  53.5 us (30%)
  Pallas kernels  38.4 us (22%)
  local copies, waits for them, and re-layouts  3.85 us (2%)
    ppermute x15, waiting for transfers between devices, along_x(): return lax.ppermute(value, 'slab', route)  45.1 us
    ppermute x8, waiting for transfers between devices, along_slab(): lax.ppermute(value, 'slab', [(i, (i + step) % count) for i in range(count)])  29.5 us
    ppermute x8, starting transfers between devices, along_slab(): lax.ppermute(value, 'slab', [(i, (i + step) % count) for i in range(count)])  19.6 us
    pallas_call x1, Pallas kernels, on_device(): call(warp_kernel, (half,) * 2 + (block,) * 9, [SMEM] + [VMEM] * 3 + [ANY]...  19.6 us
    ppermute x15, starting transfers between devices, along_x(): return lax.ppermute(value, 'slab', route)  16.6 us
    ppermute x9, starting transfers between devices, other_core(): return lax.ppermute(value, 'subj', [(i, i ^ 1) for i in range(count)])  9.49 us
    ppermute x6, starting transfers between devices, along_y(): lax.ppermute(value, 'subj', [(i, (i + 2 * step) % count) for i in range(c...  7.89 us
    ppermute x6, waiting for transfers between devices, along_y(): lax.ppermute(value, 'subj', [(i, (i + 2 * step) % count) for i in range(c...  4.6 us
  transfers between devices with their start and end apart: 38, of which 17 were waited for; matrix products, arithmetic and copies ran while one was open for 1% of the time, Pallas kernels for 8%

profile of v1, /device:TPU:1, one launch (start us, length us, event | category | flops | bytes accessed | tf_op | source)
XLA Modules:
  0.0 177.1 jit_solution(12504415250906863251)
XLA Ops:
  0.7 1.1 dynamic-slice_bitcast_fusion
  1.7 2.5 %collective-permute-start.3 = (f32[256,512]{1,0:T(8,128)S(1)}, f32[256,512]{1,0:T(8,128)S(1)}, u32[]{:S(2)}, u32[]{:S(2)}) collective-permute-start(f32[256,512]{1,0:T(8,128)S(1)} %dynamic-slice_bitcast_fusion), channel_id=1, source_target_pairs={{0,4},{1,5},{2,6},{3,7},{4,8},{5,9},{6,10},{7,11},{8,12},{9,13},{1... | collective-permute-start | bytes 1572872 | tf_op jit(solution)/shard_map/ppermute | solution.py:49
  4.3 4.0 %collective-permute-start.5 = (f32[256,512]{1,0:T(8,128)S(1)}, f32[256,512]{1,0:T(8,128)S(1)}, u32[]{:S(2)}, u32[]{:S(2)}) collective-permute-start(f32[256,512]{1,0:T(8,128)S(1)} %dynamic-slice_bitcast_fusion), channel_id=1, source_target_pairs={{0,28},{1,29},{2,30},{3,31},{4,0},{5,1},{6,2},{7,3},{8,4},{9,5},{1... | collective-permute-start | bytes 1572872 | tf_op jit(solution)/shard_map/ppermute | solution.py:49
  8.3 11.6 %collective-permute-done.3.low_a = f32[256,512]{1,0:T(8,128)S(1)} collective-permute-done((f32[256,512]{1,0:T(8,128)S(1)}, f32[256,512]{1,0:T(8,128)S(1)}, u32[]{:S(2)}, u32[]{:S(2)}) %collective-permute-start.3) | collective-permute-done | bytes 524320 | tf_op jit(solution)/shard_map/ppermute | solution.py:49
  19.9 1.2 collective-permute-start.4
  21.8 2.5 %collective-permute-start = (s32[9,128]{1,0:T(8,128)S(1)}, s32[9,128]{1,0:T(8,128)S(1)}, u32[]{:S(2)}, u32[]{:S(2)}) collective-permute-start(s32[9,128]{1,0:T(8,128)S(1)} %bitcast.21), channel_id=1, source_target_pairs={{0,3},{1,0},{2,1},{3,2},{4,7},{5,4},{6,5},{7,6},{8,11},{9,8},{10,9... | collective-permute-start | bytes 13832 | tf_op jit(solution)/shard_map/ppermute | solution.py:44
  25.5 2.8 %collective-permute-done.1.lists_2 = s32[9,128]{1,0:T(8,128)S(1)} collective-permute-done((s32[9,128]{1,0:T(8,128)S(1)}, s32[9,128]{1,0:T(8,128)S(1)}, u32[]{:S(2)}, u32[]{:S(2)}) %collective-permute-start.1) | collective-permute-done | bytes 4640 | tf_op jit(solution)/shard_map/ppermute | solution.py:44
  28.5 1.2 copy-done
  29.7 3.6 %shard_map.68 = (f32[128,512]{1,0:T(8,128)S(1)}, f32[128,512]{1,0:T(8,128)S(1)}, f32[128,512]{1,0:T(8,128)S(1)}, f32[128,512]{1,0:T(8,128)S(1)}) custom-call(s32[6]{0:T(128)S(1)} %stack.19.place_ref, s32[9,128]{1,0:T(8,128)S(1)} %bitcast.24, s32[9,128]{1,0:T(8,128)S(1)} %collective-permute-done.lists_1, s32[9,128]{1,0:T(8,128)S(1)} %collective-permute-done.1.lists_2, ...), custom_call_target="tpu_custom_call" | custom-call | flops 1048576 | bytes 1048576 | tf_op jit(solution)/shard_map/pallas_call | solution.py:342
  33.4 0.7 reshape.386
  34.1 1.7 collective-permute-start.9
  35.8 2.0 %collective-permute-start.11 = (f32[128,512]{1,0:T(8,128)S(1)}, f32[128,512]{1,0:T(8,128)S(1)}, u32[]{:S(2)}, u32[]{:S(2)}) collective-permute-start(f32[128,512]{1,0:T(8,128)S(1)} %get-tuple-element.37), channel_id=1, source_target_pairs={{0,3},{1,0},{2,1},{3,2},{4,7},{5,4},{6,5},{7,6},{8,11},{9,8},{10,9... | collective-permute-start | bytes 786440 | tf_op jit(solution)/shard_map/ppermute | solution.py:44
  37.8 4.5 %shard_map.69 = (f32[128,512]{1,0:T(8,128)S(1)}, f32[128,512]{1,0:T(8,128)S(1)}, f32[128,512]{1,0:T(8,128)S(1)}, f32[128,512]{1,0:T(8,128)S(1)}, f32[128,512]{1,0:T(8,128)S(1)}) custom-call(s32[6]{0:T(128)S(1)} %stack.19.place_ref, s32[9,128]{1,0:T(8,128)S(1)} %bitcast.25, s32[9,128]{1,0:T(8,128)S(1)} %collective-permute-done.lists_1, ...), custom_call_target="tpu_custom_call" | custom-call | flops 1048576 | bytes 1048576 | tf_op jit(solution)/shard_map/pallas_call | solution.py:347
  42.5 1.5 collective-permute-start.10
  44.0 2.0 %collective-permute-start.12 = (f32[128,512]{1,0:T(8,128)S(1)}, f32[128,512]{1,0:T(8,128)S(1)}, u32[]{:S(2)}, u32[]{:S(2)}) collective-permute-start(f32[128,512]{1,0:T(8,128)S(1)} %get-tuple-element.38), channel_id=1, source_target_pairs={{0,3},{1,0},{2,1},{3,2},{4,7},{5,4},{6,5},{7,6},{8,11},{9,8},{10,9... | collective-permute-start | bytes 786440 | tf_op jit(solution)/shard_map/ppermute | solution.py:44
  46.2 4.1 %collective-permute-done.11.refs_11_ = f32[128,512]{1,0:T(8,128)S(1)} collective-permute-done((f32[128,512]{1,0:T(8,128)S(1)}, f32[128,512]{1,0:T(8,128)S(1)}, u32[]{:S(2)}, u32[]{:S(2)}) %collective-permute-start.11) | collective-permute-done | bytes 262176 | tf_op jit(solution)/shard_map/ppermute | solution.py:44
  50.3 4.9 %collective-permute-done.8.refs_8_ = f32[128,512]{1,0:T(8,128)S(1)} collective-permute-done((f32[128,512]{1,0:T(8,128)S(1)}, f32[128,512]{1,0:T(8,128)S(1)}, u32[]{:S(2)}, u32[]{:S(2)}) %collective-permute-start.8) | collective-permute-done | bytes 262176 | tf_op jit(solution)/shard_map/ppermute | solution.py:44
  55.1 1.3 collective-permute-done.10.refs_10_
  56.4 3.2 %collective-permute-done.12.refs_12_ = f32[128,512]{1,0:T(8,128)S(1)} collective-permute-done((f32[128,512]{1,0:T(8,128)S(1)}, f32[128,512]{1,0:T(8,128)S(1)}, u32[]{:S(2)}, u32[]{:S(2)}) %collective-permute-start.12) | collective-permute-done | bytes 262176 | tf_op jit(solution)/shard_map/ppermute | solution.py:44
  59.6 19.6 %shard_map.70 = (f32[256,512]{1,0:T(8,128)S(1)}, f32[256,512]{1,0:T(8,128)S(1)}, f32[128,512]{1,0:T(8,128)S(1)}, f32[128,512]{1,0:T(8,128)S(1)}, f32[128,512]{1,...) custom-call(s32[4,512]{1,0:T(4,128)S(1)} %fusion.22.refs_0_, ...), custom_call_target="tpu_custom_call" | custom-call | flops 16777216 | bytes 16777216 | tf_op jit(solution)/shard_map/pallas_call | solution.py:369
  79.2 3.5 %collective-permute-start.17 = (f32[128,512]{1,0:T(8,128)}, f32[128,512]{1,0:T(8,128)S(1)}, u32[]{:S(2)}, u32[]{:S(2)}) collective-permute-start(f32[128,512]{1,0:T(8,128)} %get-tuple-element.47), channel_id=1, source_target_pairs={{0,3},{1,0},{2,1},{3,2},{4,7},{5,4},{6,5},{7,6},{8,11},{9,8},{10,9... | collective-permute-start | bytes 786440 | tf_op jit(solution)/shard_map/ppermute | solution.py:44
  83.8 5.6 %collective-permute-done.17.in_1 = f32[128,512]{1,0:T(8,128)S(1)} collective-permute-done((f32[128,512]{1,0:T(8,128)}, f32[128,512]{1,0:T(8,128)S(1)}, u32[]{:S(2)}, u32[]{:S(2)}) %collective-permute-start.17) | collective-permute-done | bytes 262176 | tf_op jit(solution)/shard_map/ppermute | solution.py:44
  89.4 1.6 collective-permute-done.18.in_2
  91.0 7.2 %collective-permute-done.19.in_3 = f32[128,512]{1,0:T(8,128)S(1)} collective-permute-done((f32[128,512]{1,0:T(8,128)}, f32[128,512]{1,0:T(8,128)S(1)}, u32[]{:S(2)}, u32[]{:S(2)}) %collective-permute-start.19) | collective-permute-done | bytes 262176 | tf_op jit(solution)/shard_map/ppermute | solution.py:44
  98.2 2.6 %shard_map.72 = (f32[288,512]{1,0:T(8,128)S(1)}, f32[288,512]{1,0:T(8,128)S(1)}, f32[288,512]{1,0:T(8,128)S(1)}, f32[288,512]{1,0:T(8,128)S(1)}) custom-call(s32[6]{0:T(128)S(1)} %stack.19.place_ref, s32[9,128]{1,0:T(8,128)S(1)} %bitcast.26, s32[9,128]{1,0:T(8,128)S(1)} %collective-permute-done.lists_1, s32[9,128]{1,0:T(8,128)S(1)} %collective-permute-done.1.lists_2, ...), custom_call_target="tpu_custom_call" | custom-call | flops 4194304 | bytes 4194304 | tf_op jit(solution)/shard_map/pallas_call | solution.py:402
  102.2 0.8 collective-permute-start.15
  103.0 6.0 %collective-permute-done.13.in_1 = f32[128,512]{1,0:T(8,128)S(1)} collective-permute-done((f32[128,512]{1,0:T(8,128)S(1)}, f32[128,512]{1,0:T(8,128)S(1)}, u32[]{:S(2)}, u32[]{:S(2)}) %collective-permute-start.13) | collective-permute-done | bytes 262176 | tf_op jit(solution)/shard_map/ppermute | solution.py:44
  109.0 1.6 collective-permute-done.14.in_2
  110.6 6.6 %collective-permute-done.15.in_3 = f32[128,512]{1,0:T(8,128)S(1)} collective-permute-done((f32[128,512]{1,0:T(8,128)S(1)}, f32[128,512]{1,0:T(8,128)S(1)}, u32[]{:S(2)}, u32[]{:S(2)}) %collective-permute-start.15) | collective-permute-done | bytes 262176 | tf_op jit(solution)/shard_map/ppermute | solution.py:44
  117.2 1.4 shard_map.71
  118.6 0.8 collective-permute-start.16
  119.7 3.3 %collective-permute-start.21 = (f32[288,512]{1,0:T(8,128)S(1)}, f32[288,512]{1,0:T(8,128)S(1)}, u32[]{:S(2)}, u32[]{:S(2)}) collective-permute-start(f32[288,512]{1,0:T(8,128)S(1)} %add.249), channel_id=1, source_target_pairs={{0,28},{1,29},{2,30},{3,31},{4,0},{5,1},{6,2},{7,3},{8,4},{9,5},{1... | collective-permute-start | bytes 1769480 | tf_op jit(solution)/shard_map/ppermute | solution.py:49
  123.0 13.4 %collective-permute-done.23 = f32[288,512]{1,0:T(8,128)S(1)} collective-permute-done((f32[288,512]{1,0:T(8,128)S(1)}, f32[288,512]{1,0:T(8,128)S(1)}, u32[]{:S(2)}, u32[]{:S(2)}) %collective-permute-start.23) | collective-permute-done | bytes 589856 | tf_op jit(solution)/shard_map/ppermute | solution.py:49
  136.7 2.8 %collective-permute-start.26 = (f32[72,512]{1,0:T(8,128)S(1)}, f32[72,512]{1,0:T(8,128)S(1)}, u32[]{:S(2)}, u32[]{:S(2)}) collective-permute-start(f32[72,512]{1,0:T(8,128)S(1)} %get-tuple-element.59), channel_id=1, source_target_pairs={{0,192},{32,224},{64,0},{96,32},{128,64},{160,96},{192,128},{224,1... | collective-permute-start | bytes 442376 | tf_op jit(solution)/shard_map/ppermute | solution.py:63
  139.9 0.7 collective-permute-start.24
  140.6 4.8 %collective-permute-start.37 = (f32[256,512]{1,0:T(8,128)S(1)}, f32[256,512]{1,0:T(8,128)S(1)}, u32[]{:S(2)}, u32[]{:S(2)}) collective-permute-start(f32[256,512]{1,0:T(8,128)S(1)} %get-tuple-element.57.plane_0), channel_id=1, source_target_pairs={{0,31},{1,0},{2,1},{3,2},{4,3},{5,4},{6,5},{7,6},{8,7},{9,8},{10,9... | collective-permute-start | bytes 1572872 | tf_op jit(solution)/shard_map/ppermute | solution.py:49
  145.6 4.4 %collective-permute-done.24 = f32[72,512]{1,0:T(8,128)S(1)} collective-permute-done((f32[72,512]{1,0:T(8,128)S(1)}, f32[72,512]{1,0:T(8,128)S(1)}, u32[]{:S(2)}, u32[]{:S(2)}) %collective-permute-start.24) | collective-permute-done | bytes 147488 | tf_op jit(solution)/shard_map/ppermute | solution.py:63
  150.1 4.8 %collective-permute-start.28 = (f32[72,512]{1,0:T(8,128)S(1)}, f32[72,512]{1,0:T(8,128)S(1)}, u32[]{:S(2)}, u32[]{:S(2)}) collective-permute-start(f32[72,512]{1,0:T(8,128)S(1)} %fusion.17.piece), channel_id=1, source_target_pairs={{0,31},{1,0},{2,1},{3,2},{4,3},{5,4},{6,5},{7,6},{8,7},{9,8},{10,9... | collective-permute-start | bytes 442376 | tf_op jit(solution)/shard_map/ppermute | solution.py:49
  154.9 4.5 %collective-permute-done.27.before = f32[72,512]{1,0:T(8,128)S(1)} collective-permute-done((f32[72,512]{1,0:T(8,128)S(1)}, f32[72,512]{1,0:T(8,128)S(1)}, u32[]{:S(2)}, u32[]{:S(2)}) %collective-permute-start.27) | collective-permute-done | bytes 147488 | tf_op jit(solution)/shard_map/ppermute | solution.py:49
  159.4 1.2 shard_map.73.refs_0_
  160.6 1.4 collective-permute-start.29
  161.9 1.6 collective-permute-start.30
  163.5 1.1 collective-permute-start.31
  164.6 2.9 %collective-permute-start.32 = (f32[64,512]{1,0:T(8,128)S(1)}, f32[64,512]{1,0:T(8,128)S(1)}, u32[]{:S(2)}, u32[]{:S(2)}) collective-permute-start(f32[64,512]{1,0:T(8,128)S(1)} %shard_map.73.refs_0_), channel_id=1, source_target_pairs={{0,32},{32,0},{64,96},{96,64},{128,160},{160,128},{192,224},{224,1... | collective-permute-start | bytes 393224 | tf_op jit(solution)/shard_map/ppermute | solution.py:58
  167.5 1.8 %collective-permute-start.33 = (f32[64,512]{1,0:T(8,128)S(1)}, f32[64,512]{1,0:T(8,128)S(1)}, u32[]{:S(2)}, u32[]{:S(2)}) collective-permute-start(f32[64,512]{1,0:T(8,128)S(1)} %collective-permute-done.29.refs_1_), channel_id=1, source_target_pairs={{0,32},{32,0},{64,96},{96,64},{128,160},{160,128},{192,224},{224,1... | collective-permute-start | bytes 393224 | tf_op jit(solution)/shard_map/ppermute | solution.py:58
  169.3 1.7 collective-permute-start.34
  171.4 3.9 %shard_map.75 = f32[3,2,256,512]{3,2,1,0:T(8,128)} custom-call(s32[6]{0:T(128)S(1)} %stack.19.place_ref, f32[256,512]{1,0:T(8,128)S(1)} %collective-permute-done.36.before, f32[256,512]{1,0:T(8,128)S(1)} %get-tuple-element.57.plane_0, f32[256,512]{1,0:T(8,128)S(1)} %get-tuple-element.56.plane_1, f32[256,512]{1,0:T(8,128)S(1)} %collective-permute-done.37.after, ...), custom_call_target="tpu_custom_call" | custom-call | flops 4194304 | bytes 4194304 | tf_op jit(solution)/shard_map/pallas_call | solution.py:425
  175.3 1.6 shard_map.74
  (57 shorter events, 6.6 us)
Async XLA Ops:
  0.6 45.5 %copy-start.3 = (s32[1,4,2,256]{3,2,1,0:T(2,128)S(1)}, s32[1,4,2,256]{3,2,1,0:T(2,128)}, u32[]{:S(2)}) copy-start(s32[1,4,2,256]{3,2,1,0:T(2,128)} %param.9) | copy-start | bytes 24580
  1.7 18.1 %collective-permute-start.3 = (f32[256,512]{1,0:T(8,128)S(1)}, f32[256,512]{1,0:T(8,128)S(1)}, u32[]{:S(2)}, u32[]{:S(2)}) collective-permute-start(f32[256,512]{1,0:T(8,128)S(1)} %dynamic-slice_bitcast_fusion), channel_id=1, source_target_pairs={{0,4},{1,5},{2,6},{3,7},{4,8},{5,9},{6,10},{7,11},{8,12},{9,13},{1... | collective-permute-start | bytes 1572872 | tf_op jit(solution)/shard_map/ppermute | solution.py:49
  4.3 16.8 %collective-permute-start.5 = (f32[256,512]{1,0:T(8,128)S(1)}, f32[256,512]{1,0:T(8,128)S(1)}, u32[]{:S(2)}, u32[]{:S(2)}) collective-permute-start(f32[256,512]{1,0:T(8,128)S(1)} %dynamic-slice_bitcast_fusion), channel_id=1, source_target_pairs={{0,28},{1,29},{2,30},{3,31},{4,0},{5,1},{6,2},{7,3},{8,4},{9,5},{1... | collective-permute-start | bytes 1572872 | tf_op jit(solution)/shard_map/ppermute | solution.py:49
  19.9 17.9 %collective-permute-start.4 = (f32[256,512]{1,0:T(8,128)S(1)}, f32[256,512]{1,0:T(8,128)S(1)}, u32[]{:S(2)}, u32[]{:S(2)}) collective-permute-start(f32[256,512]{1,0:T(8,128)S(1)} %collective-permute-done.3.low_a), channel_id=1, source_target_pairs={{0,32},{32,0},{64,96},{96,64},{128,160},{160,128},{192,224},{224,1... | collective-permute-start | bytes 1572872 | tf_op jit(solution)/shard_map/ppermute | solution.py:58
  21.1 16.7 %collective-permute-start.6 = (f32[256,512]{1,0:T(8,128)S(1)}, f32[256,512]{1,0:T(8,128)S(1)}, u32[]{:S(2)}, u32[]{:S(2)}) collective-permute-start(f32[256,512]{1,0:T(8,128)S(1)} %collective-permute-done.5.high_a), channel_id=1, source_target_pairs={{0,32},{32,0},{64,96},{96,64},{128,160},{160,128},{192,224},{224,1... | collective-permute-start | bytes 1572872 | tf_op jit(solution)/shard_map/ppermute | solution.py:58
  21.8 3.7 %collective-permute-start = (s32[9,128]{1,0:T(8,128)S(1)}, s32[9,128]{1,0:T(8,128)S(1)}, u32[]{:S(2)}, u32[]{:S(2)}) collective-permute-start(s32[9,128]{1,0:T(8,128)S(1)} %bitcast.21), channel_id=1, source_target_pairs={{0,3},{1,0},{2,1},{3,2},{4,7},{5,4},{6,5},{7,6},{8,11},{9,8},{10,9... | collective-permute-start | bytes 13832 | tf_op jit(solution)/shard_map/ppermute | solution.py:44
  24.3 4.0 %collective-permute-start.1 = (s32[9,128]{1,0:T(8,128)S(1)}, s32[9,128]{1,0:T(8,128)S(1)}, u32[]{:S(2)}, u32[]{:S(2)}) collective-permute-start(s32[9,128]{1,0:T(8,128)S(1)} %bitcast.22), channel_id=1, source_target_pairs={{0,2},{1,3},{2,0},{3,1},{4,6},{5,7},{6,4},{7,5},{8,10},{9,11},{10,... | collective-permute-start | bytes 13832 | tf_op jit(solution)/shard_map/ppermute | solution.py:44
  24.8 3.7 %collective-permute-start.2 = (s32[9,128]{1,0:T(8,128)S(1)}, s32[9,128]{1,0:T(8,128)S(1)}, u32[]{:S(2)}, u32[]{:S(2)}) collective-permute-start(s32[9,128]{1,0:T(8,128)S(1)} %bitcast.23), channel_id=1, source_target_pairs={{0,1},{1,2},{2,3},{3,0},{4,5},{5,6},{6,7},{7,4},{8,9},{9,10},{10,1... | collective-permute-start | bytes 13832 | tf_op jit(solution)/shard_map/ppermute | solution.py:44
  28.5 1.2 copy-start
  33.3 10.7 %collective-permute-start.7 = (f32[128,512]{1,0:T(8,128)S(1)}, f32[128,512]{1,0:T(8,128)S(1)}, u32[]{:S(2)}, u32[]{:S(2)}) collective-permute-start(f32[128,512]{1,0:T(8,128)S(1)} %get-tuple-element.33), channel_id=1, source_target_pairs={{0,1},{1,2},{2,3},{3,0},{4,5},{5,6},{6,7},{7,4},{8,9},{9,10},{10,1... | collective-permute-start | bytes 786440 | tf_op jit(solution)/shard_map/ppermute | solution.py:44
  34.1 12.0 %collective-permute-start.9 = (f32[128,512]{1,0:T(8,128)S(1)}, f32[128,512]{1,0:T(8,128)S(1)}, u32[]{:S(2)}, u32[]{:S(2)}) collective-permute-start(f32[128,512]{1,0:T(8,128)S(1)} %get-tuple-element.35), channel_id=1, source_target_pairs={{0,2},{1,3},{2,0},{3,1},{4,6},{5,7},{6,4},{7,5},{8,10},{9,11},{10,... | collective-permute-start | bytes 786440 | tf_op jit(solution)/shard_map/ppermute | solution.py:44
  35.8 14.4 %collective-permute-start.11 = (f32[128,512]{1,0:T(8,128)S(1)}, f32[128,512]{1,0:T(8,128)S(1)}, u32[]{:S(2)}, u32[]{:S(2)}) collective-permute-start(f32[128,512]{1,0:T(8,128)S(1)} %get-tuple-element.37), channel_id=1, source_target_pairs={{0,3},{1,0},{2,1},{3,2},{4,7},{5,4},{6,5},{7,6},{8,11},{9,8},{10,9... | collective-permute-start | bytes 786440 | tf_op jit(solution)/shard_map/ppermute | solution.py:44
  42.4 12.8 %collective-permute-start.8 = (f32[128,512]{1,0:T(8,128)S(1)}, f32[128,512]{1,0:T(8,128)S(1)}, u32[]{:S(2)}, u32[]{:S(2)}) collective-permute-start(f32[128,512]{1,0:T(8,128)S(1)} %get-tuple-element.34), channel_id=1, source_target_pairs={{0,1},{1,2},{2,3},{3,0},{4,5},{5,6},{6,7},{7,4},{8,9},{9,10},{10,1... | collective-permute-start | bytes 786440 | tf_op jit(solution)/shard_map/ppermute | solution.py:44
  42.5 13.9 %collective-permute-start.10 = (f32[128,512]{1,0:T(8,128)S(1)}, f32[128,512]{1,0:T(8,128)S(1)}, u32[]{:S(2)}, u32[]{:S(2)}) collective-permute-start(f32[128,512]{1,0:T(8,128)S(1)} %get-tuple-element.36), channel_id=1, source_target_pairs={{0,2},{1,3},{2,0},{3,1},{4,6},{5,7},{6,4},{7,5},{8,10},{9,11},{10,... | collective-permute-start | bytes 786440 | tf_op jit(solution)/shard_map/ppermute | solution.py:44
  44.0 15.6 %collective-permute-start.12 = (f32[128,512]{1,0:T(8,128)S(1)}, f32[128,512]{1,0:T(8,128)S(1)}, u32[]{:S(2)}, u32[]{:S(2)}) collective-permute-start(f32[128,512]{1,0:T(8,128)S(1)} %get-tuple-element.38), channel_id=1, source_target_pairs={{0,3},{1,0},{2,1},{3,2},{4,7},{5,4},{6,5},{7,6},{8,11},{9,8},{10,9... | collective-permute-start | bytes 786440 | tf_op jit(solution)/shard_map/ppermute | solution.py:44
  79.2 10.2 %collective-permute-start.17 = (f32[128,512]{1,0:T(8,128)}, f32[128,512]{1,0:T(8,128)S(1)}, u32[]{:S(2)}, u32[]{:S(2)}) collective-permute-start(f32[128,512]{1,0:T(8,128)} %get-tuple-element.47), channel_id=1, source_target_pairs={{0,3},{1,0},{2,1},{3,2},{4,7},{5,4},{6,5},{7,6},{8,11},{9,8},{10,9... | collective-permute-start | bytes 786440 | tf_op jit(solution)/shard_map/ppermute | solution.py:44
  82.7 8.3 %collective-permute-start.18 = (f32[128,512]{1,0:T(8,128)}, f32[128,512]{1,0:T(8,128)S(1)}, u32[]{:S(2)}, u32[]{:S(2)}) collective-permute-start(f32[128,512]{1,0:T(8,128)} %get-tuple-element.48), channel_id=1, source_target_pairs={{0,2},{1,3},{2,0},{3,1},{4,6},{5,7},{6,4},{7,5},{8,10},{9,11},{10,... | collective-permute-start | bytes 786440 | tf_op jit(solution)/shard_map/ppermute | solution.py:44
  83.1 15.2 %collective-permute-start.19 = (f32[128,512]{1,0:T(8,128)}, f32[128,512]{1,0:T(8,128)S(1)}, u32[]{:S(2)}, u32[]{:S(2)}) collective-permute-start(f32[128,512]{1,0:T(8,128)} %get-tuple-element.49), channel_id=1, source_target_pairs={{0,1},{1,2},{2,3},{3,0},{4,5},{5,6},{6,7},{7,4},{8,9},{9,10},{10,1... | collective-permute-start | bytes 786440 | tf_op jit(solution)/shard_map/ppermute | solution.py:44
  100.8 18.5 %collective-permute-start.22 = (f32[288,512]{1,0:T(8,128)S(1)}, f32[288,512]{1,0:T(8,128)S(1)}, u32[]{:S(2)}, u32[]{:S(2)}) collective-permute-start(f32[288,512]{1,0:T(8,128)S(1)} %get-tuple-element.53), channel_id=1, source_target_pairs={{0,32},{32,0},{64,96},{96,64},{128,160},{160,128},{192,224},{224,1... | collective-permute-start | bytes 1769480 | tf_op jit(solution)/shard_map/ppermute | solution.py:58
  101.4 18.1 %collective-permute-start.20 = (f32[288,512]{1,0:T(8,128)S(1)}, f32[288,512]{1,0:T(8,128)S(1)}, u32[]{:S(2)}, u32[]{:S(2)}) collective-permute-start(f32[288,512]{1,0:T(8,128)S(1)} %get-tuple-element.51), channel_id=1, source_target_pairs={{0,32},{32,0},{64,96},{96,64},{128,160},{160,128},{192,224},{224,1... | collective-permute-start | bytes 1769480 | tf_op jit(solution)/shard_map/ppermute | solution.py:58
  101.5 7.5 %collective-permute-start.13 = (f32[128,512]{1,0:T(8,128)S(1)}, f32[128,512]{1,0:T(8,128)S(1)}, u32[]{:S(2)}, u32[]{:S(2)}) collective-permute-start(f32[128,512]{1,0:T(8,128)S(1)} %get-tuple-element.40), channel_id=1, source_target_pairs={{0,3},{1,0},{2,1},{3,2},{4,7},{5,4},{6,5},{7,6},{8,11},{9,8},{10,9... | collective-permute-start | bytes 786440 | tf_op jit(solution)/shard_map/ppermute | solution.py:44
  101.8 8.7 %collective-permute-start.14 = (f32[128,512]{1,0:T(8,128)S(1)}, f32[128,512]{1,0:T(8,128)S(1)}, u32[]{:S(2)}, u32[]{:S(2)}) collective-permute-start(f32[128,512]{1,0:T(8,128)S(1)} %get-tuple-element.41), channel_id=1, source_target_pairs={{0,2},{1,3},{2,0},{3,1},{4,6},{5,7},{6,4},{7,5},{8,10},{9,11},{10,... | collective-permute-start | bytes 786440 | tf_op jit(solution)/shard_map/ppermute | solution.py:44
  102.2 15.0 %collective-permute-start.15 = (f32[128,512]{1,0:T(8,128)S(1)}, f32[128,512]{1,0:T(8,128)S(1)}, u32[]{:S(2)}, u32[]{:S(2)}) collective-permute-start(f32[128,512]{1,0:T(8,128)S(1)} %get-tuple-element.42), channel_id=1, source_target_pairs={{0,1},{1,2},{2,3},{3,0},{4,5},{5,6},{6,7},{7,4},{8,9},{9,10},{10,1... | collective-permute-start | bytes 786440 | tf_op jit(solution)/shard_map/ppermute | solution.py:44
  118.6 4.4 %collective-permute-start.16 = (f32[288,512]{1,0:T(8,128)S(1)}, f32[288,512]{1,0:T(8,128)S(1)}, u32[]{:S(2)}, u32[]{:S(2)}) collective-permute-start(f32[288,512]{1,0:T(8,128)S(1)} %get-tuple-element.44), channel_id=1, source_target_pairs={{0,32},{32,0},{64,96},{96,64},{128,160},{160,128},{192,224},{224,1... | collective-permute-start | bytes 1769480 | tf_op jit(solution)/shard_map/ppermute | solution.py:58
  119.5 17.0 %collective-permute-start.23 = (f32[288,512]{1,0:T(8,128)S(1)}, f32[288,512]{1,0:T(8,128)S(1)}, u32[]{:S(2)}, u32[]{:S(2)}) collective-permute-start(f32[288,512]{1,0:T(8,128)S(1)} %add.251), channel_id=1, source_target_pairs={{0,4},{1,5},{2,6},{3,7},{4,8},{5,9},{6,10},{7,11},{8,12},{9,13},{1... | collective-permute-start | bytes 1769480 | tf_op jit(solution)/shard_map/ppermute | solution.py:49
  119.6 39.8 %copy-start.1 = (f32[2,256,512]{2,1,0:T(8,128)S(1)}, f32[2,256,512]{2,1,0:T(8,128)}, u32[]{:S(2)}) copy-start(f32[2,256,512]{2,1,0:T(8,128)} %param.5) | copy-start | bytes 3145732
  119.7 51.7 %copy-start.2 = (f32[1,2,256,512]{3,2,1,0:T(8,128)S(1)}, f32[1,2,256,512]{3,2,1,0:T(8,128)}, u32[]{:S(2)}) copy-start(f32[1,2,256,512]{3,2,1,0:T(8,128)} %param.6) | copy-start | bytes 3145732
  119.7 16.7 %collective-permute-start.21 = (f32[288,512]{1,0:T(8,128)S(1)}, f32[288,512]{1,0:T(8,128)S(1)}, u32[]{:S(2)}, u32[]{:S(2)}) collective-permute-start(f32[288,512]{1,0:T(8,128)S(1)} %add.249), channel_id=1, source_target_pairs={{0,28},{1,29},{2,30},{3,31},{4,0},{5,1},{6,2},{7,3},{8,4},{9,5},{1... | collective-permute-start | bytes 1769480 | tf_op jit(solution)/shard_map/ppermute | solution.py:49
  136.7 8.6 %collective-permute-start.26 = (f32[72,512]{1,0:T(8,128)S(1)}, f32[72,512]{1,0:T(8,128)S(1)}, u32[]{:S(2)}, u32[]{:S(2)}) collective-permute-start(f32[72,512]{1,0:T(8,128)S(1)} %get-tuple-element.59), channel_id=1, source_target_pairs={{0,192},{32,224},{64,0},{96,32},{128,64},{160,96},{192,128},{224,1... | collective-permute-start | bytes 442376 | tf_op jit(solution)/shard_map/ppermute | solution.py:63
  139.5 6.0 %collective-permute-start.25 = (f32[72,512]{1,0:T(8,128)S(1)}, f32[72,512]{1,0:T(8,128)S(1)}, u32[]{:S(2)}, u32[]{:S(2)}) collective-permute-start(f32[72,512]{1,0:T(8,128)S(1)} %get-tuple-element.60), channel_id=1, source_target_pairs={{0,128},{32,160},{64,192},{96,224},{128,0},{160,32},{192,64},{224,... | collective-permute-start | bytes 442376 | tf_op jit(solution)/shard_map/ppermute | solution.py:63
  139.9 10.1 %collective-permute-start.24 = (f32[72,512]{1,0:T(8,128)S(1)}, f32[72,512]{1,0:T(8,128)S(1)}, u32[]{:S(2)}, u32[]{:S(2)}) collective-permute-start(f32[72,512]{1,0:T(8,128)S(1)} %get-tuple-element.58), channel_id=1, source_target_pairs={{0,64},{32,96},{64,128},{96,160},{128,192},{160,224},{192,0},{224,... | collective-permute-start | bytes 442376 | tf_op jit(solution)/shard_map/ppermute | solution.py:63
  140.6 24.0 %collective-permute-start.36 = (f32[256,512]{1,0:T(8,128)S(1)}, f32[256,512]{1,0:T(8,128)S(1)}, u32[]{:S(2)}, u32[]{:S(2)}) collective-permute-start(f32[256,512]{1,0:T(8,128)S(1)} %get-tuple-element.56.plane_1), channel_id=1, source_target_pairs={{0,1},{1,2},{2,3},{3,4},{4,5},{5,6},{6,7},{7,8},{8,9},{9,10},{10,1... | collective-permute-start | bytes 1572872 | tf_op jit(solution)/shard_map/ppermute | solution.py:49
  140.6 30.8 %collective-permute-start.37 = (f32[256,512]{1,0:T(8,128)S(1)}, f32[256,512]{1,0:T(8,128)S(1)}, u32[]{:S(2)}, u32[]{:S(2)}) collective-permute-start(f32[256,512]{1,0:T(8,128)S(1)} %get-tuple-element.57.plane_0), channel_id=1, source_target_pairs={{0,31},{1,0},{2,1},{3,2},{4,3},{5,4},{6,5},{7,6},{8,7},{9,8},{10,9... | collective-permute-start | bytes 1572872 | tf_op jit(solution)/shard_map/ppermute | solution.py:49
  150.0 9.3 %collective-permute-start.27 = (f32[72,512]{1,0:T(8,128)S(1)}, f32[72,512]{1,0:T(8,128)S(1)}, u32[]{:S(2)}, u32[]{:S(2)}) collective-permute-start(f32[72,512]{1,0:T(8,128)S(1)} %fusion.17.piece), channel_id=1, source_target_pairs={{0,1},{1,2},{2,3},{3,4},{4,5},{5,6},{6,7},{7,8},{8,9},{9,10},{10,1... | collective-permute-start | bytes 442376 | tf_op jit(solution)/shard_map/ppermute | solution.py:49
  150.1 9.2 %collective-permute-start.28 = (f32[72,512]{1,0:T(8,128)S(1)}, f32[72,512]{1,0:T(8,128)S(1)}, u32[]{:S(2)}, u32[]{:S(2)}) collective-permute-start(f32[72,512]{1,0:T(8,128)S(1)} %fusion.17.piece), channel_id=1, source_target_pairs={{0,31},{1,0},{2,1},{3,2},{4,3},{5,4},{6,5},{7,6},{8,7},{9,8},{10,9... | collective-permute-start | bytes 442376 | tf_op jit(solution)/shard_map/ppermute | solution.py:49
  160.6 7.0 %collective-permute-start.29 = (f32[64,512]{1,0:T(8,128)S(1)}, f32[64,512]{1,0:T(8,128)S(1)}, u32[]{:S(2)}, u32[]{:S(2)}) collective-permute-start(f32[64,512]{1,0:T(8,128)S(1)} %shard_map.73.refs_0_), channel_id=1, source_target_pairs={{0,64},{32,96},{64,128},{96,160},{128,192},{160,224},{192,0},{224,... | collective-permute-start | bytes 393224 | tf_op jit(solution)/shard_map/ppermute | solution.py:63
  161.9 7.4 %collective-permute-start.30 = (f32[64,512]{1,0:T(8,128)S(1)}, f32[64,512]{1,0:T(8,128)S(1)}, u32[]{:S(2)}, u32[]{:S(2)}) collective-permute-start(f32[64,512]{1,0:T(8,128)S(1)} %shard_map.73.refs_0_), channel_id=1, source_target_pairs={{0,128},{32,160},{64,192},{96,224},{128,0},{160,32},{192,64},{224,... | collective-permute-start | bytes 393224 | tf_op jit(solution)/shard_map/ppermute | solution.py:63
  163.5 7.6 %collective-permute-start.31 = (f32[64,512]{1,0:T(8,128)S(1)}, f32[64,512]{1,0:T(8,128)S(1)}, u32[]{:S(2)}, u32[]{:S(2)}) collective-permute-start(f32[64,512]{1,0:T(8,128)S(1)} %shard_map.73.refs_0_), channel_id=1, source_target_pairs={{0,192},{32,224},{64,0},{96,32},{128,64},{160,96},{192,128},{224,1... | collective-permute-start | bytes 393224 | tf_op jit(solution)/shard_map/ppermute | solution.py:63
  164.6 10.7 %collective-permute-start.32 = (f32[64,512]{1,0:T(8,128)S(1)}, f32[64,512]{1,0:T(8,128)S(1)}, u32[]{:S(2)}, u32[]{:S(2)}) collective-permute-start(f32[64,512]{1,0:T(8,128)S(1)} %shard_map.73.refs_0_), channel_id=1, source_target_pairs={{0,32},{32,0},{64,96},{96,64},{128,160},{160,128},{192,224},{224,1... | collective-permute-start | bytes 393224 | tf_op jit(solution)/shard_map/ppermute | solution.py:58
  167.5 7.8 %collective-permute-start.33 = (f32[64,512]{1,0:T(8,128)S(1)}, f32[64,512]{1,0:T(8,128)S(1)}, u32[]{:S(2)}, u32[]{:S(2)}) collective-permute-start(f32[64,512]{1,0:T(8,128)S(1)} %collective-permute-done.29.refs_1_), channel_id=1, source_target_pairs={{0,32},{32,0},{64,96},{96,64},{128,160},{160,128},{192,224},{224,1... | collective-permute-start | bytes 393224 | tf_op jit(solution)/shard_map/ppermute | solution.py:58
  169.3 6.0 %collective-permute-start.34 = (f32[64,512]{1,0:T(8,128)S(1)}, f32[64,512]{1,0:T(8,128)S(1)}, u32[]{:S(2)}, u32[]{:S(2)}) collective-permute-start(f32[64,512]{1,0:T(8,128)S(1)} %collective-permute-done.30.refs_2_), channel_id=1, source_target_pairs={{0,32},{32,0},{64,96},{96,64},{128,160},{160,128},{192,224},{224,1... | collective-permute-start | bytes 393224 | tf_op jit(solution)/shard_map/ppermute | solution.py:58
  171.0 4.3 %collective-permute-start.35 = (f32[64,512]{1,0:T(8,128)S(1)}, f32[64,512]{1,0:T(8,128)S(1)}, u32[]{:S(2)}, u32[]{:S(2)}) collective-permute-start(f32[64,512]{1,0:T(8,128)S(1)} %collective-permute-done.31.refs_3_), channel_id=1, source_target_pairs={{0,32},{32,0},{64,96},{96,64},{128,160},{160,128},{192,224},{224,1... | collective-permute-start | bytes 393224 | tf_op jit(solution)/shard_map/ppermute | solution.py:58

commit v2 on v1

v2 whole, which is shorter than its diff:
```python
import functools

import jax
import jax.numpy as jnp
from jax import lax
from jax.experimental import pallas as pl
from jax.experimental.pallas import tpu as pltpu
from jax.sharding import PartitionSpec as P

SMOOTH = 2
REACH = 4
RING = 4
diffusion = 0.15
HALO = SMOOTH
LANES = 128
WARP_ROWS = 32

F32 = jnp.float32
BF16 = jnp.bfloat16
I32 = jnp.int32
VMEM = pl.BlockSpec(memory_space=pltpu.VMEM)
SMEM = pl.BlockSpec(memory_space=pltpu.SMEM)
ANY = pl.BlockSpec(memory_space=pl.ANY)
LIMIT = 8 * 2**20


def call(body, outs, in_specs, out_specs, scratch=(), aliases={}):
    return pl.pallas_call(
        body,
        out_shape=outs,
        in_specs=in_specs,
        out_specs=out_specs,
        scratch_shapes=list(scratch),
        input_output_aliases=aliases,
        compiler_params=pltpu.CompilerParams(vmem_limit_bytes=LIMIT),
    )


def f32s(*shape):
    return jax.ShapeDtypeStruct(shape, F32)


def along_x(value, step):
    count = lax.axis_size("slab")
    route = [(i, i // RING * RING + (i + step) % RING) for i in range(count)]
    return lax.ppermute(value, "slab", route)


def along_slab(value, step):
    count = lax.axis_size("slab")
    return lax.ppermute(value, "slab", [(i, (i + step) % count) for i in range(count)])


def along_z(value, step):
    return along_slab(value, RING * step)


def other_core(value):
    count = lax.axis_size("subj")
    return lax.ppermute(value, "subj", [(i, i ^ 1) for i in range(count)])


def along_y(value, step):
    count = lax.axis_size("subj")
    return lax.ppermute(value, "subj", [(i, (i + 2 * step) % count) for i in range(count)])


def spread_kernel(place_ref, source_ref, all_ref, half_ref):
    count, width = source_ref.shape
    parts = width // LANES
    rows = count // 2

    def group(block, carry):
        first = pl.multiple_of(block * 8, 8)
        for part in range(parts):
            all_ref[pl.ds(first * parts + part, 8, stride=parts), :] = source_ref[
                pl.ds(first, 8), part * LANES:(part + 1) * LANES
            ]
        return carry

    lax.fori_loop(0, count // 8, group, 0, unroll=4)
    unit = 64
    start = place_ref[1] * rows * parts

    def copy(block, carry):
        first = pl.multiple_of(block * unit, unit)
        half_ref[pl.ds(first, unit), :] = all_ref[pl.ds(pl.multiple_of(start + first, unit), unit), :]
        return carry

    lax.fori_loop(0, rows * parts // unit, copy, 0, unroll=4)


def request_kernel(place_ref, lists_ref, self_ref, out_1, out_2, out_3):
    here = place_ref[0]
    line_count = place_ref[6]
    parts = place_ref[7]
    flip = place_ref[1] * (line_count // 2) * parts

    def across(row, above):
        return ((lists_ref[pl.ds(row, 1), :] * parts) ^ flip) + above * line_count * parts

    self_ref[0:1, :] = lists_ref[REACH:REACH + 1, :] * parts
    self_ref[1:2, :] = across(0, 0)
    self_ref[2:3, :] = across(2 * REACH, 1)
    for step, out in ((1, out_1), (2, out_2), (3, out_3)):
        server = lax.rem(here + RING - step, RING)
        above = (here > server).astype(I32)
        out[0:1, :] = lists_ref[pl.ds(server - here + REACH, 1), :] * parts
        out[1:2, :] = across(server - here + 2 * REACH * above, above)


def copy_lines(list_ref, list_row, held, out_ref):
    count = list_ref.shape[1]
    parts = out_ref.shape[0] // count
    unit = 16

    def group(block, carry):
        found = [
            held[pl.ds(pl.multiple_of(list_ref[list_row, block * unit + at], parts), parts), :] for at in range(unit)
        ]
        for at in range(unit):
            place = pl.multiple_of((block * unit + at) * parts, parts)
            out_ref[pl.ds(place, parts), :] = found[at]
        return carry

    lax.fori_loop(0, count // unit, group, 0, unroll=2)


def own_lines_kernel(lists_0, lists_1, lists_2, lists_3, held, out_0, out_1, out_2, out_3):
    for lists, out in ((lists_1, out_1), (lists_2, out_2), (lists_3, out_3), (lists_0, out_0)):
        copy_lines(lists, 0, held, out)


def cross_lines_kernel(
    lists_0, lists_1, lists_2, lists_3, low_a, low_b, high_a, high_b,
    out_low, out_high, out_1, out_2, out_3, held, sems,
):
    size = low_a.shape[0]
    copies = [
        pltpu.make_async_copy(part, held.at[pl.ds(at * size, size)], sems.at[at])
        for at, part in enumerate((low_a, low_b, high_a, high_b))
    ]
    for copy in copies:
        copy.start()
    for copy in copies:
        copy.wait()
    for lists, row, out in (
        (lists_1, 1, out_1), (lists_2, 1, out_2), (lists_3, 1, out_3), (lists_0, 1, out_low), (lists_0, 2, out_high),
    ):
        copy_lines(lists, row, held, out)


def split_parts(value):
    high = value.astype(BF16)
    low = (value - high.astype(F32)).astype(BF16)
    return high, low


def shift_down(value):
    width = value.shape[1]
    lane = lax.broadcasted_iota(I32, value.shape, 1)
    return jnp.where(lane == width - 1, 0.0, pltpu.roll(value, width - 1, 1))


def shift_up(value):
    lane = lax.broadcasted_iota(I32, value.shape, 1)
    return jnp.where(lane == 0, 0.0, pltpu.roll(value, 1, 1))


def corner_parts(scale, depth_part, row_part):
    above, below = scale * depth_part, scale * (1.0 - depth_part)
    rest = 1.0 - row_part
    return below * rest, below * row_part, above * rest, above * row_part


def weight_kernel(fraction_ref, here_ref, ahead_ref):
    line_count, width = fraction_ref.shape[1:]
    rows = 16
    lane = lax.broadcasted_iota(I32, (rows, width), 1)

    def step(block, carry):
        first = pl.multiple_of(block * rows, rows)
        depth_part, row_part, across = [fraction_ref[at, pl.ds(first, rows), :].astype(F32) for at in range(3)]
        here = corner_parts(1.0 - across, depth_part, row_part)
        ahead = corner_parts(
            jnp.where(lane == 0, 0.0, pltpu.roll(across, 1, 1)),
            pltpu.roll(depth_part, 1, 1), pltpu.roll(row_part, 1, 1),
        )
        for corner in range(4):
            here_ref[corner, pl.ds(first, rows), :] = here[corner]
            ahead_ref[corner, pl.ds(first, rows), :] = ahead[corner]
        return carry

    lax.fori_loop(0, line_count // rows, step, 0)


def warp_kernel(*refs):
    slot_ref, here_ref, ahead_ref, image_ref = refs[:4]
    blocks = refs[4:13]
    warped_refs, push_high, push_low = refs[13:15], refs[15], refs[16]
    held, stage_0, stage_1, sems = refs[17:]
    size = blocks[0].shape[0]
    line_count, width = image_ref.shape
    parts = width // LANES
    rows_plane = line_count // 2
    rows = WARP_ROWS
    copies = [
        pltpu.make_async_copy(block, held.at[pl.ds(at * size, size)], sems.at[at])
        for at, block in enumerate(blocks)
    ]
    for copy in copies:
        copy.start()
    for copy in copies:
        copy.wait()

    def gather(block, stage, corner, low, high):
        first = block * rows
        found = []
        for row in range(low, high):
            line = slot_ref[corner, first + row]
            found.append(held[pl.ds(pl.multiple_of(line * parts, parts), parts), :])
        for row in range(low, high):
            at = (corner * rows + row) * parts
            stage[at:at + parts, :] = found[row - low]

    lane = lax.broadcasted_iota(I32, (rows, width), 1)

    def combine(plane, block, stage, following, stage_after):
        first = pl.multiple_of(block * rows, rows)
        near, far = None, None
        for corner in range(4):
            lines = jnp.concatenate(
                [stage[pl.ds(corner * rows * parts + part, rows, stride=parts), :] for part in range(parts)],
                axis=1,
            )
            near_term = here_ref[corner, pl.ds(first, rows), :] * lines
            far_term = ahead_ref[corner, pl.ds(first, rows), :] * lines
            gather(following, stage_after, corner, 0, rows // 2)
            near = near_term if near is None else near + near_term
            far = far_term if far is None else far + far_term
        warped = near + jnp.where(lane == width - 1, 0.0, pltpu.roll(far, width - 1, 1))
        warped_refs[plane][pl.ds(pl.multiple_of(first - plane * rows_plane, rows), rows), :] = warped
        mismatch = warped - image_ref[pl.ds(first, rows), :]
        behind = pltpu.roll(mismatch, 1, 1)
        for corner in range(4):
            here, ahead = here_ref[corner, pl.ds(first, rows), :], ahead_ref[corner, pl.ds(first, rows), :]
            high, low = split_parts(here * mismatch + ahead * behind)
            gather(following, stage_after, corner, rows // 2, rows)
            at = pl.multiple_of(corner * line_count + first, rows)
            push_high[pl.ds(at, rows), :] = high
            push_low[pl.ds(at, rows), :] = low

    blocks_plane = rows_plane // rows
    last = 2 * blocks_plane - 1
    for corner in range(4):
        gather(0, stage_0, corner, 0, rows)
    for plane in range(2):
        def step(pair, carry):
            block = plane * blocks_plane + 2 * pair
            combine(plane, block, stage_0, block + 1, stage_1)
            combine(plane, block + 1, stage_1, jnp.minimum(block + 2, last), stage_0)
            return carry

        lax.fori_loop(0, blocks_plane // 2, step, 0)


def slot_sum_kernel(first, ids_ref, push_high, push_low, *outs):
    capacity = outs[0].shape[0]
    slot = lax.broadcasted_iota(I32, (capacity, push_high.shape[0]), 0)
    for start in range(0, len(outs), 3):
        chosen = outs[start:start + 3]
        hot = jnp.concatenate(
            [
                jnp.where(ids_ref[...] == slot + (first + start + at) * capacity, 1.0, 0.0).astype(BF16)
                for at in range(len(chosen))
            ],
            axis=0,
        )
        summed = jnp.dot(hot, push_high[...], preferred_element_type=F32)
        summed = summed + jnp.dot(hot, push_low[...], preferred_element_type=F32)
        for at, out in enumerate(chosen):
            out[...] = summed[at * capacity:(at + 1) * capacity]


def line_hot_kernel(place_ref, lists_0, lists_1, lists_2, lists_3, rows_ref, own_ref, low_ref, high_ref):
    capacity = lists_0.shape[1]
    line_count, parts = place_ref[6], place_ref[7]
    flip = place_ref[1] * (line_count // 2) * parts
    rows = rows_ref[...] * parts

    def hot(ids):
        return jnp.where(rows == ids, 1.0, 0.0).astype(BF16)

    own_lists = (lists_0[0:1, :], lists_1[0:1, :], lists_2[0:1, :], lists_3[0:1, :])
    cross_lists = (lists_0[1:2, :], lists_0[2:3, :], lists_1[1:2, :], lists_2[1:2, :], lists_3[1:2, :])
    for at, ids in enumerate(own_lists):
        own_ref[:, at * capacity:(at + 1) * capacity] = hot(ids)
    for at, ids in enumerate(cross_lists):
        ids = ids ^ flip
        low_ref[:, at * capacity:(at + 1) * capacity] = hot(ids)
        high_ref[:, at * capacity:(at + 1) * capacity] = hot(ids - line_count * parts)


def line_sums(hot, parts):
    return jnp.dot(hot, parts[0], preferred_element_type=F32) + jnp.dot(hot, parts[1], preferred_element_type=F32)


def own_back_kernel(hot_ref, in_0, in_1, in_2, in_3, keep, send_0, send_1):
    values = split_parts(jnp.concatenate([in_0[...], in_1[...], in_2[...], in_3[...]], axis=0))
    count = keep.shape[0]
    keep[...] = line_sums(hot_ref[:count], values)
    sent = line_sums(hot_ref[count:], values)
    send_0[...] = sent[:count // 2]
    send_1[...] = sent[count // 2:]


def cross_back_kernel(hot_low, hot_high, in_low, in_high, in_1, in_2, in_3, keep_low, keep_high, send):
    values = split_parts(jnp.concatenate([in_low[...], in_high[...], in_1[...], in_2[...], in_3[...]], axis=0))
    count = keep_low.shape[0]
    for at, (hot, keep) in enumerate(((hot_low, keep_low), (hot_high, keep_high))):
        send[at * count:(at + 1) * count] = line_sums(hot[count:], values)
        keep[...] = line_sums(hot[:count], values)


def smooth_kernel(place_ref, before, piece, after, template_ref, out, field):
    device, last, core, chip = place_ref[2], place_ref[3], place_ref[1], place_ref[4]
    size = piece.shape[0]
    rows = size // 2
    total = 3 * size
    zero = jnp.zeros(piece.shape, F32)
    field[0:size, :] = jnp.where(device > 0, before[...], zero)
    field[size:2 * size, :] = piece[...]
    field[2 * size:3 * size, :] = jnp.where(device < last, after[...], zero)
    width = piece.shape[1]
    at = lax.broadcasted_iota(I32, (total, width), 0)
    row = lax.rem(at, rows)
    per_piece = rows - 2 * HALO
    index = core * RING + chip
    row = row + index * per_piece - HALO
    inside = (row >= 0) & (row < 2 * RING * per_piece)
    inside = inside & ((at >= size) | (device > 0)) & ((at < 2 * size) | (device < last))
    current = field[...]
    for repeat in range(SMOOTH):
        beside = pltpu.roll(current, rows, 0) + pltpu.roll(current, total - rows, 0)
        beside = beside + pltpu.roll(current, 1, 0) + pltpu.roll(current, total - 1, 0)
        beside = beside + shift_up(current) + shift_down(current)
        current = current + diffusion * (beside - 6.0 * current)
        if repeat < SMOOTH - 1:
            current = jnp.where(inside, current, 0.0)
    field[...] = current
    subjects = place_ref[5].astype(F32)
    plane_rows = template_ref.shape[0] // 2
    for plane in range(2):
        start = pl.multiple_of(plane * plane_rows + index * per_piece, per_piece)
        found = field[pl.ds(size + plane * rows + HALO, per_piece), :]
        out[plane * per_piece:(plane + 1) * per_piece, :] = (
            template_ref[pl.ds(start, per_piece), :] - found / subjects
        )


def assemble_kernel(place_ref, *refs):
    pieces, out, sems = refs[:2 * RING], refs[2 * RING], refs[2 * RING + 1]
    core, chip = place_ref[1], place_ref[4]
    count = pieces[0].shape[0] // 2
    plane_rows = out.shape[0] // 2
    copies = []
    for at, piece in enumerate(pieces):
        part = core if at < RING else 1 - core
        index = part * RING + lax.rem(chip + RING - at % RING, RING)
        for plane in range(2):
            start = pl.multiple_of(plane * plane_rows + index * count, count)
            copies.append(
                pltpu.make_async_copy(
                    piece.at[pl.ds(plane * count, count)], out.at[pl.ds(start, count)], sems.at[2 * at + plane]
                )
            )
    for copy in copies:
        copy.start()
    for copy in copies:
        copy.wait()


def plane_force_kernel(plane_0, plane_1, image_ref, out, held, sem):
    rows_plane, width = plane_0.shape
    rows = 32
    row = lax.broadcasted_iota(I32, (rows, width), 0)
    for plane, current in enumerate((plane_0, plane_1)):
        def step(block, carry):
            first = pl.multiple_of(block * rows, rows)
            centre = current[pl.ds(first, rows), :]
            negative = image_ref[pl.ds(plane * rows_plane + first, rows), :] - centre
            above = current[pl.ds(jnp.maximum(first - 1, 0), 1), :]
            above = jnp.where(first > 0, above, 0.0)
            below = current[pl.ds(jnp.minimum(first + rows, rows_plane - 1), 1), :]
            below = jnp.where(first + rows < rows_plane, below, 0.0)
            up = jnp.where(row == 0, above, pltpu.roll(centre, 1, 0))
            down = jnp.where(row == rows - 1, below, pltpu.roll(centre, rows - 1, 0))
            held[0, plane, pl.ds(first, rows), :] = negative * (0.5 * (down - up))
            held[1, plane, pl.ds(first, rows), :] = negative * (0.5 * (shift_down(centre) - shift_up(centre)))
            return carry

        lax.fori_loop(0, rows_plane // rows, step, 0)
    copy = pltpu.make_async_copy(held, out.at[pl.ds(1, 2)], sem)
    copy.start()
    copy.wait()


def depth_force_kernel(place_ref, before, plane_0, plane_1, after, image_ref, given, out, held, sem):
    device, last = place_ref[2], place_ref[3]
    rows_plane = plane_0.shape[0]
    rows = 32

    def step(block, carry):
        at = pl.ds(pl.multiple_of(block * rows, rows), rows)
        lower, upper = plane_0[at, :], plane_1[at, :]
        back = jnp.where(device > 0, before[at, :], 0.0)
        ahead = jnp.where(device < last, after[at, :], 0.0)
        image_0 = image_ref[at, :]
        image_1 = image_ref[pl.ds(pl.multiple_of(rows_plane + block * rows, rows), rows), :]
        held[0, 0, at, :] = (image_0 - lower) * (0.5 * (upper - back))
        held[0, 1, at, :] = (image_1 - upper) * (0.5 * (ahead - lower))
        return carry

    lax.fori_loop(0, rows_plane // rows, step, 0)
    copy = pltpu.make_async_copy(held, out.at[pl.ds(0, 1)], sem)
    copy.start()
    copy.wait()


def on_device(template, images, fractions, requests, corners):
    _, plane_count, row_count, cell_count = images.shape
    line_count = plane_count * row_count
    band_count, capacity = requests.shape[2:]
    slab = lax.axis_index("slab")
    subject = lax.axis_index("subj")
    last = lax.axis_size("slab") - 1
    here = slab % RING
    core = subject % 2
    chip = subject // 2
    fixed = [last, lax.axis_size("subj"), line_count, cell_count // LANES]
    place = jnp.stack([here, core, slab, fixed[0], chip, fixed[1], fixed[2], fixed[3]]).astype(I32)
    lists = requests.reshape(band_count, capacity)
    lines = template.reshape(line_count, cell_count)
    parts = cell_count // LANES
    packed = f32s(capacity * parts, LANES)

    spread, plane = call(
        spread_kernel, (f32s(line_count * parts, LANES), f32s(row_count * parts, LANES)), [SMEM, VMEM], (VMEM,) * 2,
    )(place, lines)
    from_low = along_z(plane, 1)
    from_high = along_z(plane, -1)
    message = jax.ShapeDtypeStruct((2, capacity), I32)
    self_lists, *messages = call(
        request_kernel, (jax.ShapeDtypeStruct((3, capacity), I32),) + (message,) * 3, [SMEM, VMEM], (VMEM,) * 4,
    )(place, lists)
    asked = [self_lists] + [along_x(messages[step - 1], -step) for step in (1, 2, 3)]

    own = call(
        own_lines_kernel, (packed,) * 4, [SMEM] * 4 + [VMEM], (VMEM,) * 4,
    )(*asked, spread)
    got_own = [along_x(own[step], step) for step in (1, 2, 3)]
    from_low, from_high, _ = lax.optimization_barrier((from_low, from_high, (got_own[0], got_own[2])))
    from_low_b, from_high_b = other_core(from_low), other_core(from_high)
    cross = call(
        cross_lines_kernel, (packed,) * 5, [SMEM] * 4 + [ANY] * 4, (VMEM,) * 5,
        [pltpu.VMEM((2 * line_count * parts, LANES), F32), pltpu.SemaphoreType.DMA((4,))],
    )(*asked, from_low, from_low_b, from_high, from_high_b)
    got_cross = [along_x(cross[1 + step], step) for step in (1, 2, 3)]

    slot_ids = corners.reshape(4, line_count)
    offset = slot_ids // capacity - REACH
    source = here + offset
    outside = (source < 0) | (source >= RING)
    behind = (here - source) % RING
    held_at = jnp.where(
        behind == 0,
        jnp.where(offset == 0, 8, jnp.where(offset < 0, 3, 4)),
        behind + jnp.where(outside, -1, 4),
    )
    slot_ids = held_at * capacity + slot_ids % capacity
    flat_ids = slot_ids.reshape(1, 4 * line_count)
    blocks = got_cross + [cross[0], cross[1]] + got_own + [own[0]]
    here_part, ahead_part = call(
        weight_kernel, (f32s(4, line_count, cell_count),) * 2, [VMEM], (VMEM,) * 2,
    )(fractions.reshape(3, line_count, cell_count))
    half = f32s(row_count, cell_count)
    push_part = jax.ShapeDtypeStruct((4 * line_count, cell_count), BF16)
    warped_0, warped_1, push_high, push_low = call(
        warp_kernel,
        (half,) * 2 + (push_part,) * 2,
        [SMEM] + [VMEM] * 3 + [ANY] * 9,
        (VMEM,) * 4,
        [
            pltpu.VMEM((band_count * capacity * parts, LANES), F32),
            pltpu.VMEM((4 * WARP_ROWS * parts, LANES), F32),
            pltpu.VMEM((4 * WARP_ROWS * parts, LANES), F32),
            pltpu.SemaphoreType.DMA((9,)),
        ],
    )(slot_ids, here_part, ahead_part, images.reshape(line_count, cell_count), *blocks)

    block = f32s(capacity, cell_count)
    pool_cross = call(
        functools.partial(slot_sum_kernel, 0), (block,) * 5, [VMEM] * 3, (VMEM,) * 5,
    )(flat_ids, push_high, push_low)
    pool_own = call(
        functools.partial(slot_sum_kernel, 5), (block,) * 4, [VMEM] * 3, (VMEM,) * 4,
    )(flat_ids, push_high, push_low)
    back_cross = [along_x(pool_cross[step - 1], -step) for step in (1, 2, 3)]
    back_cross, pool_own = lax.optimization_barrier((back_cross, pool_own))
    back_own = [along_x(pool_own[step - 1], -step) for step in (1, 2, 3)]

    per_piece = row_count // (2 * RING)
    wide = per_piece + 2 * HALO
    at = jnp.arange(2 * RING * 2 * wide, dtype=I32)
    piece = at // (2 * wide)
    part = jnp.where(piece < RING, core, 1 - core)
    index = part * RING + (chip + piece) % RING
    row = index * per_piece - HALO + at % wide
    target = jnp.where((row >= 0) & (row < row_count), at // wide % 2 * row_count + row, -(2**20))
    target = target.reshape(-1, 1)
    core_part = f32s(RING * 2 * wide, cell_count)
    core_rows = core_part.shape[0]
    all_rows = 2 * core_rows
    hot_own, hot_low, hot_high = call(
        line_hot_kernel,
        (jax.ShapeDtypeStruct((all_rows, 4 * capacity), BF16),) + (jax.ShapeDtypeStruct((all_rows, 5 * capacity), BF16),) * 2,
        [SMEM] + [VMEM] * 5, (VMEM,) * 3,
    )(place, *asked, target)
    keep_low, keep_high, send = call(
        cross_back_kernel, (core_part,) * 2 + (f32s(2 * core_rows, cell_count),),
        [VMEM] * 7, (VMEM,) * 3,
    )(hot_low, hot_high, *pool_cross[3:], *back_cross)
    received = other_core(send)
    sum_low = keep_low + received[:core_rows]
    sum_high = keep_high + received[core_rows:]
    in_from_high = along_z(sum_low, -1)
    in_from_low = along_z(sum_high, 1)
    back_own, sum_low, sum_high = lax.optimization_barrier((back_own, sum_low, sum_high))
    size = 2 * wide
    keep_own, *send_own = call(
        own_back_kernel, (core_part,) + (f32s(core_rows // 2, cell_count),) * 2,
        [VMEM] * 5, (VMEM,) * 3,
    )(hot_own, pool_own[3], *back_own)
    got_parts = [other_core(part) for part in send_own]
    pieces = [
        keep_own[at * size:(at + 1) * size]
        + got_parts[at // 2][at % 2 * size:(at % 2 + 1) * size]
        + in_from_high[at * size:(at + 1) * size]
        + in_from_low[at * size:(at + 1) * size]
        for at in range(RING)
    ]
    piece_sum = pieces[0] + along_y(pieces[1], 1) + along_y(pieces[2], 2) + along_y(pieces[3], 3)
    edge_0, edge_1, _ = lax.optimization_barrier((warped_0, warped_1, piece_sum))
    edge_before, edge_after = along_slab(edge_1, 1), along_slab(edge_0, -1)
    before, after = along_slab(piece_sum, 1), along_slab(piece_sum, -1)
    new_piece = call(
        smooth_kernel, f32s(2 * per_piece, cell_count), [SMEM] + [VMEM] * 4, VMEM,
        [pltpu.VMEM((3 * size, cell_count), F32)],
    )(place, before, piece_sum, after, lines)

    image_lines = images.reshape(line_count, cell_count)
    force = f32s(3, plane_count, row_count, cell_count)
    part_force = call(
        plane_force_kernel, force, [VMEM] * 3, ANY,
        [pltpu.VMEM((2, plane_count, row_count, cell_count), F32), pltpu.SemaphoreType.DMA],
    )(warped_0, warped_1, image_lines)
    image_force = call(
        depth_force_kernel, force, [SMEM] + [VMEM] * 5 + [ANY], ANY,
        [pltpu.VMEM((1, plane_count, row_count, cell_count), F32), pltpu.SemaphoreType.DMA], {6: 0},
    )(place, edge_before, warped_0, warped_1, edge_after, image_lines, part_force)
    mine = [new_piece] + [along_y(new_piece, step) for step in (1, 2, 3)]
    theirs = [other_core(value) for value in mine]
    new_template = call(
        assemble_kernel, f32s(line_count, cell_count), [SMEM] + [ANY] * 8, ANY,
        [pltpu.SemaphoreType.DMA((16,))],
    )(place, *mine, *theirs)
    return new_template.reshape(template.shape), image_force[None]


def solution(mesh):
    return jax.shard_map(
        on_device,
        mesh=mesh,
        in_specs=(
            P("slab", None, None),
            P("subj", "slab", None, None),
            P("subj", None, "slab", None, None),
            P("subj", "slab", None, None),
            P("subj", None, "slab", None),
        ),
        out_specs=(P("slab", None, None), P("subj", None, "slab", None, None)),
        check_vma=False,
    )
```

time: 177 us -> 147 us (0.83)
  waiting for transfers between devices: 79.2 us -> 52.8 us
  Pallas kernels: 38.4 us -> 33.8 us
  local copies, waits for them, and re-layouts: 3.85 us -> 5.76 us
    ppermute x8, waiting for transfers between devices: 29.5 us -> 0.02 us  [along_slab(): lax.ppermute(value, 'slab', [(i, (i + step) % count) for i in range(count)])]
    ppermute x9, waiting for transfers between devices: 0.02 us -> 5.93 us  [other_core(): return lax.ppermute(value, 'subj', [(i, i ^ 1) for i in range(count)])]
    ppermute x15, waiting for transfers between devices: 45.1 us -> 39.9 us  [along_x(): return lax.ppermute(value, 'slab', route)]
    pallas_call x6 -> x13, Pallas kernels: 35.6 us -> 31 us  [the longest x1 6.56 us: on_device(): call(warp_kernel, (half,) * 2 + (push_part,) * 2, [SMEM] + [VMEM] * 3 + [...]
    unnamed x10 -> x38, local copies, waits for them, and re-layouts: 1.94 us -> 5.66 us
    ppermute x15, starting transfers between devices: 16.6 us -> 14.2 us  [along_x(): return lax.ppermute(value, 'slab', route)]
    ppermute x6, waiting for transfers between devices: 4.6 us -> 6.94 us  [along_y(): lax.ppermute(value, 'subj', [(i, (i + 2 * step) % count) for i in range(c...]
  transfers between devices with their start and end apart: 38 -> 38, of which waited for: 17 -> 20; matrix products, arithmetic and copies ran while one was open for 1% -> 1% of each run, Pallas kernels for 8% -> 12%
where the time goes in v2:
time: 147 us
  waiting for transfers between devices  52.8 us (36%)
  starting transfers between devices  52.5 us (36%)
  Pallas kernels  33.8 us (23%)
  local copies, waits for them, and re-layouts  5.76 us (4%)
    ppermute x15, waiting for transfers between devices, along_x(): return lax.ppermute(value, 'slab', route)  39.9 us
    ppermute x8, starting transfers between devices, along_slab(): lax.ppermute(value, 'slab', [(i, (i + step) % count) for i in range(count)])  17.9 us
    ppermute x15, starting transfers between devices, along_x(): return lax.ppermute(value, 'slab', route)  14.2 us
    ppermute x9, starting transfers between devices, other_core(): return lax.ppermute(value, 'subj', [(i, i ^ 1) for i in range(count)])  11.1 us
    ppermute x6, starting transfers between devices, along_y(): lax.ppermute(value, 'subj', [(i, (i + 2 * step) % count) for i in range(c...  9.22 us
    ppermute x6, waiting for transfers between devices, along_y(): lax.ppermute(value, 'subj', [(i, (i + 2 * step) % count) for i in range(c...  6.94 us
    pallas_call x1, Pallas kernels, on_device(): call(warp_kernel, (half,) * 2 + (push_part,) * 2, [SMEM] + [VMEM] * 3 + [...  6.56 us
    ppermute x9, waiting for transfers between devices, other_core(): return lax.ppermute(value, 'subj', [(i, i ^ 1) for i in range(count)])  5.93 us
  transfers between devices with their start and end apart: 38, of which 20 were waited for; matrix products, arithmetic and copies ran while one was open for 1% of the time, Pallas kernels for 12%

profile of v2, /device:TPU:1, one launch (start us, length us, event | category | flops | bytes accessed | tf_op | source)
XLA Modules:
  0.0 147.2 jit_solution(17289543818033894664)
XLA Ops:
  0.8 1.2 copy-done.3
  2.8 2.5 %collective-permute-start.3 = (f32[1024,128]{1,0:T(8,128)S(1)}, f32[1024,128]{1,0:T(8,128)S(1)}, u32[]{:S(2)}, u32[]{:S(2)}) collective-permute-start(f32[1024,128]{1,0:T(8,128)S(1)} %get-tuple-element.62), channel_id=1, source_target_pairs={{0,4},{1,5},{2,6},{3,7},{4,8},{5,9},{6,10},{7,11},{8,12},{9,13},{1... | collective-permute-start | bytes 1572872 | tf_op jit(solution)/shard_map/ppermute | solution.py:51
  5.3 4.0 %collective-permute-start.4 = (f32[1024,128]{1,0:T(8,128)S(1)}, f32[1024,128]{1,0:T(8,128)}, u32[]{:S(2)}, u32[]{:S(2)}) collective-permute-start(f32[1024,128]{1,0:T(8,128)S(1)} %get-tuple-element.62), channel_id=1, source_target_pairs={{0,28},{1,29},{2,30},{3,31},{4,0},{5,1},{6,2},{7,3},{8,4},{9,5},{1... | collective-permute-start | bytes 1572872 | tf_op jit(solution)/shard_map/ppermute | solution.py:51
  10.6 2.6 %collective-permute-start = (s32[2,128]{1,0:T(2,128)S(1)}, s32[2,128]{1,0:T(2,128)S(1)}, u32[]{:S(2)}, u32[]{:S(2)}) collective-permute-start(s32[2,128]{1,0:T(2,128)S(1)} %get-tuple-element.56), channel_id=1, source_target_pairs={{0,3},{1,0},{2,1},{3,2},{4,7},{5,4},{6,5},{7,6},{8,11},{9,8},{10,9... | collective-permute-start | bytes 3080 | tf_op jit(solution)/shard_map/ppermute | solution.py:46
  14.3 2.8 %collective-permute-done.1.lists_2 = s32[2,128]{1,0:T(2,128)S(1)} collective-permute-done((s32[2,128]{1,0:T(2,128)S(1)}, s32[2,128]{1,0:T(2,128)S(1)}, u32[]{:S(2)}, u32[]{:S(2)}) %collective-permute-start.1) | collective-permute-done | bytes 1056 | tf_op jit(solution)/shard_map/ppermute | solution.py:46
  17.6 1.1 shard_map.72
  18.8 2.7 %collective-permute-start.6 = (f32[512,128]{1,0:T(8,128)S(1)}, f32[512,128]{1,0:T(8,128)S(1)}, u32[]{:S(2)}, u32[]{:S(2)}) collective-permute-start(f32[512,128]{1,0:T(8,128)S(1)} %get-tuple-element.65), channel_id=1, source_target_pairs={{0,3},{1,0},{2,1},{3,2},{4,7},{5,4},{6,5},{7,6},{8,11},{9,8},{10,9... | collective-permute-start | bytes 786440 | tf_op jit(solution)/shard_map/ppermute | solution.py:46
  21.5 3.8 %collective-permute-done.5.refs_9_ = f32[512,128]{1,0:T(8,128)S(1)} collective-permute-done((f32[512,128]{1,0:T(8,128)S(1)}, f32[512,128]{1,0:T(8,128)S(1)}, u32[]{:S(2)}, u32[]{:S(2)}) %collective-permute-start.5) | collective-permute-done | bytes 262176 | tf_op jit(solution)/shard_map/ppermute | solution.py:46
  26.6 3.6 %collective-permute-start.7 = (f32[1024,128]{1,0:T(8,128)S(1)}, f32[1024,128]{1,0:T(8,128)}, u32[]{:S(2)}, u32[]{:S(2)}) collective-permute-start(f32[1024,128]{1,0:T(8,128)S(1)} %collective-permute-done.3.low_a), channel_id=1, source_target_pairs={{0,32},{32,0},{64,96},{96,64},{128,160},{160,128},{192,224},{224,1... | collective-permute-start | bytes 1572872 | tf_op jit(solution)/shard_map/ppermute | solution.py:60
  31.0 1.0 collective-permute-done.7.low_b
  31.9 1.0 collective-permute-done.8.high_b
  32.9 3.5 %shard_map.73 = (f32[512,128]{1,0:T(8,128)S(1)}, f32[512,128]{1,0:T(8,128)S(1)}, f32[512,128]{1,0:T(8,128)S(1)}, f32[512,128]{1,0:T(8,128)S(1)}, f32[512,128]{1,0:T(8,128)S(1)}) custom-call(s32[3,128]{1,0:T(4,128)S(1)} %get-tuple-element.55.lists_0, s32[2,128]{1,0:T(2,128)S(1)} %collective-permute-done.lists_1, s32[2,128]{1,0:T(2,128)S(1)} %collective-permute-done.1.lists_2, ...), custom_call_target="tpu_custom_call" | custom-call | tf_op jit(solution)/shard_map/pallas_call | solution.py:464
  37.0 2.2 %collective-permute-start.11 = (f32[512,128]{1,0:T(8,128)S(1)}, f32[512,128]{1,0:T(8,128)S(1)}, u32[]{:S(2)}, u32[]{:S(2)}) collective-permute-start(f32[512,128]{1,0:T(8,128)S(1)} %get-tuple-element.70), channel_id=1, source_target_pairs={{0,3},{1,0},{2,1},{3,2},{4,7},{5,4},{6,5},{7,6},{8,11},{9,8},{10,9... | collective-permute-start | bytes 786440 | tf_op jit(solution)/shard_map/ppermute | solution.py:46
  39.4 3.0 %shard_map.70 = (f32[4,512,512]{2,1,0:T(8,128)S(1)}, f32[4,512,512]{2,1,0:T(8,128)S(1)}) custom-call(bf16[3,512,512]{2,1,0:T(8,128)(2,1)S(1)} %bitcast.20), custom_call_target="tpu_custom_call" | custom-call | tf_op jit(solution)/shard_map/pallas_call | solution.py:483
  42.5 3.0 %collective-permute-done.10.refs_5_ = f32[512,128]{1,0:T(8,128)S(1)} collective-permute-done((f32[512,128]{1,0:T(8,128)S(1)}, f32[512,128]{1,0:T(8,128)S(1)}, u32[]{:S(2)}, u32[]{:S(2)}) %collective-permute-start.10) | collective-permute-done | bytes 262176 | tf_op jit(solution)/shard_map/ppermute | solution.py:46
  45.5 5.5 %collective-permute-done.11.refs_6_ = f32[512,128]{1,0:T(8,128)S(1)} collective-permute-done((f32[512,128]{1,0:T(8,128)S(1)}, f32[512,128]{1,0:T(8,128)S(1)}, u32[]{:S(2)}, u32[]{:S(2)}) %collective-permute-start.11) | collective-permute-done | bytes 262176 | tf_op jit(solution)/shard_map/ppermute | solution.py:46
  51.8 6.6 %shard_map.74 = (f32[256,512]{1,0:T(8,128)S(1)}, f32[256,512]{1,0:T(8,128)S(1)}, bf16[2048,512]{1,0:T(8,128)(2,1)S(1)}, bf16[2048,512]{1,0:T(8,128)(2,1)S(1)}) custom-call(s32[4,512]{1,0:T(4,128)S(1)} %fusion.23.refs_0_, f32[4,512,512]{2,1,0:T(8,128)S(1)} %get-tuple-element.60.refs_1_, f32[4,512,512]{2,1,0:T(8,128)S(1)} %get-tuple-element.61.refs_2_, ...), custom_call_target="tpu_custom_call" | custom-call | tf_op jit(solution)/shard_map/pallas_call | solution.py:488
  58.4 3.5 %shard_map.75 = (f32[128,512]{1,0:T(8,128)}, f32[128,512]{1,0:T(8,128)}, f32[128,512]{1,0:T(8,128)}, f32[128,512]{1,0:T(8,128)S(1)}, f32[128,512]{1,0:T(8,128)S(1)}) custom-call(s32[1,2048]{1,0:T(1,128)S(1)} %fusion.20.ids_ref, bf16[2048,512]{1,0:T(8,128)(2,1)S(1)} %get-tuple-element.75.push_high, bf16[2048,512]{1,0:T(8,128)(2,1)S(1)} %get-tuple-element.76.push_low), custom_call_target="tpu_custom_call" | custom-call | tf_op jit(solution)/shard_map/pallas_call | solution.py:502
  62.6 2.3 %collective-permute-start.13 = (f32[128,512]{1,0:T(8,128)}, f32[128,512]{1,0:T(8,128)}, u32[]{:S(2)}, u32[]{:S(2)}) collective-permute-start(f32[128,512]{1,0:T(8,128)} %get-tuple-element.77), channel_id=1, source_target_pairs={{0,3},{1,0},{2,1},{3,2},{4,7},{5,4},{6,5},{7,6},{8,11},{9,8},{10,9... | collective-permute-start | bytes 786440 | tf_op jit(solution)/shard_map/ppermute | solution.py:46
  65.9 1.0 shard_map.69
  66.9 1.6 %copy-done.2 = bf16[2048,512]{1,0:T(8,128)(2,1)S(1)} copy-done((bf16[2048,512]{1,0:T(8,128)(2,1)S(1)}, bf16[2048,512]{1,0:T(8,128)(2,1)}, u32[]{:S(2)}) %copy-start.2) | copy-done | bytes 2097176
  68.5 2.3 %shard_map.76 = (f32[128,512]{1,0:T(8,128)S(1)}, f32[128,512]{1,0:T(8,128)S(1)}, f32[128,512]{1,0:T(8,128)S(1)}, f32[128,512]{1,0:T(8,128)S(1)}) custom-call(s32[1,2048]{1,0:T(1,128)S(1)} %fusion.20.ids_ref, bf16[2048,512]{1,0:T(8,128)(2,1)S(1)} %get-tuple-element.75.push_high, bf16[2048,512]{1,0:T(8,128)(2,1)S(1)} %copy-done.2), custom_call_target="tpu_custom_call" | custom-call | tf_op jit(solution)/shard_map/pallas_call | solution.py:505
  70.9 2.9 %collective-permute-done.14.in_2 = f32[128,512]{1,0:T(8,128)} collective-permute-done((f32[128,512]{1,0:T(8,128)}, f32[128,512]{1,0:T(8,128)}, u32[]{:S(2)}, u32[]{:S(2)}) %collective-permute-start.14) | collective-permute-done | bytes 262176 | tf_op jit(solution)/shard_map/ppermute | solution.py:46
  73.8 6.1 %collective-permute-done.15.in_3 = f32[128,512]{1,0:T(8,128)} collective-permute-done((f32[128,512]{1,0:T(8,128)}, f32[128,512]{1,0:T(8,128)}, u32[]{:S(2)}, u32[]{:S(2)}) %collective-permute-start.15) | collective-permute-done | bytes 262176 | tf_op jit(solution)/shard_map/ppermute | solution.py:46
  79.9 3.1 %shard_map.77 = (f32[288,512]{1,0:T(8,128)S(1)}, f32[288,512]{1,0:T(8,128)S(1)}, f32[576,512]{1,0:T(8,128)S(1)}) custom-call(bf16[576,640]{1,0:T(8,128)(2,1)S(1)} %get-tuple-element.88.hot_low, bf16[576,640]{1,0:T(8,128)(2,1)S(1)} %get-tuple-element.89.hot_high, f32[128,512]{1,0:T(8,128)S(1)} %get-tuple-element.90.in_low, f32[128,512]{1,0:T(8,128)S(1)} %copy-done.15, ...), custom_call_target="tpu_custom_call" | custom-call | tf_op jit(solution)/shard_map/pallas_call | solution.py:529
  83.0 0.9 collective-permute-start.19
  83.9 2.5 %collective-permute-done.19 = f32[576,512]{1,0:T(8,128)S(1)} collective-permute-done((f32[576,512]{1,0:T(8,128)S(1)}, f32[576,512]{1,0:T(8,128)S(1)}, u32[]{:S(2)}, u32[]{:S(2)}) %collective-permute-start.19) | collective-permute-done | bytes 1179680 | tf_op jit(solution)/shard_map/ppermute | solution.py:60
  86.7 1.7 %collective-permute-start.21 = (f32[288,512]{1,0:T(8,128)S(1)}, f32[288,512]{1,0:T(8,128)S(1)}, u32[]{:S(2)}, u32[]{:S(2)}) collective-permute-start(f32[288,512]{1,0:T(8,128)S(1)} %get-tuple-element.111), channel_id=1, source_target_pairs={{0,28},{1,29},{2,30},{3,31},{4,0},{5,1},{6,2},{7,3},{8,4},{9,5},{1... | collective-permute-start | bytes 1769480 | tf_op jit(solution)/shard_map/ppermute | solution.py:51
  89.9 5.6 %collective-permute-done.16.in_1 = f32[128,512]{1,0:T(8,128)S(1)} collective-permute-done((f32[128,512]{1,0:T(8,128)S(1)}, f32[128,512]{1,0:T(8,128)S(1)}, u32[]{:S(2)}, u32[]{:S(2)}) %collective-permute-start.16) | collective-permute-done | bytes 262176 | tf_op jit(solution)/shard_map/ppermute | solution.py:46
  95.5 1.9 %collective-permute-done.17.in_2 = f32[128,512]{1,0:T(8,128)S(1)} collective-permute-done((f32[128,512]{1,0:T(8,128)S(1)}, f32[128,512]{1,0:T(8,128)S(1)}, u32[]{:S(2)}, u32[]{:S(2)}) %collective-permute-start.17) | collective-permute-done | bytes 262176 | tf_op jit(solution)/shard_map/ppermute | solution.py:46
  97.3 7.0 %collective-permute-done.18.in_3 = f32[128,512]{1,0:T(8,128)S(1)} collective-permute-done((f32[128,512]{1,0:T(8,128)S(1)}, f32[128,512]{1,0:T(8,128)S(1)}, u32[]{:S(2)}, u32[]{:S(2)}) %collective-permute-start.18) | collective-permute-done | bytes 262176 | tf_op jit(solution)/shard_map/ppermute | solution.py:46
  105.9 1.1 collective-permute-done.20
  107.6 1.4 collective-permute-start.23
  109.0 2.6 %collective-permute-start.25 = (f32[72,512]{1,0:T(8,128)S(1)}, f32[72,512]{1,0:T(8,128)S(1)}, u32[]{:S(2)}, u32[]{:S(2)}) collective-permute-start(f32[72,512]{1,0:T(8,128)S(1)} %get-tuple-element.108), channel_id=1, source_target_pairs={{0,128},{32,160},{64,192},{96,224},{128,0},{160,32},{192,64},{224,... | collective-permute-start | bytes 442376 | tf_op jit(solution)/shard_map/ppermute | solution.py:65
  111.6 1.1 collective-permute-start.26
  112.7 1.4 collective-permute-done.23
  114.1 4.3 %collective-permute-done.25 = f32[72,512]{1,0:T(8,128)S(1)} collective-permute-done((f32[72,512]{1,0:T(8,128)S(1)}, f32[72,512]{1,0:T(8,128)S(1)}, u32[]{:S(2)}, u32[]{:S(2)}) %collective-permute-start.25) | collective-permute-done | bytes 147488 | tf_op jit(solution)/shard_map/ppermute | solution.py:65
  118.6 4.8 %collective-permute-start.28 = (f32[72,512]{1,0:T(8,128)S(1)}, f32[72,512]{1,0:T(8,128)S(1)}, u32[]{:S(2)}, u32[]{:S(2)}) collective-permute-start(f32[72,512]{1,0:T(8,128)S(1)} %fusion.18.piece), channel_id=1, source_target_pairs={{0,31},{1,0},{2,1},{3,2},{4,3},{5,4},{6,5},{7,6},{8,7},{9,8},{10,9... | collective-permute-start | bytes 442376 | tf_op jit(solution)/shard_map/ppermute | solution.py:51
  123.4 4.8 %collective-permute-start.37 = (f32[256,512]{1,0:T(8,128)S(1)}, f32[256,512]{1,0:T(8,128)S(1)}, u32[]{:S(2)}, u32[]{:S(2)}) collective-permute-start(f32[256,512]{1,0:T(8,128)S(1)} %copy-done.6), channel_id=1, source_target_pairs={{0,31},{1,0},{2,1},{3,2},{4,3},{5,4},{6,5},{7,6},{8,7},{9,8},{10,9... | collective-permute-start | bytes 1572872 | tf_op jit(solution)/shard_map/ppermute | solution.py:51
  128.1 1.2 shard_map.79.refs_0_
  129.3 1.0 collective-permute-start.29
  130.4 2.4 %collective-permute-start.30 = (f32[64,512]{1,0:T(8,128)S(1)}, f32[64,512]{1,0:T(8,128)S(1)}, u32[]{:S(2)}, u32[]{:S(2)}) collective-permute-start(f32[64,512]{1,0:T(8,128)S(1)} %shard_map.79.refs_0_), channel_id=1, source_target_pairs={{0,128},{32,160},{64,192},{96,224},{128,0},{160,32},{192,64},{224,... | collective-permute-start | bytes 393224 | tf_op jit(solution)/shard_map/ppermute | solution.py:65
  133.5 1.2 collective-permute-done.29.refs_1_
  134.7 3.8 %collective-permute-start.32 = (f32[64,512]{1,0:T(8,128)S(1)}, f32[64,512]{1,0:T(8,128)S(1)}, u32[]{:S(2)}, u32[]{:S(2)}) collective-permute-start(f32[64,512]{1,0:T(8,128)S(1)} %shard_map.79.refs_0_), channel_id=1, source_target_pairs={{0,32},{32,0},{64,96},{96,64},{128,160},{160,128},{192,224},{224,1... | collective-permute-start | bytes 393224 | tf_op jit(solution)/shard_map/ppermute | solution.py:60
  138.6 1.4 collective-permute-start.33
  140.5 3.0 %shard_map.81.given = f32[3,2,256,512]{3,2,1,0:T(8,128)} custom-call(f32[256,512]{1,0:T(8,128)S(1)} %copy-done.6, f32[256,512]{1,0:T(8,128)S(1)} %copy-done.8, f32[512,512]{1,0:T(8,128)S(1)} %bitcast.16), custom_call_target="tpu_custom_call" | custom-call | tf_op jit(solution)/shard_map/pallas_call | solution.py:563
  143.6 1.6 %shard_map.80 = f32[512,512]{1,0:T(8,128)} custom-call(s32[8]{0:T(128)S(1)} %stack.19.place_ref, f32[64,512]{1,0:T(8,128)S(1)} %shard_map.79.refs_0_, f32[64,512]{1,0:T(8,128)S(1)} %collective-permute-done.29.refs_1_, f32[64,512]{1,0:T(8,128)S(1)} %collective-permute-done.30.refs_2_, f32[64,512]{1,0:T(8,128)S(1)} %collective-permute-done.31.refs_3_, ...), custom_call_target="tpu_custom_call" | custom-call | tf_op jit(solution)/shard_map/pallas_call | solution.py:573
  145.2 1.8 %shard_map.82 = f32[3,2,256,512]{3,2,1,0:T(8,128)} custom-call(s32[8]{0:T(128)S(1)} %stack.19.place_ref, f32[256,512]{1,0:T(8,128)S(1)} %collective-permute-done.36.before, f32[256,512]{1,0:T(8,128)S(1)} %copy-done.6, f32[256,512]{1,0:T(8,128)S(1)} %copy-done.8, f32[256,512]{1,0:T(8,128)S(1)} %collective-permute-done.37.after, ...), custom_call_target="tpu_custom_call", output_to_operand_aliasing={{}: (6, {})} | custom-call | tf_op jit(solution)/shard_map/pallas_call | solution.py:567
  (89 shorter events, 14.8 us)
Async XLA Ops:
  0.6 29.7 %copy-start.17 = (s32[1,4,2,256]{3,2,1,0:T(2,128)S(1)}, s32[1,4,2,256]{3,2,1,0:T(2,128)}, u32[]{:S(2)}) copy-start(s32[1,4,2,256]{3,2,1,0:T(2,128)} %param.9) | copy-start | bytes 24580
  2.0 37.4 %copy-start.9 = (bf16[1,3,2,256,512]{4,3,2,1,0:T(8,128)(2,1)S(1)}, bf16[1,3,2,256,512]{4,3,2,1,0:T(8,128)(2,1)}, u32[]{:S(2)}) copy-start(bf16[1,3,2,256,512]{4,3,2,1,0:T(8,128)(2,1)} %param.7) | copy-start | bytes 4718596
  2.8 23.9 %collective-permute-start.3 = (f32[1024,128]{1,0:T(8,128)S(1)}, f32[1024,128]{1,0:T(8,128)S(1)}, u32[]{:S(2)}, u32[]{:S(2)}) collective-permute-start(f32[1024,128]{1,0:T(8,128)S(1)} %get-tuple-element.62), channel_id=1, source_target_pairs={{0,4},{1,5},{2,6},{3,7},{4,8},{5,9},{6,10},{7,11},{8,12},{9,13},{1... | collective-permute-start | bytes 1572872 | tf_op jit(solution)/shard_map/ppermute | solution.py:51
  5.3 21.3 %collective-permute-start.4 = (f32[1024,128]{1,0:T(8,128)S(1)}, f32[1024,128]{1,0:T(8,128)}, u32[]{:S(2)}, u32[]{:S(2)}) collective-permute-start(f32[1024,128]{1,0:T(8,128)S(1)} %get-tuple-element.62), channel_id=1, source_target_pairs={{0,28},{1,29},{2,30},{3,31},{4,0},{5,1},{6,2},{7,3},{8,4},{9,5},{1... | collective-permute-start | bytes 1572872 | tf_op jit(solution)/shard_map/ppermute | solution.py:51
  10.6 3.7 %collective-permute-start = (s32[2,128]{1,0:T(2,128)S(1)}, s32[2,128]{1,0:T(2,128)S(1)}, u32[]{:S(2)}, u32[]{:S(2)}) collective-permute-start(s32[2,128]{1,0:T(2,128)S(1)} %get-tuple-element.56), channel_id=1, source_target_pairs={{0,3},{1,0},{2,1},{3,2},{4,7},{5,4},{6,5},{7,6},{8,11},{9,8},{10,9... | collective-permute-start | bytes 3080 | tf_op jit(solution)/shard_map/ppermute | solution.py:46
  13.2 3.9 %collective-permute-start.1 = (s32[2,128]{1,0:T(2,128)S(1)}, s32[2,128]{1,0:T(2,128)S(1)}, u32[]{:S(2)}, u32[]{:S(2)}) collective-permute-start(s32[2,128]{1,0:T(2,128)S(1)} %get-tuple-element.57), channel_id=1, source_target_pairs={{0,2},{1,3},{2,0},{3,1},{4,6},{5,7},{6,4},{7,5},{8,10},{9,11},{10,... | collective-permute-start | bytes 3080 | tf_op jit(solution)/shard_map/ppermute | solution.py:46
  13.7 3.9 %collective-permute-start.2 = (s32[2,128]{1,0:T(2,128)S(1)}, s32[2,128]{1,0:T(2,128)S(1)}, u32[]{:S(2)}, u32[]{:S(2)}) collective-permute-start(s32[2,128]{1,0:T(2,128)S(1)} %get-tuple-element.58), channel_id=1, source_target_pairs={{0,1},{1,2},{2,3},{3,0},{4,5},{5,6},{6,7},{7,4},{8,9},{9,10},{10,1... | collective-permute-start | bytes 3080 | tf_op jit(solution)/shard_map/ppermute | solution.py:46
  18.7 7.9 %copy-start.16 = (f32[512,128]{1,0:T(8,128)}, f32[512,128]{1,0:T(8,128)S(1)}, u32[]{:S(2)}) copy-start(f32[512,128]{1,0:T(8,128)S(1)} %get-tuple-element.73) | copy-start | bytes 786436
  18.7 33.1 %copy-start = (f32[1,2,256,512]{3,2,1,0:T(8,128)S(1)}, f32[1,2,256,512]{3,2,1,0:T(8,128)}, u32[]{:S(2)}) copy-start(f32[1,2,256,512]{3,2,1,0:T(8,128)} %param.6) | copy-start | bytes 3145732
  18.7 6.5 %collective-permute-start.5 = (f32[512,128]{1,0:T(8,128)S(1)}, f32[512,128]{1,0:T(8,128)S(1)}, u32[]{:S(2)}, u32[]{:S(2)}) collective-permute-start(f32[512,128]{1,0:T(8,128)S(1)} %get-tuple-element.64), channel_id=1, source_target_pairs={{0,1},{1,2},{2,3},{3,0},{4,5},{5,6},{6,7},{7,4},{8,9},{9,10},{10,1... | collective-permute-start | bytes 786440 | tf_op jit(solution)/shard_map/ppermute | solution.py:46
  18.8 7.1 %collective-permute-start.6 = (f32[512,128]{1,0:T(8,128)S(1)}, f32[512,128]{1,0:T(8,128)S(1)}, u32[]{:S(2)}, u32[]{:S(2)}) collective-permute-start(f32[512,128]{1,0:T(8,128)S(1)} %get-tuple-element.65), channel_id=1, source_target_pairs={{0,3},{1,0},{2,1},{3,2},{4,7},{5,4},{6,5},{7,6},{8,11},{9,8},{10,9... | collective-permute-start | bytes 786440 | tf_op jit(solution)/shard_map/ppermute | solution.py:46
  26.6 5.3 %collective-permute-start.7 = (f32[1024,128]{1,0:T(8,128)S(1)}, f32[1024,128]{1,0:T(8,128)}, u32[]{:S(2)}, u32[]{:S(2)}) collective-permute-start(f32[1024,128]{1,0:T(8,128)S(1)} %collective-permute-done.3.low_a), channel_id=1, source_target_pairs={{0,32},{32,0},{64,96},{96,64},{128,160},{160,128},{192,224},{224,1... | collective-permute-start | bytes 1572872 | tf_op jit(solution)/shard_map/ppermute | solution.py:60
  30.3 2.6 %collective-permute-start.8 = (f32[1024,128]{1,0:T(8,128)}, f32[1024,128]{1,0:T(8,128)}, u32[]{:S(2)}, u32[]{:S(2)}) collective-permute-start(f32[1024,128]{1,0:T(8,128)} %collective-permute-done.4.high_a), channel_id=1, source_target_pairs={{0,32},{32,0},{64,96},{96,64},{128,160},{160,128},{192,224},{224,1... | collective-permute-start | bytes 1572872 | tf_op jit(solution)/shard_map/ppermute | solution.py:60
  30.4 21.4 %copy-start.11 = (f32[512,128]{1,0:T(8,128)S(1)}, f32[512,128]{1,0:T(8,128)}, u32[]{:S(2)}) copy-start(f32[512,128]{1,0:T(8,128)} %copy-done.10) | copy-start | bytes 786436
  30.4 21.4 %copy-start.13 = (f32[512,128]{1,0:T(8,128)S(1)}, f32[512,128]{1,0:T(8,128)}, u32[]{:S(2)}) copy-start(f32[512,128]{1,0:T(8,128)} %copy-done.12) | copy-start | bytes 786436
  30.4 12.1 %collective-permute-start.12 = (f32[512,128]{1,0:T(8,128)}, f32[512,128]{1,0:T(8,128)S(1)}, u32[]{:S(2)}, u32[]{:S(2)}) collective-permute-start(f32[512,128]{1,0:T(8,128)} %copy-done.16), channel_id=1, source_target_pairs={{0,2},{1,3},{2,0},{3,1},{4,6},{5,7},{6,4},{7,5},{8,10},{9,11},{10,... | collective-permute-start | bytes 786440 | tf_op jit(solution)/shard_map/ppermute | solution.py:46
  36.4 9.2 %collective-permute-start.10 = (f32[512,128]{1,0:T(8,128)S(1)}, f32[512,128]{1,0:T(8,128)S(1)}, u32[]{:S(2)}, u32[]{:S(2)}) collective-permute-start(f32[512,128]{1,0:T(8,128)S(1)} %get-tuple-element.69), channel_id=1, source_target_pairs={{0,2},{1,3},{2,0},{3,1},{4,6},{5,7},{6,4},{7,5},{8,10},{9,11},{10,... | collective-permute-start | bytes 786440 | tf_op jit(solution)/shard_map/ppermute | solution.py:46
  37.0 14.0 %collective-permute-start.11 = (f32[512,128]{1,0:T(8,128)S(1)}, f32[512,128]{1,0:T(8,128)S(1)}, u32[]{:S(2)}, u32[]{:S(2)}) collective-permute-start(f32[512,128]{1,0:T(8,128)S(1)} %get-tuple-element.70), channel_id=1, source_target_pairs={{0,3},{1,0},{2,1},{3,2},{4,7},{5,4},{6,5},{7,6},{8,11},{9,8},{10,9... | collective-permute-start | bytes 786440 | tf_op jit(solution)/shard_map/ppermute | solution.py:46
  39.3 12.5 %collective-permute-start.9 = (f32[512,128]{1,0:T(8,128)S(1)}, f32[512,128]{1,0:T(8,128)S(1)}, u32[]{:S(2)}, u32[]{:S(2)}) collective-permute-start(f32[512,128]{1,0:T(8,128)S(1)} %get-tuple-element.68), channel_id=1, source_target_pairs={{0,1},{1,2},{2,3},{3,0},{4,5},{5,6},{6,7},{7,4},{8,9},{9,10},{10,1... | collective-permute-start | bytes 786440 | tf_op jit(solution)/shard_map/ppermute | solution.py:46
  62.6 8.3 %collective-permute-start.13 = (f32[128,512]{1,0:T(8,128)}, f32[128,512]{1,0:T(8,128)}, u32[]{:S(2)}, u32[]{:S(2)}) collective-permute-start(f32[128,512]{1,0:T(8,128)} %get-tuple-element.77), channel_id=1, source_target_pairs={{0,3},{1,0},{2,1},{3,2},{4,7},{5,4},{6,5},{7,6},{8,11},{9,8},{10,9... | collective-permute-start | bytes 786440 | tf_op jit(solution)/shard_map/ppermute | solution.py:46
  64.8 9.0 %collective-permute-start.14 = (f32[128,512]{1,0:T(8,128)}, f32[128,512]{1,0:T(8,128)}, u32[]{:S(2)}, u32[]{:S(2)}) collective-permute-start(f32[128,512]{1,0:T(8,128)} %get-tuple-element.78), channel_id=1, source_target_pairs={{0,2},{1,3},{2,0},{3,1},{4,6},{5,7},{6,4},{7,5},{8,10},{9,11},{10,... | collective-permute-start | bytes 786440 | tf_op jit(solution)/shard_map/ppermute | solution.py:46
  64.9 15.0 %collective-permute-start.15 = (f32[128,512]{1,0:T(8,128)}, f32[128,512]{1,0:T(8,128)}, u32[]{:S(2)}, u32[]{:S(2)}) collective-permute-start(f32[128,512]{1,0:T(8,128)} %get-tuple-element.79), channel_id=1, source_target_pairs={{0,1},{1,2},{2,3},{3,0},{4,5},{5,6},{6,7},{7,4},{8,9},{9,10},{10,1... | collective-permute-start | bytes 786440 | tf_op jit(solution)/shard_map/ppermute | solution.py:46
  68.5 11.4 %copy-start.15 = (f32[128,512]{1,0:T(8,128)S(1)}, f32[128,512]{1,0:T(8,128)}, u32[]{:S(2)}) copy-start(f32[128,512]{1,0:T(8,128)} %copy-done.14) | copy-start | bytes 786436
  83.0 3.4 %collective-permute-start.19 = (f32[576,512]{1,0:T(8,128)S(1)}, f32[576,512]{1,0:T(8,128)S(1)}, u32[]{:S(2)}, u32[]{:S(2)}) collective-permute-start(f32[576,512]{1,0:T(8,128)S(1)} %get-tuple-element.96), channel_id=1, source_target_pairs={{0,32},{32,0},{64,96},{96,64},{128,160},{160,128},{192,224},{224,1... | collective-permute-start | bytes 3538952 | tf_op jit(solution)/shard_map/ppermute | solution.py:60
  86.7 20.8 %collective-permute-start.21 = (f32[288,512]{1,0:T(8,128)S(1)}, f32[288,512]{1,0:T(8,128)S(1)}, u32[]{:S(2)}, u32[]{:S(2)}) collective-permute-start(f32[288,512]{1,0:T(8,128)S(1)} %get-tuple-element.111), channel_id=1, source_target_pairs={{0,28},{1,29},{2,30},{3,31},{4,0},{5,1},{6,2},{7,3},{8,4},{9,5},{1... | collective-permute-start | bytes 1769480 | tf_op jit(solution)/shard_map/ppermute | solution.py:51
  88.4 19.0 %collective-permute-start.22 = (f32[288,512]{1,0:T(8,128)S(1)}, f32[288,512]{1,0:T(8,128)S(1)}, u32[]{:S(2)}, u32[]{:S(2)}) collective-permute-start(f32[288,512]{1,0:T(8,128)S(1)} %get-tuple-element.112), channel_id=1, source_target_pairs={{0,4},{1,5},{2,6},{3,7},{4,8},{5,9},{6,10},{7,11},{8,12},{9,13},{1... | collective-permute-start | bytes 1769480 | tf_op jit(solution)/shard_map/ppermute | solution.py:51
  88.4 7.1 %collective-permute-start.16 = (f32[128,512]{1,0:T(8,128)S(1)}, f32[128,512]{1,0:T(8,128)S(1)}, u32[]{:S(2)}, u32[]{:S(2)}) collective-permute-start(f32[128,512]{1,0:T(8,128)S(1)} %get-tuple-element.85), channel_id=1, source_target_pairs={{0,3},{1,0},{2,1},{3,2},{4,7},{5,4},{6,5},{7,6},{8,11},{9,8},{10,9... | collective-permute-start | bytes 786440 | tf_op jit(solution)/shard_map/ppermute | solution.py:46
  89.0 8.3 %collective-permute-start.17 = (f32[128,512]{1,0:T(8,128)S(1)}, f32[128,512]{1,0:T(8,128)S(1)}, u32[]{:S(2)}, u32[]{:S(2)}) collective-permute-start(f32[128,512]{1,0:T(8,128)S(1)} %get-tuple-element.86), channel_id=1, source_target_pairs={{0,2},{1,3},{2,0},{3,1},{4,6},{5,7},{6,4},{7,5},{8,10},{9,11},{10,... | collective-permute-start | bytes 786440 | tf_op jit(solution)/shard_map/ppermute | solution.py:46
  89.0 15.3 %collective-permute-start.18 = (f32[128,512]{1,0:T(8,128)S(1)}, f32[128,512]{1,0:T(8,128)S(1)}, u32[]{:S(2)}, u32[]{:S(2)}) collective-permute-start(f32[128,512]{1,0:T(8,128)S(1)} %get-tuple-element.87), channel_id=1, source_target_pairs={{0,1},{1,2},{2,3},{3,0},{4,5},{5,6},{6,7},{7,4},{8,9},{9,10},{10,1... | collective-permute-start | bytes 786440 | tf_op jit(solution)/shard_map/ppermute | solution.py:46
  105.2 18.2 %copy-start.8 = (f32[256,512]{1,0:T(8,128)S(1)}, f32[256,512]{1,0:T(8,128)}, u32[]{:S(2)}) copy-start(f32[256,512]{1,0:T(8,128)} %copy-done.7) | copy-start | bytes 1572868
  105.2 18.2 %copy-start.6 = (f32[256,512]{1,0:T(8,128)S(1)}, f32[256,512]{1,0:T(8,128)}, u32[]{:S(2)}) copy-start(f32[256,512]{1,0:T(8,128)} %copy-done.5) | copy-start | bytes 1572868
  105.2 22.9 %copy-start.4 = (f32[2,256,512]{2,1,0:T(8,128)S(1)}, f32[2,256,512]{2,1,0:T(8,128)}, u32[]{:S(2)}) copy-start(f32[2,256,512]{2,1,0:T(8,128)} %param.5) | copy-start | bytes 3145732
  105.2 1.8 %collective-permute-start.20 = (f32[144,512]{1,0:T(8,128)S(1)}, f32[144,512]{1,0:T(8,128)S(1)}, u32[]{:S(2)}, u32[]{:S(2)}) collective-permute-start(f32[144,512]{1,0:T(8,128)S(1)} %get-tuple-element.102), channel_id=1, source_target_pairs={{0,32},{32,0},{64,96},{96,64},{128,160},{160,128},{192,224},{224,1... | collective-permute-start | bytes 884744 | tf_op jit(solution)/shard_map/ppermute | solution.py:60
  105.8 1.6 %collective-permute-start.24 = (f32[144,512]{1,0:T(8,128)S(1)}, f32[144,512]{1,0:T(8,128)S(1)}, u32[]{:S(2)}, u32[]{:S(2)}) collective-permute-start(f32[144,512]{1,0:T(8,128)S(1)} %get-tuple-element.103), channel_id=1, source_target_pairs={{0,32},{32,0},{64,96},{96,64},{128,160},{160,128},{192,224},{224,1... | collective-permute-start | bytes 884744 | tf_op jit(solution)/shard_map/ppermute | solution.py:60
  107.6 6.5 %collective-permute-start.23 = (f32[72,512]{1,0:T(8,128)S(1)}, f32[72,512]{1,0:T(8,128)S(1)}, u32[]{:S(2)}, u32[]{:S(2)}) collective-permute-start(f32[72,512]{1,0:T(8,128)S(1)} %get-tuple-element.110), channel_id=1, source_target_pairs={{0,64},{32,96},{64,128},{96,160},{128,192},{160,224},{192,0},{224,... | collective-permute-start | bytes 442376 | tf_op jit(solution)/shard_map/ppermute | solution.py:65
  109.0 9.4 %collective-permute-start.25 = (f32[72,512]{1,0:T(8,128)S(1)}, f32[72,512]{1,0:T(8,128)S(1)}, u32[]{:S(2)}, u32[]{:S(2)}) collective-permute-start(f32[72,512]{1,0:T(8,128)S(1)} %get-tuple-element.108), channel_id=1, source_target_pairs={{0,128},{32,160},{64,192},{96,224},{128,0},{160,32},{192,64},{224,... | collective-permute-start | bytes 442376 | tf_op jit(solution)/shard_map/ppermute | solution.py:65
  111.6 6.8 %collective-permute-start.26 = (f32[72,512]{1,0:T(8,128)S(1)}, f32[72,512]{1,0:T(8,128)S(1)}, u32[]{:S(2)}, u32[]{:S(2)}) collective-permute-start(f32[72,512]{1,0:T(8,128)S(1)} %get-tuple-element.109), channel_id=1, source_target_pairs={{0,192},{32,224},{64,0},{96,32},{128,64},{160,96},{192,128},{224,1... | collective-permute-start | bytes 442376 | tf_op jit(solution)/shard_map/ppermute | solution.py:65
  118.5 9.7 %collective-permute-start.27 = (f32[72,512]{1,0:T(8,128)S(1)}, f32[72,512]{1,0:T(8,128)S(1)}, u32[]{:S(2)}, u32[]{:S(2)}) collective-permute-start(f32[72,512]{1,0:T(8,128)S(1)} %fusion.18.piece), channel_id=1, source_target_pairs={{0,1},{1,2},{2,3},{3,4},{4,5},{5,6},{6,7},{7,8},{8,9},{9,10},{10,1... | collective-permute-start | bytes 442376 | tf_op jit(solution)/shard_map/ppermute | solution.py:51
  118.6 9.6 %collective-permute-start.28 = (f32[72,512]{1,0:T(8,128)S(1)}, f32[72,512]{1,0:T(8,128)S(1)}, u32[]{:S(2)}, u32[]{:S(2)}) collective-permute-start(f32[72,512]{1,0:T(8,128)S(1)} %fusion.18.piece), channel_id=1, source_target_pairs={{0,31},{1,0},{2,1},{3,2},{4,3},{5,4},{6,5},{7,6},{8,7},{9,8},{10,9... | collective-permute-start | bytes 442376 | tf_op jit(solution)/shard_map/ppermute | solution.py:51
  123.3 21.9 %collective-permute-start.36 = (f32[256,512]{1,0:T(8,128)S(1)}, f32[256,512]{1,0:T(8,128)S(1)}, u32[]{:S(2)}, u32[]{:S(2)}) collective-permute-start(f32[256,512]{1,0:T(8,128)S(1)} %copy-done.8), channel_id=1, source_target_pairs={{0,1},{1,2},{2,3},{3,4},{4,5},{5,6},{6,7},{7,8},{8,9},{9,10},{10,1... | collective-permute-start | bytes 1572872 | tf_op jit(solution)/shard_map/ppermute | solution.py:51
  123.4 21.9 %collective-permute-start.37 = (f32[256,512]{1,0:T(8,128)S(1)}, f32[256,512]{1,0:T(8,128)S(1)}, u32[]{:S(2)}, u32[]{:S(2)}) collective-permute-start(f32[256,512]{1,0:T(8,128)S(1)} %copy-done.6), channel_id=1, source_target_pairs={{0,31},{1,0},{2,1},{3,2},{4,3},{5,4},{6,5},{7,6},{8,7},{9,8},{10,9... | collective-permute-start | bytes 1572872 | tf_op jit(solution)/shard_map/ppermute | solution.py:51
  129.3 5.4 %collective-permute-start.29 = (f32[64,512]{1,0:T(8,128)S(1)}, f32[64,512]{1,0:T(8,128)S(1)}, u32[]{:S(2)}, u32[]{:S(2)}) collective-permute-start(f32[64,512]{1,0:T(8,128)S(1)} %shard_map.79.refs_0_), channel_id=1, source_target_pairs={{0,64},{32,96},{64,128},{96,160},{128,192},{160,224},{192,0},{224,... | collective-permute-start | bytes 393224 | tf_op jit(solution)/shard_map/ppermute | solution.py:65
  130.4 8.2 %collective-permute-start.30 = (f32[64,512]{1,0:T(8,128)S(1)}, f32[64,512]{1,0:T(8,128)S(1)}, u32[]{:S(2)}, u32[]{:S(2)}) collective-permute-start(f32[64,512]{1,0:T(8,128)S(1)} %shard_map.79.refs_0_), channel_id=1, source_target_pairs={{0,128},{32,160},{64,192},{96,224},{128,0},{160,32},{192,64},{224,... | collective-permute-start | bytes 393224 | tf_op jit(solution)/shard_map/ppermute | solution.py:65
  132.7 7.3 %collective-permute-start.31 = (f32[64,512]{1,0:T(8,128)S(1)}, f32[64,512]{1,0:T(8,128)S(1)}, u32[]{:S(2)}, u32[]{:S(2)}) collective-permute-start(f32[64,512]{1,0:T(8,128)S(1)} %shard_map.79.refs_0_), channel_id=1, source_target_pairs={{0,192},{32,224},{64,0},{96,32},{128,64},{160,96},{192,128},{224,1... | collective-permute-start | bytes 393224 | tf_op jit(solution)/shard_map/ppermute | solution.py:65
  134.7 5.6 %collective-permute-start.32 = (f32[64,512]{1,0:T(8,128)S(1)}, f32[64,512]{1,0:T(8,128)S(1)}, u32[]{:S(2)}, u32[]{:S(2)}) collective-permute-start(f32[64,512]{1,0:T(8,128)S(1)} %shard_map.79.refs_0_), channel_id=1, source_target_pairs={{0,32},{32,0},{64,96},{96,64},{128,160},{160,128},{192,224},{224,1... | collective-permute-start | bytes 393224 | tf_op jit(solution)/shard_map/ppermute | solution.py:60
  138.6 5.0 %collective-permute-start.33 = (f32[64,512]{1,0:T(8,128)S(1)}, f32[64,512]{1,0:T(8,128)S(1)}, u32[]{:S(2)}, u32[]{:S(2)}) collective-permute-start(f32[64,512]{1,0:T(8,128)S(1)} %collective-permute-done.29.refs_1_), channel_id=1, source_target_pairs={{0,32},{32,0},{64,96},{96,64},{128,160},{160,128},{192,224},{224,1... | collective-permute-start | bytes 393224 | tf_op jit(solution)/shard_map/ppermute | solution.py:60
  140.0 3.6 %collective-permute-start.34 = (f32[64,512]{1,0:T(8,128)S(1)}, f32[64,512]{1,0:T(8,128)S(1)}, u32[]{:S(2)}, u32[]{:S(2)}) collective-permute-start(f32[64,512]{1,0:T(8,128)S(1)} %collective-permute-done.30.refs_2_), channel_id=1, source_target_pairs={{0,32},{32,0},{64,96},{96,64},{128,160},{160,128},{192,224},{224,1... | collective-permute-start | bytes 393224 | tf_op jit(solution)/shard_map/ppermute | solution.py:60
  140.3 3.2 %collective-permute-start.35 = (f32[64,512]{1,0:T(8,128)S(1)}, f32[64,512]{1,0:T(8,128)S(1)}, u32[]{:S(2)}, u32[]{:S(2)}) collective-permute-start(f32[64,512]{1,0:T(8,128)S(1)} %collective-permute-done.31.refs_3_), channel_id=1, source_target_pairs={{0,32},{32,0},{64,96},{96,64},{128,160},{160,128},{192,224},{224,1... | collective-permute-start | bytes 393224 | tf_op jit(solution)/shard_map/ppermute | solution.py:60
  (8 other events, 15.4 us)

commit v3 on v2

--- a/solution.py
+++ b/solution.py
@@ -55,6 +55,11 @@
     return along_slab(value, RING * step)
 
 
+def ring_of(move, values, sign):
+    moved = {step: move(values[step - 1], sign * step) for step in (2, 1, 3)}
+    return [moved[step] for step in (1, 2, 3)]
+
+
 def other_core(value):
     count = lax.axis_size("subj")
     return lax.ppermute(value, "subj", [(i, i ^ 1) for i in range(count)])
@@ -65,29 +70,28 @@
     return lax.ppermute(value, "subj", [(i, (i + 2 * step) % count) for i in range(count)])
 
 
-def spread_kernel(place_ref, source_ref, all_ref, half_ref):
+def spread_rows(source_ref, out_ref):
     count, width = source_ref.shape
     parts = width // LANES
-    rows = count // 2
 
     def group(block, carry):
         first = pl.multiple_of(block * 8, 8)
         for part in range(parts):
-            all_ref[pl.ds(first * parts + part, 8, stride=parts), :] = source_ref[
+            out_ref[pl.ds(first * parts + part, 8, stride=parts), :] = source_ref[
                 pl.ds(first, 8), part * LANES:(part + 1) * LANES
             ]
         return carry
 
     lax.fori_loop(0, count // 8, group, 0, unroll=4)
-    unit = 64
-    start = place_ref[1] * rows * parts
-
-    def copy(block, carry):
-        first = pl.multiple_of(block * unit, unit)
-        half_ref[pl.ds(first, unit), :] = all_ref[pl.ds(pl.multiple_of(start + first, unit), unit), :]
-        return carry
-
-    lax.fori_loop(0, rows * parts // unit, copy, 0, unroll=4)
+
+
+def spread_plane_kernel(place_ref, source_ref, out_ref, held, sem):
+    rows = held.shape[0]
+    start = pl.multiple_of(place_ref[1] * rows, rows)
+    copy = pltpu.make_async_copy(source_ref.at[pl.ds(start, rows)], held, sem)
+    copy.start()
+    copy.wait()
+    spread_rows(held, out_ref)
 
 
 def request_kernel(place_ref, lists_ref, self_ref, out_1, out_2, out_3):
@@ -109,6 +113,18 @@
         out[1:2, :] = across(server - here + 2 * REACH * above, above)
 
 
+def fill(held, parts):
+    size = parts[0].shape[0]
+    unit = 64
+    for at, part in enumerate(parts):
+        def group(block, carry):
+            first = pl.multiple_of(block * unit, unit)
+            held[pl.ds(at * size + first, unit), :] = part[pl.ds(first, unit), :]
+            return carry
+
+        lax.fori_loop(0, size // unit, group, 0, unroll=4)
+
+
 def copy_lines(list_ref, list_row, held, out_ref):
     count = list_ref.shape[1]
     parts = out_ref.shape[0] // count
@@ -133,17 +149,9 @@
 
 def cross_lines_kernel(
     lists_0, lists_1, lists_2, lists_3, low_a, low_b, high_a, high_b,
-    out_low, out_high, out_1, out_2, out_3, held, sems,
+    out_low, out_high, out_1, out_2, out_3, held,
 ):
-    size = low_a.shape[0]
-    copies = [
-        pltpu.make_async_copy(part, held.at[pl.ds(at * size, size)], sems.at[at])
-        for at, part in enumerate((low_a, low_b, high_a, high_b))
-    ]
-    for copy in copies:
-        copy.start()
-    for copy in copies:
-        copy.wait()
+    fill(held, (low_a, low_b, high_a, high_b))
     for lists, row, out in (
         (lists_1, 1, out_1), (lists_2, 1, out_2), (lists_3, 1, out_3), (lists_0, 1, out_low), (lists_0, 2, out_high),
     ):
@@ -198,27 +206,19 @@
     slot_ref, here_ref, ahead_ref, image_ref = refs[:4]
     blocks = refs[4:13]
     warped_refs, push_high, push_low = refs[13:15], refs[15], refs[16]
-    held, stage_0, stage_1, sems = refs[17:]
-    size = blocks[0].shape[0]
+    held, stage_0, stage_1 = refs[17:]
     line_count, width = image_ref.shape
     parts = width // LANES
     rows_plane = line_count // 2
     rows = WARP_ROWS
-    copies = [
-        pltpu.make_async_copy(block, held.at[pl.ds(at * size, size)], sems.at[at])
-        for at, block in enumerate(blocks)
-    ]
-    for copy in copies:
-        copy.start()
-    for copy in copies:
-        copy.wait()
+    fill(held, blocks)
 
     def gather(block, stage, corner, low, high):
         first = block * rows
         found = []
         for row in range(low, high):
             line = slot_ref[corner, first + row]
-            found.append(held[pl.ds(pl.multiple_of(line * parts, parts), parts), :])
+            found.append(held[pl.ds(pl.multiple_of(line, parts), parts), :])
         for row in range(low, high):
             at = (corner * rows + row) * parts
             stage[at:at + parts, :] = found[row - low]
@@ -293,33 +293,33 @@
 
     own_lists = (lists_0[0:1, :], lists_1[0:1, :], lists_2[0:1, :], lists_3[0:1, :])
     cross_lists = (lists_0[1:2, :], lists_0[2:3, :], lists_1[1:2, :], lists_2[1:2, :], lists_3[1:2, :])
-    for at, ids in enumerate(own_lists):
+    for at, ids in enumerate(own_lists + own_lists):
         own_ref[:, at * capacity:(at + 1) * capacity] = hot(ids)
-    for at, ids in enumerate(cross_lists):
+    for at, ids in enumerate(cross_lists + cross_lists):
         ids = ids ^ flip
         low_ref[:, at * capacity:(at + 1) * capacity] = hot(ids)
         high_ref[:, at * capacity:(at + 1) * capacity] = hot(ids - line_count * parts)
 
 
-def line_sums(hot, parts):
-    return jnp.dot(hot, parts[0], preferred_element_type=F32) + jnp.dot(hot, parts[1], preferred_element_type=F32)
+def stacked_parts(blocks):
+    return jnp.concatenate(split_parts(jnp.concatenate([block[...] for block in blocks], axis=0)), axis=0)
 
 
 def own_back_kernel(hot_ref, in_0, in_1, in_2, in_3, keep, send_0, send_1):
-    values = split_parts(jnp.concatenate([in_0[...], in_1[...], in_2[...], in_3[...]], axis=0))
-    count = keep.shape[0]
-    keep[...] = line_sums(hot_ref[:count], values)
-    sent = line_sums(hot_ref[count:], values)
-    send_0[...] = sent[:count // 2]
-    send_1[...] = sent[count // 2:]
+    summed = jnp.dot(hot_ref[...], stacked_parts((in_0, in_1, in_2, in_3)), preferred_element_type=F32)
+    count, first = keep.shape[0], send_0.shape[0]
+    keep[...] = summed[:count]
+    send_0[...] = summed[count:count + first]
+    send_1[...] = summed[count + first:]
 
 
 def cross_back_kernel(hot_low, hot_high, in_low, in_high, in_1, in_2, in_3, keep_low, keep_high, send):
-    values = split_parts(jnp.concatenate([in_low[...], in_high[...], in_1[...], in_2[...], in_3[...]], axis=0))
+    values = stacked_parts((in_low, in_high, in_1, in_2, in_3))
     count = keep_low.shape[0]
     for at, (hot, keep) in enumerate(((hot_low, keep_low), (hot_high, keep_high))):
-        send[at * count:(at + 1) * count] = line_sums(hot[count:], values)
-        keep[...] = line_sums(hot[:count], values)
+        summed = jnp.dot(hot[...], values, preferred_element_type=F32)
+        keep[...] = summed[:count]
+        send[at * count:(at + 1) * count] = summed[count:]
 
 
 def smooth_kernel(place_ref, before, piece, after, template_ref, out, field):
@@ -358,28 +358,6 @@
         )
 
 
-def assemble_kernel(place_ref, *refs):
-    pieces, out, sems = refs[:2 * RING], refs[2 * RING], refs[2 * RING + 1]
-    core, chip = place_ref[1], place_ref[4]
-    count = pieces[0].shape[0] // 2
-    plane_rows = out.shape[0] // 2
-    copies = []
-    for at, piece in enumerate(pieces):
-        part = core if at < RING else 1 - core
-        index = part * RING + lax.rem(chip + RING - at % RING, RING)
-        for plane in range(2):
-            start = pl.multiple_of(plane * plane_rows + index * count, count)
-            copies.append(
-                pltpu.make_async_copy(
-                    piece.at[pl.ds(plane * count, count)], out.at[pl.ds(start, count)], sems.at[2 * at + plane]
-                )
-            )
-    for copy in copies:
-        copy.start()
-    for copy in copies:
-        copy.wait()
-
-
 def plane_force_kernel(plane_0, plane_1, image_ref, out, held, sem):
     rows_plane, width = plane_0.shape
     rows = 32
@@ -405,26 +383,43 @@
     copy.wait()
 
 
-def depth_force_kernel(place_ref, before, plane_0, plane_1, after, image_ref, given, out, held, sem):
-    device, last = place_ref[2], place_ref[3]
+def finish_kernel(place_ref, before, plane_0, plane_1, after, image_ref, *refs):
+    pieces = refs[:2 * RING]
+    template_out, out, held, sems = refs[2 * RING + 1:]
+    device, last, core, chip = place_ref[2], place_ref[3], place_ref[1], place_ref[4]
+    count = pieces[0].shape[0] // 2
     rows_plane = plane_0.shape[0]
+    copies = []
+    for at, piece in enumerate(pieces):
+        part = core if at < RING else 1 - core
+        index = part * RING + lax.rem(chip + RING - at % RING, RING)
+        for plane in range(2):
+            start = pl.multiple_of(plane * rows_plane + index * count, count)
+            copies.append(
+                pltpu.make_async_copy(
+                    piece.at[pl.ds(plane * count, count)], template_out.at[pl.ds(start, count)], sems.at[2 * at + plane]
+                )
+            )
+    for copy in copies:
+        copy.start()
     rows = 32
-
-    def step(block, carry):
-        at = pl.ds(pl.multiple_of(block * rows, rows), rows)
-        lower, upper = plane_0[at, :], plane_1[at, :]
-        back = jnp.where(device > 0, before[at, :], 0.0)
-        ahead = jnp.where(device < last, after[at, :], 0.0)
-        image_0 = image_ref[at, :]
-        image_1 = image_ref[pl.ds(pl.multiple_of(rows_plane + block * rows, rows), rows), :]
-        held[0, 0, at, :] = (image_0 - lower) * (0.5 * (upper - back))
-        held[0, 1, at, :] = (image_1 - upper) * (0.5 * (ahead - lower))
-        return carry
-
-    lax.fori_loop(0, rows_plane // rows, step, 0)
-    copy = pltpu.make_async_copy(held, out.at[pl.ds(0, 1)], sem)
-    copy.start()
-    copy.wait()
+    for plane in range(2):
+        def step(block, carry):
+            at = pl.ds(pl.multiple_of(block * rows, rows), rows)
+            image = image_ref[pl.ds(pl.multiple_of(plane * rows_plane + block * rows, rows), rows), :]
+            if plane == 0:
+                centre, back, ahead = plane_0[at, :], jnp.where(device > 0, before[at, :], 0.0), plane_1[at, :]
+            else:
+                centre, back, ahead = plane_1[at, :], plane_0[at, :], jnp.where(device < last, after[at, :], 0.0)
+            held[plane, at, :] = (image - centre) * (0.5 * (ahead - back))
+            return carry
+
+        lax.fori_loop(0, rows_plane // rows, step, 0)
+        copy = pltpu.make_async_copy(held.at[plane], out.at[0, plane], sems.at[4 * RING + plane])
+        copy.start()
+        copies.append(copy)
+    for copy in copies:
+        copy.wait()
 
 
 def on_device(template, images, fractions, requests, corners):
@@ -444,28 +439,30 @@
     parts = cell_count // LANES
     packed = f32s(capacity * parts, LANES)
 
-    spread, plane = call(
-        spread_kernel, (f32s(line_count * parts, LANES), f32s(row_count * parts, LANES)), [SMEM, VMEM], (VMEM,) * 2,
-    )(place, lines)
-    from_low = along_z(plane, 1)
-    from_high = along_z(plane, -1)
     message = jax.ShapeDtypeStruct((2, capacity), I32)
     self_lists, *messages = call(
         request_kernel, (jax.ShapeDtypeStruct((3, capacity), I32),) + (message,) * 3, [SMEM, VMEM], (VMEM,) * 4,
     )(place, lists)
-    asked = [self_lists] + [along_x(messages[step - 1], -step) for step in (1, 2, 3)]
+    plane = call(
+        spread_plane_kernel, f32s(row_count * parts, LANES), [SMEM, ANY], VMEM,
+        [pltpu.VMEM((row_count, cell_count), F32), pltpu.SemaphoreType.DMA],
+    )(place, lines)
+    spread = call(spread_rows, f32s(line_count * parts, LANES), [VMEM], VMEM)(lines)
+    from_low = along_z(plane, 1)
+    from_high = along_z(plane, -1)
+    asked = [self_lists] + ring_of(along_x, messages, -1)
 
     own = call(
         own_lines_kernel, (packed,) * 4, [SMEM] * 4 + [VMEM], (VMEM,) * 4,
     )(*asked, spread)
-    got_own = [along_x(own[step], step) for step in (1, 2, 3)]
+    got_own = ring_of(along_x, own[1:], 1)
     from_low, from_high, _ = lax.optimization_barrier((from_low, from_high, (got_own[0], got_own[2])))
     from_low_b, from_high_b = other_core(from_low), other_core(from_high)
     cross = call(
-        cross_lines_kernel, (packed,) * 5, [SMEM] * 4 + [ANY] * 4, (VMEM,) * 5,
-        [pltpu.VMEM((2 * line_count * parts, LANES), F32), pltpu.SemaphoreType.DMA((4,))],
+        cross_lines_kernel, (packed,) * 5, [SMEM] * 4 + [VMEM] * 4, (VMEM,) * 5,
+        [pltpu.VMEM((2 * line_count * parts, LANES), F32)],
     )(*asked, from_low, from_low_b, from_high, from_high_b)
-    got_cross = [along_x(cross[1 + step], step) for step in (1, 2, 3)]
+    got_cross = ring_of(along_x, cross[2:], 1)
 
     slot_ids = corners.reshape(4, line_count)
     offset = slot_ids // capacity - REACH
@@ -488,26 +485,31 @@
     warped_0, warped_1, push_high, push_low = call(
         warp_kernel,
         (half,) * 2 + (push_part,) * 2,
-        [SMEM] + [VMEM] * 3 + [ANY] * 9,
+        [SMEM] + [VMEM] * 12,
         (VMEM,) * 4,
         [
             pltpu.VMEM((band_count * capacity * parts, LANES), F32),
             pltpu.VMEM((4 * WARP_ROWS * parts, LANES), F32),
             pltpu.VMEM((4 * WARP_ROWS * parts, LANES), F32),
-            pltpu.SemaphoreType.DMA((9,)),
         ],
-    )(slot_ids, here_part, ahead_part, images.reshape(line_count, cell_count), *blocks)
+    )(slot_ids * parts, here_part, ahead_part, images.reshape(line_count, cell_count), *blocks)
 
     block = f32s(capacity, cell_count)
     pool_cross = call(
-        functools.partial(slot_sum_kernel, 0), (block,) * 5, [VMEM] * 3, (VMEM,) * 5,
+        functools.partial(slot_sum_kernel, 0), (block,) * 3, [VMEM] * 3, (VMEM,) * 3,
     )(flat_ids, push_high, push_low)
-    pool_own = call(
-        functools.partial(slot_sum_kernel, 5), (block,) * 4, [VMEM] * 3, (VMEM,) * 4,
+    pool_low, pool_high, *pool_own = call(
+        functools.partial(slot_sum_kernel, 3), (block,) * 6, [VMEM] * 3, (VMEM,) * 6,
     )(flat_ids, push_high, push_low)
-    back_cross = [along_x(pool_cross[step - 1], -step) for step in (1, 2, 3)]
-    back_cross, pool_own = lax.optimization_barrier((back_cross, pool_own))
-    back_own = [along_x(pool_own[step - 1], -step) for step in (1, 2, 3)]
+    back_cross = ring_of(along_x, pool_cross, -1)
+    image_lines = images.reshape(line_count, cell_count)
+    force = f32s(3, plane_count, row_count, cell_count)
+    part_force = call(
+        plane_force_kernel, force, [VMEM] * 3, ANY,
+        [pltpu.VMEM((2, plane_count, row_count, cell_count), F32), pltpu.SemaphoreType.DMA],
+    )(warped_0, warped_1, image_lines)
+    back_cross, pool_own, part_force = lax.optimization_barrier((back_cross, pool_own, part_force))
+    back_own = ring_of(along_x, pool_own, -1)
 
     per_piece = row_count // (2 * RING)
     wide = per_piece + 2 * HALO
@@ -523,13 +525,13 @@
     all_rows = 2 * core_rows
     hot_own, hot_low, hot_high = call(
         line_hot_kernel,
-        (jax.ShapeDtypeStruct((all_rows, 4 * capacity), BF16),) + (jax.ShapeDtypeStruct((all_rows, 5 * capacity), BF16),) * 2,
+        (jax.ShapeDtypeStruct((all_rows, 8 * capacity), BF16),) + (jax.ShapeDtypeStruct((all_rows, 10 * capacity), BF16),) * 2,
         [SMEM] + [VMEM] * 5, (VMEM,) * 3,
     )(place, *asked, target)
     keep_low, keep_high, send = call(
         cross_back_kernel, (core_part,) * 2 + (f32s(2 * core_rows, cell_count),),
         [VMEM] * 7, (VMEM,) * 3,
-    )(hot_low, hot_high, *pool_cross[3:], *back_cross)
+    )(hot_low, hot_high, pool_low, pool_high, *back_cross)
     received = other_core(send)
     sum_low = keep_low + received[:core_rows]
     sum_high = keep_high + received[core_rows:]
@@ -538,18 +540,19 @@
     back_own, sum_low, sum_high = lax.optimization_barrier((back_own, sum_low, sum_high))
     size = 2 * wide
     keep_own, *send_own = call(
-        own_back_kernel, (core_part,) + (f32s(core_rows // 2, cell_count),) * 2,
+        own_back_kernel, (core_part, f32s(core_rows - size, cell_count), f32s(size, cell_count)),
         [VMEM] * 5, (VMEM,) * 3,
     )(hot_own, pool_own[3], *back_own)
     got_parts = [other_core(part) for part in send_own]
     pieces = [
         keep_own[at * size:(at + 1) * size]
-        + got_parts[at // 2][at % 2 * size:(at % 2 + 1) * size]
+        + (got_parts[0][at * size:(at + 1) * size] if at < RING - 1 else got_parts[1])
         + in_from_high[at * size:(at + 1) * size]
         + in_from_low[at * size:(at + 1) * size]
         for at in range(RING)
     ]
-    piece_sum = pieces[0] + along_y(pieces[1], 1) + along_y(pieces[2], 2) + along_y(pieces[3], 3)
+    got_pieces = ring_of(along_y, pieces[1:], 1)
+    piece_sum = pieces[0] + got_pieces[0] + got_pieces[1] + got_pieces[2]
     edge_0, edge_1, _ = lax.optimization_barrier((warped_0, warped_1, piece_sum))
     edge_before, edge_after = along_slab(edge_1, 1), along_slab(edge_0, -1)
     before, after = along_slab(piece_sum, 1), along_slab(piece_sum, -1)
@@ -558,22 +561,13 @@
         [pltpu.VMEM((3 * size, cell_count), F32)],
     )(place, before, piece_sum, after, lines)
 
-    image_lines = images.reshape(line_count, cell_count)
-    force = f32s(3, plane_count, row_count, cell_count)
-    part_force = call(
-        plane_force_kernel, force, [VMEM] * 3, ANY,
-        [pltpu.VMEM((2, plane_count, row_count, cell_count), F32), pltpu.SemaphoreType.DMA],
-    )(warped_0, warped_1, image_lines)
-    image_force = call(
-        depth_force_kernel, force, [SMEM] + [VMEM] * 5 + [ANY], ANY,
-        [pltpu.VMEM((1, plane_count, row_count, cell_count), F32), pltpu.SemaphoreType.DMA], {6: 0},
-    )(place, edge_before, warped_0, warped_1, edge_after, image_lines, part_force)
-    mine = [new_piece] + [along_y(new_piece, step) for step in (1, 2, 3)]
+    mine = [new_piece] + ring_of(along_y, [new_piece] * 3, 1)
     theirs = [other_core(value) for value in mine]
-    new_template = call(
-        assemble_kernel, f32s(line_count, cell_count), [SMEM] + [ANY] * 8, ANY,
-        [pltpu.SemaphoreType.DMA((16,))],
-    )(place, *mine, *theirs)
+    new_template, image_force = call(
+        finish_kernel, (f32s(line_count, cell_count), force), [SMEM] + [VMEM] * 5 + [ANY] * 9, (ANY, ANY),
+        [pltpu.VMEM((plane_count, row_count, cell_count), F32), pltpu.SemaphoreType.DMA((4 * RING + 2,))],
+        {14: 1},
+    )(place, edge_before, warped_0, warped_1, edge_after, image_lines, *mine, *theirs, part_force)
     return new_template.reshape(template.shape), image_force[None]
 
 

time: 147 us -> 138 us (0.939)
  waiting for transfers between devices: 52.8 us -> 41.9 us
  Pallas kernels: 33.8 us -> 31.2 us
  local copies, waits for them, and re-layouts: 5.76 us -> 8.09 us
  starting transfers between devices: 52.5 us -> 54.4 us
    ppermute x15, waiting for transfers between devices: 39.9 us -> 29.7 us  [along_x(): return lax.ppermute(value, 'slab', route)]
    unnamed x38 -> x32, local copies, waits for them, and re-layouts: 5.66 us -> 7.99 us
    pallas_call x9, Pallas kernels: 21.8 us -> 19.6 us  [the longest x1 5.88 us: on_device(): call(warp_kernel, (half,) * 2 + (push_part,) * 2, [SMEM] + [VMEM] * 12, (...]
  transfers between devices with their start and end apart: 38 -> 38, of which waited for: 20 -> 22; matrix products, arithmetic and copies ran while one was open for 1% -> 1% of each run, Pallas kernels for 12% -> 13%
where the time goes in v3:
time: 138 us
  starting transfers between devices  54.4 us (39%)
  waiting for transfers between devices  41.9 us (30%)
  Pallas kernels  31.2 us (23%)
  local copies, waits for them, and re-layouts  8.09 us (6%)
    ppermute x15, waiting for transfers between devices, along_x(): return lax.ppermute(value, 'slab', route)  29.7 us
    ppermute x8, starting transfers between devices, along_slab(): lax.ppermute(value, 'slab', [(i, (i + step) % count) for i in range(count)])  18.2 us
    ppermute x15, starting transfers between devices, along_x(): return lax.ppermute(value, 'slab', route)  14.5 us
    ppermute x9, starting transfers between devices, other_core(): return lax.ppermute(value, 'subj', [(i, i ^ 1) for i in range(count)])  12.4 us
    ppermute x6, starting transfers between devices, along_y(): lax.ppermute(value, 'subj', [(i, (i + 2 * step) % count) for i in range(c...  9.36 us
    unnamed x32, local copies, waits for them, and re-layouts  7.99 us
    pallas_call x1, Pallas kernels, on_device(): call(warp_kernel, (half,) * 2 + (push_part,) * 2, [SMEM] + [VMEM] * 12, (...  5.88 us
    ppermute x9, waiting for transfers between devices, other_core(): return lax.ppermute(value, 'subj', [(i, i ^ 1) for i in range(count)])  5.57 us
  transfers between devices with their start and end apart: 38, of which 22 were waited for; matrix products, arithmetic and copies ran while one was open for 1% of the time, Pallas kernels for 13%

profile of v3, /device:TPU:1, one launch (start us, length us, event | category | flops | bytes accessed | tf_op | source)
XLA Modules:
  0.0 137.8 jit_solution(7231303104696215542)
XLA Ops:
  0.8 1.2 copy-done
  2.7 2.5 %collective-permute-start.3 = (f32[1024,128]{1,0:T(8,128)S(1)}, f32[1024,128]{1,0:T(8,128)S(1)}, u32[]{:S(2)}, u32[]{:S(2)}) collective-permute-start(f32[1024,128]{1,0:T(8,128)S(1)} %shard_map.70), channel_id=1, source_target_pairs={{0,4},{1,5},{2,6},{3,7},{4,8},{5,9},{6,10},{7,11},{8,12},{9,13},{1... | collective-permute-start | bytes 1572872 | tf_op jit(solution)/shard_map/ppermute | solution.py:51
  5.2 4.0 %collective-permute-start.4 = (f32[1024,128]{1,0:T(8,128)S(1)}, f32[1024,128]{1,0:T(8,128)S(1)}, u32[]{:S(2)}, u32[]{:S(2)}) collective-permute-start(f32[1024,128]{1,0:T(8,128)S(1)} %shard_map.70), channel_id=1, source_target_pairs={{0,28},{1,29},{2,30},{3,31},{4,0},{5,1},{6,2},{7,3},{8,4},{9,5},{1... | collective-permute-start | bytes 1572872 | tf_op jit(solution)/shard_map/ppermute | solution.py:51
  9.8 2.6 %collective-permute-start = (s32[2,128]{1,0:T(2,128)S(1)}, s32[2,128]{1,0:T(2,128)S(1)}, u32[]{:S(2)}, u32[]{:S(2)}) collective-permute-start(s32[2,128]{1,0:T(2,128)S(1)} %get-tuple-element.59), channel_id=1, source_target_pairs={{0,3},{1,0},{2,1},{3,2},{4,7},{5,4},{6,5},{7,6},{8,11},{9,8},{10,9... | collective-permute-start | bytes 3080 | tf_op jit(solution)/shard_map/ppermute | solution.py:46
  13.7 2.6 %collective-permute-done.1.lists_2 = s32[2,128]{1,0:T(2,128)S(1)} collective-permute-done((s32[2,128]{1,0:T(2,128)S(1)}, s32[2,128]{1,0:T(2,128)S(1)}, u32[]{:S(2)}, u32[]{:S(2)}) %collective-permute-start.1) | collective-permute-done | bytes 1056 | tf_op jit(solution)/shard_map/ppermute | solution.py:46
  16.8 1.1 shard_map.72
  18.6 2.7 %collective-permute-start.6 = (f32[512,128]{1,0:T(8,128)S(1)}, f32[512,128]{1,0:T(8,128)S(1)}, u32[]{:S(2)}, u32[]{:S(2)}) collective-permute-start(f32[512,128]{1,0:T(8,128)S(1)} %get-tuple-element.63), channel_id=1, source_target_pairs={{0,3},{1,0},{2,1},{3,2},{4,7},{5,4},{6,5},{7,6},{8,11},{9,8},{10,9... | collective-permute-start | bytes 786440 | tf_op jit(solution)/shard_map/ppermute | solution.py:46
  21.3 3.8 %collective-permute-done.5.refs_9_ = f32[512,128]{1,0:T(8,128)S(1)} collective-permute-done((f32[512,128]{1,0:T(8,128)S(1)}, f32[512,128]{1,0:T(8,128)S(1)}, u32[]{:S(2)}, u32[]{:S(2)}) %collective-permute-start.5) | collective-permute-done | bytes 262176 | tf_op jit(solution)/shard_map/ppermute | solution.py:46
  26.5 3.5 %collective-permute-start.7 = (f32[1024,128]{1,0:T(8,128)S(1)}, f32[1024,128]{1,0:T(8,128)}, u32[]{:S(2)}, u32[]{:S(2)}) collective-permute-start(f32[1024,128]{1,0:T(8,128)S(1)} %collective-permute-done.3.low_a), channel_id=1, source_target_pairs={{0,32},{32,0},{64,96},{96,64},{128,160},{160,128},{192,224},{224,1... | collective-permute-start | bytes 1572872 | tf_op jit(solution)/shard_map/ppermute | solution.py:65
  30.8 0.9 collective-permute-done.7.low_b
  32.5 2.8 %shard_map.73 = (f32[512,128]{1,0:T(8,128)S(1)}, f32[512,128]{1,0:T(8,128)S(1)}, f32[512,128]{1,0:T(8,128)S(1)}, f32[512,128]{1,0:T(8,128)S(1)}, f32[512,128]{1,0:T(8,128)S(1)}) custom-call(s32[3,128]{1,0:T(4,128)S(1)} %get-tuple-element.58.lists_0, s32[2,128]{1,0:T(2,128)S(1)} %collective-permute-done.lists_1, s32[2,128]{1,0:T(2,128)S(1)} %collective-permute-done.1.lists_2, ...), custom_call_target="tpu_custom_call" | custom-call | tf_op jit(solution)/shard_map/pallas_call | solution.py:461
  35.3 0.9 collective-permute-start.10
  36.2 2.2 %collective-permute-start.11 = (f32[512,128]{1,0:T(8,128)S(1)}, f32[512,128]{1,0:T(8,128)S(1)}, u32[]{:S(2)}, u32[]{:S(2)}) collective-permute-start(f32[512,128]{1,0:T(8,128)S(1)} %get-tuple-element.68), channel_id=1, source_target_pairs={{0,3},{1,0},{2,1},{3,2},{4,7},{5,4},{6,5},{7,6},{8,11},{9,8},{10,9... | collective-permute-start | bytes 786440 | tf_op jit(solution)/shard_map/ppermute | solution.py:46
  38.6 1.4 %copy-done.7 = bf16[1,3,2,256,512]{4,3,2,1,0:T(8,128)(2,1)S(1)} copy-done((bf16[1,3,2,256,512]{4,3,2,1,0:T(8,128)(2,1)S(1)}, bf16[1,3,2,256,512]{4,3,2,1,0:T(8,128)(2,1)}, u32[]{:S(2)}) %copy-start.7) | copy-done | bytes 1572888
  40.0 3.0 %shard_map.68 = (f32[4,512,512]{2,1,0:T(8,128)S(1)}, f32[4,512,512]{2,1,0:T(8,128)S(1)}) custom-call(bf16[3,512,512]{2,1,0:T(8,128)(2,1)S(1)} %bitcast.21), custom_call_target="tpu_custom_call" | custom-call | tf_op jit(solution)/shard_map/pallas_call | solution.py:480
  43.1 2.3 %collective-permute-done.10.refs_5_ = f32[512,128]{1,0:T(8,128)S(1)} collective-permute-done((f32[512,128]{1,0:T(8,128)S(1)}, f32[512,128]{1,0:T(8,128)S(1)}, u32[]{:S(2)}, u32[]{:S(2)}) %collective-permute-start.10) | collective-permute-done | bytes 262176 | tf_op jit(solution)/shard_map/ppermute | solution.py:46
  45.3 5.5 %collective-permute-done.11.refs_6_ = f32[512,128]{1,0:T(8,128)S(1)} collective-permute-done((f32[512,128]{1,0:T(8,128)S(1)}, f32[512,128]{1,0:T(8,128)S(1)}, u32[]{:S(2)}, u32[]{:S(2)}) %collective-permute-start.11) | collective-permute-done | bytes 262176 | tf_op jit(solution)/shard_map/ppermute | solution.py:46
  51.5 5.9 %shard_map.74 = (f32[256,512]{1,0:T(8,128)S(1)}, f32[256,512]{1,0:T(8,128)S(1)}, bf16[2048,512]{1,0:T(8,128)(2,1)S(1)}, bf16[2048,512]{1,0:T(8,128)(2,1)S(1)}) custom-call(s32[4,512]{1,0:T(4,128)S(1)} %fusion.24.refs_0_, f32[4,512,512]{2,1,0:T(8,128)S(1)} %get-tuple-element.56.refs_1_, f32[4,512,512]{2,1,0:T(8,128)S(1)} %get-tuple-element.57.refs_2_, ...), custom_call_target="tpu_custom_call" | custom-call | tf_op jit(solution)/shard_map/pallas_call | solution.py:485
  57.4 2.7 %shard_map.76 = (f32[128,512]{1,0:T(8,128)}, f32[128,512]{1,0:T(8,128)}, f32[128,512]{1,0:T(8,128)}) custom-call(s32[1,2048]{1,0:T(1,128)S(1)} %fusion.20.ids_ref, bf16[2048,512]{1,0:T(8,128)(2,1)S(1)} %get-tuple-element.76.push_high, bf16[2048,512]{1,0:T(8,128)(2,1)S(1)} %get-tuple-element.77.push_low), custom_call_target="tpu_custom_call" | custom-call | tf_op jit(solution)/shard_map/pallas_call | solution.py:498
  60.0 2.3 %collective-permute-start.13 = (f32[128,512]{1,0:T(8,128)}, f32[128,512]{1,0:T(8,128)S(1)}, u32[]{:S(2)}, u32[]{:S(2)}) collective-permute-start(f32[128,512]{1,0:T(8,128)} %get-tuple-element.78), channel_id=1, source_target_pairs={{0,3},{1,0},{2,1},{3,2},{4,7},{5,4},{6,5},{7,6},{8,11},{9,8},{10,9... | collective-permute-start | bytes 786440 | tf_op jit(solution)/shard_map/ppermute | solution.py:46
  63.4 1.1 shard_map.75
  64.6 1.6 %copy-done.4 = bf16[2048,512]{1,0:T(8,128)(2,1)S(1)} copy-done((bf16[2048,512]{1,0:T(8,128)(2,1)S(1)}, bf16[2048,512]{1,0:T(8,128)(2,1)}, u32[]{:S(2)}) %copy-start.4) | copy-done | bytes 2097176
  66.2 1.6 %copy-done.6 = bf16[2048,512]{1,0:T(8,128)(2,1)S(1)} copy-done((bf16[2048,512]{1,0:T(8,128)(2,1)S(1)}, bf16[2048,512]{1,0:T(8,128)(2,1)}, u32[]{:S(2)}) %copy-start.6) | copy-done | bytes 2097176
  67.8 3.4 %shard_map.77 = (f32[128,512]{1,0:T(8,128)S(1)}, f32[128,512]{1,0:T(8,128)S(1)}, f32[128,512]{1,0:T(8,128)S(1)}, f32[128,512]{1,0:T(8,128)S(1)}, f32[128,512]{1,0:T(8,128)S(1)}, /*index=5*/f32[128,512]{1,0:T(8,128)S(1)}) custom-call(s32[1,2048]{1,0:T(1,128)S(1)} %fusion.20.ids_ref, bf16[2048,512]{1,0:T(8,128)(2,1)S(1)} %copy-done.4, ...), custom_call_target="tpu_custom_call" | custom-call | tf_op jit(solution)/shard_map/pallas_call | solution.py:501
  71.2 3.0 %shard_map.78.refs_8_ = f32[3,2,256,512]{3,2,1,0:T(8,128)} custom-call(f32[256,512]{1,0:T(8,128)S(1)} %get-tuple-element.106.plane_0, f32[256,512]{1,0:T(8,128)S(1)} %get-tuple-element.105.plane_1, f32[512,512]{1,0:T(8,128)S(1)} %bitcast.19), custom_call_target="tpu_custom_call" | custom-call | tf_op jit(solution)/shard_map/pallas_call | solution.py:507
  74.3 3.1 %collective-permute-done.15.in_3 = f32[128,512]{1,0:T(8,128)} collective-permute-done((f32[128,512]{1,0:T(8,128)}, f32[128,512]{1,0:T(8,128)}, u32[]{:S(2)}, u32[]{:S(2)}) %collective-permute-start.15) | collective-permute-done | bytes 262176 | tf_op jit(solution)/shard_map/ppermute | solution.py:46
  77.4 2.7 %shard_map.79 = (f32[288,512]{1,0:T(8,128)S(1)}, f32[288,512]{1,0:T(8,128)S(1)}, f32[576,512]{1,0:T(8,128)S(1)}) custom-call(bf16[576,1280]{1,0:T(8,128)(2,1)S(1)} %get-tuple-element.89.hot_low, bf16[576,1280]{1,0:T(8,128)(2,1)S(1)} %get-tuple-element.90.hot_high, f32[128,512]{1,0:T(8,128)S(1)} %get-tuple-element.91.in_low, ...), custom_call_target="tpu_custom_call" | custom-call | tf_op jit(solution)/shard_map/pallas_call | solution.py:531
  80.1 0.9 collective-permute-start.19
  82.5 1.0 collective-permute-done.19
  83.7 2.0 %collective-permute-start.21 = (f32[288,512]{1,0:T(8,128)S(1)}, f32[288,512]{1,0:T(8,128)S(1)}, u32[]{:S(2)}, u32[]{:S(2)}) collective-permute-start(f32[288,512]{1,0:T(8,128)S(1)} %get-tuple-element.113), channel_id=1, source_target_pairs={{0,28},{1,29},{2,30},{3,31},{4,0},{5,1},{6,2},{7,3},{8,4},{9,5},{1... | collective-permute-start | bytes 1769480 | tf_op jit(solution)/shard_map/ppermute | solution.py:51
  85.7 3.2 %collective-permute-done.16.in_1 = f32[128,512]{1,0:T(8,128)S(1)} collective-permute-done((f32[128,512]{1,0:T(8,128)S(1)}, f32[128,512]{1,0:T(8,128)S(1)}, u32[]{:S(2)}, u32[]{:S(2)}) %collective-permute-start.16) | collective-permute-done | bytes 262176 | tf_op jit(solution)/shard_map/ppermute | solution.py:46
  88.9 1.8 %collective-permute-done.17.in_2 = f32[128,512]{1,0:T(8,128)S(1)} collective-permute-done((f32[128,512]{1,0:T(8,128)S(1)}, f32[128,512]{1,0:T(8,128)S(1)}, u32[]{:S(2)}, u32[]{:S(2)}) %collective-permute-start.17) | collective-permute-done | bytes 262176 | tf_op jit(solution)/shard_map/ppermute | solution.py:46
  90.7 6.3 %collective-permute-done.18.in_3 = f32[128,512]{1,0:T(8,128)S(1)} collective-permute-done((f32[128,512]{1,0:T(8,128)S(1)}, f32[128,512]{1,0:T(8,128)S(1)}, u32[]{:S(2)}, u32[]{:S(2)}) %collective-permute-start.18) | collective-permute-done | bytes 262176 | tf_op jit(solution)/shard_map/ppermute | solution.py:46
  98.4 1.5 %collective-permute-done.25 = f32[72,512]{1,0:T(8,128)S(1)} collective-permute-done((f32[72,512]{1,0:T(8,128)S(1)}, f32[72,512]{1,0:T(8,128)S(1)}, u32[]{:S(2)}, u32[]{:S(2)}) %collective-permute-start.25) | collective-permute-done | bytes 147488 | tf_op jit(solution)/shard_map/ppermute | solution.py:65
  100.0 1.1 collective-permute-done.22
  101.3 1.3 collective-permute-start.23
  102.6 2.6 %collective-permute-start.24 = (f32[72,512]{1,0:T(8,128)S(1)}, f32[72,512]{1,0:T(8,128)S(1)}, u32[]{:S(2)}, u32[]{:S(2)}) collective-permute-start(f32[72,512]{1,0:T(8,128)S(1)} %get-tuple-element.111), channel_id=1, source_target_pairs={{0,128},{32,160},{64,192},{96,224},{128,0},{160,32},{192,64},{224,... | collective-permute-start | bytes 442376 | tf_op jit(solution)/shard_map/ppermute | solution.py:70
  105.3 1.1 collective-permute-start.26
  106.6 3.9 %collective-permute-done.24 = f32[72,512]{1,0:T(8,128)S(1)} collective-permute-done((f32[72,512]{1,0:T(8,128)S(1)}, f32[72,512]{1,0:T(8,128)S(1)}, u32[]{:S(2)}, u32[]{:S(2)}) %collective-permute-start.24) | collective-permute-done | bytes 147488 | tf_op jit(solution)/shard_map/ppermute | solution.py:70
  110.9 4.8 %collective-permute-start.30 = (f32[72,512]{1,0:T(8,128)S(1)}, f32[72,512]{1,0:T(8,128)S(1)}, u32[]{:S(2)}, u32[]{:S(2)}) collective-permute-start(f32[72,512]{1,0:T(8,128)S(1)} %fusion.18.piece), channel_id=1, source_target_pairs={{0,31},{1,0},{2,1},{3,2},{4,3},{5,4},{6,5},{7,6},{8,7},{9,8},{10,9... | collective-permute-start | bytes 442376 | tf_op jit(solution)/shard_map/ppermute | solution.py:51
  115.6 4.8 %collective-permute-start.28 = (f32[256,512]{1,0:T(8,128)S(1)}, f32[256,512]{1,0:T(8,128)S(1)}, u32[]{:S(2)}, u32[]{:S(2)}) collective-permute-start(f32[256,512]{1,0:T(8,128)S(1)} %get-tuple-element.106.plane_0), channel_id=1, source_target_pairs={{0,31},{1,0},{2,1},{3,2},{4,3},{5,4},{6,5},{7,6},{8,7},{9,8},{10,9... | collective-permute-start | bytes 1572872 | tf_op jit(solution)/shard_map/ppermute | solution.py:51
  120.4 1.2 shard_map.81.refs_0_
  121.6 1.5 %collective-permute-start.31 = (f32[64,512]{1,0:T(8,128)S(1)}, f32[64,512]{1,0:T(8,128)S(1)}, u32[]{:S(2)}, u32[]{:S(2)}) collective-permute-start(f32[64,512]{1,0:T(8,128)S(1)} %shard_map.81.refs_0_), channel_id=1, source_target_pairs={{0,64},{32,96},{64,128},{96,160},{128,192},{160,224},{192,0},{224,... | collective-permute-start | bytes 393224 | tf_op jit(solution)/shard_map/ppermute | solution.py:70
  123.2 2.4 %collective-permute-start.32 = (f32[64,512]{1,0:T(8,128)S(1)}, f32[64,512]{1,0:T(8,128)S(1)}, u32[]{:S(2)}, u32[]{:S(2)}) collective-permute-start(f32[64,512]{1,0:T(8,128)S(1)} %shard_map.81.refs_0_), channel_id=1, source_target_pairs={{0,128},{32,160},{64,192},{96,224},{128,0},{160,32},{192,64},{224,... | collective-permute-start | bytes 393224 | tf_op jit(solution)/shard_map/ppermute | solution.py:70
  125.9 1.1 collective-permute-done.31.refs_1_
  127.1 4.5 %collective-permute-start.34 = (f32[64,512]{1,0:T(8,128)S(1)}, f32[64,512]{1,0:T(8,128)S(1)}, u32[]{:S(2)}, u32[]{:S(2)}) collective-permute-start(f32[64,512]{1,0:T(8,128)S(1)} %shard_map.81.refs_0_), channel_id=1, source_target_pairs={{0,32},{32,0},{64,96},{96,64},{128,160},{160,128},{192,224},{224,1... | collective-permute-start | bytes 393224 | tf_op jit(solution)/shard_map/ppermute | solution.py:65
  131.5 2.1 %collective-permute-start.35 = (f32[64,512]{1,0:T(8,128)S(1)}, f32[64,512]{1,0:T(8,128)S(1)}, u32[]{:S(2)}, u32[]{:S(2)}) collective-permute-start(f32[64,512]{1,0:T(8,128)S(1)} %collective-permute-done.31.refs_1_), channel_id=1, source_target_pairs={{0,32},{32,0},{64,96},{96,64},{128,160},{160,128},{192,224},{224,1... | collective-permute-start | bytes 393224 | tf_op jit(solution)/shard_map/ppermute | solution.py:65
  135.6 2.0 %shard_map.82 = (f32[512,512]{1,0:T(8,128)}, f32[3,2,256,512]{3,2,1,0:T(8,128)}) custom-call(s32[8]{0:T(128)S(1)} %stack.19.place_ref, f32[256,512]{1,0:T(8,128)S(1)} %collective-permute-done.27.before, f32[256,512]{1,0:T(8,128)S(1)} %get-tuple-element.106.plane_0, f32[256,512]{1,0:T(8,128)S(1)} %get-tuple-element.105.plane_1, ...), custom_call_target="tpu_custom_call", output_to_operand_aliasing={{1}: (14, {})} | custom-call | tf_op jit(solution)/shard_map/pallas_call | solution.py:566
  (83 shorter events, 15.1 us)
Async XLA Ops:
  0.6 8.6 %copy-start.14 = (s32[1,1,9,128]{3,1,2,0:T(1,128)S(1)}, s32[1,1,9,128]{3,1,2,0:T(1,128)}, u32[]{:S(2)}) copy-start(s32[1,1,9,128]{3,1,2,0:T(1,128)} %param.8) | copy-start | bytes 13828
  2.0 11.5 %copy-start.1 = (f32[2,256,512]{2,1,0:T(8,128)S(1)}, f32[2,256,512]{2,1,0:T(8,128)}, u32[]{:S(2)}) copy-start(f32[2,256,512]{2,1,0:T(8,128)} %param.5) | copy-start | bytes 3145732
  2.7 23.8 %collective-permute-start.3 = (f32[1024,128]{1,0:T(8,128)S(1)}, f32[1024,128]{1,0:T(8,128)S(1)}, u32[]{:S(2)}, u32[]{:S(2)}) collective-permute-start(f32[1024,128]{1,0:T(8,128)S(1)} %shard_map.70), channel_id=1, source_target_pairs={{0,4},{1,5},{2,6},{3,7},{4,8},{5,9},{6,10},{7,11},{8,12},{9,13},{1... | collective-permute-start | bytes 1572872 | tf_op jit(solution)/shard_map/ppermute | solution.py:51
  5.2 21.3 %collective-permute-start.4 = (f32[1024,128]{1,0:T(8,128)S(1)}, f32[1024,128]{1,0:T(8,128)S(1)}, u32[]{:S(2)}, u32[]{:S(2)}) collective-permute-start(f32[1024,128]{1,0:T(8,128)S(1)} %shard_map.70), channel_id=1, source_target_pairs={{0,28},{1,29},{2,30},{3,31},{4,0},{5,1},{6,2},{7,3},{8,4},{9,5},{1... | collective-permute-start | bytes 1572872 | tf_op jit(solution)/shard_map/ppermute | solution.py:51
  9.8 3.9 %collective-permute-start = (s32[2,128]{1,0:T(2,128)S(1)}, s32[2,128]{1,0:T(2,128)S(1)}, u32[]{:S(2)}, u32[]{:S(2)}) collective-permute-start(s32[2,128]{1,0:T(2,128)S(1)} %get-tuple-element.59), channel_id=1, source_target_pairs={{0,3},{1,0},{2,1},{3,2},{4,7},{5,4},{6,5},{7,6},{8,11},{9,8},{10,9... | collective-permute-start | bytes 3080 | tf_op jit(solution)/shard_map/ppermute | solution.py:46
  12.4 3.9 %collective-permute-start.1 = (s32[2,128]{1,0:T(2,128)S(1)}, s32[2,128]{1,0:T(2,128)S(1)}, u32[]{:S(2)}, u32[]{:S(2)}) collective-permute-start(s32[2,128]{1,0:T(2,128)S(1)} %get-tuple-element.60), channel_id=1, source_target_pairs={{0,2},{1,3},{2,0},{3,1},{4,6},{5,7},{6,4},{7,5},{8,10},{9,11},{10,... | collective-permute-start | bytes 3080 | tf_op jit(solution)/shard_map/ppermute | solution.py:46
  12.9 17.2 %copy-start.13 = (s32[1,4,2,256]{3,2,1,0:T(2,128)S(1)}, s32[1,4,2,256]{3,2,1,0:T(2,128)}, u32[]{:S(2)}) copy-start(s32[1,4,2,256]{3,2,1,0:T(2,128)} %param.9) | copy-start | bytes 24580
  12.9 3.9 %collective-permute-start.2 = (s32[2,128]{1,0:T(2,128)S(1)}, s32[2,128]{1,0:T(2,128)S(1)}, u32[]{:S(2)}, u32[]{:S(2)}) collective-permute-start(s32[2,128]{1,0:T(2,128)S(1)} %get-tuple-element.61), channel_id=1, source_target_pairs={{0,1},{1,2},{2,3},{3,0},{4,5},{5,6},{6,7},{7,4},{8,9},{9,10},{10,1... | collective-permute-start | bytes 3080 | tf_op jit(solution)/shard_map/ppermute | solution.py:46
  18.6 6.4 %collective-permute-start.5 = (f32[512,128]{1,0:T(8,128)S(1)}, f32[512,128]{1,0:T(8,128)S(1)}, u32[]{:S(2)}, u32[]{:S(2)}) collective-permute-start(f32[512,128]{1,0:T(8,128)S(1)} %get-tuple-element.62), channel_id=1, source_target_pairs={{0,1},{1,2},{2,3},{3,0},{4,5},{5,6},{6,7},{7,4},{8,9},{9,10},{10,1... | collective-permute-start | bytes 786440 | tf_op jit(solution)/shard_map/ppermute | solution.py:46
  18.6 7.1 %collective-permute-start.6 = (f32[512,128]{1,0:T(8,128)S(1)}, f32[512,128]{1,0:T(8,128)S(1)}, u32[]{:S(2)}, u32[]{:S(2)}) collective-permute-start(f32[512,128]{1,0:T(8,128)S(1)} %get-tuple-element.63), channel_id=1, source_target_pairs={{0,3},{1,0},{2,1},{3,2},{4,7},{5,4},{6,5},{7,6},{8,11},{9,8},{10,9... | collective-permute-start | bytes 786440 | tf_op jit(solution)/shard_map/ppermute | solution.py:46
  26.5 5.2 %collective-permute-start.7 = (f32[1024,128]{1,0:T(8,128)S(1)}, f32[1024,128]{1,0:T(8,128)}, u32[]{:S(2)}, u32[]{:S(2)}) collective-permute-start(f32[1024,128]{1,0:T(8,128)S(1)} %collective-permute-done.3.low_a), channel_id=1, source_target_pairs={{0,32},{32,0},{64,96},{96,64},{128,160},{160,128},{192,224},{224,1... | collective-permute-start | bytes 1572872 | tf_op jit(solution)/shard_map/ppermute | solution.py:65
  30.0 2.4 %collective-permute-start.8 = (f32[1024,128]{1,0:T(8,128)S(1)}, f32[1024,128]{1,0:T(8,128)}, u32[]{:S(2)}, u32[]{:S(2)}) collective-permute-start(f32[1024,128]{1,0:T(8,128)S(1)} %collective-permute-done.4.high_a), channel_id=1, source_target_pairs={{0,32},{32,0},{64,96},{96,64},{128,160},{160,128},{192,224},{224,1... | collective-permute-start | bytes 1572872 | tf_op jit(solution)/shard_map/ppermute | solution.py:65
  30.2 21.3 %copy-start.2 = (f32[1,2,256,512]{3,2,1,0:T(8,128)S(1)}, f32[1,2,256,512]{3,2,1,0:T(8,128)}, u32[]{:S(2)}) copy-start(f32[1,2,256,512]{3,2,1,0:T(8,128)} %param.6) | copy-start | bytes 3145732
  30.2 21.3 %copy-start.9 = (f32[512,128]{1,0:T(8,128)S(1)}, f32[512,128]{1,0:T(8,128)}, u32[]{:S(2)}) copy-start(f32[512,128]{1,0:T(8,128)} %copy-done.8) | copy-start | bytes 786436
  30.2 21.3 %copy-start.11 = (f32[512,128]{1,0:T(8,128)S(1)}, f32[512,128]{1,0:T(8,128)}, u32[]{:S(2)}) copy-start(f32[512,128]{1,0:T(8,128)} %copy-done.10) | copy-start | bytes 786436
  30.2 12.9 %collective-permute-start.12 = (f32[512,128]{1,0:T(8,128)}, f32[512,128]{1,0:T(8,128)S(1)}, u32[]{:S(2)}, u32[]{:S(2)}) collective-permute-start(f32[512,128]{1,0:T(8,128)} %copy-done.12), channel_id=1, source_target_pairs={{0,2},{1,3},{2,0},{3,1},{4,6},{5,7},{6,4},{7,5},{8,10},{9,11},{10,... | collective-permute-start | bytes 786440 | tf_op jit(solution)/shard_map/ppermute | solution.py:46
  35.3 10.0 %collective-permute-start.10 = (f32[512,128]{1,0:T(8,128)S(1)}, f32[512,128]{1,0:T(8,128)S(1)}, u32[]{:S(2)}, u32[]{:S(2)}) collective-permute-start(f32[512,128]{1,0:T(8,128)S(1)} %get-tuple-element.67), channel_id=1, source_target_pairs={{0,2},{1,3},{2,0},{3,1},{4,6},{5,7},{6,4},{7,5},{8,10},{9,11},{10,... | collective-permute-start | bytes 786440 | tf_op jit(solution)/shard_map/ppermute | solution.py:46
  36.2 14.6 %collective-permute-start.11 = (f32[512,128]{1,0:T(8,128)S(1)}, f32[512,128]{1,0:T(8,128)S(1)}, u32[]{:S(2)}, u32[]{:S(2)}) collective-permute-start(f32[512,128]{1,0:T(8,128)S(1)} %get-tuple-element.68), channel_id=1, source_target_pairs={{0,3},{1,0},{2,1},{3,2},{4,7},{5,4},{6,5},{7,6},{8,11},{9,8},{10,9... | collective-permute-start | bytes 786440 | tf_op jit(solution)/shard_map/ppermute | solution.py:46
  38.4 13.0 %collective-permute-start.9 = (f32[512,128]{1,0:T(8,128)S(1)}, f32[512,128]{1,0:T(8,128)S(1)}, u32[]{:S(2)}, u32[]{:S(2)}) collective-permute-start(f32[512,128]{1,0:T(8,128)S(1)} %get-tuple-element.66), channel_id=1, source_target_pairs={{0,1},{1,2},{2,3},{3,0},{4,5},{5,6},{6,7},{7,4},{8,9},{9,10},{10,1... | collective-permute-start | bytes 786440 | tf_op jit(solution)/shard_map/ppermute | solution.py:46
  57.3 2.7 %copy-start.3 = (bf16[2048,512]{1,0:T(8,128)(2,1)}, bf16[2048,512]{1,0:T(8,128)(2,1)S(1)}, u32[]{:S(2)}) copy-start(bf16[2048,512]{1,0:T(8,128)(2,1)S(1)} %get-tuple-element.76.push_high) | copy-start | bytes 6291460
  57.4 2.7 %copy-start.5 = (bf16[2048,512]{1,0:T(8,128)(2,1)}, bf16[2048,512]{1,0:T(8,128)(2,1)S(1)}, u32[]{:S(2)}) copy-start(bf16[2048,512]{1,0:T(8,128)(2,1)S(1)} %get-tuple-element.77.push_low) | copy-start | bytes 6291460
  60.0 14.2 %collective-permute-start.13 = (f32[128,512]{1,0:T(8,128)}, f32[128,512]{1,0:T(8,128)S(1)}, u32[]{:S(2)}, u32[]{:S(2)}) collective-permute-start(f32[128,512]{1,0:T(8,128)} %get-tuple-element.78), channel_id=1, source_target_pairs={{0,3},{1,0},{2,1},{3,2},{4,7},{5,4},{6,5},{7,6},{8,11},{9,8},{10,9... | collective-permute-start | bytes 786440 | tf_op jit(solution)/shard_map/ppermute | solution.py:46
  62.3 12.0 %collective-permute-start.14 = (f32[128,512]{1,0:T(8,128)}, f32[128,512]{1,0:T(8,128)}, u32[]{:S(2)}, u32[]{:S(2)}) collective-permute-start(f32[128,512]{1,0:T(8,128)} %get-tuple-element.79), channel_id=1, source_target_pairs={{0,2},{1,3},{2,0},{3,1},{4,6},{5,7},{6,4},{7,5},{8,10},{9,11},{10,... | collective-permute-start | bytes 786440 | tf_op jit(solution)/shard_map/ppermute | solution.py:46
  62.3 15.1 %collective-permute-start.15 = (f32[128,512]{1,0:T(8,128)}, f32[128,512]{1,0:T(8,128)}, u32[]{:S(2)}, u32[]{:S(2)}) collective-permute-start(f32[128,512]{1,0:T(8,128)} %get-tuple-element.80), channel_id=1, source_target_pairs={{0,1},{1,2},{2,3},{3,0},{4,5},{5,6},{6,7},{7,4},{8,9},{9,10},{10,1... | collective-permute-start | bytes 786440 | tf_op jit(solution)/shard_map/ppermute | solution.py:46
  64.6 1.6 %copy-start.4 = (bf16[2048,512]{1,0:T(8,128)(2,1)S(1)}, bf16[2048,512]{1,0:T(8,128)(2,1)}, u32[]{:S(2)}) copy-start(bf16[2048,512]{1,0:T(8,128)(2,1)} %copy-done.3) | copy-start | bytes 6291460
  66.2 1.6 %copy-start.6 = (bf16[2048,512]{1,0:T(8,128)(2,1)S(1)}, bf16[2048,512]{1,0:T(8,128)(2,1)}, u32[]{:S(2)}) copy-start(bf16[2048,512]{1,0:T(8,128)(2,1)} %copy-done.5) | copy-start | bytes 6291460
  80.1 3.4 %collective-permute-start.19 = (f32[576,512]{1,0:T(8,128)S(1)}, f32[576,512]{1,0:T(8,128)S(1)}, u32[]{:S(2)}, u32[]{:S(2)}) collective-permute-start(f32[576,512]{1,0:T(8,128)S(1)} %get-tuple-element.97), channel_id=1, source_target_pairs={{0,32},{32,0},{64,96},{96,64},{128,160},{160,128},{192,224},{224,1... | collective-permute-start | bytes 3538952 | tf_op jit(solution)/shard_map/ppermute | solution.py:65
  81.0 7.9 %collective-permute-start.16 = (f32[128,512]{1,0:T(8,128)S(1)}, f32[128,512]{1,0:T(8,128)S(1)}, u32[]{:S(2)}, u32[]{:S(2)}) collective-permute-start(f32[128,512]{1,0:T(8,128)S(1)} %get-tuple-element.86), channel_id=1, source_target_pairs={{0,3},{1,0},{2,1},{3,2},{4,7},{5,4},{6,5},{7,6},{8,11},{9,8},{10,9... | collective-permute-start | bytes 786440 | tf_op jit(solution)/shard_map/ppermute | solution.py:46
  81.6 9.1 %collective-permute-start.17 = (f32[128,512]{1,0:T(8,128)S(1)}, f32[128,512]{1,0:T(8,128)S(1)}, u32[]{:S(2)}, u32[]{:S(2)}) collective-permute-start(f32[128,512]{1,0:T(8,128)S(1)} %get-tuple-element.87), channel_id=1, source_target_pairs={{0,2},{1,3},{2,0},{3,1},{4,6},{5,7},{6,4},{7,5},{8,10},{9,11},{10,... | collective-permute-start | bytes 786440 | tf_op jit(solution)/shard_map/ppermute | solution.py:46
  82.2 14.8 %collective-permute-start.18 = (f32[128,512]{1,0:T(8,128)S(1)}, f32[128,512]{1,0:T(8,128)S(1)}, u32[]{:S(2)}, u32[]{:S(2)}) collective-permute-start(f32[128,512]{1,0:T(8,128)S(1)} %get-tuple-element.88), channel_id=1, source_target_pairs={{0,1},{1,2},{2,3},{3,0},{4,5},{5,6},{6,7},{7,4},{8,9},{9,10},{10,1... | collective-permute-start | bytes 786440 | tf_op jit(solution)/shard_map/ppermute | solution.py:46
  83.7 16.3 %collective-permute-start.21 = (f32[288,512]{1,0:T(8,128)S(1)}, f32[288,512]{1,0:T(8,128)S(1)}, u32[]{:S(2)}, u32[]{:S(2)}) collective-permute-start(f32[288,512]{1,0:T(8,128)S(1)} %get-tuple-element.113), channel_id=1, source_target_pairs={{0,28},{1,29},{2,30},{3,31},{4,0},{5,1},{6,2},{7,3},{8,4},{9,5},{1... | collective-permute-start | bytes 1769480 | tf_op jit(solution)/shard_map/ppermute | solution.py:51
  85.7 15.4 %collective-permute-start.22 = (f32[288,512]{1,0:T(8,128)S(1)}, f32[288,512]{1,0:T(8,128)S(1)}, u32[]{:S(2)}, u32[]{:S(2)}) collective-permute-start(f32[288,512]{1,0:T(8,128)S(1)} %get-tuple-element.114), channel_id=1, source_target_pairs={{0,4},{1,5},{2,6},{3,7},{4,8},{5,9},{6,10},{7,11},{8,12},{9,13},{1... | collective-permute-start | bytes 1769480 | tf_op jit(solution)/shard_map/ppermute | solution.py:51
  97.8 2.2 %collective-permute-start.20 = (f32[216,512]{1,0:T(8,128)S(1)}, f32[216,512]{1,0:T(8,128)S(1)}, u32[]{:S(2)}, u32[]{:S(2)}) collective-permute-start(f32[216,512]{1,0:T(8,128)S(1)} %get-tuple-element.103), channel_id=1, source_target_pairs={{0,32},{32,0},{64,96},{96,64},{128,160},{160,128},{192,224},{224,1... | collective-permute-start | bytes 1327112 | tf_op jit(solution)/shard_map/ppermute | solution.py:65
  98.3 1.6 %collective-permute-start.25 = (f32[72,512]{1,0:T(8,128)S(1)}, f32[72,512]{1,0:T(8,128)S(1)}, u32[]{:S(2)}, u32[]{:S(2)}) collective-permute-start(f32[72,512]{1,0:T(8,128)S(1)} %get-tuple-element.104), channel_id=1, source_target_pairs={{0,32},{32,0},{64,96},{96,64},{128,160},{160,128},{192,224},{224,1... | collective-permute-start | bytes 442376 | tf_op jit(solution)/shard_map/ppermute | solution.py:65
  101.3 5.3 %collective-permute-start.23 = (f32[72,512]{1,0:T(8,128)S(1)}, f32[72,512]{1,0:T(8,128)S(1)}, u32[]{:S(2)}, u32[]{:S(2)}) collective-permute-start(f32[72,512]{1,0:T(8,128)S(1)} %get-tuple-element.110), channel_id=1, source_target_pairs={{0,64},{32,96},{64,128},{96,160},{128,192},{160,224},{192,0},{224,... | collective-permute-start | bytes 442376 | tf_op jit(solution)/shard_map/ppermute | solution.py:70
  102.6 7.8 %collective-permute-start.24 = (f32[72,512]{1,0:T(8,128)S(1)}, f32[72,512]{1,0:T(8,128)S(1)}, u32[]{:S(2)}, u32[]{:S(2)}) collective-permute-start(f32[72,512]{1,0:T(8,128)S(1)} %get-tuple-element.111), channel_id=1, source_target_pairs={{0,128},{32,160},{64,192},{96,224},{128,0},{160,32},{192,64},{224,... | collective-permute-start | bytes 442376 | tf_op jit(solution)/shard_map/ppermute | solution.py:70
  105.3 5.4 %collective-permute-start.26 = (f32[72,512]{1,0:T(8,128)S(1)}, f32[72,512]{1,0:T(8,128)S(1)}, u32[]{:S(2)}, u32[]{:S(2)}) collective-permute-start(f32[72,512]{1,0:T(8,128)S(1)} %get-tuple-element.112), channel_id=1, source_target_pairs={{0,192},{32,224},{64,0},{96,32},{128,64},{160,96},{192,128},{224,1... | collective-permute-start | bytes 442376 | tf_op jit(solution)/shard_map/ppermute | solution.py:70
  110.8 9.7 %collective-permute-start.29 = (f32[72,512]{1,0:T(8,128)S(1)}, f32[72,512]{1,0:T(8,128)S(1)}, u32[]{:S(2)}, u32[]{:S(2)}) collective-permute-start(f32[72,512]{1,0:T(8,128)S(1)} %fusion.18.piece), channel_id=1, source_target_pairs={{0,1},{1,2},{2,3},{3,4},{4,5},{5,6},{6,7},{7,8},{8,9},{9,10},{10,1... | collective-permute-start | bytes 442376 | tf_op jit(solution)/shard_map/ppermute | solution.py:51
  110.9 9.6 %collective-permute-start.30 = (f32[72,512]{1,0:T(8,128)S(1)}, f32[72,512]{1,0:T(8,128)S(1)}, u32[]{:S(2)}, u32[]{:S(2)}) collective-permute-start(f32[72,512]{1,0:T(8,128)S(1)} %fusion.18.piece), channel_id=1, source_target_pairs={{0,31},{1,0},{2,1},{3,2},{4,3},{5,4},{6,5},{7,6},{8,7},{9,8},{10,9... | collective-permute-start | bytes 442376 | tf_op jit(solution)/shard_map/ppermute | solution.py:51
  115.6 20.0 %collective-permute-start.27 = (f32[256,512]{1,0:T(8,128)S(1)}, f32[256,512]{1,0:T(8,128)S(1)}, u32[]{:S(2)}, u32[]{:S(2)}) collective-permute-start(f32[256,512]{1,0:T(8,128)S(1)} %get-tuple-element.105.plane_1), channel_id=1, source_target_pairs={{0,1},{1,2},{2,3},{3,4},{4,5},{5,6},{6,7},{7,8},{8,9},{9,10},{10,1... | collective-permute-start | bytes 1572872 | tf_op jit(solution)/shard_map/ppermute | solution.py:51
  115.6 20.0 %collective-permute-start.28 = (f32[256,512]{1,0:T(8,128)S(1)}, f32[256,512]{1,0:T(8,128)S(1)}, u32[]{:S(2)}, u32[]{:S(2)}) collective-permute-start(f32[256,512]{1,0:T(8,128)S(1)} %get-tuple-element.106.plane_0), channel_id=1, source_target_pairs={{0,31},{1,0},{2,1},{3,2},{4,3},{5,4},{6,5},{7,6},{8,7},{9,8},{10,9... | collective-permute-start | bytes 1572872 | tf_op jit(solution)/shard_map/ppermute | solution.py:51
  121.6 5.4 %collective-permute-start.31 = (f32[64,512]{1,0:T(8,128)S(1)}, f32[64,512]{1,0:T(8,128)S(1)}, u32[]{:S(2)}, u32[]{:S(2)}) collective-permute-start(f32[64,512]{1,0:T(8,128)S(1)} %shard_map.81.refs_0_), channel_id=1, source_target_pairs={{0,64},{32,96},{64,128},{96,160},{128,192},{160,224},{192,0},{224,... | collective-permute-start | bytes 393224 | tf_op jit(solution)/shard_map/ppermute | solution.py:70
  123.2 8.4 %collective-permute-start.32 = (f32[64,512]{1,0:T(8,128)S(1)}, f32[64,512]{1,0:T(8,128)S(1)}, u32[]{:S(2)}, u32[]{:S(2)}) collective-permute-start(f32[64,512]{1,0:T(8,128)S(1)} %shard_map.81.refs_0_), channel_id=1, source_target_pairs={{0,128},{32,160},{64,192},{96,224},{128,0},{160,32},{192,64},{224,... | collective-permute-start | bytes 393224 | tf_op jit(solution)/shard_map/ppermute | solution.py:70
  125.6 8.0 %collective-permute-start.33 = (f32[64,512]{1,0:T(8,128)S(1)}, f32[64,512]{1,0:T(8,128)S(1)}, u32[]{:S(2)}, u32[]{:S(2)}) collective-permute-start(f32[64,512]{1,0:T(8,128)S(1)} %shard_map.81.refs_0_), channel_id=1, source_target_pairs={{0,192},{32,224},{64,0},{96,32},{128,64},{160,96},{192,128},{224,1... | collective-permute-start | bytes 393224 | tf_op jit(solution)/shard_map/ppermute | solution.py:70
  127.1 7.2 %collective-permute-start.34 = (f32[64,512]{1,0:T(8,128)S(1)}, f32[64,512]{1,0:T(8,128)S(1)}, u32[]{:S(2)}, u32[]{:S(2)}) collective-permute-start(f32[64,512]{1,0:T(8,128)S(1)} %shard_map.81.refs_0_), channel_id=1, source_target_pairs={{0,32},{32,0},{64,96},{96,64},{128,160},{160,128},{192,224},{224,1... | collective-permute-start | bytes 393224 | tf_op jit(solution)/shard_map/ppermute | solution.py:65
  131.5 3.1 %collective-permute-start.35 = (f32[64,512]{1,0:T(8,128)S(1)}, f32[64,512]{1,0:T(8,128)S(1)}, u32[]{:S(2)}, u32[]{:S(2)}) collective-permute-start(f32[64,512]{1,0:T(8,128)S(1)} %collective-permute-done.31.refs_1_), channel_id=1, source_target_pairs={{0,32},{32,0},{64,96},{96,64},{128,160},{160,128},{192,224},{224,1... | collective-permute-start | bytes 393224 | tf_op jit(solution)/shard_map/ppermute | solution.py:65
  133.6 1.6 %collective-permute-start.36 = (f32[64,512]{1,0:T(8,128)S(1)}, f32[64,512]{1,0:T(8,128)S(1)}, u32[]{:S(2)}, u32[]{:S(2)}) collective-permute-start(f32[64,512]{1,0:T(8,128)S(1)} %collective-permute-done.32.refs_2_), channel_id=1, source_target_pairs={{0,32},{32,0},{64,96},{96,64},{128,160},{160,128},{192,224},{224,1... | collective-permute-start | bytes 393224 | tf_op jit(solution)/shard_map/ppermute | solution.py:65
  134.2 1.3 collective-permute-start.37
  (5 other events, 4.8 us)

commit v4 on v3

--- a/solution.py
+++ b/solution.py
@@ -70,28 +70,27 @@
     return lax.ppermute(value, "subj", [(i, (i + 2 * step) % count) for i in range(count)])
 
 
-def spread_rows(source_ref, out_ref):
-    count, width = source_ref.shape
-    parts = width // LANES
+def spread_rows(source_ref, start, count, out_ref):
+    parts = source_ref.shape[1] // LANES
 
     def group(block, carry):
         first = pl.multiple_of(block * 8, 8)
         for part in range(parts):
             out_ref[pl.ds(first * parts + part, 8, stride=parts), :] = source_ref[
-                pl.ds(first, 8), part * LANES:(part + 1) * LANES
+                pl.ds(pl.multiple_of(start + first, 8), 8), part * LANES:(part + 1) * LANES
             ]
         return carry
 
     lax.fori_loop(0, count // 8, group, 0, unroll=4)
 
 
-def spread_plane_kernel(place_ref, source_ref, out_ref, held, sem):
-    rows = held.shape[0]
-    start = pl.multiple_of(place_ref[1] * rows, rows)
-    copy = pltpu.make_async_copy(source_ref.at[pl.ds(start, rows)], held, sem)
-    copy.start()
-    copy.wait()
-    spread_rows(held, out_ref)
+def spread_plane_kernel(place_ref, source_ref, out_ref):
+    rows = source_ref.shape[0] // 2
+    spread_rows(source_ref, place_ref[1] * rows, rows, out_ref)
+
+
+def spread_kernel(source_ref, out_ref):
+    spread_rows(source_ref, 0, source_ref.shape[0], out_ref)
 
 
 def request_kernel(place_ref, lists_ref, self_ref, out_1, out_2, out_3):
@@ -142,20 +141,22 @@
     lax.fori_loop(0, count // unit, group, 0, unroll=2)
 
 
-def own_lines_kernel(lists_0, lists_1, lists_2, lists_3, held, out_0, out_1, out_2, out_3):
-    for lists, out in ((lists_1, out_1), (lists_2, out_2), (lists_3, out_3), (lists_0, out_0)):
+def own_lines_kernel(lists_1, lists_2, lists_3, held, out_1, out_2, out_3):
+    for lists, out in ((lists_1, out_1), (lists_2, out_2), (lists_3, out_3)):
         copy_lines(lists, 0, held, out)
 
 
-def cross_lines_kernel(
-    lists_0, lists_1, lists_2, lists_3, low_a, low_b, high_a, high_b,
-    out_low, out_high, out_1, out_2, out_3, held,
-):
+def cross_lines_kernel(lists_1, lists_2, lists_3, low_a, low_b, high_a, high_b, out_1, out_2, out_3, held):
     fill(held, (low_a, low_b, high_a, high_b))
-    for lists, row, out in (
-        (lists_1, 1, out_1), (lists_2, 1, out_2), (lists_3, 1, out_3), (lists_0, 1, out_low), (lists_0, 2, out_high),
-    ):
-        copy_lines(lists, row, held, out)
+    for lists, out in ((lists_1, out_1), (lists_2, out_2), (lists_3, out_3)):
+        copy_lines(lists, 1, held, out)
+
+
+def self_lines_kernel(lists, own, low_a, low_b, high_a, high_b, out_low, out_high, out_own, held):
+    fill(held, (low_a, low_b, high_a, high_b))
+    copy_lines(lists, 0, own, out_own)
+    copy_lines(lists, 1, held, out_low)
+    copy_lines(lists, 2, held, out_high)
 
 
 def split_parts(value):
@@ -444,25 +445,28 @@
         request_kernel, (jax.ShapeDtypeStruct((3, capacity), I32),) + (message,) * 3, [SMEM, VMEM], (VMEM,) * 4,
     )(place, lists)
     plane = call(
-        spread_plane_kernel, f32s(row_count * parts, LANES), [SMEM, ANY], VMEM,
-        [pltpu.VMEM((row_count, cell_count), F32), pltpu.SemaphoreType.DMA],
+        spread_plane_kernel, f32s(row_count * parts, LANES), [SMEM, VMEM], VMEM,
     )(place, lines)
-    spread = call(spread_rows, f32s(line_count * parts, LANES), [VMEM], VMEM)(lines)
+    spread = call(spread_kernel, f32s(line_count * parts, LANES), [VMEM], VMEM)(lines)
     from_low = along_z(plane, 1)
     from_high = along_z(plane, -1)
     asked = [self_lists] + ring_of(along_x, messages, -1)
 
     own = call(
-        own_lines_kernel, (packed,) * 4, [SMEM] * 4 + [VMEM], (VMEM,) * 4,
-    )(*asked, spread)
-    got_own = ring_of(along_x, own[1:], 1)
+        own_lines_kernel, (packed,) * 3, [SMEM] * 3 + [VMEM], (VMEM,) * 3,
+    )(*asked[1:], spread)
+    got_own = ring_of(along_x, own, 1)
     from_low, from_high, _ = lax.optimization_barrier((from_low, from_high, (got_own[0], got_own[2])))
     from_low_b, from_high_b = other_core(from_low), other_core(from_high)
+    slabs = (from_low, from_low_b, from_high, from_high_b)
+    held_slabs = [pltpu.VMEM((2 * line_count * parts, LANES), F32)]
     cross = call(
-        cross_lines_kernel, (packed,) * 5, [SMEM] * 4 + [VMEM] * 4, (VMEM,) * 5,
-        [pltpu.VMEM((2 * line_count * parts, LANES), F32)],
-    )(*asked, from_low, from_low_b, from_high, from_high_b)
-    got_cross = ring_of(along_x, cross[2:], 1)
+        cross_lines_kernel, (packed,) * 3, [SMEM] * 3 + [VMEM] * 4, (VMEM,) * 3, held_slabs,
+    )(*asked[1:], *slabs)
+    got_cross = ring_of(along_x, cross, 1)
+    self_low, self_high, self_own = call(
+        self_lines_kernel, (packed,) * 3, [SMEM] + [VMEM] * 5, (VMEM,) * 3, held_slabs,
+    )(self_lists, spread, *slabs)
 
     slot_ids = corners.reshape(4, line_count)
     offset = slot_ids // capacity - REACH
@@ -476,7 +480,7 @@
     )
     slot_ids = held_at * capacity + slot_ids % capacity
     flat_ids = slot_ids.reshape(1, 4 * line_count)
-    blocks = got_cross + [cross[0], cross[1]] + got_own + [own[0]]
+    blocks = got_cross + [self_low, self_high] + got_own + [self_own]
     here_part, ahead_part = call(
         weight_kernel, (f32s(4, line_count, cell_count),) * 2, [VMEM], (VMEM,) * 2,
     )(fractions.reshape(3, line_count, cell_count))

time: 138 us -> 138 us (level)
  waiting for transfers between devices: 41.9 us -> 38.2 us
  starting transfers between devices: 54.4 us -> 56.3 us
  Pallas kernels: 31.2 us -> 32.6 us
    ppermute x15, waiting for transfers between devices: 29.7 us -> 26.9 us  [along_x(): return lax.ppermute(value, 'slab', route)]
    ppermute x15, starting transfers between devices: 14.5 us -> 16.6 us  [along_x(): return lax.ppermute(value, 'slab', route)]
    pallas_call x4 -> x5, Pallas kernels: 4.78 us -> 6.17 us  [the longest x1 2.25 us: on_device(): call(cross_lines_kernel, (packed,) * 3, [SMEM] * 3 + [VMEM] * 4, (VMEM,)...]
    unnamed x32 -> x36, local copies, waits for them, and re-layouts: 7.99 us -> 7.93 us
  transfers between devices with their start and end apart: 38 -> 38, of which waited for: 22 -> 21; matrix products, arithmetic and copies ran while one was open for 1% -> 1% of each run, Pallas kernels for 13% -> 14%
where the time goes in v4:
time: 138 us; the launch traced here: 137 us
  starting transfers between devices  56.3 us (41%)
  waiting for transfers between devices  38.2 us (28%)
  Pallas kernels  32.6 us (24%)
  local copies, waits for them, and re-layouts  8.03 us (6%)
    ppermute x15, waiting for transfers between devices, along_x(): return lax.ppermute(value, 'slab', route)  26.9 us
    ppermute x8, starting transfers between devices, along_slab(): lax.ppermute(value, 'slab', [(i, (i + step) % count) for i in range(count)])  17.9 us
    ppermute x15, starting transfers between devices, along_x(): return lax.ppermute(value, 'slab', route)  16.6 us
    ppermute x9, starting transfers between devices, other_core(): return lax.ppermute(value, 'subj', [(i, i ^ 1) for i in range(count)])  12.5 us
    ppermute x6, starting transfers between devices, along_y(): lax.ppermute(value, 'subj', [(i, (i + 2 * step) % count) for i in range(c...  9.36 us
    unnamed x36, local copies, waits for them, and re-layouts  7.93 us
    pallas_call x1, Pallas kernels, on_device(): call(warp_kernel, (half,) * 2 + (push_part,) * 2, [SMEM] + [VMEM] * 12, (...  5.86 us
    ppermute x6, waiting for transfers between devices, along_y(): lax.ppermute(value, 'subj', [(i, (i + 2 * step) % count) for i in range(c...  5.49 us
  transfers between devices with their start and end apart: 38, of which 21 were waited for; matrix products, arithmetic and copies ran while one was open for 1% of the time, Pallas kernels for 14%

profile of v4, /device:TPU:1, one launch (start us, length us, event | category | flops | bytes accessed | tf_op | source)
XLA Modules:
  0.0 137.4 jit_solution(972454835698930695)
XLA Ops:
  0.8 1.2 copy-done
  2.6 2.5 %collective-permute-start.3 = (f32[1024,128]{1,0:T(8,128)S(1)}, f32[1024,128]{1,0:T(8,128)S(1)}, u32[]{:S(2)}, u32[]{:S(2)}) collective-permute-start(f32[1024,128]{1,0:T(8,128)S(1)} %shard_map.70), channel_id=1, source_target_pairs={{0,4},{1,5},{2,6},{3,7},{4,8},{5,9},{6,10},{7,11},{8,12},{9,13},{1... | collective-permute-start | bytes 1572872 | tf_op jit(solution)/shard_map/ppermute | solution.py:51
  5.2 4.0 %collective-permute-start.4 = (f32[1024,128]{1,0:T(8,128)S(1)}, f32[1024,128]{1,0:T(8,128)S(1)}, u32[]{:S(2)}, u32[]{:S(2)}) collective-permute-start(f32[1024,128]{1,0:T(8,128)S(1)} %shard_map.70), channel_id=1, source_target_pairs={{0,28},{1,29},{2,30},{3,31},{4,0},{5,1},{6,2},{7,3},{8,4},{9,5},{1... | collective-permute-start | bytes 1572872 | tf_op jit(solution)/shard_map/ppermute | solution.py:51
  9.8 2.6 %collective-permute-start = (s32[2,128]{1,0:T(2,128)S(1)}, s32[2,128]{1,0:T(2,128)S(1)}, u32[]{:S(2)}, u32[]{:S(2)}) collective-permute-start(s32[2,128]{1,0:T(2,128)S(1)} %get-tuple-element.58), channel_id=1, source_target_pairs={{0,3},{1,0},{2,1},{3,2},{4,7},{5,4},{6,5},{7,6},{8,11},{9,8},{10,9... | collective-permute-start | bytes 3080 | tf_op jit(solution)/shard_map/ppermute | solution.py:46
  13.7 2.6 %collective-permute-done.1.lists_2 = s32[2,128]{1,0:T(2,128)S(1)} collective-permute-done((s32[2,128]{1,0:T(2,128)S(1)}, s32[2,128]{1,0:T(2,128)S(1)}, u32[]{:S(2)}, u32[]{:S(2)}) %collective-permute-start.1) | collective-permute-done | bytes 1056 | tf_op jit(solution)/shard_map/ppermute | solution.py:46
  16.8 0.9 shard_map.72
  18.4 2.7 %collective-permute-start.6 = (f32[512,128]{1,0:T(8,128)S(1)}, f32[512,128]{1,0:T(8,128)S(1)}, u32[]{:S(2)}, u32[]{:S(2)}) collective-permute-start(f32[512,128]{1,0:T(8,128)S(1)} %get-tuple-element.62), channel_id=1, source_target_pairs={{0,3},{1,0},{2,1},{3,2},{4,7},{5,4},{6,5},{7,6},{8,11},{9,8},{10,9... | collective-permute-start | bytes 786440 | tf_op jit(solution)/shard_map/ppermute | solution.py:46
  21.1 3.8 %collective-permute-done.5.refs_9_ = f32[512,128]{1,0:T(8,128)S(1)} collective-permute-done((f32[512,128]{1,0:T(8,128)S(1)}, f32[512,128]{1,0:T(8,128)S(1)}, u32[]{:S(2)}, u32[]{:S(2)}) %collective-permute-start.5) | collective-permute-done | bytes 262176 | tf_op jit(solution)/shard_map/ppermute | solution.py:46
  25.6 3.6 %collective-permute-start.7 = (f32[1024,128]{1,0:T(8,128)S(1)}, f32[1024,128]{1,0:T(8,128)}, u32[]{:S(2)}, u32[]{:S(2)}) collective-permute-start(f32[1024,128]{1,0:T(8,128)S(1)} %collective-permute-done.3.low_a), channel_id=1, source_target_pairs={{0,32},{32,0},{64,96},{96,64},{128,160},{160,128},{192,224},{224,1... | collective-permute-start | bytes 1572872 | tf_op jit(solution)/shard_map/ppermute | solution.py:65
  29.3 1.3 collective-permute-start.12
  31.6 2.2 %shard_map.73 = (f32[512,128]{1,0:T(8,128)S(1)}, f32[512,128]{1,0:T(8,128)S(1)}, f32[512,128]{1,0:T(8,128)S(1)}) custom-call(s32[2,128]{1,0:T(2,128)S(1)} %collective-permute-done.lists_1, s32[2,128]{1,0:T(2,128)S(1)} %collective-permute-done.1.lists_2, s32[2,128]{1,0:T(2,128)S(1)} %collective-permute-done.2.lists_3, ...), custom_call_target="tpu_custom_call" | custom-call | tf_op jit(solution)/shard_map/pallas_call | solution.py:463
  33.9 1.3 collective-permute-start.10
  35.1 2.6 %collective-permute-start.11 = (f32[512,128]{1,0:T(8,128)S(1)}, f32[512,128]{1,0:T(8,128)S(1)}, u32[]{:S(2)}, u32[]{:S(2)}) collective-permute-start(f32[512,128]{1,0:T(8,128)S(1)} %get-tuple-element.67), channel_id=1, source_target_pairs={{0,3},{1,0},{2,1},{3,2},{4,7},{5,4},{6,5},{7,6},{8,11},{9,8},{10,9... | collective-permute-start | bytes 786440 | tf_op jit(solution)/shard_map/ppermute | solution.py:46
  37.8 3.0 %shard_map.68 = (f32[4,512,512]{2,1,0:T(8,128)S(1)}, f32[4,512,512]{2,1,0:T(8,128)S(1)}) custom-call(bf16[3,512,512]{2,1,0:T(8,128)(2,1)S(1)} %bitcast.21), custom_call_target="tpu_custom_call" | custom-call | tf_op jit(solution)/shard_map/pallas_call | solution.py:484
  40.9 1.0 copy-done.8
  42.0 1.0 copy-done.10
  43.0 2.2 %shard_map.74 = (f32[512,128]{1,0:T(8,128)S(1)}, f32[512,128]{1,0:T(8,128)S(1)}, f32[512,128]{1,0:T(8,128)S(1)}) custom-call(s32[3,128]{1,0:T(4,128)S(1)} %get-tuple-element.68.lists.lists_0, f32[2048,128]{1,0:T(8,128)S(1)} %shard_map.71.held.own, f32[1024,128]{1,0:T(8,128)S(1)} %copy-done.8, f32[1024,128]{1,0:T(8,128)} %collective-permute-done.7.low_b, ...), custom_call_target="tpu_custom_call" | custom-call | tf_op jit(solution)/shard_map/pallas_call | solution.py:467
  45.2 5.2 %collective-permute-done.11.refs_6_ = f32[512,128]{1,0:T(8,128)S(1)} collective-permute-done((f32[512,128]{1,0:T(8,128)S(1)}, f32[512,128]{1,0:T(8,128)S(1)}, u32[]{:S(2)}, u32[]{:S(2)}) %collective-permute-start.11) | collective-permute-done | bytes 262176 | tf_op jit(solution)/shard_map/ppermute | solution.py:46
  50.6 5.9 %shard_map.75 = (f32[256,512]{1,0:T(8,128)S(1)}, f32[256,512]{1,0:T(8,128)S(1)}, bf16[2048,512]{1,0:T(8,128)(2,1)S(1)}, bf16[2048,512]{1,0:T(8,128)(2,1)S(1)}) custom-call(s32[4,512]{1,0:T(4,128)S(1)} %fusion.24.refs_0_, f32[4,512,512]{2,1,0:T(8,128)S(1)} %get-tuple-element.56.refs_1_, f32[4,512,512]{2,1,0:T(8,128)S(1)} %get-tuple-element.57.refs_2_, ...), custom_call_target="tpu_custom_call" | custom-call | tf_op jit(solution)/shard_map/pallas_call | solution.py:489
  56.5 2.6 %shard_map.77 = (f32[128,512]{1,0:T(8,128)}, f32[128,512]{1,0:T(8,128)}, f32[128,512]{1,0:T(8,128)}) custom-call(s32[1,2048]{1,0:T(1,128)S(1)} %fusion.20.ids_ref, bf16[2048,512]{1,0:T(8,128)(2,1)S(1)} %get-tuple-element.76.push_high, bf16[2048,512]{1,0:T(8,128)(2,1)S(1)} %get-tuple-element.77.push_low), custom_call_target="tpu_custom_call" | custom-call | tf_op jit(solution)/shard_map/pallas_call | solution.py:502
  59.1 3.0 %collective-permute-start.13 = (f32[128,512]{1,0:T(8,128)}, f32[128,512]{1,0:T(8,128)S(1)}, u32[]{:S(2)}, u32[]{:S(2)}) collective-permute-start(f32[128,512]{1,0:T(8,128)} %get-tuple-element.78), channel_id=1, source_target_pairs={{0,3},{1,0},{2,1},{3,2},{4,7},{5,4},{6,5},{7,6},{8,11},{9,8},{10,9... | collective-permute-start | bytes 786440 | tf_op jit(solution)/shard_map/ppermute | solution.py:46
  63.2 1.1 shard_map.76
  64.4 1.6 %copy-done.4 = bf16[2048,512]{1,0:T(8,128)(2,1)S(1)} copy-done((bf16[2048,512]{1,0:T(8,128)(2,1)S(1)}, bf16[2048,512]{1,0:T(8,128)(2,1)}, u32[]{:S(2)}) %copy-start.4) | copy-done | bytes 2097176
  66.0 1.6 %copy-done.6 = bf16[2048,512]{1,0:T(8,128)(2,1)S(1)} copy-done((bf16[2048,512]{1,0:T(8,128)(2,1)S(1)}, bf16[2048,512]{1,0:T(8,128)(2,1)}, u32[]{:S(2)}) %copy-start.6) | copy-done | bytes 2097176
  67.6 3.4 %shard_map.78 = (f32[128,512]{1,0:T(8,128)S(1)}, f32[128,512]{1,0:T(8,128)S(1)}, f32[128,512]{1,0:T(8,128)S(1)}, f32[128,512]{1,0:T(8,128)S(1)}, f32[128,512]{1,0:T(8,128)S(1)}, /*index=5*/f32[128,512]{1,0:T(8,128)S(1)}) custom-call(s32[1,2048]{1,0:T(1,128)S(1)} %fusion.20.ids_ref, bf16[2048,512]{1,0:T(8,128)(2,1)S(1)} %copy-done.4, ...), custom_call_target="tpu_custom_call" | custom-call | tf_op jit(solution)/shard_map/pallas_call | solution.py:505
  71.0 3.0 %shard_map.79.refs_8_ = f32[3,2,256,512]{3,2,1,0:T(8,128)} custom-call(f32[256,512]{1,0:T(8,128)S(1)} %get-tuple-element.106.plane_0, f32[256,512]{1,0:T(8,128)S(1)} %get-tuple-element.105.plane_1, f32[512,512]{1,0:T(8,128)S(1)} %bitcast.19), custom_call_target="tpu_custom_call" | custom-call | tf_op jit(solution)/shard_map/pallas_call | solution.py:511
  74.1 3.1 %collective-permute-done.15.in_3 = f32[128,512]{1,0:T(8,128)} collective-permute-done((f32[128,512]{1,0:T(8,128)}, f32[128,512]{1,0:T(8,128)}, u32[]{:S(2)}, u32[]{:S(2)}) %collective-permute-start.15) | collective-permute-done | bytes 262176 | tf_op jit(solution)/shard_map/ppermute | solution.py:46
  77.2 2.7 %shard_map.80 = (f32[288,512]{1,0:T(8,128)S(1)}, f32[288,512]{1,0:T(8,128)S(1)}, f32[576,512]{1,0:T(8,128)S(1)}) custom-call(bf16[576,1280]{1,0:T(8,128)(2,1)S(1)} %get-tuple-element.89.hot_low, bf16[576,1280]{1,0:T(8,128)(2,1)S(1)} %get-tuple-element.90.hot_high, f32[128,512]{1,0:T(8,128)S(1)} %get-tuple-element.91.in_low, ...), custom_call_target="tpu_custom_call" | custom-call | tf_op jit(solution)/shard_map/pallas_call | solution.py:535
  82.3 1.0 collective-permute-done.19
  83.5 1.7 %collective-permute-start.21 = (f32[288,512]{1,0:T(8,128)S(1)}, f32[288,512]{1,0:T(8,128)S(1)}, u32[]{:S(2)}, u32[]{:S(2)}) collective-permute-start(f32[288,512]{1,0:T(8,128)S(1)} %get-tuple-element.113), channel_id=1, source_target_pairs={{0,28},{1,29},{2,30},{3,31},{4,0},{5,1},{6,2},{7,3},{8,4},{9,5},{1... | collective-permute-start | bytes 1769480 | tf_op jit(solution)/shard_map/ppermute | solution.py:51
  85.3 3.4 %collective-permute-done.16.in_1 = f32[128,512]{1,0:T(8,128)S(1)} collective-permute-done((f32[128,512]{1,0:T(8,128)S(1)}, f32[128,512]{1,0:T(8,128)S(1)}, u32[]{:S(2)}, u32[]{:S(2)}) %collective-permute-start.16) | collective-permute-done | bytes 262176 | tf_op jit(solution)/shard_map/ppermute | solution.py:46
  88.7 1.8 %collective-permute-done.17.in_2 = f32[128,512]{1,0:T(8,128)S(1)} collective-permute-done((f32[128,512]{1,0:T(8,128)S(1)}, f32[128,512]{1,0:T(8,128)S(1)}, u32[]{:S(2)}, u32[]{:S(2)}) %collective-permute-start.17) | collective-permute-done | bytes 262176 | tf_op jit(solution)/shard_map/ppermute | solution.py:46
  90.5 6.3 %collective-permute-done.18.in_3 = f32[128,512]{1,0:T(8,128)S(1)} collective-permute-done((f32[128,512]{1,0:T(8,128)S(1)}, f32[128,512]{1,0:T(8,128)S(1)}, u32[]{:S(2)}, u32[]{:S(2)}) %collective-permute-start.18) | collective-permute-done | bytes 262176 | tf_op jit(solution)/shard_map/ppermute | solution.py:46
  98.2 1.5 %collective-permute-done.25 = f32[72,512]{1,0:T(8,128)S(1)} collective-permute-done((f32[72,512]{1,0:T(8,128)S(1)}, f32[72,512]{1,0:T(8,128)S(1)}, u32[]{:S(2)}, u32[]{:S(2)}) %collective-permute-start.25) | collective-permute-done | bytes 147488 | tf_op jit(solution)/shard_map/ppermute | solution.py:65
  99.8 0.9 collective-permute-done.22
  100.9 1.4 collective-permute-start.23
  102.2 2.6 %collective-permute-start.24 = (f32[72,512]{1,0:T(8,128)S(1)}, f32[72,512]{1,0:T(8,128)S(1)}, u32[]{:S(2)}, u32[]{:S(2)}) collective-permute-start(f32[72,512]{1,0:T(8,128)S(1)} %get-tuple-element.111), channel_id=1, source_target_pairs={{0,128},{32,160},{64,192},{96,224},{128,0},{160,32},{192,64},{224,... | collective-permute-start | bytes 442376 | tf_op jit(solution)/shard_map/ppermute | solution.py:70
  104.9 1.1 collective-permute-start.26
  106.2 3.9 %collective-permute-done.24 = f32[72,512]{1,0:T(8,128)S(1)} collective-permute-done((f32[72,512]{1,0:T(8,128)S(1)}, f32[72,512]{1,0:T(8,128)S(1)}, u32[]{:S(2)}, u32[]{:S(2)}) %collective-permute-start.24) | collective-permute-done | bytes 147488 | tf_op jit(solution)/shard_map/ppermute | solution.py:70
  110.5 4.8 %collective-permute-start.30 = (f32[72,512]{1,0:T(8,128)S(1)}, f32[72,512]{1,0:T(8,128)S(1)}, u32[]{:S(2)}, u32[]{:S(2)}) collective-permute-start(f32[72,512]{1,0:T(8,128)S(1)} %fusion.18.piece), channel_id=1, source_target_pairs={{0,31},{1,0},{2,1},{3,2},{4,3},{5,4},{6,5},{7,6},{8,7},{9,8},{10,9... | collective-permute-start | bytes 442376 | tf_op jit(solution)/shard_map/ppermute | solution.py:51
  115.2 4.8 %collective-permute-start.28 = (f32[256,512]{1,0:T(8,128)S(1)}, f32[256,512]{1,0:T(8,128)S(1)}, u32[]{:S(2)}, u32[]{:S(2)}) collective-permute-start(f32[256,512]{1,0:T(8,128)S(1)} %get-tuple-element.106.plane_0), channel_id=1, source_target_pairs={{0,31},{1,0},{2,1},{3,2},{4,3},{5,4},{6,5},{7,6},{8,7},{9,8},{10,9... | collective-permute-start | bytes 1572872 | tf_op jit(solution)/shard_map/ppermute | solution.py:51
  120.0 1.2 shard_map.82.refs_0_
  121.2 1.6 %collective-permute-start.31 = (f32[64,512]{1,0:T(8,128)S(1)}, f32[64,512]{1,0:T(8,128)S(1)}, u32[]{:S(2)}, u32[]{:S(2)}) collective-permute-start(f32[64,512]{1,0:T(8,128)S(1)} %shard_map.82.refs_0_), channel_id=1, source_target_pairs={{0,64},{32,96},{64,128},{96,160},{128,192},{160,224},{192,0},{224,... | collective-permute-start | bytes 393224 | tf_op jit(solution)/shard_map/ppermute | solution.py:70
  122.8 2.4 %collective-permute-start.32 = (f32[64,512]{1,0:T(8,128)S(1)}, f32[64,512]{1,0:T(8,128)S(1)}, u32[]{:S(2)}, u32[]{:S(2)}) collective-permute-start(f32[64,512]{1,0:T(8,128)S(1)} %shard_map.82.refs_0_), channel_id=1, source_target_pairs={{0,128},{32,160},{64,192},{96,224},{128,0},{160,32},{192,64},{224,... | collective-permute-start | bytes 393224 | tf_op jit(solution)/shard_map/ppermute | solution.py:70
  125.5 1.1 collective-permute-done.31.refs_1_
  126.7 4.5 %collective-permute-start.34 = (f32[64,512]{1,0:T(8,128)S(1)}, f32[64,512]{1,0:T(8,128)S(1)}, u32[]{:S(2)}, u32[]{:S(2)}) collective-permute-start(f32[64,512]{1,0:T(8,128)S(1)} %shard_map.82.refs_0_), channel_id=1, source_target_pairs={{0,32},{32,0},{64,96},{96,64},{128,160},{160,128},{192,224},{224,1... | collective-permute-start | bytes 393224 | tf_op jit(solution)/shard_map/ppermute | solution.py:65
  131.1 2.1 %collective-permute-start.35 = (f32[64,512]{1,0:T(8,128)S(1)}, f32[64,512]{1,0:T(8,128)S(1)}, u32[]{:S(2)}, u32[]{:S(2)}) collective-permute-start(f32[64,512]{1,0:T(8,128)S(1)} %collective-permute-done.31.refs_1_), channel_id=1, source_target_pairs={{0,32},{32,0},{64,96},{96,64},{128,160},{160,128},{192,224},{224,1... | collective-permute-start | bytes 393224 | tf_op jit(solution)/shard_map/ppermute | solution.py:65
  135.2 2.0 %shard_map.83 = (f32[512,512]{1,0:T(8,128)}, f32[3,2,256,512]{3,2,1,0:T(8,128)}) custom-call(s32[8]{0:T(128)S(1)} %stack.19.place_ref, f32[256,512]{1,0:T(8,128)S(1)} %collective-permute-done.27.before, f32[256,512]{1,0:T(8,128)S(1)} %get-tuple-element.106.plane_0, f32[256,512]{1,0:T(8,128)S(1)} %get-tuple-element.105.plane_1, ...), custom_call_target="tpu_custom_call", output_to_operand_aliasing={{1}: (14, {})} | custom-call | tf_op jit(solution)/shard_map/pallas_call | solution.py:570
  (88 shorter events, 14.4 us)
Async XLA Ops:
  0.6 8.6 %copy-start.16 = (s32[1,1,9,128]{3,1,2,0:T(1,128)S(1)}, s32[1,1,9,128]{3,1,2,0:T(1,128)}, u32[]{:S(2)}) copy-start(s32[1,1,9,128]{3,1,2,0:T(1,128)} %param.8) | copy-start | bytes 13828
  2.0 11.5 %copy-start.1 = (f32[2,256,512]{2,1,0:T(8,128)S(1)}, f32[2,256,512]{2,1,0:T(8,128)}, u32[]{:S(2)}) copy-start(f32[2,256,512]{2,1,0:T(8,128)} %param.5) | copy-start | bytes 3145732
  2.6 22.9 %collective-permute-start.3 = (f32[1024,128]{1,0:T(8,128)S(1)}, f32[1024,128]{1,0:T(8,128)S(1)}, u32[]{:S(2)}, u32[]{:S(2)}) collective-permute-start(f32[1024,128]{1,0:T(8,128)S(1)} %shard_map.70), channel_id=1, source_target_pairs={{0,4},{1,5},{2,6},{3,7},{4,8},{5,9},{6,10},{7,11},{8,12},{9,13},{1... | collective-permute-start | bytes 1572872 | tf_op jit(solution)/shard_map/ppermute | solution.py:51
  5.2 20.4 %collective-permute-start.4 = (f32[1024,128]{1,0:T(8,128)S(1)}, f32[1024,128]{1,0:T(8,128)S(1)}, u32[]{:S(2)}, u32[]{:S(2)}) collective-permute-start(f32[1024,128]{1,0:T(8,128)S(1)} %shard_map.70), channel_id=1, source_target_pairs={{0,28},{1,29},{2,30},{3,31},{4,0},{5,1},{6,2},{7,3},{8,4},{9,5},{1... | collective-permute-start | bytes 1572872 | tf_op jit(solution)/shard_map/ppermute | solution.py:51
  9.8 3.9 %collective-permute-start = (s32[2,128]{1,0:T(2,128)S(1)}, s32[2,128]{1,0:T(2,128)S(1)}, u32[]{:S(2)}, u32[]{:S(2)}) collective-permute-start(s32[2,128]{1,0:T(2,128)S(1)} %get-tuple-element.58), channel_id=1, source_target_pairs={{0,3},{1,0},{2,1},{3,2},{4,7},{5,4},{6,5},{7,6},{8,11},{9,8},{10,9... | collective-permute-start | bytes 3080 | tf_op jit(solution)/shard_map/ppermute | solution.py:46
  12.3 3.9 %collective-permute-start.1 = (s32[2,128]{1,0:T(2,128)S(1)}, s32[2,128]{1,0:T(2,128)S(1)}, u32[]{:S(2)}, u32[]{:S(2)}) collective-permute-start(s32[2,128]{1,0:T(2,128)S(1)} %get-tuple-element.59), channel_id=1, source_target_pairs={{0,2},{1,3},{2,0},{3,1},{4,6},{5,7},{6,4},{7,5},{8,10},{9,11},{10,... | collective-permute-start | bytes 3080 | tf_op jit(solution)/shard_map/ppermute | solution.py:46
  12.9 16.4 %copy-start.15 = (s32[1,4,2,256]{3,2,1,0:T(2,128)S(1)}, s32[1,4,2,256]{3,2,1,0:T(2,128)}, u32[]{:S(2)}) copy-start(s32[1,4,2,256]{3,2,1,0:T(2,128)} %param.9) | copy-start | bytes 24580
  12.9 3.9 %collective-permute-start.2 = (s32[2,128]{1,0:T(2,128)S(1)}, s32[2,128]{1,0:T(2,128)S(1)}, u32[]{:S(2)}, u32[]{:S(2)}) collective-permute-start(s32[2,128]{1,0:T(2,128)S(1)} %get-tuple-element.60), channel_id=1, source_target_pairs={{0,1},{1,2},{2,3},{3,0},{4,5},{5,6},{6,7},{7,4},{8,9},{9,10},{10,1... | collective-permute-start | bytes 3080 | tf_op jit(solution)/shard_map/ppermute | solution.py:46
  18.4 6.4 %collective-permute-start.5 = (f32[512,128]{1,0:T(8,128)S(1)}, f32[512,128]{1,0:T(8,128)S(1)}, u32[]{:S(2)}, u32[]{:S(2)}) collective-permute-start(f32[512,128]{1,0:T(8,128)S(1)} %get-tuple-element.61), channel_id=1, source_target_pairs={{0,1},{1,2},{2,3},{3,0},{4,5},{5,6},{6,7},{7,4},{8,9},{9,10},{10,1... | collective-permute-start | bytes 786440 | tf_op jit(solution)/shard_map/ppermute | solution.py:46
  18.4 6.4 %collective-permute-start.6 = (f32[512,128]{1,0:T(8,128)S(1)}, f32[512,128]{1,0:T(8,128)S(1)}, u32[]{:S(2)}, u32[]{:S(2)}) collective-permute-start(f32[512,128]{1,0:T(8,128)S(1)} %get-tuple-element.62), channel_id=1, source_target_pairs={{0,3},{1,0},{2,1},{3,2},{4,7},{5,4},{6,5},{7,6},{8,11},{9,8},{10,9... | collective-permute-start | bytes 786440 | tf_op jit(solution)/shard_map/ppermute | solution.py:46
  25.6 15.3 %copy-start.7 = (f32[1024,128]{1,0:T(8,128)}, f32[1024,128]{1,0:T(8,128)S(1)}, u32[]{:S(2)}) copy-start(f32[1024,128]{1,0:T(8,128)S(1)} %collective-permute-done.3.low_a) | copy-start | bytes 1572868
  25.6 15.3 %copy-start.9 = (f32[1024,128]{1,0:T(8,128)}, f32[1024,128]{1,0:T(8,128)S(1)}, u32[]{:S(2)}) copy-start(f32[1024,128]{1,0:T(8,128)S(1)} %collective-permute-done.4.high_a) | copy-start | bytes 1572868
  25.6 5.3 %collective-permute-start.7 = (f32[1024,128]{1,0:T(8,128)S(1)}, f32[1024,128]{1,0:T(8,128)}, u32[]{:S(2)}, u32[]{:S(2)}) collective-permute-start(f32[1024,128]{1,0:T(8,128)S(1)} %collective-permute-done.3.low_a), channel_id=1, source_target_pairs={{0,32},{32,0},{64,96},{96,64},{128,160},{160,128},{192,224},{224,1... | collective-permute-start | bytes 1572872 | tf_op jit(solution)/shard_map/ppermute | solution.py:65
  29.2 2.4 %collective-permute-start.8 = (f32[1024,128]{1,0:T(8,128)S(1)}, f32[1024,128]{1,0:T(8,128)}, u32[]{:S(2)}, u32[]{:S(2)}) collective-permute-start(f32[1024,128]{1,0:T(8,128)S(1)} %collective-permute-done.4.high_a), channel_id=1, source_target_pairs={{0,32},{32,0},{64,96},{96,64},{128,160},{160,128},{192,224},{224,1... | collective-permute-start | bytes 1572872 | tf_op jit(solution)/shard_map/ppermute | solution.py:65
  29.3 8.5 %copy-start.11 = (bf16[1,3,2,256,512]{4,3,2,1,0:T(8,128)(2,1)S(1)}, bf16[1,3,2,256,512]{4,3,2,1,0:T(8,128)(2,1)}, u32[]{:S(2)}) copy-start(bf16[1,3,2,256,512]{4,3,2,1,0:T(8,128)(2,1)} %param.7) | copy-start | bytes 4718596
  29.3 15.9 %collective-permute-start.12 = (f32[512,128]{1,0:T(8,128)}, f32[512,128]{1,0:T(8,128)S(1)}, u32[]{:S(2)}, u32[]{:S(2)}) collective-permute-start(f32[512,128]{1,0:T(8,128)} %copy-done.14), channel_id=1, source_target_pairs={{0,2},{1,3},{2,0},{3,1},{4,6},{5,7},{6,4},{7,5},{8,10},{9,11},{10,... | collective-permute-start | bytes 786440 | tf_op jit(solution)/shard_map/ppermute | solution.py:46
  33.9 11.4 %collective-permute-start.10 = (f32[512,128]{1,0:T(8,128)S(1)}, f32[512,128]{1,0:T(8,128)S(1)}, u32[]{:S(2)}, u32[]{:S(2)}) collective-permute-start(f32[512,128]{1,0:T(8,128)S(1)} %get-tuple-element.66), channel_id=1, source_target_pairs={{0,2},{1,3},{2,0},{3,1},{4,6},{5,7},{6,4},{7,5},{8,10},{9,11},{10,... | collective-permute-start | bytes 786440 | tf_op jit(solution)/shard_map/ppermute | solution.py:46
  35.1 15.3 %collective-permute-start.11 = (f32[512,128]{1,0:T(8,128)S(1)}, f32[512,128]{1,0:T(8,128)S(1)}, u32[]{:S(2)}, u32[]{:S(2)}) collective-permute-start(f32[512,128]{1,0:T(8,128)S(1)} %get-tuple-element.67), channel_id=1, source_target_pairs={{0,3},{1,0},{2,1},{3,2},{4,7},{5,4},{6,5},{7,6},{8,11},{9,8},{10,9... | collective-permute-start | bytes 786440 | tf_op jit(solution)/shard_map/ppermute | solution.py:46
  37.7 12.9 %collective-permute-start.9 = (f32[512,128]{1,0:T(8,128)S(1)}, f32[512,128]{1,0:T(8,128)S(1)}, u32[]{:S(2)}, u32[]{:S(2)}) collective-permute-start(f32[512,128]{1,0:T(8,128)S(1)} %get-tuple-element.65), channel_id=1, source_target_pairs={{0,1},{1,2},{2,3},{3,0},{4,5},{5,6},{6,7},{7,4},{8,9},{9,10},{10,1... | collective-permute-start | bytes 786440 | tf_op jit(solution)/shard_map/ppermute | solution.py:46
  43.0 7.6 %copy-start.2 = (f32[1,2,256,512]{3,2,1,0:T(8,128)S(1)}, f32[1,2,256,512]{3,2,1,0:T(8,128)}, u32[]{:S(2)}) copy-start(f32[1,2,256,512]{3,2,1,0:T(8,128)} %param.6) | copy-start | bytes 3145732
  43.0 7.6 %copy-start.13 = (f32[512,128]{1,0:T(8,128)S(1)}, f32[512,128]{1,0:T(8,128)}, u32[]{:S(2)}) copy-start(f32[512,128]{1,0:T(8,128)} %copy-done.12) | copy-start | bytes 786436
  56.5 2.7 %copy-start.3 = (bf16[2048,512]{1,0:T(8,128)(2,1)}, bf16[2048,512]{1,0:T(8,128)(2,1)S(1)}, u32[]{:S(2)}) copy-start(bf16[2048,512]{1,0:T(8,128)(2,1)S(1)} %get-tuple-element.76.push_high) | copy-start | bytes 6291460
  56.5 2.6 %copy-start.5 = (bf16[2048,512]{1,0:T(8,128)(2,1)}, bf16[2048,512]{1,0:T(8,128)(2,1)S(1)}, u32[]{:S(2)}) copy-start(bf16[2048,512]{1,0:T(8,128)(2,1)S(1)} %get-tuple-element.77.push_low) | copy-start | bytes 6291460
  59.1 14.9 %collective-permute-start.13 = (f32[128,512]{1,0:T(8,128)}, f32[128,512]{1,0:T(8,128)S(1)}, u32[]{:S(2)}, u32[]{:S(2)}) collective-permute-start(f32[128,512]{1,0:T(8,128)} %get-tuple-element.78), channel_id=1, source_target_pairs={{0,3},{1,0},{2,1},{3,2},{4,7},{5,4},{6,5},{7,6},{8,11},{9,8},{10,9... | collective-permute-start | bytes 786440 | tf_op jit(solution)/shard_map/ppermute | solution.py:46
  62.1 12.0 %collective-permute-start.14 = (f32[128,512]{1,0:T(8,128)}, f32[128,512]{1,0:T(8,128)}, u32[]{:S(2)}, u32[]{:S(2)}) collective-permute-start(f32[128,512]{1,0:T(8,128)} %get-tuple-element.79), channel_id=1, source_target_pairs={{0,2},{1,3},{2,0},{3,1},{4,6},{5,7},{6,4},{7,5},{8,10},{9,11},{10,... | collective-permute-start | bytes 786440 | tf_op jit(solution)/shard_map/ppermute | solution.py:46
  62.1 15.1 %collective-permute-start.15 = (f32[128,512]{1,0:T(8,128)}, f32[128,512]{1,0:T(8,128)}, u32[]{:S(2)}, u32[]{:S(2)}) collective-permute-start(f32[128,512]{1,0:T(8,128)} %get-tuple-element.80), channel_id=1, source_target_pairs={{0,1},{1,2},{2,3},{3,0},{4,5},{5,6},{6,7},{7,4},{8,9},{9,10},{10,1... | collective-permute-start | bytes 786440 | tf_op jit(solution)/shard_map/ppermute | solution.py:46
  79.9 3.4 %collective-permute-start.19 = (f32[576,512]{1,0:T(8,128)S(1)}, f32[576,512]{1,0:T(8,128)S(1)}, u32[]{:S(2)}, u32[]{:S(2)}) collective-permute-start(f32[576,512]{1,0:T(8,128)S(1)} %get-tuple-element.97), channel_id=1, source_target_pairs={{0,32},{32,0},{64,96},{96,64},{128,160},{160,128},{192,224},{224,1... | collective-permute-start | bytes 3538952 | tf_op jit(solution)/shard_map/ppermute | solution.py:65
  80.8 7.9 %collective-permute-start.16 = (f32[128,512]{1,0:T(8,128)S(1)}, f32[128,512]{1,0:T(8,128)S(1)}, u32[]{:S(2)}, u32[]{:S(2)}) collective-permute-start(f32[128,512]{1,0:T(8,128)S(1)} %get-tuple-element.86), channel_id=1, source_target_pairs={{0,3},{1,0},{2,1},{3,2},{4,7},{5,4},{6,5},{7,6},{8,11},{9,8},{10,9... | collective-permute-start | bytes 786440 | tf_op jit(solution)/shard_map/ppermute | solution.py:46
  81.4 9.1 %collective-permute-start.17 = (f32[128,512]{1,0:T(8,128)S(1)}, f32[128,512]{1,0:T(8,128)S(1)}, u32[]{:S(2)}, u32[]{:S(2)}) collective-permute-start(f32[128,512]{1,0:T(8,128)S(1)} %get-tuple-element.87), channel_id=1, source_target_pairs={{0,2},{1,3},{2,0},{3,1},{4,6},{5,7},{6,4},{7,5},{8,10},{9,11},{10,... | collective-permute-start | bytes 786440 | tf_op jit(solution)/shard_map/ppermute | solution.py:46
  82.0 14.8 %collective-permute-start.18 = (f32[128,512]{1,0:T(8,128)S(1)}, f32[128,512]{1,0:T(8,128)S(1)}, u32[]{:S(2)}, u32[]{:S(2)}) collective-permute-start(f32[128,512]{1,0:T(8,128)S(1)} %get-tuple-element.88), channel_id=1, source_target_pairs={{0,1},{1,2},{2,3},{3,0},{4,5},{5,6},{6,7},{7,4},{8,9},{9,10},{10,1... | collective-permute-start | bytes 786440 | tf_op jit(solution)/shard_map/ppermute | solution.py:46
  83.5 16.3 %collective-permute-start.21 = (f32[288,512]{1,0:T(8,128)S(1)}, f32[288,512]{1,0:T(8,128)S(1)}, u32[]{:S(2)}, u32[]{:S(2)}) collective-permute-start(f32[288,512]{1,0:T(8,128)S(1)} %get-tuple-element.113), channel_id=1, source_target_pairs={{0,28},{1,29},{2,30},{3,31},{4,0},{5,1},{6,2},{7,3},{8,4},{9,5},{1... | collective-permute-start | bytes 1769480 | tf_op jit(solution)/shard_map/ppermute | solution.py:51
  85.3 15.4 %collective-permute-start.22 = (f32[288,512]{1,0:T(8,128)S(1)}, f32[288,512]{1,0:T(8,128)S(1)}, u32[]{:S(2)}, u32[]{:S(2)}) collective-permute-start(f32[288,512]{1,0:T(8,128)S(1)} %get-tuple-element.114), channel_id=1, source_target_pairs={{0,4},{1,5},{2,6},{3,7},{4,8},{5,9},{6,10},{7,11},{8,12},{9,13},{1... | collective-permute-start | bytes 1769480 | tf_op jit(solution)/shard_map/ppermute | solution.py:51
  97.6 2.2 %collective-permute-start.20 = (f32[216,512]{1,0:T(8,128)S(1)}, f32[216,512]{1,0:T(8,128)S(1)}, u32[]{:S(2)}, u32[]{:S(2)}) collective-permute-start(f32[216,512]{1,0:T(8,128)S(1)} %get-tuple-element.103), channel_id=1, source_target_pairs={{0,32},{32,0},{64,96},{96,64},{128,160},{160,128},{192,224},{224,1... | collective-permute-start | bytes 1327112 | tf_op jit(solution)/shard_map/ppermute | solution.py:65
  98.1 1.6 %collective-permute-start.25 = (f32[72,512]{1,0:T(8,128)S(1)}, f32[72,512]{1,0:T(8,128)S(1)}, u32[]{:S(2)}, u32[]{:S(2)}) collective-permute-start(f32[72,512]{1,0:T(8,128)S(1)} %get-tuple-element.104), channel_id=1, source_target_pairs={{0,32},{32,0},{64,96},{96,64},{128,160},{160,128},{192,224},{224,1... | collective-permute-start | bytes 442376 | tf_op jit(solution)/shard_map/ppermute | solution.py:65
  100.9 5.3 %collective-permute-start.23 = (f32[72,512]{1,0:T(8,128)S(1)}, f32[72,512]{1,0:T(8,128)S(1)}, u32[]{:S(2)}, u32[]{:S(2)}) collective-permute-start(f32[72,512]{1,0:T(8,128)S(1)} %get-tuple-element.110), channel_id=1, source_target_pairs={{0,64},{32,96},{64,128},{96,160},{128,192},{160,224},{192,0},{224,... | collective-permute-start | bytes 442376 | tf_op jit(solution)/shard_map/ppermute | solution.py:70
  102.2 7.8 %collective-permute-start.24 = (f32[72,512]{1,0:T(8,128)S(1)}, f32[72,512]{1,0:T(8,128)S(1)}, u32[]{:S(2)}, u32[]{:S(2)}) collective-permute-start(f32[72,512]{1,0:T(8,128)S(1)} %get-tuple-element.111), channel_id=1, source_target_pairs={{0,128},{32,160},{64,192},{96,224},{128,0},{160,32},{192,64},{224,... | collective-permute-start | bytes 442376 | tf_op jit(solution)/shard_map/ppermute | solution.py:70
  104.9 5.4 %collective-permute-start.26 = (f32[72,512]{1,0:T(8,128)S(1)}, f32[72,512]{1,0:T(8,128)S(1)}, u32[]{:S(2)}, u32[]{:S(2)}) collective-permute-start(f32[72,512]{1,0:T(8,128)S(1)} %get-tuple-element.112), channel_id=1, source_target_pairs={{0,192},{32,224},{64,0},{96,32},{128,64},{160,96},{192,128},{224,1... | collective-permute-start | bytes 442376 | tf_op jit(solution)/shard_map/ppermute | solution.py:70
  110.4 9.7 %collective-permute-start.29 = (f32[72,512]{1,0:T(8,128)S(1)}, f32[72,512]{1,0:T(8,128)S(1)}, u32[]{:S(2)}, u32[]{:S(2)}) collective-permute-start(f32[72,512]{1,0:T(8,128)S(1)} %fusion.18.piece), channel_id=1, source_target_pairs={{0,1},{1,2},{2,3},{3,4},{4,5},{5,6},{6,7},{7,8},{8,9},{9,10},{10,1... | collective-permute-start | bytes 442376 | tf_op jit(solution)/shard_map/ppermute | solution.py:51
  110.5 9.6 %collective-permute-start.30 = (f32[72,512]{1,0:T(8,128)S(1)}, f32[72,512]{1,0:T(8,128)S(1)}, u32[]{:S(2)}, u32[]{:S(2)}) collective-permute-start(f32[72,512]{1,0:T(8,128)S(1)} %fusion.18.piece), channel_id=1, source_target_pairs={{0,31},{1,0},{2,1},{3,2},{4,3},{5,4},{6,5},{7,6},{8,7},{9,8},{10,9... | collective-permute-start | bytes 442376 | tf_op jit(solution)/shard_map/ppermute | solution.py:51
  115.2 20.0 %collective-permute-start.27 = (f32[256,512]{1,0:T(8,128)S(1)}, f32[256,512]{1,0:T(8,128)S(1)}, u32[]{:S(2)}, u32[]{:S(2)}) collective-permute-start(f32[256,512]{1,0:T(8,128)S(1)} %get-tuple-element.105.plane_1), channel_id=1, source_target_pairs={{0,1},{1,2},{2,3},{3,4},{4,5},{5,6},{6,7},{7,8},{8,9},{9,10},{10,1... | collective-permute-start | bytes 1572872 | tf_op jit(solution)/shard_map/ppermute | solution.py:51
  115.2 20.0 %collective-permute-start.28 = (f32[256,512]{1,0:T(8,128)S(1)}, f32[256,512]{1,0:T(8,128)S(1)}, u32[]{:S(2)}, u32[]{:S(2)}) collective-permute-start(f32[256,512]{1,0:T(8,128)S(1)} %get-tuple-element.106.plane_0), channel_id=1, source_target_pairs={{0,31},{1,0},{2,1},{3,2},{4,3},{5,4},{6,5},{7,6},{8,7},{9,8},{10,9... | collective-permute-start | bytes 1572872 | tf_op jit(solution)/shard_map/ppermute | solution.py:51
  121.2 5.4 %collective-permute-start.31 = (f32[64,512]{1,0:T(8,128)S(1)}, f32[64,512]{1,0:T(8,128)S(1)}, u32[]{:S(2)}, u32[]{:S(2)}) collective-permute-start(f32[64,512]{1,0:T(8,128)S(1)} %shard_map.82.refs_0_), channel_id=1, source_target_pairs={{0,64},{32,96},{64,128},{96,160},{128,192},{160,224},{192,0},{224,... | collective-permute-start | bytes 393224 | tf_op jit(solution)/shard_map/ppermute | solution.py:70
  122.8 8.4 %collective-permute-start.32 = (f32[64,512]{1,0:T(8,128)S(1)}, f32[64,512]{1,0:T(8,128)S(1)}, u32[]{:S(2)}, u32[]{:S(2)}) collective-permute-start(f32[64,512]{1,0:T(8,128)S(1)} %shard_map.82.refs_0_), channel_id=1, source_target_pairs={{0,128},{32,160},{64,192},{96,224},{128,0},{160,32},{192,64},{224,... | collective-permute-start | bytes 393224 | tf_op jit(solution)/shard_map/ppermute | solution.py:70
  125.2 8.0 %collective-permute-start.33 = (f32[64,512]{1,0:T(8,128)S(1)}, f32[64,512]{1,0:T(8,128)S(1)}, u32[]{:S(2)}, u32[]{:S(2)}) collective-permute-start(f32[64,512]{1,0:T(8,128)S(1)} %shard_map.82.refs_0_), channel_id=1, source_target_pairs={{0,192},{32,224},{64,0},{96,32},{128,64},{160,96},{192,128},{224,1... | collective-permute-start | bytes 393224 | tf_op jit(solution)/shard_map/ppermute | solution.py:70
  126.7 7.2 %collective-permute-start.34 = (f32[64,512]{1,0:T(8,128)S(1)}, f32[64,512]{1,0:T(8,128)S(1)}, u32[]{:S(2)}, u32[]{:S(2)}) collective-permute-start(f32[64,512]{1,0:T(8,128)S(1)} %shard_map.82.refs_0_), channel_id=1, source_target_pairs={{0,32},{32,0},{64,96},{96,64},{128,160},{160,128},{192,224},{224,1... | collective-permute-start | bytes 393224 | tf_op jit(solution)/shard_map/ppermute | solution.py:65
  131.1 3.1 %collective-permute-start.35 = (f32[64,512]{1,0:T(8,128)S(1)}, f32[64,512]{1,0:T(8,128)S(1)}, u32[]{:S(2)}, u32[]{:S(2)}) collective-permute-start(f32[64,512]{1,0:T(8,128)S(1)} %collective-permute-done.31.refs_1_), channel_id=1, source_target_pairs={{0,32},{32,0},{64,96},{96,64},{128,160},{160,128},{192,224},{224,1... | collective-permute-start | bytes 393224 | tf_op jit(solution)/shard_map/ppermute | solution.py:65
  133.2 1.6 %collective-permute-start.36 = (f32[64,512]{1,0:T(8,128)S(1)}, f32[64,512]{1,0:T(8,128)S(1)}, u32[]{:S(2)}, u32[]{:S(2)}) collective-permute-start(f32[64,512]{1,0:T(8,128)S(1)} %collective-permute-done.32.refs_2_), channel_id=1, source_target_pairs={{0,32},{32,0},{64,96},{96,64},{128,160},{160,128},{192,224},{224,1... | collective-permute-start | bytes 393224 | tf_op jit(solution)/shard_map/ppermute | solution.py:65
  133.8 1.3 collective-permute-start.37
  (7 other events, 7.9 us)

commit v5 on v4

--- a/solution.py
+++ b/solution.py
@@ -141,9 +141,13 @@
     lax.fori_loop(0, count // unit, group, 0, unroll=2)
 
 
-def own_lines_kernel(lists_1, lists_2, lists_3, held, out_1, out_2, out_3):
-    for lists, out in ((lists_1, out_1), (lists_2, out_2), (lists_3, out_3)):
+def near_lines_kernel(lists_1, lists_3, held, out_1, out_3):
+    for lists, out in ((lists_1, out_1), (lists_3, out_3)):
         copy_lines(lists, 0, held, out)
+
+
+def far_lines_kernel(lists, held, out):
+    copy_lines(lists, 0, held, out)
 
 
 def cross_lines_kernel(lists_1, lists_2, lists_3, low_a, low_b, high_a, high_b, out_1, out_2, out_3, held):
@@ -314,13 +318,18 @@
     send_1[...] = summed[count + first:]
 
 
-def cross_back_kernel(hot_low, hot_high, in_low, in_high, in_1, in_2, in_3, keep_low, keep_high, send):
-    values = stacked_parts((in_low, in_high, in_1, in_2, in_3))
+def cross_send_kernel(hot_low, hot_high, in_low, in_high, in_1, in_2, in_3, send, values):
+    stacked = stacked_parts((in_low, in_high, in_1, in_2, in_3))
+    count = send.shape[0] // 2
+    for at, hot in enumerate((hot_low, hot_high)):
+        send[at * count:(at + 1) * count] = jnp.dot(hot[count:], stacked, preferred_element_type=F32)
+    values[...] = stacked
+
+
+def cross_keep_kernel(hot_low, hot_high, values, keep_low, keep_high):
     count = keep_low.shape[0]
-    for at, (hot, keep) in enumerate(((hot_low, keep_low), (hot_high, keep_high))):
-        summed = jnp.dot(hot[...], values, preferred_element_type=F32)
-        keep[...] = summed[:count]
-        send[at * count:(at + 1) * count] = summed[count:]
+    keep_low[...] = jnp.dot(hot_low[:count], values[...], preferred_element_type=F32)
+    keep_high[...] = jnp.dot(hot_high[:count], values[...], preferred_element_type=F32)
 
 
 def smooth_kernel(place_ref, before, piece, after, template_ref, out, field):
@@ -450,13 +459,16 @@
     spread = call(spread_kernel, f32s(line_count * parts, LANES), [VMEM], VMEM)(lines)
     from_low = along_z(plane, 1)
     from_high = along_z(plane, -1)
-    asked = [self_lists] + ring_of(along_x, messages, -1)
-
-    own = call(
-        own_lines_kernel, (packed,) * 3, [SMEM] * 3 + [VMEM], (VMEM,) * 3,
-    )(*asked[1:], spread)
-    got_own = ring_of(along_x, own, 1)
-    from_low, from_high, _ = lax.optimization_barrier((from_low, from_high, (got_own[0], got_own[2])))
+    asked = [self_lists] + lax.optimization_barrier(ring_of(along_x, messages, -1))
+
+    own_1, own_3 = call(
+        near_lines_kernel, (packed,) * 2, [SMEM] * 2 + [VMEM], (VMEM,) * 2,
+    )(asked[1], asked[3], spread)
+    got_1, got_3 = along_x(own_1, 1), along_x(own_3, 3)
+    from_low, from_high, _ = lax.optimization_barrier((from_low, from_high, (got_1, got_3)))
+    far_list, _ = lax.optimization_barrier((asked[2], got_3))
+    own_2 = call(far_lines_kernel, packed, [SMEM, VMEM], VMEM)(far_list, spread)
+    got_own = [got_1, along_x(own_2, 2), got_3]
     from_low_b, from_high_b = other_core(from_low), other_core(from_high)
     slabs = (from_low, from_low_b, from_high, from_high_b)
     held_slabs = [pltpu.VMEM((2 * line_count * parts, LANES), F32)]
@@ -532,10 +544,14 @@
         (jax.ShapeDtypeStruct((all_rows, 8 * capacity), BF16),) + (jax.ShapeDtypeStruct((all_rows, 10 * capacity), BF16),) * 2,
         [SMEM] + [VMEM] * 5, (VMEM,) * 3,
     )(place, *asked, target)
-    keep_low, keep_high, send = call(
-        cross_back_kernel, (core_part,) * 2 + (f32s(2 * core_rows, cell_count),),
-        [VMEM] * 7, (VMEM,) * 3,
+    send, stacked = call(
+        cross_send_kernel,
+        (f32s(2 * core_rows, cell_count), jax.ShapeDtypeStruct((10 * capacity, cell_count), BF16)),
+        [VMEM] * 7, (VMEM,) * 2,
     )(hot_low, hot_high, pool_low, pool_high, *back_cross)
+    keep_low, keep_high = call(
+        cross_keep_kernel, (core_part,) * 2, [VMEM] * 3, (VMEM,) * 2,
+    )(hot_low, hot_high, stacked)
     received = other_core(send)
     sum_low = keep_low + received[:core_rows]
     sum_high = keep_high + received[core_rows:]

time: 138 us -> 137 us (level)
  local copies, waits for them, and re-layouts: 8.03 us -> 5.28 us
    ppermute x15, waiting for transfers between devices: 26.9 us -> 29.7 us  [along_x(): return lax.ppermute(value, 'slab', route)]
    unnamed x36 -> x34, local copies, waits for them, and re-layouts: 7.93 us -> 5.18 us
    ppermute x9, waiting for transfers between devices: 4.88 us -> 3.22 us  [other_core(): return lax.ppermute(value, 'subj', [(i, i ^ 1) for i in range(count)])]
    pallas_call x2 -> x4, Pallas kernels: 3.67 us -> 4.34 us  [the longest x1 1.96 us: on_device(): call(cross_send_kernel, (f32s(2 * core_rows, cell_count), jax.ShapeDtypeS...]
  transfers between devices with their start and end apart: 38 -> 38, of which waited for: 21 -> 19; matrix products, arithmetic and copies ran while one was open for 1% -> 1% of each run, Pallas kernels for 14% -> 15%
where the time goes in v5:
time: 137 us; the launch traced here: 136 us
  starting transfers between devices  56.9 us (42%)
  waiting for transfers between devices  38.7 us (28%)
  Pallas kernels  33.2 us (24%)
  local copies, waits for them, and re-layouts  5.28 us (4%)
    ppermute x15, waiting for transfers between devices, along_x(): return lax.ppermute(value, 'slab', route)  29.7 us
    ppermute x8, starting transfers between devices, along_slab(): lax.ppermute(value, 'slab', [(i, (i + step) % count) for i in range(count)])  17.9 us
    ppermute x15, starting transfers between devices, along_x(): return lax.ppermute(value, 'slab', route)  17.4 us
    ppermute x9, starting transfers between devices, other_core(): return lax.ppermute(value, 'subj', [(i, i ^ 1) for i in range(count)])  12.2 us
    ppermute x6, starting transfers between devices, along_y(): lax.ppermute(value, 'subj', [(i, (i + 2 * step) % count) for i in range(c...  9.33 us
    pallas_call x1, Pallas kernels, on_device(): call(warp_kernel, (half,) * 2 + (push_part,) * 2, [SMEM] + [VMEM] * 12, (...  5.84 us
    ppermute x6, waiting for transfers between devices, along_y(): lax.ppermute(value, 'subj', [(i, (i + 2 * step) % count) for i in range(c...  5.74 us
    unnamed x34, local copies, waits for them, and re-layouts  5.18 us
  transfers between devices with their start and end apart: 38, of which 19 were waited for; matrix products, arithmetic and copies ran while one was open for 1% of the time, Pallas kernels for 15%

profile of v5, /device:TPU:1, one launch (start us, length us, event | category | flops | bytes accessed | tf_op | source)
XLA Modules:
  0.0 136.4 jit_solution(2632919142460966349)
XLA Ops:
  0.8 1.2 copy-done
  2.6 2.5 %collective-permute-start.3 = (f32[1024,128]{1,0:T(8,128)S(1)}, f32[1024,128]{1,0:T(8,128)S(1)}, u32[]{:S(2)}, u32[]{:S(2)}) collective-permute-start(f32[1024,128]{1,0:T(8,128)S(1)} %shard_map.70), channel_id=1, source_target_pairs={{0,4},{1,5},{2,6},{3,7},{4,8},{5,9},{6,10},{7,11},{8,12},{9,13},{1... | collective-permute-start | bytes 1572872 | tf_op jit(solution)/shard_map/ppermute | solution.py:51
  5.2 4.0 %collective-permute-start.4 = (f32[1024,128]{1,0:T(8,128)S(1)}, f32[1024,128]{1,0:T(8,128)S(1)}, u32[]{:S(2)}, u32[]{:S(2)}) collective-permute-start(f32[1024,128]{1,0:T(8,128)S(1)} %shard_map.70), channel_id=1, source_target_pairs={{0,28},{1,29},{2,30},{3,31},{4,0},{5,1},{6,2},{7,3},{8,4},{9,5},{1... | collective-permute-start | bytes 1572872 | tf_op jit(solution)/shard_map/ppermute | solution.py:51
  9.8 2.6 %collective-permute-start = (s32[2,128]{1,0:T(2,128)S(1)}, s32[2,128]{1,0:T(2,128)S(1)}, u32[]{:S(2)}, u32[]{:S(2)}) collective-permute-start(s32[2,128]{1,0:T(2,128)S(1)} %get-tuple-element.62), channel_id=1, source_target_pairs={{0,3},{1,0},{2,1},{3,2},{4,7},{5,4},{6,5},{7,6},{8,11},{9,8},{10,9... | collective-permute-start | bytes 3080 | tf_op jit(solution)/shard_map/ppermute | solution.py:46
  13.7 2.6 %collective-permute-done.1.lists_2.lists = s32[2,128]{1,0:T(2,128)S(1)} collective-permute-done((s32[2,128]{1,0:T(2,128)S(1)}, s32[2,128]{1,0:T(2,128)S(1)}, u32[]{:S(2)}, u32[]{:S(2)}) %collective-permute-start.1) | collective-permute-done | bytes 1056 | tf_op jit(solution)/shard_map/ppermute | solution.py:46
  16.8 0.8 shard_map.72
  17.7 2.7 %collective-permute-start.6 = (f32[512,128]{1,0:T(8,128)S(1)}, f32[512,128]{1,0:T(8,128)S(1)}, u32[]{:S(2)}, u32[]{:S(2)}) collective-permute-start(f32[512,128]{1,0:T(8,128)S(1)} %get-tuple-element.69), channel_id=1, source_target_pairs={{0,3},{1,0},{2,1},{3,2},{4,7},{5,4},{6,5},{7,6},{8,11},{9,8},{10,9... | collective-permute-start | bytes 786440 | tf_op jit(solution)/shard_map/ppermute | solution.py:46
  20.3 3.8 %collective-permute-done.5.refs_9_ = f32[512,128]{1,0:T(8,128)S(1)} collective-permute-done((f32[512,128]{1,0:T(8,128)S(1)}, f32[512,128]{1,0:T(8,128)S(1)}, u32[]{:S(2)}, u32[]{:S(2)}) %collective-permute-start.5) | collective-permute-done | bytes 262176 | tf_op jit(solution)/shard_map/ppermute | solution.py:46
  24.8 3.6 %collective-permute-start.7 = (f32[1024,128]{1,0:T(8,128)S(1)}, f32[1024,128]{1,0:T(8,128)}, u32[]{:S(2)}, u32[]{:S(2)}) collective-permute-start(f32[1024,128]{1,0:T(8,128)S(1)} %collective-permute-done.3.low_a), channel_id=1, source_target_pairs={{0,32},{32,0},{64,96},{96,64},{128,160},{160,128},{192,224},{224,1... | collective-permute-start | bytes 1572872 | tf_op jit(solution)/shard_map/ppermute | solution.py:65
  29.3 1.3 collective-permute-start.12
  30.9 2.2 %shard_map.73 = (f32[512,128]{1,0:T(8,128)S(1)}, f32[512,128]{1,0:T(8,128)S(1)}, f32[512,128]{1,0:T(8,128)S(1)}) custom-call(s32[2,128]{1,0:T(2,128)S(1)} %collective-permute-done.lists_1, s32[2,128]{1,0:T(2,128)S(1)} %collective-permute-done.1.lists_2.lists, s32[2,128]{1,0:T(2,128)S(1)} %collective-permute-done.2.lists_3, ...), custom_call_target="tpu_custom_call" | custom-call | tf_op jit(solution)/shard_map/pallas_call | solution.py:475
  33.2 1.5 %collective-permute-start.10 = (f32[512,128]{1,0:T(8,128)S(1)}, f32[512,128]{1,0:T(8,128)S(1)}, u32[]{:S(2)}, u32[]{:S(2)}) collective-permute-start(f32[512,128]{1,0:T(8,128)S(1)} %get-tuple-element.73), channel_id=1, source_target_pairs={{0,2},{1,3},{2,0},{3,1},{4,6},{5,7},{6,4},{7,5},{8,10},{9,11},{10,... | collective-permute-start | bytes 786440 | tf_op jit(solution)/shard_map/ppermute | solution.py:46
  34.7 3.0 %collective-permute-start.11 = (f32[512,128]{1,0:T(8,128)S(1)}, f32[512,128]{1,0:T(8,128)S(1)}, u32[]{:S(2)}, u32[]{:S(2)}) collective-permute-start(f32[512,128]{1,0:T(8,128)S(1)} %get-tuple-element.74), channel_id=1, source_target_pairs={{0,3},{1,0},{2,1},{3,2},{4,7},{5,4},{6,5},{7,6},{8,11},{9,8},{10,9... | collective-permute-start | bytes 786440 | tf_op jit(solution)/shard_map/ppermute | solution.py:46
  37.8 3.0 %shard_map.68 = (f32[4,512,512]{2,1,0:T(8,128)S(1)}, f32[4,512,512]{2,1,0:T(8,128)S(1)}) custom-call(bf16[3,512,512]{2,1,0:T(8,128)(2,1)S(1)} %bitcast.21), custom_call_target="tpu_custom_call" | custom-call | tf_op jit(solution)/shard_map/pallas_call | solution.py:496
  40.9 2.2 %shard_map.74 = (f32[512,128]{1,0:T(8,128)S(1)}, f32[512,128]{1,0:T(8,128)S(1)}, f32[512,128]{1,0:T(8,128)S(1)}) custom-call(s32[3,128]{1,0:T(4,128)S(1)} %get-tuple-element.75.lists.lists_0, f32[2048,128]{1,0:T(8,128)S(1)} %shard_map.71.held.own, f32[1024,128]{1,0:T(8,128)S(1)} %copy-done.8, f32[1024,128]{1,0:T(8,128)} %collective-permute-done.7.low_b, ...), custom_call_target="tpu_custom_call" | custom-call | tf_op jit(solution)/shard_map/pallas_call | solution.py:479
  43.1 0.9 collective-permute-done.10.refs_5_
  44.0 6.2 %collective-permute-done.11.refs_6_ = f32[512,128]{1,0:T(8,128)S(1)} collective-permute-done((f32[512,128]{1,0:T(8,128)S(1)}, f32[512,128]{1,0:T(8,128)S(1)}, u32[]{:S(2)}, u32[]{:S(2)}) %collective-permute-start.11) | collective-permute-done | bytes 262176 | tf_op jit(solution)/shard_map/ppermute | solution.py:46
  50.3 5.8 %shard_map.76 = (f32[256,512]{1,0:T(8,128)S(1)}, f32[256,512]{1,0:T(8,128)S(1)}, bf16[2048,512]{1,0:T(8,128)(2,1)S(1)}, bf16[2048,512]{1,0:T(8,128)(2,1)S(1)}) custom-call(s32[4,512]{1,0:T(4,128)S(1)} %fusion.24.refs_0_, f32[4,512,512]{2,1,0:T(8,128)S(1)} %get-tuple-element.60.refs_1_, f32[4,512,512]{2,1,0:T(8,128)S(1)} %get-tuple-element.61.refs_2_, ...), custom_call_target="tpu_custom_call" | custom-call | tf_op jit(solution)/shard_map/pallas_call | solution.py:501
  56.2 2.6 %shard_map.78 = (f32[128,512]{1,0:T(8,128)}, f32[128,512]{1,0:T(8,128)}, f32[128,512]{1,0:T(8,128)}) custom-call(s32[1,2048]{1,0:T(1,128)S(1)} %fusion.20.ids_ref, bf16[2048,512]{1,0:T(8,128)(2,1)S(1)} %get-tuple-element.83.push_high, bf16[2048,512]{1,0:T(8,128)(2,1)S(1)} %get-tuple-element.84.push_low), custom_call_target="tpu_custom_call" | custom-call | tf_op jit(solution)/shard_map/pallas_call | solution.py:514
  58.8 3.0 %collective-permute-start.13 = (f32[128,512]{1,0:T(8,128)}, f32[128,512]{1,0:T(8,128)S(1)}, u32[]{:S(2)}, u32[]{:S(2)}) collective-permute-start(f32[128,512]{1,0:T(8,128)} %get-tuple-element.85), channel_id=1, source_target_pairs={{0,3},{1,0},{2,1},{3,2},{4,7},{5,4},{6,5},{7,6},{8,11},{9,8},{10,9... | collective-permute-start | bytes 786440 | tf_op jit(solution)/shard_map/ppermute | solution.py:46
  62.9 1.1 shard_map.77
  64.1 1.6 %copy-done.4 = bf16[2048,512]{1,0:T(8,128)(2,1)S(1)} copy-done((bf16[2048,512]{1,0:T(8,128)(2,1)S(1)}, bf16[2048,512]{1,0:T(8,128)(2,1)}, u32[]{:S(2)}) %copy-start.4) | copy-done | bytes 2097176
  65.7 1.6 %copy-done.6 = bf16[2048,512]{1,0:T(8,128)(2,1)S(1)} copy-done((bf16[2048,512]{1,0:T(8,128)(2,1)S(1)}, bf16[2048,512]{1,0:T(8,128)(2,1)}, u32[]{:S(2)}) %copy-start.6) | copy-done | bytes 2097176
  67.3 3.4 %shard_map.79 = (f32[128,512]{1,0:T(8,128)S(1)}, f32[128,512]{1,0:T(8,128)S(1)}, f32[128,512]{1,0:T(8,128)S(1)}, f32[128,512]{1,0:T(8,128)S(1)}, f32[128,512]{1,0:T(8,128)S(1)}, /*index=5*/f32[128,512]{1,0:T(8,128)S(1)}) custom-call(s32[1,2048]{1,0:T(1,128)S(1)} %fusion.20.ids_ref, bf16[2048,512]{1,0:T(8,128)(2,1)S(1)} %copy-done.4, ...), custom_call_target="tpu_custom_call" | custom-call | tf_op jit(solution)/shard_map/pallas_call | solution.py:517
  70.7 3.0 %shard_map.80.refs_8_ = f32[3,2,256,512]{3,2,1,0:T(8,128)} custom-call(f32[256,512]{1,0:T(8,128)S(1)} %get-tuple-element.114.plane_0, f32[256,512]{1,0:T(8,128)S(1)} %get-tuple-element.113.plane_1, f32[512,512]{1,0:T(8,128)S(1)} %bitcast.19), custom_call_target="tpu_custom_call" | custom-call | tf_op jit(solution)/shard_map/pallas_call | solution.py:523
  73.7 3.1 %collective-permute-done.15.in_3 = f32[128,512]{1,0:T(8,128)} collective-permute-done((f32[128,512]{1,0:T(8,128)}, f32[128,512]{1,0:T(8,128)}, u32[]{:S(2)}, u32[]{:S(2)}) %collective-permute-start.15) | collective-permute-done | bytes 262176 | tf_op jit(solution)/shard_map/ppermute | solution.py:46
  76.9 2.0 %shard_map.81 = (f32[576,512]{1,0:T(8,128)S(1)}, bf16[1280,512]{1,0:T(8,128)(2,1)S(1)}) custom-call(bf16[576,1280]{1,0:T(8,128)(2,1)S(1)} %get-tuple-element.96.hot_low, bf16[576,1280]{1,0:T(8,128)(2,1)S(1)} %get-tuple-element.97.hot_high, f32[128,512]{1,0:T(8,128)S(1)} %get-tuple-element.98.in_low, f32[128,512]{1,0:T(8,128)S(1)} %get-tuple-element.99.in_high, ...), custom_call_target="tpu_custom_call" | custom-call | tf_op jit(solution)/shard_map/pallas_call | solution.py:547
  78.8 0.9 collective-permute-start.19
  79.7 0.9 shard_map.82
  82.4 1.7 %collective-permute-start.21 = (f32[288,512]{1,0:T(8,128)S(1)}, f32[288,512]{1,0:T(8,128)S(1)}, u32[]{:S(2)}, u32[]{:S(2)}) collective-permute-start(f32[288,512]{1,0:T(8,128)S(1)} %get-tuple-element.121), channel_id=1, source_target_pairs={{0,28},{1,29},{2,30},{3,31},{4,0},{5,1},{6,2},{7,3},{8,4},{9,5},{1... | collective-permute-start | bytes 1769480 | tf_op jit(solution)/shard_map/ppermute | solution.py:51
  84.2 4.5 %collective-permute-done.16.in_1 = f32[128,512]{1,0:T(8,128)S(1)} collective-permute-done((f32[128,512]{1,0:T(8,128)S(1)}, f32[128,512]{1,0:T(8,128)S(1)}, u32[]{:S(2)}, u32[]{:S(2)}) %collective-permute-start.16) | collective-permute-done | bytes 262176 | tf_op jit(solution)/shard_map/ppermute | solution.py:46
  88.6 1.8 %collective-permute-done.17.in_2 = f32[128,512]{1,0:T(8,128)S(1)} collective-permute-done((f32[128,512]{1,0:T(8,128)S(1)}, f32[128,512]{1,0:T(8,128)S(1)}, u32[]{:S(2)}, u32[]{:S(2)}) %collective-permute-start.17) | collective-permute-done | bytes 262176 | tf_op jit(solution)/shard_map/ppermute | solution.py:46
  90.5 6.2 %collective-permute-done.18.in_3 = f32[128,512]{1,0:T(8,128)S(1)} collective-permute-done((f32[128,512]{1,0:T(8,128)S(1)}, f32[128,512]{1,0:T(8,128)S(1)}, u32[]{:S(2)}, u32[]{:S(2)}) %collective-permute-start.18) | collective-permute-done | bytes 262176 | tf_op jit(solution)/shard_map/ppermute | solution.py:46
  98.2 1.5 %collective-permute-done.25 = f32[72,512]{1,0:T(8,128)S(1)} collective-permute-done((f32[72,512]{1,0:T(8,128)S(1)}, f32[72,512]{1,0:T(8,128)S(1)}, u32[]{:S(2)}, u32[]{:S(2)}) %collective-permute-start.25) | collective-permute-done | bytes 147488 | tf_op jit(solution)/shard_map/ppermute | solution.py:65
  99.9 1.4 %collective-permute-start.23 = (f32[72,512]{1,0:T(8,128)S(1)}, f32[72,512]{1,0:T(8,128)S(1)}, u32[]{:S(2)}, u32[]{:S(2)}) collective-permute-start(f32[72,512]{1,0:T(8,128)S(1)} %get-tuple-element.118), channel_id=1, source_target_pairs={{0,64},{32,96},{64,128},{96,160},{128,192},{160,224},{192,0},{224,... | collective-permute-start | bytes 442376 | tf_op jit(solution)/shard_map/ppermute | solution.py:70
  101.3 2.6 %collective-permute-start.24 = (f32[72,512]{1,0:T(8,128)S(1)}, f32[72,512]{1,0:T(8,128)S(1)}, u32[]{:S(2)}, u32[]{:S(2)}) collective-permute-start(f32[72,512]{1,0:T(8,128)S(1)} %get-tuple-element.119), channel_id=1, source_target_pairs={{0,128},{32,160},{64,192},{96,224},{128,0},{160,32},{192,64},{224,... | collective-permute-start | bytes 442376 | tf_op jit(solution)/shard_map/ppermute | solution.py:70
  103.9 1.1 collective-permute-start.26
  105.2 4.0 %collective-permute-done.24 = f32[72,512]{1,0:T(8,128)S(1)} collective-permute-done((f32[72,512]{1,0:T(8,128)S(1)}, f32[72,512]{1,0:T(8,128)S(1)}, u32[]{:S(2)}, u32[]{:S(2)}) %collective-permute-start.24) | collective-permute-done | bytes 147488 | tf_op jit(solution)/shard_map/ppermute | solution.py:70
  109.5 1.0 collective-permute-start.29
  110.5 3.9 %collective-permute-start.30 = (f32[72,512]{1,0:T(8,128)S(1)}, f32[72,512]{1,0:T(8,128)S(1)}, u32[]{:S(2)}, u32[]{:S(2)}) collective-permute-start(f32[72,512]{1,0:T(8,128)S(1)} %fusion.18.piece), channel_id=1, source_target_pairs={{0,31},{1,0},{2,1},{3,2},{4,3},{5,4},{6,5},{7,6},{8,7},{9,8},{10,9... | collective-permute-start | bytes 442376 | tf_op jit(solution)/shard_map/ppermute | solution.py:51
  114.4 4.8 %collective-permute-start.28 = (f32[256,512]{1,0:T(8,128)S(1)}, f32[256,512]{1,0:T(8,128)S(1)}, u32[]{:S(2)}, u32[]{:S(2)}) collective-permute-start(f32[256,512]{1,0:T(8,128)S(1)} %get-tuple-element.114.plane_0), channel_id=1, source_target_pairs={{0,31},{1,0},{2,1},{3,2},{4,3},{5,4},{6,5},{7,6},{8,7},{9,8},{10,9... | collective-permute-start | bytes 1572872 | tf_op jit(solution)/shard_map/ppermute | solution.py:51
  119.2 1.2 shard_map.84.refs_0_
  120.4 1.6 %collective-permute-start.31 = (f32[64,512]{1,0:T(8,128)S(1)}, f32[64,512]{1,0:T(8,128)S(1)}, u32[]{:S(2)}, u32[]{:S(2)}) collective-permute-start(f32[64,512]{1,0:T(8,128)S(1)} %shard_map.84.refs_0_), channel_id=1, source_target_pairs={{0,64},{32,96},{64,128},{96,160},{128,192},{160,224},{192,0},{224,... | collective-permute-start | bytes 393224 | tf_op jit(solution)/shard_map/ppermute | solution.py:70
  122.0 2.4 %collective-permute-start.32 = (f32[64,512]{1,0:T(8,128)S(1)}, f32[64,512]{1,0:T(8,128)S(1)}, u32[]{:S(2)}, u32[]{:S(2)}) collective-permute-start(f32[64,512]{1,0:T(8,128)S(1)} %shard_map.84.refs_0_), channel_id=1, source_target_pairs={{0,128},{32,160},{64,192},{96,224},{128,0},{160,32},{192,64},{224,... | collective-permute-start | bytes 393224 | tf_op jit(solution)/shard_map/ppermute | solution.py:70
  124.6 1.2 collective-permute-done.31.refs_1_
  125.9 4.4 %collective-permute-start.34 = (f32[64,512]{1,0:T(8,128)S(1)}, f32[64,512]{1,0:T(8,128)S(1)}, u32[]{:S(2)}, u32[]{:S(2)}) collective-permute-start(f32[64,512]{1,0:T(8,128)S(1)} %shard_map.84.refs_0_), channel_id=1, source_target_pairs={{0,32},{32,0},{64,96},{96,64},{128,160},{160,128},{192,224},{224,1... | collective-permute-start | bytes 393224 | tf_op jit(solution)/shard_map/ppermute | solution.py:65
  130.3 1.9 %collective-permute-start.35 = (f32[64,512]{1,0:T(8,128)S(1)}, f32[64,512]{1,0:T(8,128)S(1)}, u32[]{:S(2)}, u32[]{:S(2)}) collective-permute-start(f32[64,512]{1,0:T(8,128)S(1)} %collective-permute-done.31.refs_1_), channel_id=1, source_target_pairs={{0,32},{32,0},{64,96},{96,64},{128,160},{160,128},{192,224},{224,1... | collective-permute-start | bytes 393224 | tf_op jit(solution)/shard_map/ppermute | solution.py:65
  134.2 2.0 %shard_map.85 = (f32[512,512]{1,0:T(8,128)}, f32[3,2,256,512]{3,2,1,0:T(8,128)}) custom-call(s32[8]{0:T(128)S(1)} %stack.19.place_ref, f32[256,512]{1,0:T(8,128)S(1)} %collective-permute-done.27.before, f32[256,512]{1,0:T(8,128)S(1)} %get-tuple-element.114.plane_0, f32[256,512]{1,0:T(8,128)S(1)} %get-tuple-element.113.plane_1, ...), custom_call_target="tpu_custom_call", output_to_operand_aliasing={{1}: (14, {})} | custom-call | tf_op jit(solution)/shard_map/pallas_call | solution.py:586
  (88 shorter events, 12.8 us)
Async XLA Ops:
  0.6 8.6 %copy-start.15 = (s32[1,1,9,128]{3,1,2,0:T(1,128)S(1)}, s32[1,1,9,128]{3,1,2,0:T(1,128)}, u32[]{:S(2)}) copy-start(s32[1,1,9,128]{3,1,2,0:T(1,128)} %param.8) | copy-start | bytes 13828
  2.0 11.5 %copy-start.1 = (f32[2,256,512]{2,1,0:T(8,128)S(1)}, f32[2,256,512]{2,1,0:T(8,128)}, u32[]{:S(2)}) copy-start(f32[2,256,512]{2,1,0:T(8,128)} %param.5) | copy-start | bytes 3145732
  2.6 22.2 %collective-permute-start.3 = (f32[1024,128]{1,0:T(8,128)S(1)}, f32[1024,128]{1,0:T(8,128)S(1)}, u32[]{:S(2)}, u32[]{:S(2)}) collective-permute-start(f32[1024,128]{1,0:T(8,128)S(1)} %shard_map.70), channel_id=1, source_target_pairs={{0,4},{1,5},{2,6},{3,7},{4,8},{5,9},{6,10},{7,11},{8,12},{9,13},{1... | collective-permute-start | bytes 1572872 | tf_op jit(solution)/shard_map/ppermute | solution.py:51
  5.2 19.6 %collective-permute-start.4 = (f32[1024,128]{1,0:T(8,128)S(1)}, f32[1024,128]{1,0:T(8,128)S(1)}, u32[]{:S(2)}, u32[]{:S(2)}) collective-permute-start(f32[1024,128]{1,0:T(8,128)S(1)} %shard_map.70), channel_id=1, source_target_pairs={{0,28},{1,29},{2,30},{3,31},{4,0},{5,1},{6,2},{7,3},{8,4},{9,5},{1... | collective-permute-start | bytes 1572872 | tf_op jit(solution)/shard_map/ppermute | solution.py:51
  9.8 3.9 %collective-permute-start = (s32[2,128]{1,0:T(2,128)S(1)}, s32[2,128]{1,0:T(2,128)S(1)}, u32[]{:S(2)}, u32[]{:S(2)}) collective-permute-start(s32[2,128]{1,0:T(2,128)S(1)} %get-tuple-element.62), channel_id=1, source_target_pairs={{0,3},{1,0},{2,1},{3,2},{4,7},{5,4},{6,5},{7,6},{8,11},{9,8},{10,9... | collective-permute-start | bytes 3080 | tf_op jit(solution)/shard_map/ppermute | solution.py:46
  12.3 3.9 %collective-permute-start.1 = (s32[2,128]{1,0:T(2,128)S(1)}, s32[2,128]{1,0:T(2,128)S(1)}, u32[]{:S(2)}, u32[]{:S(2)}) collective-permute-start(s32[2,128]{1,0:T(2,128)S(1)} %get-tuple-element.63), channel_id=1, source_target_pairs={{0,2},{1,3},{2,0},{3,1},{4,6},{5,7},{6,4},{7,5},{8,10},{9,11},{10,... | collective-permute-start | bytes 3080 | tf_op jit(solution)/shard_map/ppermute | solution.py:46
  12.9 15.7 %copy-start.14 = (s32[1,4,2,256]{3,2,1,0:T(2,128)S(1)}, s32[1,4,2,256]{3,2,1,0:T(2,128)}, u32[]{:S(2)}) copy-start(s32[1,4,2,256]{3,2,1,0:T(2,128)} %param.9) | copy-start | bytes 24580
  12.9 3.9 %collective-permute-start.2 = (s32[2,128]{1,0:T(2,128)S(1)}, s32[2,128]{1,0:T(2,128)S(1)}, u32[]{:S(2)}, u32[]{:S(2)}) collective-permute-start(s32[2,128]{1,0:T(2,128)S(1)} %get-tuple-element.64), channel_id=1, source_target_pairs={{0,1},{1,2},{2,3},{3,0},{4,5},{5,6},{6,7},{7,4},{8,9},{9,10},{10,1... | collective-permute-start | bytes 3080 | tf_op jit(solution)/shard_map/ppermute | solution.py:46
  17.6 6.5 %collective-permute-start.5 = (f32[512,128]{1,0:T(8,128)S(1)}, f32[512,128]{1,0:T(8,128)S(1)}, u32[]{:S(2)}, u32[]{:S(2)}) collective-permute-start(f32[512,128]{1,0:T(8,128)S(1)} %get-tuple-element.68), channel_id=1, source_target_pairs={{0,1},{1,2},{2,3},{3,0},{4,5},{5,6},{6,7},{7,4},{8,9},{9,10},{10,1... | collective-permute-start | bytes 786440 | tf_op jit(solution)/shard_map/ppermute | solution.py:46
  17.7 6.4 %collective-permute-start.6 = (f32[512,128]{1,0:T(8,128)S(1)}, f32[512,128]{1,0:T(8,128)S(1)}, u32[]{:S(2)}, u32[]{:S(2)}) collective-permute-start(f32[512,128]{1,0:T(8,128)S(1)} %get-tuple-element.69), channel_id=1, source_target_pairs={{0,3},{1,0},{2,1},{3,2},{4,7},{5,4},{6,5},{7,6},{8,11},{9,8},{10,9... | collective-permute-start | bytes 786440 | tf_op jit(solution)/shard_map/ppermute | solution.py:46
  24.8 8.3 %copy-start.7 = (f32[1024,128]{1,0:T(8,128)}, f32[1024,128]{1,0:T(8,128)S(1)}, u32[]{:S(2)}) copy-start(f32[1024,128]{1,0:T(8,128)S(1)} %collective-permute-done.3.low_a) | copy-start | bytes 1572868
  24.8 8.3 %copy-start.9 = (f32[1024,128]{1,0:T(8,128)}, f32[1024,128]{1,0:T(8,128)S(1)}, u32[]{:S(2)}) copy-start(f32[1024,128]{1,0:T(8,128)S(1)} %collective-permute-done.4.high_a) | copy-start | bytes 1572868
  24.8 5.7 %collective-permute-start.7 = (f32[1024,128]{1,0:T(8,128)S(1)}, f32[1024,128]{1,0:T(8,128)}, u32[]{:S(2)}, u32[]{:S(2)}) collective-permute-start(f32[1024,128]{1,0:T(8,128)S(1)} %collective-permute-done.3.low_a), channel_id=1, source_target_pairs={{0,32},{32,0},{64,96},{96,64},{128,160},{160,128},{192,224},{224,1... | collective-permute-start | bytes 1572872 | tf_op jit(solution)/shard_map/ppermute | solution.py:65
  28.4 2.4 %collective-permute-start.8 = (f32[1024,128]{1,0:T(8,128)S(1)}, f32[1024,128]{1,0:T(8,128)}, u32[]{:S(2)}, u32[]{:S(2)}) collective-permute-start(f32[1024,128]{1,0:T(8,128)S(1)} %collective-permute-done.4.high_a), channel_id=1, source_target_pairs={{0,32},{32,0},{64,96},{96,64},{128,160},{160,128},{192,224},{224,1... | collective-permute-start | bytes 1572872 | tf_op jit(solution)/shard_map/ppermute | solution.py:65
  28.6 9.2 %copy-start.11 = (bf16[1,3,2,256,512]{4,3,2,1,0:T(8,128)(2,1)S(1)}, bf16[1,3,2,256,512]{4,3,2,1,0:T(8,128)(2,1)}, u32[]{:S(2)}) copy-start(bf16[1,3,2,256,512]{4,3,2,1,0:T(8,128)(2,1)} %param.7) | copy-start | bytes 4718596
  29.3 13.9 %collective-permute-start.12 = (f32[512,128]{1,0:T(8,128)S(1)}, f32[512,128]{1,0:T(8,128)S(1)}, u32[]{:S(2)}, u32[]{:S(2)}) collective-permute-start(f32[512,128]{1,0:T(8,128)S(1)} %shard_map.75), channel_id=1, source_target_pairs={{0,2},{1,3},{2,0},{3,1},{4,6},{5,7},{6,4},{7,5},{8,10},{9,11},{10,... | collective-permute-start | bytes 786440 | tf_op jit(solution)/shard_map/ppermute | solution.py:46
  33.1 7.8 %copy-start.8 = (f32[1024,128]{1,0:T(8,128)S(1)}, f32[1024,128]{1,0:T(8,128)}, u32[]{:S(2)}) copy-start(f32[1024,128]{1,0:T(8,128)} %copy-done.7) | copy-start | bytes 1572868
  33.1 7.7 %copy-start.10 = (f32[1024,128]{1,0:T(8,128)S(1)}, f32[1024,128]{1,0:T(8,128)}, u32[]{:S(2)}) copy-start(f32[1024,128]{1,0:T(8,128)} %copy-done.9) | copy-start | bytes 1572868
  33.2 10.8 %collective-permute-start.10 = (f32[512,128]{1,0:T(8,128)S(1)}, f32[512,128]{1,0:T(8,128)S(1)}, u32[]{:S(2)}, u32[]{:S(2)}) collective-permute-start(f32[512,128]{1,0:T(8,128)S(1)} %get-tuple-element.73), channel_id=1, source_target_pairs={{0,2},{1,3},{2,0},{3,1},{4,6},{5,7},{6,4},{7,5},{8,10},{9,11},{10,... | collective-permute-start | bytes 786440 | tf_op jit(solution)/shard_map/ppermute | solution.py:46
  34.7 15.5 %collective-permute-start.11 = (f32[512,128]{1,0:T(8,128)S(1)}, f32[512,128]{1,0:T(8,128)S(1)}, u32[]{:S(2)}, u32[]{:S(2)}) collective-permute-start(f32[512,128]{1,0:T(8,128)S(1)} %get-tuple-element.74), channel_id=1, source_target_pairs={{0,3},{1,0},{2,1},{3,2},{4,7},{5,4},{6,5},{7,6},{8,11},{9,8},{10,9... | collective-permute-start | bytes 786440 | tf_op jit(solution)/shard_map/ppermute | solution.py:46
  37.7 12.6 %collective-permute-start.9 = (f32[512,128]{1,0:T(8,128)S(1)}, f32[512,128]{1,0:T(8,128)S(1)}, u32[]{:S(2)}, u32[]{:S(2)}) collective-permute-start(f32[512,128]{1,0:T(8,128)S(1)} %get-tuple-element.72), channel_id=1, source_target_pairs={{0,1},{1,2},{2,3},{3,0},{4,5},{5,6},{6,7},{7,4},{8,9},{9,10},{10,1... | collective-permute-start | bytes 786440 | tf_op jit(solution)/shard_map/ppermute | solution.py:46
  40.9 9.4 %copy-start.2 = (f32[1,2,256,512]{3,2,1,0:T(8,128)S(1)}, f32[1,2,256,512]{3,2,1,0:T(8,128)}, u32[]{:S(2)}) copy-start(f32[1,2,256,512]{3,2,1,0:T(8,128)} %param.6) | copy-start | bytes 3145732
  40.9 9.4 %copy-start.13 = (f32[512,128]{1,0:T(8,128)S(1)}, f32[512,128]{1,0:T(8,128)}, u32[]{:S(2)}) copy-start(f32[512,128]{1,0:T(8,128)} %copy-done.12) | copy-start | bytes 786436
  58.8 14.9 %collective-permute-start.13 = (f32[128,512]{1,0:T(8,128)}, f32[128,512]{1,0:T(8,128)S(1)}, u32[]{:S(2)}, u32[]{:S(2)}) collective-permute-start(f32[128,512]{1,0:T(8,128)} %get-tuple-element.85), channel_id=1, source_target_pairs={{0,3},{1,0},{2,1},{3,2},{4,7},{5,4},{6,5},{7,6},{8,11},{9,8},{10,9... | collective-permute-start | bytes 786440 | tf_op jit(solution)/shard_map/ppermute | solution.py:46
  61.8 11.9 %collective-permute-start.14 = (f32[128,512]{1,0:T(8,128)}, f32[128,512]{1,0:T(8,128)}, u32[]{:S(2)}, u32[]{:S(2)}) collective-permute-start(f32[128,512]{1,0:T(8,128)} %get-tuple-element.86), channel_id=1, source_target_pairs={{0,2},{1,3},{2,0},{3,1},{4,6},{5,7},{6,4},{7,5},{8,10},{9,11},{10,... | collective-permute-start | bytes 786440 | tf_op jit(solution)/shard_map/ppermute | solution.py:46
  61.8 15.1 %collective-permute-start.15 = (f32[128,512]{1,0:T(8,128)}, f32[128,512]{1,0:T(8,128)}, u32[]{:S(2)}, u32[]{:S(2)}) collective-permute-start(f32[128,512]{1,0:T(8,128)} %get-tuple-element.87), channel_id=1, source_target_pairs={{0,1},{1,2},{2,3},{3,0},{4,5},{5,6},{6,7},{7,4},{8,9},{9,10},{10,1... | collective-permute-start | bytes 786440 | tf_op jit(solution)/shard_map/ppermute | solution.py:46
  78.8 3.4 %collective-permute-start.19 = (f32[576,512]{1,0:T(8,128)S(1)}, f32[576,512]{1,0:T(8,128)S(1)}, u32[]{:S(2)}, u32[]{:S(2)}) collective-permute-start(f32[576,512]{1,0:T(8,128)S(1)} %get-tuple-element.105), channel_id=1, source_target_pairs={{0,32},{32,0},{64,96},{96,64},{128,160},{160,128},{192,224},{224,1... | collective-permute-start | bytes 3538952 | tf_op jit(solution)/shard_map/ppermute | solution.py:65
  80.6 8.0 %collective-permute-start.16 = (f32[128,512]{1,0:T(8,128)S(1)}, f32[128,512]{1,0:T(8,128)S(1)}, u32[]{:S(2)}, u32[]{:S(2)}) collective-permute-start(f32[128,512]{1,0:T(8,128)S(1)} %get-tuple-element.93), channel_id=1, source_target_pairs={{0,3},{1,0},{2,1},{3,2},{4,7},{5,4},{6,5},{7,6},{8,11},{9,8},{10,9... | collective-permute-start | bytes 786440 | tf_op jit(solution)/shard_map/ppermute | solution.py:46
  81.3 9.2 %collective-permute-start.17 = (f32[128,512]{1,0:T(8,128)S(1)}, f32[128,512]{1,0:T(8,128)S(1)}, u32[]{:S(2)}, u32[]{:S(2)}) collective-permute-start(f32[128,512]{1,0:T(8,128)S(1)} %get-tuple-element.94), channel_id=1, source_target_pairs={{0,2},{1,3},{2,0},{3,1},{4,6},{5,7},{6,4},{7,5},{8,10},{9,11},{10,... | collective-permute-start | bytes 786440 | tf_op jit(solution)/shard_map/ppermute | solution.py:46
  81.9 14.8 %collective-permute-start.18 = (f32[128,512]{1,0:T(8,128)S(1)}, f32[128,512]{1,0:T(8,128)S(1)}, u32[]{:S(2)}, u32[]{:S(2)}) collective-permute-start(f32[128,512]{1,0:T(8,128)S(1)} %get-tuple-element.95), channel_id=1, source_target_pairs={{0,1},{1,2},{2,3},{3,0},{4,5},{5,6},{6,7},{7,4},{8,9},{9,10},{10,1... | collective-permute-start | bytes 786440 | tf_op jit(solution)/shard_map/ppermute | solution.py:46
  82.4 17.3 %collective-permute-start.21 = (f32[288,512]{1,0:T(8,128)S(1)}, f32[288,512]{1,0:T(8,128)S(1)}, u32[]{:S(2)}, u32[]{:S(2)}) collective-permute-start(f32[288,512]{1,0:T(8,128)S(1)} %get-tuple-element.121), channel_id=1, source_target_pairs={{0,28},{1,29},{2,30},{3,31},{4,0},{5,1},{6,2},{7,3},{8,4},{9,5},{1... | collective-permute-start | bytes 1769480 | tf_op jit(solution)/shard_map/ppermute | solution.py:51
  84.2 15.5 %collective-permute-start.22 = (f32[288,512]{1,0:T(8,128)S(1)}, f32[288,512]{1,0:T(8,128)S(1)}, u32[]{:S(2)}, u32[]{:S(2)}) collective-permute-start(f32[288,512]{1,0:T(8,128)S(1)} %get-tuple-element.122), channel_id=1, source_target_pairs={{0,4},{1,5},{2,6},{3,7},{4,8},{5,9},{6,10},{7,11},{8,12},{9,13},{1... | collective-permute-start | bytes 1769480 | tf_op jit(solution)/shard_map/ppermute | solution.py:51
  97.5 2.2 %collective-permute-start.20 = (f32[216,512]{1,0:T(8,128)S(1)}, f32[216,512]{1,0:T(8,128)S(1)}, u32[]{:S(2)}, u32[]{:S(2)}) collective-permute-start(f32[216,512]{1,0:T(8,128)S(1)} %get-tuple-element.111), channel_id=1, source_target_pairs={{0,32},{32,0},{64,96},{96,64},{128,160},{160,128},{192,224},{224,1... | collective-permute-start | bytes 1327112 | tf_op jit(solution)/shard_map/ppermute | solution.py:65
  98.1 1.6 %collective-permute-start.25 = (f32[72,512]{1,0:T(8,128)S(1)}, f32[72,512]{1,0:T(8,128)S(1)}, u32[]{:S(2)}, u32[]{:S(2)}) collective-permute-start(f32[72,512]{1,0:T(8,128)S(1)} %get-tuple-element.112), channel_id=1, source_target_pairs={{0,32},{32,0},{64,96},{96,64},{128,160},{160,128},{192,224},{224,1... | collective-permute-start | bytes 442376 | tf_op jit(solution)/shard_map/ppermute | solution.py:65
  99.9 5.3 %collective-permute-start.23 = (f32[72,512]{1,0:T(8,128)S(1)}, f32[72,512]{1,0:T(8,128)S(1)}, u32[]{:S(2)}, u32[]{:S(2)}) collective-permute-start(f32[72,512]{1,0:T(8,128)S(1)} %get-tuple-element.118), channel_id=1, source_target_pairs={{0,64},{32,96},{64,128},{96,160},{128,192},{160,224},{192,0},{224,... | collective-permute-start | bytes 442376 | tf_op jit(solution)/shard_map/ppermute | solution.py:70
  101.3 7.9 %collective-permute-start.24 = (f32[72,512]{1,0:T(8,128)S(1)}, f32[72,512]{1,0:T(8,128)S(1)}, u32[]{:S(2)}, u32[]{:S(2)}) collective-permute-start(f32[72,512]{1,0:T(8,128)S(1)} %get-tuple-element.119), channel_id=1, source_target_pairs={{0,128},{32,160},{64,192},{96,224},{128,0},{160,32},{192,64},{224,... | collective-permute-start | bytes 442376 | tf_op jit(solution)/shard_map/ppermute | solution.py:70
  103.9 5.5 %collective-permute-start.26 = (f32[72,512]{1,0:T(8,128)S(1)}, f32[72,512]{1,0:T(8,128)S(1)}, u32[]{:S(2)}, u32[]{:S(2)}) collective-permute-start(f32[72,512]{1,0:T(8,128)S(1)} %get-tuple-element.120), channel_id=1, source_target_pairs={{0,192},{32,224},{64,0},{96,32},{128,64},{160,96},{192,128},{224,1... | collective-permute-start | bytes 442376 | tf_op jit(solution)/shard_map/ppermute | solution.py:70
  109.5 9.7 %collective-permute-start.29 = (f32[72,512]{1,0:T(8,128)S(1)}, f32[72,512]{1,0:T(8,128)S(1)}, u32[]{:S(2)}, u32[]{:S(2)}) collective-permute-start(f32[72,512]{1,0:T(8,128)S(1)} %fusion.18.piece), channel_id=1, source_target_pairs={{0,1},{1,2},{2,3},{3,4},{4,5},{5,6},{6,7},{7,8},{8,9},{9,10},{10,1... | collective-permute-start | bytes 442376 | tf_op jit(solution)/shard_map/ppermute | solution.py:51
  110.5 8.7 %collective-permute-start.30 = (f32[72,512]{1,0:T(8,128)S(1)}, f32[72,512]{1,0:T(8,128)S(1)}, u32[]{:S(2)}, u32[]{:S(2)}) collective-permute-start(f32[72,512]{1,0:T(8,128)S(1)} %fusion.18.piece), channel_id=1, source_target_pairs={{0,31},{1,0},{2,1},{3,2},{4,3},{5,4},{6,5},{7,6},{8,7},{9,8},{10,9... | collective-permute-start | bytes 442376 | tf_op jit(solution)/shard_map/ppermute | solution.py:51
  114.4 19.8 %collective-permute-start.27 = (f32[256,512]{1,0:T(8,128)S(1)}, f32[256,512]{1,0:T(8,128)S(1)}, u32[]{:S(2)}, u32[]{:S(2)}) collective-permute-start(f32[256,512]{1,0:T(8,128)S(1)} %get-tuple-element.113.plane_1), channel_id=1, source_target_pairs={{0,1},{1,2},{2,3},{3,4},{4,5},{5,6},{6,7},{7,8},{8,9},{9,10},{10,1... | collective-permute-start | bytes 1572872 | tf_op jit(solution)/shard_map/ppermute | solution.py:51
  114.4 19.8 %collective-permute-start.28 = (f32[256,512]{1,0:T(8,128)S(1)}, f32[256,512]{1,0:T(8,128)S(1)}, u32[]{:S(2)}, u32[]{:S(2)}) collective-permute-start(f32[256,512]{1,0:T(8,128)S(1)} %get-tuple-element.114.plane_0), channel_id=1, source_target_pairs={{0,31},{1,0},{2,1},{3,2},{4,3},{5,4},{6,5},{7,6},{8,7},{9,8},{10,9... | collective-permute-start | bytes 1572872 | tf_op jit(solution)/shard_map/ppermute | solution.py:51
  120.4 5.5 %collective-permute-start.31 = (f32[64,512]{1,0:T(8,128)S(1)}, f32[64,512]{1,0:T(8,128)S(1)}, u32[]{:S(2)}, u32[]{:S(2)}) collective-permute-start(f32[64,512]{1,0:T(8,128)S(1)} %shard_map.84.refs_0_), channel_id=1, source_target_pairs={{0,64},{32,96},{64,128},{96,160},{128,192},{160,224},{192,0},{224,... | collective-permute-start | bytes 393224 | tf_op jit(solution)/shard_map/ppermute | solution.py:70
  122.0 8.3 %collective-permute-start.32 = (f32[64,512]{1,0:T(8,128)S(1)}, f32[64,512]{1,0:T(8,128)S(1)}, u32[]{:S(2)}, u32[]{:S(2)}) collective-permute-start(f32[64,512]{1,0:T(8,128)S(1)} %shard_map.84.refs_0_), channel_id=1, source_target_pairs={{0,128},{32,160},{64,192},{96,224},{128,0},{160,32},{192,64},{224,... | collective-permute-start | bytes 393224 | tf_op jit(solution)/shard_map/ppermute | solution.py:70
  124.4 7.8 %collective-permute-start.33 = (f32[64,512]{1,0:T(8,128)S(1)}, f32[64,512]{1,0:T(8,128)S(1)}, u32[]{:S(2)}, u32[]{:S(2)}) collective-permute-start(f32[64,512]{1,0:T(8,128)S(1)} %shard_map.84.refs_0_), channel_id=1, source_target_pairs={{0,192},{32,224},{64,0},{96,32},{128,64},{160,96},{192,128},{224,1... | collective-permute-start | bytes 393224 | tf_op jit(solution)/shard_map/ppermute | solution.py:70
  125.9 7.0 %collective-permute-start.34 = (f32[64,512]{1,0:T(8,128)S(1)}, f32[64,512]{1,0:T(8,128)S(1)}, u32[]{:S(2)}, u32[]{:S(2)}) collective-permute-start(f32[64,512]{1,0:T(8,128)S(1)} %shard_map.84.refs_0_), channel_id=1, source_target_pairs={{0,32},{32,0},{64,96},{96,64},{128,160},{160,128},{192,224},{224,1... | collective-permute-start | bytes 393224 | tf_op jit(solution)/shard_map/ppermute | solution.py:65
  130.3 2.9 %collective-permute-start.35 = (f32[64,512]{1,0:T(8,128)S(1)}, f32[64,512]{1,0:T(8,128)S(1)}, u32[]{:S(2)}, u32[]{:S(2)}) collective-permute-start(f32[64,512]{1,0:T(8,128)S(1)} %collective-permute-done.31.refs_1_), channel_id=1, source_target_pairs={{0,32},{32,0},{64,96},{96,64},{128,160},{160,128},{192,224},{224,1... | collective-permute-start | bytes 393224 | tf_op jit(solution)/shard_map/ppermute | solution.py:65
  132.2 1.6 %collective-permute-start.36 = (f32[64,512]{1,0:T(8,128)S(1)}, f32[64,512]{1,0:T(8,128)S(1)}, u32[]{:S(2)}, u32[]{:S(2)}) collective-permute-start(f32[64,512]{1,0:T(8,128)S(1)} %collective-permute-done.32.refs_2_), channel_id=1, source_target_pairs={{0,32},{32,0},{64,96},{96,64},{128,160},{160,128},{192,224},{224,1... | collective-permute-start | bytes 393224 | tf_op jit(solution)/shard_map/ppermute | solution.py:65
  132.8 1.3 collective-permute-start.37
  (6 other events, 10.4 us)

commit v6 on v5

--- a/solution.py
+++ b/solution.py
@@ -465,9 +465,8 @@
         near_lines_kernel, (packed,) * 2, [SMEM] * 2 + [VMEM], (VMEM,) * 2,
     )(asked[1], asked[3], spread)
     got_1, got_3 = along_x(own_1, 1), along_x(own_3, 3)
-    from_low, from_high, _ = lax.optimization_barrier((from_low, from_high, (got_1, got_3)))
-    far_list, _ = lax.optimization_barrier((asked[2], got_3))
-    own_2 = call(far_lines_kernel, packed, [SMEM, VMEM], VMEM)(far_list, spread)
+    own_2 = call(far_lines_kernel, packed, [SMEM, VMEM], VMEM)(asked[2], spread)
+    from_low, from_high, own_2, _ = lax.optimization_barrier((from_low, from_high, own_2, (got_1, got_3)))
     got_own = [got_1, along_x(own_2, 2), got_3]
     from_low_b, from_high_b = other_core(from_low), other_core(from_high)
     slabs = (from_low, from_low_b, from_high, from_high_b)

time: 137 us -> 136 us (level)
  local copies, waits for them, and re-layouts: 5.28 us -> 8.04 us
  waiting for transfers between devices: 38.7 us -> 36.1 us
    ppermute x15, waiting for transfers between devices: 29.7 us -> 26.5 us  [along_x(): return lax.ppermute(value, 'slab', route)]
    unnamed x34 -> x36, local copies, waits for them, and re-layouts: 5.18 us -> 7.94 us
where the time goes in v6:
time: 136 us
  starting transfers between devices  56.3 us (41%)
  waiting for transfers between devices  36.1 us (27%)
  Pallas kernels  33.2 us (24%)
  local copies, waits for them, and re-layouts  8.04 us (6%)
    ppermute x15, waiting for transfers between devices, along_x(): return lax.ppermute(value, 'slab', route)  26.5 us
    ppermute x8, starting transfers between devices, along_slab(): lax.ppermute(value, 'slab', [(i, (i + step) % count) for i in range(count)])  18 us
    ppermute x15, starting transfers between devices, along_x(): return lax.ppermute(value, 'slab', route)  16.7 us
    ppermute x9, starting transfers between devices, other_core(): return lax.ppermute(value, 'subj', [(i, i ^ 1) for i in range(count)])  12.3 us
    ppermute x6, starting transfers between devices, along_y(): lax.ppermute(value, 'subj', [(i, (i + 2 * step) % count) for i in range(c...  9.35 us
    unnamed x36, local copies, waits for them, and re-layouts  7.94 us
    pallas_call x1, Pallas kernels, on_device(): call(warp_kernel, (half,) * 2 + (push_part,) * 2, [SMEM] + [VMEM] * 12, (...  5.81 us
    ppermute x6, waiting for transfers between devices, along_y(): lax.ppermute(value, 'subj', [(i, (i + 2 * step) % count) for i in range(c...  5.7 us
  transfers between devices with their start and end apart: 38, of which 19 were waited for; matrix products, arithmetic and copies ran while one was open for 1% of the time, Pallas kernels for 15%

profile of v6, /device:TPU:1, one launch (start us, length us, event | category | flops | bytes accessed | tf_op | source)
XLA Modules:
  0.0 135.9 jit_solution(9469312830822564152)
XLA Ops:
  0.8 1.2 copy-done
  2.6 2.5 %collective-permute-start.3 = (f32[1024,128]{1,0:T(8,128)S(1)}, f32[1024,128]{1,0:T(8,128)S(1)}, u32[]{:S(2)}, u32[]{:S(2)}) collective-permute-start(f32[1024,128]{1,0:T(8,128)S(1)} %shard_map.70), channel_id=1, source_target_pairs={{0,4},{1,5},{2,6},{3,7},{4,8},{5,9},{6,10},{7,11},{8,12},{9,13},{1... | collective-permute-start | bytes 1572872 | tf_op jit(solution)/shard_map/ppermute | solution.py:51
  5.2 4.0 %collective-permute-start.4 = (f32[1024,128]{1,0:T(8,128)S(1)}, f32[1024,128]{1,0:T(8,128)S(1)}, u32[]{:S(2)}, u32[]{:S(2)}) collective-permute-start(f32[1024,128]{1,0:T(8,128)S(1)} %shard_map.70), channel_id=1, source_target_pairs={{0,28},{1,29},{2,30},{3,31},{4,0},{5,1},{6,2},{7,3},{8,4},{9,5},{1... | collective-permute-start | bytes 1572872 | tf_op jit(solution)/shard_map/ppermute | solution.py:51
  9.8 2.6 %collective-permute-start = (s32[2,128]{1,0:T(2,128)S(1)}, s32[2,128]{1,0:T(2,128)S(1)}, u32[]{:S(2)}, u32[]{:S(2)}) collective-permute-start(s32[2,128]{1,0:T(2,128)S(1)} %get-tuple-element.62), channel_id=1, source_target_pairs={{0,3},{1,0},{2,1},{3,2},{4,7},{5,4},{6,5},{7,6},{8,11},{9,8},{10,9... | collective-permute-start | bytes 3080 | tf_op jit(solution)/shard_map/ppermute | solution.py:46
  13.7 2.6 %collective-permute-done.1.lists.lists_2 = s32[2,128]{1,0:T(2,128)S(1)} collective-permute-done((s32[2,128]{1,0:T(2,128)S(1)}, s32[2,128]{1,0:T(2,128)S(1)}, u32[]{:S(2)}, u32[]{:S(2)}) %collective-permute-start.1) | collective-permute-done | bytes 1056 | tf_op jit(solution)/shard_map/ppermute | solution.py:46
  17.7 2.7 %collective-permute-start.6 = (f32[512,128]{1,0:T(8,128)S(1)}, f32[512,128]{1,0:T(8,128)S(1)}, u32[]{:S(2)}, u32[]{:S(2)}) collective-permute-start(f32[512,128]{1,0:T(8,128)S(1)} %get-tuple-element.69), channel_id=1, source_target_pairs={{0,3},{1,0},{2,1},{3,2},{4,7},{5,4},{6,5},{7,6},{8,11},{9,8},{10,9... | collective-permute-start | bytes 786440 | tf_op jit(solution)/shard_map/ppermute | solution.py:46
  21.7 2.4 %collective-permute-done.5.refs_9_ = f32[512,128]{1,0:T(8,128)S(1)} collective-permute-done((f32[512,128]{1,0:T(8,128)S(1)}, f32[512,128]{1,0:T(8,128)S(1)}, u32[]{:S(2)}, u32[]{:S(2)}) %collective-permute-start.5) | collective-permute-done | bytes 262176 | tf_op jit(solution)/shard_map/ppermute | solution.py:46
  24.8 3.6 %collective-permute-start.7 = (f32[1024,128]{1,0:T(8,128)S(1)}, f32[1024,128]{1,0:T(8,128)}, u32[]{:S(2)}, u32[]{:S(2)}) collective-permute-start(f32[1024,128]{1,0:T(8,128)S(1)} %collective-permute-done.3.low_a), channel_id=1, source_target_pairs={{0,32},{32,0},{64,96},{96,64},{128,160},{160,128},{192,224},{224,1... | collective-permute-start | bytes 1572872 | tf_op jit(solution)/shard_map/ppermute | solution.py:65
  28.6 1.3 collective-permute-start.12
  30.9 2.2 %shard_map.74 = (f32[512,128]{1,0:T(8,128)S(1)}, f32[512,128]{1,0:T(8,128)S(1)}, f32[512,128]{1,0:T(8,128)S(1)}) custom-call(s32[2,128]{1,0:T(2,128)S(1)} %collective-permute-done.lists_1, s32[2,128]{1,0:T(2,128)S(1)} %collective-permute-done.1.lists.lists_2, s32[2,128]{1,0:T(2,128)S(1)} %collective-permute-done.2.lists_3, ...), custom_call_target="tpu_custom_call" | custom-call | tf_op jit(solution)/shard_map/pallas_call | solution.py:474
  33.1 1.3 collective-permute-start.10
  34.4 2.6 %collective-permute-start.11 = (f32[512,128]{1,0:T(8,128)S(1)}, f32[512,128]{1,0:T(8,128)S(1)}, u32[]{:S(2)}, u32[]{:S(2)}) collective-permute-start(f32[512,128]{1,0:T(8,128)S(1)} %get-tuple-element.74), channel_id=1, source_target_pairs={{0,3},{1,0},{2,1},{3,2},{4,7},{5,4},{6,5},{7,6},{8,11},{9,8},{10,9... | collective-permute-start | bytes 786440 | tf_op jit(solution)/shard_map/ppermute | solution.py:46
  37.1 3.0 %shard_map.68 = (f32[4,512,512]{2,1,0:T(8,128)S(1)}, f32[4,512,512]{2,1,0:T(8,128)S(1)}) custom-call(bf16[3,512,512]{2,1,0:T(8,128)(2,1)S(1)} %bitcast.21), custom_call_target="tpu_custom_call" | custom-call | tf_op jit(solution)/shard_map/pallas_call | solution.py:495
  40.2 1.0 copy-done.8
  41.2 1.0 copy-done.10
  42.3 2.2 %shard_map.75 = (f32[512,128]{1,0:T(8,128)S(1)}, f32[512,128]{1,0:T(8,128)S(1)}, f32[512,128]{1,0:T(8,128)S(1)}) custom-call(s32[3,128]{1,0:T(4,128)S(1)} %get-tuple-element.75.lists.lists_0, f32[2048,128]{1,0:T(8,128)S(1)} %shard_map.71.held.own, f32[1024,128]{1,0:T(8,128)S(1)} %copy-done.8, f32[1024,128]{1,0:T(8,128)} %collective-permute-done.7.low_b, ...), custom_call_target="tpu_custom_call" | custom-call | tf_op jit(solution)/shard_map/pallas_call | solution.py:478
  44.5 5.2 %collective-permute-done.11.refs_6_ = f32[512,128]{1,0:T(8,128)S(1)} collective-permute-done((f32[512,128]{1,0:T(8,128)S(1)}, f32[512,128]{1,0:T(8,128)S(1)}, u32[]{:S(2)}, u32[]{:S(2)}) %collective-permute-start.11) | collective-permute-done | bytes 262176 | tf_op jit(solution)/shard_map/ppermute | solution.py:46
  49.8 5.8 %shard_map.76 = (f32[256,512]{1,0:T(8,128)S(1)}, f32[256,512]{1,0:T(8,128)S(1)}, bf16[2048,512]{1,0:T(8,128)(2,1)S(1)}, bf16[2048,512]{1,0:T(8,128)(2,1)S(1)}) custom-call(s32[4,512]{1,0:T(4,128)S(1)} %fusion.24.refs_0_, f32[4,512,512]{2,1,0:T(8,128)S(1)} %get-tuple-element.60.refs_1_, f32[4,512,512]{2,1,0:T(8,128)S(1)} %get-tuple-element.61.refs_2_, ...), custom_call_target="tpu_custom_call" | custom-call | tf_op jit(solution)/shard_map/pallas_call | solution.py:500
  55.7 2.6 %shard_map.78 = (f32[128,512]{1,0:T(8,128)}, f32[128,512]{1,0:T(8,128)}, f32[128,512]{1,0:T(8,128)}) custom-call(s32[1,2048]{1,0:T(1,128)S(1)} %fusion.20.ids_ref, bf16[2048,512]{1,0:T(8,128)(2,1)S(1)} %get-tuple-element.83.push_high, bf16[2048,512]{1,0:T(8,128)(2,1)S(1)} %get-tuple-element.84.push_low), custom_call_target="tpu_custom_call" | custom-call | tf_op jit(solution)/shard_map/pallas_call | solution.py:513
  58.3 3.0 %collective-permute-start.13 = (f32[128,512]{1,0:T(8,128)}, f32[128,512]{1,0:T(8,128)S(1)}, u32[]{:S(2)}, u32[]{:S(2)}) collective-permute-start(f32[128,512]{1,0:T(8,128)} %get-tuple-element.85), channel_id=1, source_target_pairs={{0,3},{1,0},{2,1},{3,2},{4,7},{5,4},{6,5},{7,6},{8,11},{9,8},{10,9... | collective-permute-start | bytes 786440 | tf_op jit(solution)/shard_map/ppermute | solution.py:46
  62.4 1.1 shard_map.77
  63.6 1.6 %copy-done.4 = bf16[2048,512]{1,0:T(8,128)(2,1)S(1)} copy-done((bf16[2048,512]{1,0:T(8,128)(2,1)S(1)}, bf16[2048,512]{1,0:T(8,128)(2,1)}, u32[]{:S(2)}) %copy-start.4) | copy-done | bytes 2097176
  65.2 1.6 %copy-done.6 = bf16[2048,512]{1,0:T(8,128)(2,1)S(1)} copy-done((bf16[2048,512]{1,0:T(8,128)(2,1)S(1)}, bf16[2048,512]{1,0:T(8,128)(2,1)}, u32[]{:S(2)}) %copy-start.6) | copy-done | bytes 2097176
  66.8 3.4 %shard_map.79 = (f32[128,512]{1,0:T(8,128)S(1)}, f32[128,512]{1,0:T(8,128)S(1)}, f32[128,512]{1,0:T(8,128)S(1)}, f32[128,512]{1,0:T(8,128)S(1)}, f32[128,512]{1,0:T(8,128)S(1)}, /*index=5*/f32[128,512]{1,0:T(8,128)S(1)}) custom-call(s32[1,2048]{1,0:T(1,128)S(1)} %fusion.20.ids_ref, bf16[2048,512]{1,0:T(8,128)(2,1)S(1)} %copy-done.4, ...), custom_call_target="tpu_custom_call" | custom-call | tf_op jit(solution)/shard_map/pallas_call | solution.py:516
  70.2 3.0 %shard_map.80.refs_8_ = f32[3,2,256,512]{3,2,1,0:T(8,128)} custom-call(f32[256,512]{1,0:T(8,128)S(1)} %get-tuple-element.114.plane_0, f32[256,512]{1,0:T(8,128)S(1)} %get-tuple-element.113.plane_1, f32[512,512]{1,0:T(8,128)S(1)} %bitcast.19), custom_call_target="tpu_custom_call" | custom-call | tf_op jit(solution)/shard_map/pallas_call | solution.py:522
  73.2 3.1 %collective-permute-done.15.in_3 = f32[128,512]{1,0:T(8,128)} collective-permute-done((f32[128,512]{1,0:T(8,128)}, f32[128,512]{1,0:T(8,128)}, u32[]{:S(2)}, u32[]{:S(2)}) %collective-permute-start.15) | collective-permute-done | bytes 262176 | tf_op jit(solution)/shard_map/ppermute | solution.py:46
  76.3 2.0 %shard_map.81 = (f32[576,512]{1,0:T(8,128)S(1)}, bf16[1280,512]{1,0:T(8,128)(2,1)S(1)}) custom-call(bf16[576,1280]{1,0:T(8,128)(2,1)S(1)} %get-tuple-element.96.hot_low, bf16[576,1280]{1,0:T(8,128)(2,1)S(1)} %get-tuple-element.97.hot_high, f32[128,512]{1,0:T(8,128)S(1)} %get-tuple-element.98.in_low, f32[128,512]{1,0:T(8,128)S(1)} %get-tuple-element.99.in_high, ...), custom_call_target="tpu_custom_call" | custom-call | tf_op jit(solution)/shard_map/pallas_call | solution.py:546
  78.3 0.9 collective-permute-start.19
  79.2 0.9 shard_map.82
  81.9 1.7 %collective-permute-start.21 = (f32[288,512]{1,0:T(8,128)S(1)}, f32[288,512]{1,0:T(8,128)S(1)}, u32[]{:S(2)}, u32[]{:S(2)}) collective-permute-start(f32[288,512]{1,0:T(8,128)S(1)} %get-tuple-element.121), channel_id=1, source_target_pairs={{0,28},{1,29},{2,30},{3,31},{4,0},{5,1},{6,2},{7,3},{8,4},{9,5},{1... | collective-permute-start | bytes 1769480 | tf_op jit(solution)/shard_map/ppermute | solution.py:51
  83.7 4.5 %collective-permute-done.16.in_1 = f32[128,512]{1,0:T(8,128)S(1)} collective-permute-done((f32[128,512]{1,0:T(8,128)S(1)}, f32[128,512]{1,0:T(8,128)S(1)}, u32[]{:S(2)}, u32[]{:S(2)}) %collective-permute-start.16) | collective-permute-done | bytes 262176 | tf_op jit(solution)/shard_map/ppermute | solution.py:46
  88.1 1.8 %collective-permute-done.17.in_2 = f32[128,512]{1,0:T(8,128)S(1)} collective-permute-done((f32[128,512]{1,0:T(8,128)S(1)}, f32[128,512]{1,0:T(8,128)S(1)}, u32[]{:S(2)}, u32[]{:S(2)}) %collective-permute-start.17) | collective-permute-done | bytes 262176 | tf_op jit(solution)/shard_map/ppermute | solution.py:46
  90.0 6.2 %collective-permute-done.18.in_3 = f32[128,512]{1,0:T(8,128)S(1)} collective-permute-done((f32[128,512]{1,0:T(8,128)S(1)}, f32[128,512]{1,0:T(8,128)S(1)}, u32[]{:S(2)}, u32[]{:S(2)}) %collective-permute-start.18) | collective-permute-done | bytes 262176 | tf_op jit(solution)/shard_map/ppermute | solution.py:46
  97.7 1.5 %collective-permute-done.25 = f32[72,512]{1,0:T(8,128)S(1)} collective-permute-done((f32[72,512]{1,0:T(8,128)S(1)}, f32[72,512]{1,0:T(8,128)S(1)}, u32[]{:S(2)}, u32[]{:S(2)}) %collective-permute-start.25) | collective-permute-done | bytes 147488 | tf_op jit(solution)/shard_map/ppermute | solution.py:65
  99.4 1.4 %collective-permute-start.23 = (f32[72,512]{1,0:T(8,128)S(1)}, f32[72,512]{1,0:T(8,128)S(1)}, u32[]{:S(2)}, u32[]{:S(2)}) collective-permute-start(f32[72,512]{1,0:T(8,128)S(1)} %get-tuple-element.118), channel_id=1, source_target_pairs={{0,64},{32,96},{64,128},{96,160},{128,192},{160,224},{192,0},{224,... | collective-permute-start | bytes 442376 | tf_op jit(solution)/shard_map/ppermute | solution.py:70
  100.8 2.6 %collective-permute-start.24 = (f32[72,512]{1,0:T(8,128)S(1)}, f32[72,512]{1,0:T(8,128)S(1)}, u32[]{:S(2)}, u32[]{:S(2)}) collective-permute-start(f32[72,512]{1,0:T(8,128)S(1)} %get-tuple-element.119), channel_id=1, source_target_pairs={{0,128},{32,160},{64,192},{96,224},{128,0},{160,32},{192,64},{224,... | collective-permute-start | bytes 442376 | tf_op jit(solution)/shard_map/ppermute | solution.py:70
  103.4 1.1 collective-permute-start.26
  104.7 4.0 %collective-permute-done.24 = f32[72,512]{1,0:T(8,128)S(1)} collective-permute-done((f32[72,512]{1,0:T(8,128)S(1)}, f32[72,512]{1,0:T(8,128)S(1)}, u32[]{:S(2)}, u32[]{:S(2)}) %collective-permute-start.24) | collective-permute-done | bytes 147488 | tf_op jit(solution)/shard_map/ppermute | solution.py:70
  109.0 1.0 collective-permute-start.29
  110.0 3.9 %collective-permute-start.30 = (f32[72,512]{1,0:T(8,128)S(1)}, f32[72,512]{1,0:T(8,128)S(1)}, u32[]{:S(2)}, u32[]{:S(2)}) collective-permute-start(f32[72,512]{1,0:T(8,128)S(1)} %fusion.18.piece), channel_id=1, source_target_pairs={{0,31},{1,0},{2,1},{3,2},{4,3},{5,4},{6,5},{7,6},{8,7},{9,8},{10,9... | collective-permute-start | bytes 442376 | tf_op jit(solution)/shard_map/ppermute | solution.py:51
  113.9 4.8 %collective-permute-start.28 = (f32[256,512]{1,0:T(8,128)S(1)}, f32[256,512]{1,0:T(8,128)S(1)}, u32[]{:S(2)}, u32[]{:S(2)}) collective-permute-start(f32[256,512]{1,0:T(8,128)S(1)} %get-tuple-element.114.plane_0), channel_id=1, source_target_pairs={{0,31},{1,0},{2,1},{3,2},{4,3},{5,4},{6,5},{7,6},{8,7},{9,8},{10,9... | collective-permute-start | bytes 1572872 | tf_op jit(solution)/shard_map/ppermute | solution.py:51
  118.7 1.2 shard_map.84.refs_0_
  119.9 1.6 %collective-permute-start.31 = (f32[64,512]{1,0:T(8,128)S(1)}, f32[64,512]{1,0:T(8,128)S(1)}, u32[]{:S(2)}, u32[]{:S(2)}) collective-permute-start(f32[64,512]{1,0:T(8,128)S(1)} %shard_map.84.refs_0_), channel_id=1, source_target_pairs={{0,64},{32,96},{64,128},{96,160},{128,192},{160,224},{192,0},{224,... | collective-permute-start | bytes 393224 | tf_op jit(solution)/shard_map/ppermute | solution.py:70
  121.5 2.4 %collective-permute-start.32 = (f32[64,512]{1,0:T(8,128)S(1)}, f32[64,512]{1,0:T(8,128)S(1)}, u32[]{:S(2)}, u32[]{:S(2)}) collective-permute-start(f32[64,512]{1,0:T(8,128)S(1)} %shard_map.84.refs_0_), channel_id=1, source_target_pairs={{0,128},{32,160},{64,192},{96,224},{128,0},{160,32},{192,64},{224,... | collective-permute-start | bytes 393224 | tf_op jit(solution)/shard_map/ppermute | solution.py:70
  124.2 1.2 collective-permute-done.31.refs_1_
  125.4 4.4 %collective-permute-start.34 = (f32[64,512]{1,0:T(8,128)S(1)}, f32[64,512]{1,0:T(8,128)S(1)}, u32[]{:S(2)}, u32[]{:S(2)}) collective-permute-start(f32[64,512]{1,0:T(8,128)S(1)} %shard_map.84.refs_0_), channel_id=1, source_target_pairs={{0,32},{32,0},{64,96},{96,64},{128,160},{160,128},{192,224},{224,1... | collective-permute-start | bytes 393224 | tf_op jit(solution)/shard_map/ppermute | solution.py:65
  129.8 2.0 %collective-permute-start.35 = (f32[64,512]{1,0:T(8,128)S(1)}, f32[64,512]{1,0:T(8,128)S(1)}, u32[]{:S(2)}, u32[]{:S(2)}) collective-permute-start(f32[64,512]{1,0:T(8,128)S(1)} %collective-permute-done.31.refs_1_), channel_id=1, source_target_pairs={{0,32},{32,0},{64,96},{96,64},{128,160},{160,128},{192,224},{224,1... | collective-permute-start | bytes 393224 | tf_op jit(solution)/shard_map/ppermute | solution.py:65
  133.7 2.0 %shard_map.85 = (f32[512,512]{1,0:T(8,128)}, f32[3,2,256,512]{3,2,1,0:T(8,128)}) custom-call(s32[8]{0:T(128)S(1)} %stack.19.place_ref, f32[256,512]{1,0:T(8,128)S(1)} %collective-permute-done.27.before, f32[256,512]{1,0:T(8,128)S(1)} %get-tuple-element.114.plane_0, f32[256,512]{1,0:T(8,128)S(1)} %get-tuple-element.113.plane_1, ...), custom_call_target="tpu_custom_call", output_to_operand_aliasing={{1}: (14, {})} | custom-call | tf_op jit(solution)/shard_map/pallas_call | solution.py:585
  (90 shorter events, 15.0 us)
Async XLA Ops:
  0.6 8.6 %copy-start.16 = (s32[1,1,9,128]{3,1,2,0:T(1,128)S(1)}, s32[1,1,9,128]{3,1,2,0:T(1,128)}, u32[]{:S(2)}) copy-start(s32[1,1,9,128]{3,1,2,0:T(1,128)} %param.8) | copy-start | bytes 13828
  2.0 11.5 %copy-start.1 = (f32[2,256,512]{2,1,0:T(8,128)S(1)}, f32[2,256,512]{2,1,0:T(8,128)}, u32[]{:S(2)}) copy-start(f32[2,256,512]{2,1,0:T(8,128)} %param.5) | copy-start | bytes 3145732
  2.6 22.2 %collective-permute-start.3 = (f32[1024,128]{1,0:T(8,128)S(1)}, f32[1024,128]{1,0:T(8,128)S(1)}, u32[]{:S(2)}, u32[]{:S(2)}) collective-permute-start(f32[1024,128]{1,0:T(8,128)S(1)} %shard_map.70), channel_id=1, source_target_pairs={{0,4},{1,5},{2,6},{3,7},{4,8},{5,9},{6,10},{7,11},{8,12},{9,13},{1... | collective-permute-start | bytes 1572872 | tf_op jit(solution)/shard_map/ppermute | solution.py:51
  5.2 19.6 %collective-permute-start.4 = (f32[1024,128]{1,0:T(8,128)S(1)}, f32[1024,128]{1,0:T(8,128)S(1)}, u32[]{:S(2)}, u32[]{:S(2)}) collective-permute-start(f32[1024,128]{1,0:T(8,128)S(1)} %shard_map.70), channel_id=1, source_target_pairs={{0,28},{1,29},{2,30},{3,31},{4,0},{5,1},{6,2},{7,3},{8,4},{9,5},{1... | collective-permute-start | bytes 1572872 | tf_op jit(solution)/shard_map/ppermute | solution.py:51
  9.8 3.9 %collective-permute-start = (s32[2,128]{1,0:T(2,128)S(1)}, s32[2,128]{1,0:T(2,128)S(1)}, u32[]{:S(2)}, u32[]{:S(2)}) collective-permute-start(s32[2,128]{1,0:T(2,128)S(1)} %get-tuple-element.62), channel_id=1, source_target_pairs={{0,3},{1,0},{2,1},{3,2},{4,7},{5,4},{6,5},{7,6},{8,11},{9,8},{10,9... | collective-permute-start | bytes 3080 | tf_op jit(solution)/shard_map/ppermute | solution.py:46
  12.3 3.9 %collective-permute-start.1 = (s32[2,128]{1,0:T(2,128)S(1)}, s32[2,128]{1,0:T(2,128)S(1)}, u32[]{:S(2)}, u32[]{:S(2)}) collective-permute-start(s32[2,128]{1,0:T(2,128)S(1)} %get-tuple-element.63), channel_id=1, source_target_pairs={{0,2},{1,3},{2,0},{3,1},{4,6},{5,7},{6,4},{7,5},{8,10},{9,11},{10,... | collective-permute-start | bytes 3080 | tf_op jit(solution)/shard_map/ppermute | solution.py:46
  12.9 3.9 %collective-permute-start.2 = (s32[2,128]{1,0:T(2,128)S(1)}, s32[2,128]{1,0:T(2,128)S(1)}, u32[]{:S(2)}, u32[]{:S(2)}) collective-permute-start(s32[2,128]{1,0:T(2,128)S(1)} %get-tuple-element.64), channel_id=1, source_target_pairs={{0,1},{1,2},{2,3},{3,0},{4,5},{5,6},{6,7},{7,4},{8,9},{9,10},{10,1... | collective-permute-start | bytes 3080 | tf_op jit(solution)/shard_map/ppermute | solution.py:46
  13.7 14.9 %copy-start.15 = (s32[1,4,2,256]{3,2,1,0:T(2,128)S(1)}, s32[1,4,2,256]{3,2,1,0:T(2,128)}, u32[]{:S(2)}) copy-start(s32[1,4,2,256]{3,2,1,0:T(2,128)} %param.9) | copy-start | bytes 24580
  17.6 6.5 %collective-permute-start.5 = (f32[512,128]{1,0:T(8,128)S(1)}, f32[512,128]{1,0:T(8,128)S(1)}, u32[]{:S(2)}, u32[]{:S(2)}) collective-permute-start(f32[512,128]{1,0:T(8,128)S(1)} %get-tuple-element.68), channel_id=1, source_target_pairs={{0,1},{1,2},{2,3},{3,0},{4,5},{5,6},{6,7},{7,4},{8,9},{9,10},{10,1... | collective-permute-start | bytes 786440 | tf_op jit(solution)/shard_map/ppermute | solution.py:46
  17.7 6.4 %collective-permute-start.6 = (f32[512,128]{1,0:T(8,128)S(1)}, f32[512,128]{1,0:T(8,128)S(1)}, u32[]{:S(2)}, u32[]{:S(2)}) collective-permute-start(f32[512,128]{1,0:T(8,128)S(1)} %get-tuple-element.69), channel_id=1, source_target_pairs={{0,3},{1,0},{2,1},{3,2},{4,7},{5,4},{6,5},{7,6},{8,11},{9,8},{10,9... | collective-permute-start | bytes 786440 | tf_op jit(solution)/shard_map/ppermute | solution.py:46
  24.8 15.3 %copy-start.7 = (f32[1024,128]{1,0:T(8,128)}, f32[1024,128]{1,0:T(8,128)S(1)}, u32[]{:S(2)}) copy-start(f32[1024,128]{1,0:T(8,128)S(1)} %collective-permute-done.3.low_a) | copy-start | bytes 1572868
  24.8 15.3 %copy-start.9 = (f32[1024,128]{1,0:T(8,128)}, f32[1024,128]{1,0:T(8,128)S(1)}, u32[]{:S(2)}) copy-start(f32[1024,128]{1,0:T(8,128)S(1)} %collective-permute-done.4.high_a) | copy-start | bytes 1572868
  24.8 5.3 %collective-permute-start.7 = (f32[1024,128]{1,0:T(8,128)S(1)}, f32[1024,128]{1,0:T(8,128)}, u32[]{:S(2)}, u32[]{:S(2)}) collective-permute-start(f32[1024,128]{1,0:T(8,128)S(1)} %collective-permute-done.3.low_a), channel_id=1, source_target_pairs={{0,32},{32,0},{64,96},{96,64},{128,160},{160,128},{192,224},{224,1... | collective-permute-start | bytes 1572872 | tf_op jit(solution)/shard_map/ppermute | solution.py:65
  28.4 2.4 %collective-permute-start.8 = (f32[1024,128]{1,0:T(8,128)S(1)}, f32[1024,128]{1,0:T(8,128)}, u32[]{:S(2)}, u32[]{:S(2)}) collective-permute-start(f32[1024,128]{1,0:T(8,128)S(1)} %collective-permute-done.4.high_a), channel_id=1, source_target_pairs={{0,32},{32,0},{64,96},{96,64},{128,160},{160,128},{192,224},{224,1... | collective-permute-start | bytes 1572872 | tf_op jit(solution)/shard_map/ppermute | solution.py:65
  28.6 8.5 %copy-start.11 = (bf16[1,3,2,256,512]{4,3,2,1,0:T(8,128)(2,1)S(1)}, bf16[1,3,2,256,512]{4,3,2,1,0:T(8,128)(2,1)}, u32[]{:S(2)}) copy-start(bf16[1,3,2,256,512]{4,3,2,1,0:T(8,128)(2,1)} %param.7) | copy-start | bytes 4718596
  28.6 15.9 %collective-permute-start.12 = (f32[512,128]{1,0:T(8,128)}, f32[512,128]{1,0:T(8,128)S(1)}, u32[]{:S(2)}, u32[]{:S(2)}) collective-permute-start(f32[512,128]{1,0:T(8,128)} %copy-done.14), channel_id=1, source_target_pairs={{0,2},{1,3},{2,0},{3,1},{4,6},{5,7},{6,4},{7,5},{8,10},{9,11},{10,... | collective-permute-start | bytes 786440 | tf_op jit(solution)/shard_map/ppermute | solution.py:46
  33.1 11.4 %collective-permute-start.10 = (f32[512,128]{1,0:T(8,128)S(1)}, f32[512,128]{1,0:T(8,128)S(1)}, u32[]{:S(2)}, u32[]{:S(2)}) collective-permute-start(f32[512,128]{1,0:T(8,128)S(1)} %get-tuple-element.73), channel_id=1, source_target_pairs={{0,2},{1,3},{2,0},{3,1},{4,6},{5,7},{6,4},{7,5},{8,10},{9,11},{10,... | collective-permute-start | bytes 786440 | tf_op jit(solution)/shard_map/ppermute | solution.py:46
  34.4 15.3 %collective-permute-start.11 = (f32[512,128]{1,0:T(8,128)S(1)}, f32[512,128]{1,0:T(8,128)S(1)}, u32[]{:S(2)}, u32[]{:S(2)}) collective-permute-start(f32[512,128]{1,0:T(8,128)S(1)} %get-tuple-element.74), channel_id=1, source_target_pairs={{0,3},{1,0},{2,1},{3,2},{4,7},{5,4},{6,5},{7,6},{8,11},{9,8},{10,9... | collective-permute-start | bytes 786440 | tf_op jit(solution)/shard_map/ppermute | solution.py:46
  36.9 12.9 %collective-permute-start.9 = (f32[512,128]{1,0:T(8,128)S(1)}, f32[512,128]{1,0:T(8,128)S(1)}, u32[]{:S(2)}, u32[]{:S(2)}) collective-permute-start(f32[512,128]{1,0:T(8,128)S(1)} %get-tuple-element.72), channel_id=1, source_target_pairs={{0,1},{1,2},{2,3},{3,0},{4,5},{5,6},{6,7},{7,4},{8,9},{9,10},{10,1... | collective-permute-start | bytes 786440 | tf_op jit(solution)/shard_map/ppermute | solution.py:46
  42.3 7.6 %copy-start.2 = (f32[1,2,256,512]{3,2,1,0:T(8,128)S(1)}, f32[1,2,256,512]{3,2,1,0:T(8,128)}, u32[]{:S(2)}) copy-start(f32[1,2,256,512]{3,2,1,0:T(8,128)} %param.6) | copy-start | bytes 3145732
  42.3 7.6 %copy-start.13 = (f32[512,128]{1,0:T(8,128)S(1)}, f32[512,128]{1,0:T(8,128)}, u32[]{:S(2)}) copy-start(f32[512,128]{1,0:T(8,128)} %copy-done.12) | copy-start | bytes 786436
  55.7 2.7 %copy-start.3 = (bf16[2048,512]{1,0:T(8,128)(2,1)}, bf16[2048,512]{1,0:T(8,128)(2,1)S(1)}, u32[]{:S(2)}) copy-start(bf16[2048,512]{1,0:T(8,128)(2,1)S(1)} %get-tuple-element.83.push_high) | copy-start | bytes 6291460
  55.7 2.7 %copy-start.5 = (bf16[2048,512]{1,0:T(8,128)(2,1)}, bf16[2048,512]{1,0:T(8,128)(2,1)S(1)}, u32[]{:S(2)}) copy-start(bf16[2048,512]{1,0:T(8,128)(2,1)S(1)} %get-tuple-element.84.push_low) | copy-start | bytes 6291460
  58.3 14.9 %collective-permute-start.13 = (f32[128,512]{1,0:T(8,128)}, f32[128,512]{1,0:T(8,128)S(1)}, u32[]{:S(2)}, u32[]{:S(2)}) collective-permute-start(f32[128,512]{1,0:T(8,128)} %get-tuple-element.85), channel_id=1, source_target_pairs={{0,3},{1,0},{2,1},{3,2},{4,7},{5,4},{6,5},{7,6},{8,11},{9,8},{10,9... | collective-permute-start | bytes 786440 | tf_op jit(solution)/shard_map/ppermute | solution.py:46
  61.3 11.9 %collective-permute-start.14 = (f32[128,512]{1,0:T(8,128)}, f32[128,512]{1,0:T(8,128)}, u32[]{:S(2)}, u32[]{:S(2)}) collective-permute-start(f32[128,512]{1,0:T(8,128)} %get-tuple-element.86), channel_id=1, source_target_pairs={{0,2},{1,3},{2,0},{3,1},{4,6},{5,7},{6,4},{7,5},{8,10},{9,11},{10,... | collective-permute-start | bytes 786440 | tf_op jit(solution)/shard_map/ppermute | solution.py:46
  61.3 15.0 %collective-permute-start.15 = (f32[128,512]{1,0:T(8,128)}, f32[128,512]{1,0:T(8,128)}, u32[]{:S(2)}, u32[]{:S(2)}) collective-permute-start(f32[128,512]{1,0:T(8,128)} %get-tuple-element.87), channel_id=1, source_target_pairs={{0,1},{1,2},{2,3},{3,0},{4,5},{5,6},{6,7},{7,4},{8,9},{9,10},{10,1... | collective-permute-start | bytes 786440 | tf_op jit(solution)/shard_map/ppermute | solution.py:46
  78.3 3.4 %collective-permute-start.19 = (f32[576,512]{1,0:T(8,128)S(1)}, f32[576,512]{1,0:T(8,128)S(1)}, u32[]{:S(2)}, u32[]{:S(2)}) collective-permute-start(f32[576,512]{1,0:T(8,128)S(1)} %get-tuple-element.105), channel_id=1, source_target_pairs={{0,32},{32,0},{64,96},{96,64},{128,160},{160,128},{192,224},{224,1... | collective-permute-start | bytes 3538952 | tf_op jit(solution)/shard_map/ppermute | solution.py:65
  80.1 8.0 %collective-permute-start.16 = (f32[128,512]{1,0:T(8,128)S(1)}, f32[128,512]{1,0:T(8,128)S(1)}, u32[]{:S(2)}, u32[]{:S(2)}) collective-permute-start(f32[128,512]{1,0:T(8,128)S(1)} %get-tuple-element.93), channel_id=1, source_target_pairs={{0,3},{1,0},{2,1},{3,2},{4,7},{5,4},{6,5},{7,6},{8,11},{9,8},{10,9... | collective-permute-start | bytes 786440 | tf_op jit(solution)/shard_map/ppermute | solution.py:46
  80.8 9.2 %collective-permute-start.17 = (f32[128,512]{1,0:T(8,128)S(1)}, f32[128,512]{1,0:T(8,128)S(1)}, u32[]{:S(2)}, u32[]{:S(2)}) collective-permute-start(f32[128,512]{1,0:T(8,128)S(1)} %get-tuple-element.94), channel_id=1, source_target_pairs={{0,2},{1,3},{2,0},{3,1},{4,6},{5,7},{6,4},{7,5},{8,10},{9,11},{10,... | collective-permute-start | bytes 786440 | tf_op jit(solution)/shard_map/ppermute | solution.py:46
  81.4 14.8 %collective-permute-start.18 = (f32[128,512]{1,0:T(8,128)S(1)}, f32[128,512]{1,0:T(8,128)S(1)}, u32[]{:S(2)}, u32[]{:S(2)}) collective-permute-start(f32[128,512]{1,0:T(8,128)S(1)} %get-tuple-element.95), channel_id=1, source_target_pairs={{0,1},{1,2},{2,3},{3,0},{4,5},{5,6},{6,7},{7,4},{8,9},{9,10},{10,1... | collective-permute-start | bytes 786440 | tf_op jit(solution)/shard_map/ppermute | solution.py:46
  81.9 17.3 %collective-permute-start.21 = (f32[288,512]{1,0:T(8,128)S(1)}, f32[288,512]{1,0:T(8,128)S(1)}, u32[]{:S(2)}, u32[]{:S(2)}) collective-permute-start(f32[288,512]{1,0:T(8,128)S(1)} %get-tuple-element.121), channel_id=1, source_target_pairs={{0,28},{1,29},{2,30},{3,31},{4,0},{5,1},{6,2},{7,3},{8,4},{9,5},{1... | collective-permute-start | bytes 1769480 | tf_op jit(solution)/shard_map/ppermute | solution.py:51
  83.7 15.5 %collective-permute-start.22 = (f32[288,512]{1,0:T(8,128)S(1)}, f32[288,512]{1,0:T(8,128)S(1)}, u32[]{:S(2)}, u32[]{:S(2)}) collective-permute-start(f32[288,512]{1,0:T(8,128)S(1)} %get-tuple-element.122), channel_id=1, source_target_pairs={{0,4},{1,5},{2,6},{3,7},{4,8},{5,9},{6,10},{7,11},{8,12},{9,13},{1... | collective-permute-start | bytes 1769480 | tf_op jit(solution)/shard_map/ppermute | solution.py:51
  97.0 2.2 %collective-permute-start.20 = (f32[216,512]{1,0:T(8,128)S(1)}, f32[216,512]{1,0:T(8,128)S(1)}, u32[]{:S(2)}, u32[]{:S(2)}) collective-permute-start(f32[216,512]{1,0:T(8,128)S(1)} %get-tuple-element.111), channel_id=1, source_target_pairs={{0,32},{32,0},{64,96},{96,64},{128,160},{160,128},{192,224},{224,1... | collective-permute-start | bytes 1327112 | tf_op jit(solution)/shard_map/ppermute | solution.py:65
  97.6 1.6 %collective-permute-start.25 = (f32[72,512]{1,0:T(8,128)S(1)}, f32[72,512]{1,0:T(8,128)S(1)}, u32[]{:S(2)}, u32[]{:S(2)}) collective-permute-start(f32[72,512]{1,0:T(8,128)S(1)} %get-tuple-element.112), channel_id=1, source_target_pairs={{0,32},{32,0},{64,96},{96,64},{128,160},{160,128},{192,224},{224,1... | collective-permute-start | bytes 442376 | tf_op jit(solution)/shard_map/ppermute | solution.py:65
  99.4 5.4 %collective-permute-start.23 = (f32[72,512]{1,0:T(8,128)S(1)}, f32[72,512]{1,0:T(8,128)S(1)}, u32[]{:S(2)}, u32[]{:S(2)}) collective-permute-start(f32[72,512]{1,0:T(8,128)S(1)} %get-tuple-element.118), channel_id=1, source_target_pairs={{0,64},{32,96},{64,128},{96,160},{128,192},{160,224},{192,0},{224,... | collective-permute-start | bytes 442376 | tf_op jit(solution)/shard_map/ppermute | solution.py:70
  100.8 7.9 %collective-permute-start.24 = (f32[72,512]{1,0:T(8,128)S(1)}, f32[72,512]{1,0:T(8,128)S(1)}, u32[]{:S(2)}, u32[]{:S(2)}) collective-permute-start(f32[72,512]{1,0:T(8,128)S(1)} %get-tuple-element.119), channel_id=1, source_target_pairs={{0,128},{32,160},{64,192},{96,224},{128,0},{160,32},{192,64},{224,... | collective-permute-start | bytes 442376 | tf_op jit(solution)/shard_map/ppermute | solution.py:70
  103.4 5.5 %collective-permute-start.26 = (f32[72,512]{1,0:T(8,128)S(1)}, f32[72,512]{1,0:T(8,128)S(1)}, u32[]{:S(2)}, u32[]{:S(2)}) collective-permute-start(f32[72,512]{1,0:T(8,128)S(1)} %get-tuple-element.120), channel_id=1, source_target_pairs={{0,192},{32,224},{64,0},{96,32},{128,64},{160,96},{192,128},{224,1... | collective-permute-start | bytes 442376 | tf_op jit(solution)/shard_map/ppermute | solution.py:70
  109.0 9.7 %collective-permute-start.29 = (f32[72,512]{1,0:T(8,128)S(1)}, f32[72,512]{1,0:T(8,128)S(1)}, u32[]{:S(2)}, u32[]{:S(2)}) collective-permute-start(f32[72,512]{1,0:T(8,128)S(1)} %fusion.18.piece), channel_id=1, source_target_pairs={{0,1},{1,2},{2,3},{3,4},{4,5},{5,6},{6,7},{7,8},{8,9},{9,10},{10,1... | collective-permute-start | bytes 442376 | tf_op jit(solution)/shard_map/ppermute | solution.py:51
  110.0 8.7 %collective-permute-start.30 = (f32[72,512]{1,0:T(8,128)S(1)}, f32[72,512]{1,0:T(8,128)S(1)}, u32[]{:S(2)}, u32[]{:S(2)}) collective-permute-start(f32[72,512]{1,0:T(8,128)S(1)} %fusion.18.piece), channel_id=1, source_target_pairs={{0,31},{1,0},{2,1},{3,2},{4,3},{5,4},{6,5},{7,6},{8,7},{9,8},{10,9... | collective-permute-start | bytes 442376 | tf_op jit(solution)/shard_map/ppermute | solution.py:51
  113.9 19.8 %collective-permute-start.27 = (f32[256,512]{1,0:T(8,128)S(1)}, f32[256,512]{1,0:T(8,128)S(1)}, u32[]{:S(2)}, u32[]{:S(2)}) collective-permute-start(f32[256,512]{1,0:T(8,128)S(1)} %get-tuple-element.113.plane_1), channel_id=1, source_target_pairs={{0,1},{1,2},{2,3},{3,4},{4,5},{5,6},{6,7},{7,8},{8,9},{9,10},{10,1... | collective-permute-start | bytes 1572872 | tf_op jit(solution)/shard_map/ppermute | solution.py:51
  113.9 19.8 %collective-permute-start.28 = (f32[256,512]{1,0:T(8,128)S(1)}, f32[256,512]{1,0:T(8,128)S(1)}, u32[]{:S(2)}, u32[]{:S(2)}) collective-permute-start(f32[256,512]{1,0:T(8,128)S(1)} %get-tuple-element.114.plane_0), channel_id=1, source_target_pairs={{0,31},{1,0},{2,1},{3,2},{4,3},{5,4},{6,5},{7,6},{8,7},{9,8},{10,9... | collective-permute-start | bytes 1572872 | tf_op jit(solution)/shard_map/ppermute | solution.py:51
  119.9 5.5 %collective-permute-start.31 = (f32[64,512]{1,0:T(8,128)S(1)}, f32[64,512]{1,0:T(8,128)S(1)}, u32[]{:S(2)}, u32[]{:S(2)}) collective-permute-start(f32[64,512]{1,0:T(8,128)S(1)} %shard_map.84.refs_0_), channel_id=1, source_target_pairs={{0,64},{32,96},{64,128},{96,160},{128,192},{160,224},{192,0},{224,... | collective-permute-start | bytes 393224 | tf_op jit(solution)/shard_map/ppermute | solution.py:70
  121.5 8.3 %collective-permute-start.32 = (f32[64,512]{1,0:T(8,128)S(1)}, f32[64,512]{1,0:T(8,128)S(1)}, u32[]{:S(2)}, u32[]{:S(2)}) collective-permute-start(f32[64,512]{1,0:T(8,128)S(1)} %shard_map.84.refs_0_), channel_id=1, source_target_pairs={{0,128},{32,160},{64,192},{96,224},{128,0},{160,32},{192,64},{224,... | collective-permute-start | bytes 393224 | tf_op jit(solution)/shard_map/ppermute | solution.py:70
  123.9 7.8 %collective-permute-start.33 = (f32[64,512]{1,0:T(8,128)S(1)}, f32[64,512]{1,0:T(8,128)S(1)}, u32[]{:S(2)}, u32[]{:S(2)}) collective-permute-start(f32[64,512]{1,0:T(8,128)S(1)} %shard_map.84.refs_0_), channel_id=1, source_target_pairs={{0,192},{32,224},{64,0},{96,32},{128,64},{160,96},{192,128},{224,1... | collective-permute-start | bytes 393224 | tf_op jit(solution)/shard_map/ppermute | solution.py:70
  125.4 7.0 %collective-permute-start.34 = (f32[64,512]{1,0:T(8,128)S(1)}, f32[64,512]{1,0:T(8,128)S(1)}, u32[]{:S(2)}, u32[]{:S(2)}) collective-permute-start(f32[64,512]{1,0:T(8,128)S(1)} %shard_map.84.refs_0_), channel_id=1, source_target_pairs={{0,32},{32,0},{64,96},{96,64},{128,160},{160,128},{192,224},{224,1... | collective-permute-start | bytes 393224 | tf_op jit(solution)/shard_map/ppermute | solution.py:65
  129.8 3.0 %collective-permute-start.35 = (f32[64,512]{1,0:T(8,128)S(1)}, f32[64,512]{1,0:T(8,128)S(1)}, u32[]{:S(2)}, u32[]{:S(2)}) collective-permute-start(f32[64,512]{1,0:T(8,128)S(1)} %collective-permute-done.31.refs_1_), channel_id=1, source_target_pairs={{0,32},{32,0},{64,96},{96,64},{128,160},{160,128},{192,224},{224,1... | collective-permute-start | bytes 393224 | tf_op jit(solution)/shard_map/ppermute | solution.py:65
  131.7 1.6 %collective-permute-start.36 = (f32[64,512]{1,0:T(8,128)S(1)}, f32[64,512]{1,0:T(8,128)S(1)}, u32[]{:S(2)}, u32[]{:S(2)}) collective-permute-start(f32[64,512]{1,0:T(8,128)S(1)} %collective-permute-done.32.refs_2_), channel_id=1, source_target_pairs={{0,32},{32,0},{64,96},{96,64},{128,160},{160,128},{192,224},{224,1... | collective-permute-start | bytes 393224 | tf_op jit(solution)/shard_map/ppermute | solution.py:65
  132.4 1.3 collective-permute-start.37
  (7 other events, 7.9 us)

commit v7 on v6

--- a/solution.py
+++ b/solution.py
@@ -523,7 +523,7 @@
         plane_force_kernel, force, [VMEM] * 3, ANY,
         [pltpu.VMEM((2, plane_count, row_count, cell_count), F32), pltpu.SemaphoreType.DMA],
     )(warped_0, warped_1, image_lines)
-    back_cross, pool_own, part_force = lax.optimization_barrier((back_cross, pool_own, part_force))
+    back_cross, pool_own = lax.optimization_barrier((back_cross, pool_own))
     back_own = ring_of(along_x, pool_own, -1)
 
     per_piece = row_count // (2 * RING)
@@ -556,7 +556,7 @@
     sum_high = keep_high + received[core_rows:]
     in_from_high = along_z(sum_low, -1)
     in_from_low = along_z(sum_high, 1)
-    back_own, sum_low, sum_high = lax.optimization_barrier((back_own, sum_low, sum_high))
+    back_own, sum_low, sum_high, part_force = lax.optimization_barrier((back_own, sum_low, sum_high, part_force))
     size = 2 * wide
     keep_own, *send_own = call(
         own_back_kernel, (core_part, f32s(core_rows - size, cell_count), f32s(size, cell_count)),

time: 136 us -> 136 us (level)
  transfers between devices with their start and end apart: 38 -> 38, of which waited for: 19 -> 20; matrix products, arithmetic and copies ran while one was open for 1% -> 1% of each run, Pallas kernels for 15% -> 15%
where the time goes in v7:
time: 136 us
  starting transfers between devices  56.2 us (41%)
  waiting for transfers between devices  36.2 us (27%)
  Pallas kernels  33.2 us (24%)
  local copies, waits for them, and re-layouts  8.04 us (6%)
    ppermute x15, waiting for transfers between devices, along_x(): return lax.ppermute(value, 'slab', route)  26.5 us
    ppermute x8, starting transfers between devices, along_slab(): lax.ppermute(value, 'slab', [(i, (i + step) % count) for i in range(count)])  18 us
    ppermute x15, starting transfers between devices, along_x(): return lax.ppermute(value, 'slab', route)  16.7 us
    ppermute x9, starting transfers between devices, other_core(): return lax.ppermute(value, 'subj', [(i, i ^ 1) for i in range(count)])  12.2 us
    ppermute x6, starting transfers between devices, along_y(): lax.ppermute(value, 'subj', [(i, (i + 2 * step) % count) for i in range(c...  9.38 us
    unnamed x36, local copies, waits for them, and re-layouts  7.94 us
    pallas_call x1, Pallas kernels, on_device(): call(warp_kernel, (half,) * 2 + (push_part,) * 2, [SMEM] + [VMEM] * 12, (...  5.81 us
    ppermute x6, waiting for transfers between devices, along_y(): lax.ppermute(value, 'subj', [(i, (i + 2 * step) % count) for i in range(c...  5.72 us
  transfers between devices with their start and end apart: 38, of which 20 were waited for; matrix products, arithmetic and copies ran while one was open for 1% of the time, Pallas kernels for 15%

profile of v7, /device:TPU:1, one launch (start us, length us, event | category | flops | bytes accessed | tf_op | source)
XLA Modules:
  0.0 135.9 jit_solution(662593755932650898)
XLA Ops:
  0.8 1.2 copy-done
  2.6 2.5 %collective-permute-start.3 = (f32[1024,128]{1,0:T(8,128)S(1)}, f32[1024,128]{1,0:T(8,128)S(1)}, u32[]{:S(2)}, u32[]{:S(2)}) collective-permute-start(f32[1024,128]{1,0:T(8,128)S(1)} %shard_map.70), channel_id=1, source_target_pairs={{0,4},{1,5},{2,6},{3,7},{4,8},{5,9},{6,10},{7,11},{8,12},{9,13},{1... | collective-permute-start | bytes 1572872 | tf_op jit(solution)/shard_map/ppermute | solution.py:51
  5.2 4.0 %collective-permute-start.4 = (f32[1024,128]{1,0:T(8,128)S(1)}, f32[1024,128]{1,0:T(8,128)S(1)}, u32[]{:S(2)}, u32[]{:S(2)}) collective-permute-start(f32[1024,128]{1,0:T(8,128)S(1)} %shard_map.70), channel_id=1, source_target_pairs={{0,28},{1,29},{2,30},{3,31},{4,0},{5,1},{6,2},{7,3},{8,4},{9,5},{1... | collective-permute-start | bytes 1572872 | tf_op jit(solution)/shard_map/ppermute | solution.py:51
  9.8 2.6 %collective-permute-start = (s32[2,128]{1,0:T(2,128)S(1)}, s32[2,128]{1,0:T(2,128)S(1)}, u32[]{:S(2)}, u32[]{:S(2)}) collective-permute-start(s32[2,128]{1,0:T(2,128)S(1)} %get-tuple-element.62), channel_id=1, source_target_pairs={{0,3},{1,0},{2,1},{3,2},{4,7},{5,4},{6,5},{7,6},{8,11},{9,8},{10,9... | collective-permute-start | bytes 3080 | tf_op jit(solution)/shard_map/ppermute | solution.py:46
  13.7 2.6 %collective-permute-done.1.lists.lists_2 = s32[2,128]{1,0:T(2,128)S(1)} collective-permute-done((s32[2,128]{1,0:T(2,128)S(1)}, s32[2,128]{1,0:T(2,128)S(1)}, u32[]{:S(2)}, u32[]{:S(2)}) %collective-permute-start.1) | collective-permute-done | bytes 1056 | tf_op jit(solution)/shard_map/ppermute | solution.py:46
  17.7 2.7 %collective-permute-start.6 = (f32[512,128]{1,0:T(8,128)S(1)}, f32[512,128]{1,0:T(8,128)S(1)}, u32[]{:S(2)}, u32[]{:S(2)}) collective-permute-start(f32[512,128]{1,0:T(8,128)S(1)} %get-tuple-element.69), channel_id=1, source_target_pairs={{0,3},{1,0},{2,1},{3,2},{4,7},{5,4},{6,5},{7,6},{8,11},{9,8},{10,9... | collective-permute-start | bytes 786440 | tf_op jit(solution)/shard_map/ppermute | solution.py:46
  21.7 2.4 %collective-permute-done.5.refs_9_ = f32[512,128]{1,0:T(8,128)S(1)} collective-permute-done((f32[512,128]{1,0:T(8,128)S(1)}, f32[512,128]{1,0:T(8,128)S(1)}, u32[]{:S(2)}, u32[]{:S(2)}) %collective-permute-start.5) | collective-permute-done | bytes 262176 | tf_op jit(solution)/shard_map/ppermute | solution.py:46
  24.8 3.6 %collective-permute-start.7 = (f32[1024,128]{1,0:T(8,128)S(1)}, f32[1024,128]{1,0:T(8,128)}, u32[]{:S(2)}, u32[]{:S(2)}) collective-permute-start(f32[1024,128]{1,0:T(8,128)S(1)} %collective-permute-done.3.low_a), channel_id=1, source_target_pairs={{0,32},{32,0},{64,96},{96,64},{128,160},{160,128},{192,224},{224,1... | collective-permute-start | bytes 1572872 | tf_op jit(solution)/shard_map/ppermute | solution.py:65
  28.6 1.3 collective-permute-start.12
  30.9 2.2 %shard_map.74 = (f32[512,128]{1,0:T(8,128)S(1)}, f32[512,128]{1,0:T(8,128)S(1)}, f32[512,128]{1,0:T(8,128)S(1)}) custom-call(s32[2,128]{1,0:T(2,128)S(1)} %collective-permute-done.lists_1, s32[2,128]{1,0:T(2,128)S(1)} %collective-permute-done.1.lists.lists_2, s32[2,128]{1,0:T(2,128)S(1)} %collective-permute-done.2.lists_3, ...), custom_call_target="tpu_custom_call" | custom-call | tf_op jit(solution)/shard_map/pallas_call | solution.py:474
  33.1 1.3 collective-permute-start.10
  34.4 2.6 %collective-permute-start.11 = (f32[512,128]{1,0:T(8,128)S(1)}, f32[512,128]{1,0:T(8,128)S(1)}, u32[]{:S(2)}, u32[]{:S(2)}) collective-permute-start(f32[512,128]{1,0:T(8,128)S(1)} %get-tuple-element.74), channel_id=1, source_target_pairs={{0,3},{1,0},{2,1},{3,2},{4,7},{5,4},{6,5},{7,6},{8,11},{9,8},{10,9... | collective-permute-start | bytes 786440 | tf_op jit(solution)/shard_map/ppermute | solution.py:46
  37.1 3.0 %shard_map.68 = (f32[4,512,512]{2,1,0:T(8,128)S(1)}, f32[4,512,512]{2,1,0:T(8,128)S(1)}) custom-call(bf16[3,512,512]{2,1,0:T(8,128)(2,1)S(1)} %bitcast.21), custom_call_target="tpu_custom_call" | custom-call | tf_op jit(solution)/shard_map/pallas_call | solution.py:495
  40.2 1.0 copy-done.8
  41.2 1.0 copy-done.10
  42.3 2.2 %shard_map.75 = (f32[512,128]{1,0:T(8,128)S(1)}, f32[512,128]{1,0:T(8,128)S(1)}, f32[512,128]{1,0:T(8,128)S(1)}) custom-call(s32[3,128]{1,0:T(4,128)S(1)} %get-tuple-element.75.lists.lists_0, f32[2048,128]{1,0:T(8,128)S(1)} %shard_map.71.held.own, f32[1024,128]{1,0:T(8,128)S(1)} %copy-done.8, f32[1024,128]{1,0:T(8,128)} %collective-permute-done.7.low_b, ...), custom_call_target="tpu_custom_call" | custom-call | tf_op jit(solution)/shard_map/pallas_call | solution.py:478
  44.5 5.2 %collective-permute-done.11.refs_6_ = f32[512,128]{1,0:T(8,128)S(1)} collective-permute-done((f32[512,128]{1,0:T(8,128)S(1)}, f32[512,128]{1,0:T(8,128)S(1)}, u32[]{:S(2)}, u32[]{:S(2)}) %collective-permute-start.11) | collective-permute-done | bytes 262176 | tf_op jit(solution)/shard_map/ppermute | solution.py:46
  49.8 5.8 %shard_map.76 = (f32[256,512]{1,0:T(8,128)S(1)}, f32[256,512]{1,0:T(8,128)S(1)}, bf16[2048,512]{1,0:T(8,128)(2,1)S(1)}, bf16[2048,512]{1,0:T(8,128)(2,1)S(1)}) custom-call(s32[4,512]{1,0:T(4,128)S(1)} %fusion.24.refs_0_, f32[4,512,512]{2,1,0:T(8,128)S(1)} %get-tuple-element.60.refs_1_, f32[4,512,512]{2,1,0:T(8,128)S(1)} %get-tuple-element.61.refs_2_, ...), custom_call_target="tpu_custom_call" | custom-call | tf_op jit(solution)/shard_map/pallas_call | solution.py:500
  55.7 2.6 %shard_map.78 = (f32[128,512]{1,0:T(8,128)}, f32[128,512]{1,0:T(8,128)}, f32[128,512]{1,0:T(8,128)}) custom-call(s32[1,2048]{1,0:T(1,128)S(1)} %fusion.20.ids_ref, bf16[2048,512]{1,0:T(8,128)(2,1)S(1)} %get-tuple-element.83.push_high, bf16[2048,512]{1,0:T(8,128)(2,1)S(1)} %get-tuple-element.84.push_low), custom_call_target="tpu_custom_call" | custom-call | tf_op jit(solution)/shard_map/pallas_call | solution.py:513
  58.3 3.0 %collective-permute-start.13 = (f32[128,512]{1,0:T(8,128)}, f32[128,512]{1,0:T(8,128)S(1)}, u32[]{:S(2)}, u32[]{:S(2)}) collective-permute-start(f32[128,512]{1,0:T(8,128)} %get-tuple-element.85), channel_id=1, source_target_pairs={{0,3},{1,0},{2,1},{3,2},{4,7},{5,4},{6,5},{7,6},{8,11},{9,8},{10,9... | collective-permute-start | bytes 786440 | tf_op jit(solution)/shard_map/ppermute | solution.py:46
  62.4 1.1 shard_map.77
  63.6 1.6 %copy-done.4 = bf16[2048,512]{1,0:T(8,128)(2,1)S(1)} copy-done((bf16[2048,512]{1,0:T(8,128)(2,1)S(1)}, bf16[2048,512]{1,0:T(8,128)(2,1)}, u32[]{:S(2)}) %copy-start.4) | copy-done | bytes 2097176
  65.2 1.6 %copy-done.6 = bf16[2048,512]{1,0:T(8,128)(2,1)S(1)} copy-done((bf16[2048,512]{1,0:T(8,128)(2,1)S(1)}, bf16[2048,512]{1,0:T(8,128)(2,1)}, u32[]{:S(2)}) %copy-start.6) | copy-done | bytes 2097176
  66.8 3.4 %shard_map.79 = (f32[128,512]{1,0:T(8,128)S(1)}, f32[128,512]{1,0:T(8,128)S(1)}, f32[128,512]{1,0:T(8,128)S(1)}, f32[128,512]{1,0:T(8,128)S(1)}, f32[128,512]{1,0:T(8,128)S(1)}, /*index=5*/f32[128,512]{1,0:T(8,128)S(1)}) custom-call(s32[1,2048]{1,0:T(1,128)S(1)} %fusion.20.ids_ref, bf16[2048,512]{1,0:T(8,128)(2,1)S(1)} %copy-done.4, ...), custom_call_target="tpu_custom_call" | custom-call | tf_op jit(solution)/shard_map/pallas_call | solution.py:516
  70.2 2.1 %collective-permute-done.13.in_1 = f32[128,512]{1,0:T(8,128)S(1)} collective-permute-done((f32[128,512]{1,0:T(8,128)}, f32[128,512]{1,0:T(8,128)S(1)}, u32[]{:S(2)}, u32[]{:S(2)}) %collective-permute-start.13) | collective-permute-done | bytes 262176 | tf_op jit(solution)/shard_map/ppermute | solution.py:46
  72.3 4.1 %collective-permute-done.15.in_3 = f32[128,512]{1,0:T(8,128)} collective-permute-done((f32[128,512]{1,0:T(8,128)}, f32[128,512]{1,0:T(8,128)}, u32[]{:S(2)}, u32[]{:S(2)}) %collective-permute-start.15) | collective-permute-done | bytes 262176 | tf_op jit(solution)/shard_map/ppermute | solution.py:46
  76.3 2.0 %shard_map.80 = (f32[576,512]{1,0:T(8,128)S(1)}, bf16[1280,512]{1,0:T(8,128)(2,1)S(1)}) custom-call(bf16[576,1280]{1,0:T(8,128)(2,1)S(1)} %get-tuple-element.96.hot_low, bf16[576,1280]{1,0:T(8,128)(2,1)S(1)} %get-tuple-element.97.hot_high, f32[128,512]{1,0:T(8,128)S(1)} %get-tuple-element.98.in_low, f32[128,512]{1,0:T(8,128)S(1)} %get-tuple-element.99.in_high, ...), custom_call_target="tpu_custom_call" | custom-call | tf_op jit(solution)/shard_map/pallas_call | solution.py:546
  79.2 0.9 shard_map.81
  81.9 1.7 %collective-permute-start.21 = (f32[288,512]{1,0:T(8,128)S(1)}, f32[288,512]{1,0:T(8,128)S(1)}, u32[]{:S(2)}, u32[]{:S(2)}) collective-permute-start(f32[288,512]{1,0:T(8,128)S(1)} %get-tuple-element.121), channel_id=1, source_target_pairs={{0,28},{1,29},{2,30},{3,31},{4,0},{5,1},{6,2},{7,3},{8,4},{9,5},{1... | collective-permute-start | bytes 1769480 | tf_op jit(solution)/shard_map/ppermute | solution.py:51
  83.7 3.0 %shard_map.82.refs_8_ = f32[3,2,256,512]{3,2,1,0:T(8,128)} custom-call(f32[256,512]{1,0:T(8,128)S(1)} %get-tuple-element.114.plane_0, f32[256,512]{1,0:T(8,128)S(1)} %get-tuple-element.113.plane_1, f32[512,512]{1,0:T(8,128)S(1)} %bitcast.19), custom_call_target="tpu_custom_call" | custom-call | tf_op jit(solution)/shard_map/pallas_call | solution.py:522
  86.7 1.4 %collective-permute-done.16.in_1 = f32[128,512]{1,0:T(8,128)S(1)} collective-permute-done((f32[128,512]{1,0:T(8,128)S(1)}, f32[128,512]{1,0:T(8,128)S(1)}, u32[]{:S(2)}, u32[]{:S(2)}) %collective-permute-start.16) | collective-permute-done | bytes 262176 | tf_op jit(solution)/shard_map/ppermute | solution.py:46
  88.2 1.8 %collective-permute-done.17.in_2 = f32[128,512]{1,0:T(8,128)S(1)} collective-permute-done((f32[128,512]{1,0:T(8,128)S(1)}, f32[128,512]{1,0:T(8,128)S(1)}, u32[]{:S(2)}, u32[]{:S(2)}) %collective-permute-start.17) | collective-permute-done | bytes 262176 | tf_op jit(solution)/shard_map/ppermute | solution.py:46
  90.0 6.2 %collective-permute-done.18.in_3 = f32[128,512]{1,0:T(8,128)S(1)} collective-permute-done((f32[128,512]{1,0:T(8,128)S(1)}, f32[128,512]{1,0:T(8,128)S(1)}, u32[]{:S(2)}, u32[]{:S(2)}) %collective-permute-start.18) | collective-permute-done | bytes 262176 | tf_op jit(solution)/shard_map/ppermute | solution.py:46
  97.7 1.5 %collective-permute-done.25 = f32[72,512]{1,0:T(8,128)S(1)} collective-permute-done((f32[72,512]{1,0:T(8,128)S(1)}, f32[72,512]{1,0:T(8,128)S(1)}, u32[]{:S(2)}, u32[]{:S(2)}) %collective-permute-start.25) | collective-permute-done | bytes 147488 | tf_op jit(solution)/shard_map/ppermute | solution.py:65
  99.4 1.4 %collective-permute-start.23 = (f32[72,512]{1,0:T(8,128)S(1)}, f32[72,512]{1,0:T(8,128)S(1)}, u32[]{:S(2)}, u32[]{:S(2)}) collective-permute-start(f32[72,512]{1,0:T(8,128)S(1)} %get-tuple-element.118), channel_id=1, source_target_pairs={{0,64},{32,96},{64,128},{96,160},{128,192},{160,224},{192,0},{224,... | collective-permute-start | bytes 442376 | tf_op jit(solution)/shard_map/ppermute | solution.py:70
  100.8 2.6 %collective-permute-start.24 = (f32[72,512]{1,0:T(8,128)S(1)}, f32[72,512]{1,0:T(8,128)S(1)}, u32[]{:S(2)}, u32[]{:S(2)}) collective-permute-start(f32[72,512]{1,0:T(8,128)S(1)} %get-tuple-element.119), channel_id=1, source_target_pairs={{0,128},{32,160},{64,192},{96,224},{128,0},{160,32},{192,64},{224,... | collective-permute-start | bytes 442376 | tf_op jit(solution)/shard_map/ppermute | solution.py:70
  103.4 1.1 collective-permute-start.26
  104.7 4.0 %collective-permute-done.24 = f32[72,512]{1,0:T(8,128)S(1)} collective-permute-done((f32[72,512]{1,0:T(8,128)S(1)}, f32[72,512]{1,0:T(8,128)S(1)}, u32[]{:S(2)}, u32[]{:S(2)}) %collective-permute-start.24) | collective-permute-done | bytes 147488 | tf_op jit(solution)/shard_map/ppermute | solution.py:70
  109.0 1.0 collective-permute-start.29
  110.0 3.9 %collective-permute-start.30 = (f32[72,512]{1,0:T(8,128)S(1)}, f32[72,512]{1,0:T(8,128)S(1)}, u32[]{:S(2)}, u32[]{:S(2)}) collective-permute-start(f32[72,512]{1,0:T(8,128)S(1)} %fusion.18.piece), channel_id=1, source_target_pairs={{0,31},{1,0},{2,1},{3,2},{4,3},{5,4},{6,5},{7,6},{8,7},{9,8},{10,9... | collective-permute-start | bytes 442376 | tf_op jit(solution)/shard_map/ppermute | solution.py:51
  113.9 4.8 %collective-permute-start.28 = (f32[256,512]{1,0:T(8,128)S(1)}, f32[256,512]{1,0:T(8,128)S(1)}, u32[]{:S(2)}, u32[]{:S(2)}) collective-permute-start(f32[256,512]{1,0:T(8,128)S(1)} %get-tuple-element.114.plane_0), channel_id=1, source_target_pairs={{0,31},{1,0},{2,1},{3,2},{4,3},{5,4},{6,5},{7,6},{8,7},{9,8},{10,9... | collective-permute-start | bytes 1572872 | tf_op jit(solution)/shard_map/ppermute | solution.py:51
  118.7 1.2 shard_map.84.refs_0_
  119.9 1.6 %collective-permute-start.31 = (f32[64,512]{1,0:T(8,128)S(1)}, f32[64,512]{1,0:T(8,128)S(1)}, u32[]{:S(2)}, u32[]{:S(2)}) collective-permute-start(f32[64,512]{1,0:T(8,128)S(1)} %shard_map.84.refs_0_), channel_id=1, source_target_pairs={{0,64},{32,96},{64,128},{96,160},{128,192},{160,224},{192,0},{224,... | collective-permute-start | bytes 393224 | tf_op jit(solution)/shard_map/ppermute | solution.py:70
  121.5 2.5 %collective-permute-start.32 = (f32[64,512]{1,0:T(8,128)S(1)}, f32[64,512]{1,0:T(8,128)S(1)}, u32[]{:S(2)}, u32[]{:S(2)}) collective-permute-start(f32[64,512]{1,0:T(8,128)S(1)} %shard_map.84.refs_0_), channel_id=1, source_target_pairs={{0,128},{32,160},{64,192},{96,224},{128,0},{160,32},{192,64},{224,... | collective-permute-start | bytes 393224 | tf_op jit(solution)/shard_map/ppermute | solution.py:70
  124.2 1.3 collective-permute-done.31.refs_1_
  125.4 4.4 %collective-permute-start.34 = (f32[64,512]{1,0:T(8,128)S(1)}, f32[64,512]{1,0:T(8,128)S(1)}, u32[]{:S(2)}, u32[]{:S(2)}) collective-permute-start(f32[64,512]{1,0:T(8,128)S(1)} %shard_map.84.refs_0_), channel_id=1, source_target_pairs={{0,32},{32,0},{64,96},{96,64},{128,160},{160,128},{192,224},{224,1... | collective-permute-start | bytes 393224 | tf_op jit(solution)/shard_map/ppermute | solution.py:65
  129.8 1.9 %collective-permute-start.35 = (f32[64,512]{1,0:T(8,128)S(1)}, f32[64,512]{1,0:T(8,128)S(1)}, u32[]{:S(2)}, u32[]{:S(2)}) collective-permute-start(f32[64,512]{1,0:T(8,128)S(1)} %collective-permute-done.31.refs_1_), channel_id=1, source_target_pairs={{0,32},{32,0},{64,96},{96,64},{128,160},{160,128},{192,224},{224,1... | collective-permute-start | bytes 393224 | tf_op jit(solution)/shard_map/ppermute | solution.py:65
  133.7 2.0 %shard_map.85 = (f32[512,512]{1,0:T(8,128)}, f32[3,2,256,512]{3,2,1,0:T(8,128)}) custom-call(s32[8]{0:T(128)S(1)} %stack.19.place_ref, f32[256,512]{1,0:T(8,128)S(1)} %collective-permute-done.27.before, f32[256,512]{1,0:T(8,128)S(1)} %get-tuple-element.114.plane_0, f32[256,512]{1,0:T(8,128)S(1)} %get-tuple-element.113.plane_1, ...), custom_call_target="tpu_custom_call", output_to_operand_aliasing={{1}: (14, {})} | custom-call | tf_op jit(solution)/shard_map/pallas_call | solution.py:585
  (90 shorter events, 15.8 us)
Async XLA Ops:
  0.6 8.6 %copy-start.16 = (s32[1,1,9,128]{3,1,2,0:T(1,128)S(1)}, s32[1,1,9,128]{3,1,2,0:T(1,128)}, u32[]{:S(2)}) copy-start(s32[1,1,9,128]{3,1,2,0:T(1,128)} %param.8) | copy-start | bytes 13828
  2.0 11.5 %copy-start.1 = (f32[2,256,512]{2,1,0:T(8,128)S(1)}, f32[2,256,512]{2,1,0:T(8,128)}, u32[]{:S(2)}) copy-start(f32[2,256,512]{2,1,0:T(8,128)} %param.5) | copy-start | bytes 3145732
  2.6 22.2 %collective-permute-start.3 = (f32[1024,128]{1,0:T(8,128)S(1)}, f32[1024,128]{1,0:T(8,128)S(1)}, u32[]{:S(2)}, u32[]{:S(2)}) collective-permute-start(f32[1024,128]{1,0:T(8,128)S(1)} %shard_map.70), channel_id=1, source_target_pairs={{0,4},{1,5},{2,6},{3,7},{4,8},{5,9},{6,10},{7,11},{8,12},{9,13},{1... | collective-permute-start | bytes 1572872 | tf_op jit(solution)/shard_map/ppermute | solution.py:51
  5.2 19.6 %collective-permute-start.4 = (f32[1024,128]{1,0:T(8,128)S(1)}, f32[1024,128]{1,0:T(8,128)S(1)}, u32[]{:S(2)}, u32[]{:S(2)}) collective-permute-start(f32[1024,128]{1,0:T(8,128)S(1)} %shard_map.70), channel_id=1, source_target_pairs={{0,28},{1,29},{2,30},{3,31},{4,0},{5,1},{6,2},{7,3},{8,4},{9,5},{1... | collective-permute-start | bytes 1572872 | tf_op jit(solution)/shard_map/ppermute | solution.py:51
  9.8 3.9 %collective-permute-start = (s32[2,128]{1,0:T(2,128)S(1)}, s32[2,128]{1,0:T(2,128)S(1)}, u32[]{:S(2)}, u32[]{:S(2)}) collective-permute-start(s32[2,128]{1,0:T(2,128)S(1)} %get-tuple-element.62), channel_id=1, source_target_pairs={{0,3},{1,0},{2,1},{3,2},{4,7},{5,4},{6,5},{7,6},{8,11},{9,8},{10,9... | collective-permute-start | bytes 3080 | tf_op jit(solution)/shard_map/ppermute | solution.py:46
  12.3 3.9 %collective-permute-start.1 = (s32[2,128]{1,0:T(2,128)S(1)}, s32[2,128]{1,0:T(2,128)S(1)}, u32[]{:S(2)}, u32[]{:S(2)}) collective-permute-start(s32[2,128]{1,0:T(2,128)S(1)} %get-tuple-element.63), channel_id=1, source_target_pairs={{0,2},{1,3},{2,0},{3,1},{4,6},{5,7},{6,4},{7,5},{8,10},{9,11},{10,... | collective-permute-start | bytes 3080 | tf_op jit(solution)/shard_map/ppermute | solution.py:46
  12.9 3.9 %collective-permute-start.2 = (s32[2,128]{1,0:T(2,128)S(1)}, s32[2,128]{1,0:T(2,128)S(1)}, u32[]{:S(2)}, u32[]{:S(2)}) collective-permute-start(s32[2,128]{1,0:T(2,128)S(1)} %get-tuple-element.64), channel_id=1, source_target_pairs={{0,1},{1,2},{2,3},{3,0},{4,5},{5,6},{6,7},{7,4},{8,9},{9,10},{10,1... | collective-permute-start | bytes 3080 | tf_op jit(solution)/shard_map/ppermute | solution.py:46
  13.7 14.9 %copy-start.15 = (s32[1,4,2,256]{3,2,1,0:T(2,128)S(1)}, s32[1,4,2,256]{3,2,1,0:T(2,128)}, u32[]{:S(2)}) copy-start(s32[1,4,2,256]{3,2,1,0:T(2,128)} %param.9) | copy-start | bytes 24580
  17.6 6.5 %collective-permute-start.5 = (f32[512,128]{1,0:T(8,128)S(1)}, f32[512,128]{1,0:T(8,128)S(1)}, u32[]{:S(2)}, u32[]{:S(2)}) collective-permute-start(f32[512,128]{1,0:T(8,128)S(1)} %get-tuple-element.68), channel_id=1, source_target_pairs={{0,1},{1,2},{2,3},{3,0},{4,5},{5,6},{6,7},{7,4},{8,9},{9,10},{10,1... | collective-permute-start | bytes 786440 | tf_op jit(solution)/shard_map/ppermute | solution.py:46
  17.7 6.4 %collective-permute-start.6 = (f32[512,128]{1,0:T(8,128)S(1)}, f32[512,128]{1,0:T(8,128)S(1)}, u32[]{:S(2)}, u32[]{:S(2)}) collective-permute-start(f32[512,128]{1,0:T(8,128)S(1)} %get-tuple-element.69), channel_id=1, source_target_pairs={{0,3},{1,0},{2,1},{3,2},{4,7},{5,4},{6,5},{7,6},{8,11},{9,8},{10,9... | collective-permute-start | bytes 786440 | tf_op jit(solution)/shard_map/ppermute | solution.py:46
  24.8 15.3 %copy-start.7 = (f32[1024,128]{1,0:T(8,128)}, f32[1024,128]{1,0:T(8,128)S(1)}, u32[]{:S(2)}) copy-start(f32[1024,128]{1,0:T(8,128)S(1)} %collective-permute-done.3.low_a) | copy-start | bytes 1572868
  24.8 15.3 %copy-start.9 = (f32[1024,128]{1,0:T(8,128)}, f32[1024,128]{1,0:T(8,128)S(1)}, u32[]{:S(2)}) copy-start(f32[1024,128]{1,0:T(8,128)S(1)} %collective-permute-done.4.high_a) | copy-start | bytes 1572868
  24.8 5.3 %collective-permute-start.7 = (f32[1024,128]{1,0:T(8,128)S(1)}, f32[1024,128]{1,0:T(8,128)}, u32[]{:S(2)}, u32[]{:S(2)}) collective-permute-start(f32[1024,128]{1,0:T(8,128)S(1)} %collective-permute-done.3.low_a), channel_id=1, source_target_pairs={{0,32},{32,0},{64,96},{96,64},{128,160},{160,128},{192,224},{224,1... | collective-permute-start | bytes 1572872 | tf_op jit(solution)/shard_map/ppermute | solution.py:65
  28.4 2.4 %collective-permute-start.8 = (f32[1024,128]{1,0:T(8,128)S(1)}, f32[1024,128]{1,0:T(8,128)}, u32[]{:S(2)}, u32[]{:S(2)}) collective-permute-start(f32[1024,128]{1,0:T(8,128)S(1)} %collective-permute-done.4.high_a), channel_id=1, source_target_pairs={{0,32},{32,0},{64,96},{96,64},{128,160},{160,128},{192,224},{224,1... | collective-permute-start | bytes 1572872 | tf_op jit(solution)/shard_map/ppermute | solution.py:65
  28.6 8.5 %copy-start.11 = (bf16[1,3,2,256,512]{4,3,2,1,0:T(8,128)(2,1)S(1)}, bf16[1,3,2,256,512]{4,3,2,1,0:T(8,128)(2,1)}, u32[]{:S(2)}) copy-start(bf16[1,3,2,256,512]{4,3,2,1,0:T(8,128)(2,1)} %param.7) | copy-start | bytes 4718596
  28.6 15.9 %collective-permute-start.12 = (f32[512,128]{1,0:T(8,128)}, f32[512,128]{1,0:T(8,128)S(1)}, u32[]{:S(2)}, u32[]{:S(2)}) collective-permute-start(f32[512,128]{1,0:T(8,128)} %copy-done.14), channel_id=1, source_target_pairs={{0,2},{1,3},{2,0},{3,1},{4,6},{5,7},{6,4},{7,5},{8,10},{9,11},{10,... | collective-permute-start | bytes 786440 | tf_op jit(solution)/shard_map/ppermute | solution.py:46
  33.1 11.4 %collective-permute-start.10 = (f32[512,128]{1,0:T(8,128)S(1)}, f32[512,128]{1,0:T(8,128)S(1)}, u32[]{:S(2)}, u32[]{:S(2)}) collective-permute-start(f32[512,128]{1,0:T(8,128)S(1)} %get-tuple-element.73), channel_id=1, source_target_pairs={{0,2},{1,3},{2,0},{3,1},{4,6},{5,7},{6,4},{7,5},{8,10},{9,11},{10,... | collective-permute-start | bytes 786440 | tf_op jit(solution)/shard_map/ppermute | solution.py:46
  34.4 15.3 %collective-permute-start.11 = (f32[512,128]{1,0:T(8,128)S(1)}, f32[512,128]{1,0:T(8,128)S(1)}, u32[]{:S(2)}, u32[]{:S(2)}) collective-permute-start(f32[512,128]{1,0:T(8,128)S(1)} %get-tuple-element.74), channel_id=1, source_target_pairs={{0,3},{1,0},{2,1},{3,2},{4,7},{5,4},{6,5},{7,6},{8,11},{9,8},{10,9... | collective-permute-start | bytes 786440 | tf_op jit(solution)/shard_map/ppermute | solution.py:46
  36.9 12.9 %collective-permute-start.9 = (f32[512,128]{1,0:T(8,128)S(1)}, f32[512,128]{1,0:T(8,128)S(1)}, u32[]{:S(2)}, u32[]{:S(2)}) collective-permute-start(f32[512,128]{1,0:T(8,128)S(1)} %get-tuple-element.72), channel_id=1, source_target_pairs={{0,1},{1,2},{2,3},{3,0},{4,5},{5,6},{6,7},{7,4},{8,9},{9,10},{10,1... | collective-permute-start | bytes 786440 | tf_op jit(solution)/shard_map/ppermute | solution.py:46
  42.3 7.6 %copy-start.2 = (f32[1,2,256,512]{3,2,1,0:T(8,128)S(1)}, f32[1,2,256,512]{3,2,1,0:T(8,128)}, u32[]{:S(2)}) copy-start(f32[1,2,256,512]{3,2,1,0:T(8,128)} %param.6) | copy-start | bytes 3145732
  42.3 7.6 %copy-start.13 = (f32[512,128]{1,0:T(8,128)S(1)}, f32[512,128]{1,0:T(8,128)}, u32[]{:S(2)}) copy-start(f32[512,128]{1,0:T(8,128)} %copy-done.12) | copy-start | bytes 786436
  55.7 2.7 %copy-start.3 = (bf16[2048,512]{1,0:T(8,128)(2,1)}, bf16[2048,512]{1,0:T(8,128)(2,1)S(1)}, u32[]{:S(2)}) copy-start(bf16[2048,512]{1,0:T(8,128)(2,1)S(1)} %get-tuple-element.83.push_high) | copy-start | bytes 6291460
  55.7 2.7 %copy-start.5 = (bf16[2048,512]{1,0:T(8,128)(2,1)}, bf16[2048,512]{1,0:T(8,128)(2,1)S(1)}, u32[]{:S(2)}) copy-start(bf16[2048,512]{1,0:T(8,128)(2,1)S(1)} %get-tuple-element.84.push_low) | copy-start | bytes 6291460
  58.3 13.9 %collective-permute-start.13 = (f32[128,512]{1,0:T(8,128)}, f32[128,512]{1,0:T(8,128)S(1)}, u32[]{:S(2)}, u32[]{:S(2)}) collective-permute-start(f32[128,512]{1,0:T(8,128)} %get-tuple-element.85), channel_id=1, source_target_pairs={{0,3},{1,0},{2,1},{3,2},{4,7},{5,4},{6,5},{7,6},{8,11},{9,8},{10,9... | collective-permute-start | bytes 786440 | tf_op jit(solution)/shard_map/ppermute | solution.py:46
  61.3 11.0 %collective-permute-start.14 = (f32[128,512]{1,0:T(8,128)}, f32[128,512]{1,0:T(8,128)}, u32[]{:S(2)}, u32[]{:S(2)}) collective-permute-start(f32[128,512]{1,0:T(8,128)} %get-tuple-element.86), channel_id=1, source_target_pairs={{0,2},{1,3},{2,0},{3,1},{4,6},{5,7},{6,4},{7,5},{8,10},{9,11},{10,... | collective-permute-start | bytes 786440 | tf_op jit(solution)/shard_map/ppermute | solution.py:46
  61.3 15.0 %collective-permute-start.15 = (f32[128,512]{1,0:T(8,128)}, f32[128,512]{1,0:T(8,128)}, u32[]{:S(2)}, u32[]{:S(2)}) collective-permute-start(f32[128,512]{1,0:T(8,128)} %get-tuple-element.87), channel_id=1, source_target_pairs={{0,1},{1,2},{2,3},{3,0},{4,5},{5,6},{6,7},{7,4},{8,9},{9,10},{10,1... | collective-permute-start | bytes 786440 | tf_op jit(solution)/shard_map/ppermute | solution.py:46
  78.3 3.4 %collective-permute-start.19 = (f32[576,512]{1,0:T(8,128)S(1)}, f32[576,512]{1,0:T(8,128)S(1)}, u32[]{:S(2)}, u32[]{:S(2)}) collective-permute-start(f32[576,512]{1,0:T(8,128)S(1)} %get-tuple-element.105), channel_id=1, source_target_pairs={{0,32},{32,0},{64,96},{96,64},{128,160},{160,128},{192,224},{224,1... | collective-permute-start | bytes 3538952 | tf_op jit(solution)/shard_map/ppermute | solution.py:65
  80.1 8.0 %collective-permute-start.16 = (f32[128,512]{1,0:T(8,128)S(1)}, f32[128,512]{1,0:T(8,128)S(1)}, u32[]{:S(2)}, u32[]{:S(2)}) collective-permute-start(f32[128,512]{1,0:T(8,128)S(1)} %get-tuple-element.93), channel_id=1, source_target_pairs={{0,3},{1,0},{2,1},{3,2},{4,7},{5,4},{6,5},{7,6},{8,11},{9,8},{10,9... | collective-permute-start | bytes 786440 | tf_op jit(solution)/shard_map/ppermute | solution.py:46
  80.8 9.2 %collective-permute-start.17 = (f32[128,512]{1,0:T(8,128)S(1)}, f32[128,512]{1,0:T(8,128)S(1)}, u32[]{:S(2)}, u32[]{:S(2)}) collective-permute-start(f32[128,512]{1,0:T(8,128)S(1)} %get-tuple-element.94), channel_id=1, source_target_pairs={{0,2},{1,3},{2,0},{3,1},{4,6},{5,7},{6,4},{7,5},{8,10},{9,11},{10,... | collective-permute-start | bytes 786440 | tf_op jit(solution)/shard_map/ppermute | solution.py:46
  80.8 15.4 %collective-permute-start.18 = (f32[128,512]{1,0:T(8,128)S(1)}, f32[128,512]{1,0:T(8,128)S(1)}, u32[]{:S(2)}, u32[]{:S(2)}) collective-permute-start(f32[128,512]{1,0:T(8,128)S(1)} %get-tuple-element.95), channel_id=1, source_target_pairs={{0,1},{1,2},{2,3},{3,0},{4,5},{5,6},{6,7},{7,4},{8,9},{9,10},{10,1... | collective-permute-start | bytes 786440 | tf_op jit(solution)/shard_map/ppermute | solution.py:46
  81.9 17.3 %collective-permute-start.21 = (f32[288,512]{1,0:T(8,128)S(1)}, f32[288,512]{1,0:T(8,128)S(1)}, u32[]{:S(2)}, u32[]{:S(2)}) collective-permute-start(f32[288,512]{1,0:T(8,128)S(1)} %get-tuple-element.121), channel_id=1, source_target_pairs={{0,28},{1,29},{2,30},{3,31},{4,0},{5,1},{6,2},{7,3},{8,4},{9,5},{1... | collective-permute-start | bytes 1769480 | tf_op jit(solution)/shard_map/ppermute | solution.py:51
  83.7 15.5 %collective-permute-start.22 = (f32[288,512]{1,0:T(8,128)S(1)}, f32[288,512]{1,0:T(8,128)S(1)}, u32[]{:S(2)}, u32[]{:S(2)}) collective-permute-start(f32[288,512]{1,0:T(8,128)S(1)} %get-tuple-element.122), channel_id=1, source_target_pairs={{0,4},{1,5},{2,6},{3,7},{4,8},{5,9},{6,10},{7,11},{8,12},{9,13},{1... | collective-permute-start | bytes 1769480 | tf_op jit(solution)/shard_map/ppermute | solution.py:51
  97.0 2.2 %collective-permute-start.20 = (f32[216,512]{1,0:T(8,128)S(1)}, f32[216,512]{1,0:T(8,128)S(1)}, u32[]{:S(2)}, u32[]{:S(2)}) collective-permute-start(f32[216,512]{1,0:T(8,128)S(1)} %get-tuple-element.111), channel_id=1, source_target_pairs={{0,32},{32,0},{64,96},{96,64},{128,160},{160,128},{192,224},{224,1... | collective-permute-start | bytes 1327112 | tf_op jit(solution)/shard_map/ppermute | solution.py:65
  97.6 1.6 %collective-permute-start.25 = (f32[72,512]{1,0:T(8,128)S(1)}, f32[72,512]{1,0:T(8,128)S(1)}, u32[]{:S(2)}, u32[]{:S(2)}) collective-permute-start(f32[72,512]{1,0:T(8,128)S(1)} %get-tuple-element.112), channel_id=1, source_target_pairs={{0,32},{32,0},{64,96},{96,64},{128,160},{160,128},{192,224},{224,1... | collective-permute-start | bytes 442376 | tf_op jit(solution)/shard_map/ppermute | solution.py:65
  99.4 5.3 %collective-permute-start.23 = (f32[72,512]{1,0:T(8,128)S(1)}, f32[72,512]{1,0:T(8,128)S(1)}, u32[]{:S(2)}, u32[]{:S(2)}) collective-permute-start(f32[72,512]{1,0:T(8,128)S(1)} %get-tuple-element.118), channel_id=1, source_target_pairs={{0,64},{32,96},{64,128},{96,160},{128,192},{160,224},{192,0},{224,... | collective-permute-start | bytes 442376 | tf_op jit(solution)/shard_map/ppermute | solution.py:70
  100.8 7.9 %collective-permute-start.24 = (f32[72,512]{1,0:T(8,128)S(1)}, f32[72,512]{1,0:T(8,128)S(1)}, u32[]{:S(2)}, u32[]{:S(2)}) collective-permute-start(f32[72,512]{1,0:T(8,128)S(1)} %get-tuple-element.119), channel_id=1, source_target_pairs={{0,128},{32,160},{64,192},{96,224},{128,0},{160,32},{192,64},{224,... | collective-permute-start | bytes 442376 | tf_op jit(solution)/shard_map/ppermute | solution.py:70
  103.4 5.5 %collective-permute-start.26 = (f32[72,512]{1,0:T(8,128)S(1)}, f32[72,512]{1,0:T(8,128)S(1)}, u32[]{:S(2)}, u32[]{:S(2)}) collective-permute-start(f32[72,512]{1,0:T(8,128)S(1)} %get-tuple-element.120), channel_id=1, source_target_pairs={{0,192},{32,224},{64,0},{96,32},{128,64},{160,96},{192,128},{224,1... | collective-permute-start | bytes 442376 | tf_op jit(solution)/shard_map/ppermute | solution.py:70
  109.0 9.7 %collective-permute-start.29 = (f32[72,512]{1,0:T(8,128)S(1)}, f32[72,512]{1,0:T(8,128)S(1)}, u32[]{:S(2)}, u32[]{:S(2)}) collective-permute-start(f32[72,512]{1,0:T(8,128)S(1)} %fusion.18.piece), channel_id=1, source_target_pairs={{0,1},{1,2},{2,3},{3,4},{4,5},{5,6},{6,7},{7,8},{8,9},{9,10},{10,1... | collective-permute-start | bytes 442376 | tf_op jit(solution)/shard_map/ppermute | solution.py:51
  110.0 8.7 %collective-permute-start.30 = (f32[72,512]{1,0:T(8,128)S(1)}, f32[72,512]{1,0:T(8,128)S(1)}, u32[]{:S(2)}, u32[]{:S(2)}) collective-permute-start(f32[72,512]{1,0:T(8,128)S(1)} %fusion.18.piece), channel_id=1, source_target_pairs={{0,31},{1,0},{2,1},{3,2},{4,3},{5,4},{6,5},{7,6},{8,7},{9,8},{10,9... | collective-permute-start | bytes 442376 | tf_op jit(solution)/shard_map/ppermute | solution.py:51
  113.9 19.8 %collective-permute-start.27 = (f32[256,512]{1,0:T(8,128)S(1)}, f32[256,512]{1,0:T(8,128)S(1)}, u32[]{:S(2)}, u32[]{:S(2)}) collective-permute-start(f32[256,512]{1,0:T(8,128)S(1)} %get-tuple-element.113.plane_1), channel_id=1, source_target_pairs={{0,1},{1,2},{2,3},{3,4},{4,5},{5,6},{6,7},{7,8},{8,9},{9,10},{10,1... | collective-permute-start | bytes 1572872 | tf_op jit(solution)/shard_map/ppermute | solution.py:51
  113.9 19.8 %collective-permute-start.28 = (f32[256,512]{1,0:T(8,128)S(1)}, f32[256,512]{1,0:T(8,128)S(1)}, u32[]{:S(2)}, u32[]{:S(2)}) collective-permute-start(f32[256,512]{1,0:T(8,128)S(1)} %get-tuple-element.114.plane_0), channel_id=1, source_target_pairs={{0,31},{1,0},{2,1},{3,2},{4,3},{5,4},{6,5},{7,6},{8,7},{9,8},{10,9... | collective-permute-start | bytes 1572872 | tf_op jit(solution)/shard_map/ppermute | solution.py:51
  119.9 5.6 %collective-permute-start.31 = (f32[64,512]{1,0:T(8,128)S(1)}, f32[64,512]{1,0:T(8,128)S(1)}, u32[]{:S(2)}, u32[]{:S(2)}) collective-permute-start(f32[64,512]{1,0:T(8,128)S(1)} %shard_map.84.refs_0_), channel_id=1, source_target_pairs={{0,64},{32,96},{64,128},{96,160},{128,192},{160,224},{192,0},{224,... | collective-permute-start | bytes 393224 | tf_op jit(solution)/shard_map/ppermute | solution.py:70
  121.5 8.4 %collective-permute-start.32 = (f32[64,512]{1,0:T(8,128)S(1)}, f32[64,512]{1,0:T(8,128)S(1)}, u32[]{:S(2)}, u32[]{:S(2)}) collective-permute-start(f32[64,512]{1,0:T(8,128)S(1)} %shard_map.84.refs_0_), channel_id=1, source_target_pairs={{0,128},{32,160},{64,192},{96,224},{128,0},{160,32},{192,64},{224,... | collective-permute-start | bytes 393224 | tf_op jit(solution)/shard_map/ppermute | solution.py:70
  124.0 7.8 %collective-permute-start.33 = (f32[64,512]{1,0:T(8,128)S(1)}, f32[64,512]{1,0:T(8,128)S(1)}, u32[]{:S(2)}, u32[]{:S(2)}) collective-permute-start(f32[64,512]{1,0:T(8,128)S(1)} %shard_map.84.refs_0_), channel_id=1, source_target_pairs={{0,192},{32,224},{64,0},{96,32},{128,64},{160,96},{192,128},{224,1... | collective-permute-start | bytes 393224 | tf_op jit(solution)/shard_map/ppermute | solution.py:70
  125.4 6.9 %collective-permute-start.34 = (f32[64,512]{1,0:T(8,128)S(1)}, f32[64,512]{1,0:T(8,128)S(1)}, u32[]{:S(2)}, u32[]{:S(2)}) collective-permute-start(f32[64,512]{1,0:T(8,128)S(1)} %shard_map.84.refs_0_), channel_id=1, source_target_pairs={{0,32},{32,0},{64,96},{96,64},{128,160},{160,128},{192,224},{224,1... | collective-permute-start | bytes 393224 | tf_op jit(solution)/shard_map/ppermute | solution.py:65
  129.8 2.9 %collective-permute-start.35 = (f32[64,512]{1,0:T(8,128)S(1)}, f32[64,512]{1,0:T(8,128)S(1)}, u32[]{:S(2)}, u32[]{:S(2)}) collective-permute-start(f32[64,512]{1,0:T(8,128)S(1)} %collective-permute-done.31.refs_1_), channel_id=1, source_target_pairs={{0,32},{32,0},{64,96},{96,64},{128,160},{160,128},{192,224},{224,1... | collective-permute-start | bytes 393224 | tf_op jit(solution)/shard_map/ppermute | solution.py:65
  131.7 1.6 %collective-permute-start.36 = (f32[64,512]{1,0:T(8,128)S(1)}, f32[64,512]{1,0:T(8,128)S(1)}, u32[]{:S(2)}, u32[]{:S(2)}) collective-permute-start(f32[64,512]{1,0:T(8,128)S(1)} %collective-permute-done.32.refs_2_), channel_id=1, source_target_pairs={{0,32},{32,0},{64,96},{96,64},{128,160},{160,128},{192,224},{224,1... | collective-permute-start | bytes 393224 | tf_op jit(solution)/shard_map/ppermute | solution.py:65
  132.4 1.3 collective-permute-start.37
  (7 other events, 7.9 us)
